TPU v7x, 32 devices: a whole 2x2x4 slice. The times are simulated.
32 devices in a mesh: wide: 16 (over z, y, x), narrow: 2 (over core).
Axes of the slice: x: 2, y: 2, z: 4, core: 2. Of those that a mesh axis runs over, the one named last changes fastest.
Arguments:
- tokens: bfloat16 [16384, 640], P(('wide', 'narrow')), may hold values from -6 to 6
- lengths: int32 [32], P(('wide', 'narrow')), may hold values from 0 to 512, as said below
- w_qkv: bfloat16 [2, 1228800], P(None, ('wide', 'narrow')), may hold values from -0.25 to 0.25
- w_out: bfloat16 [2, 409600], P(None, ('wide', 'narrow')), may hold values from -0.625 to 0.625
- w_up: bfloat16 [2, 1638400], P(None, ('wide', 'narrow')), may hold values from -0.25 to 0.25
- w_down: bfloat16 [2, 1638400], P(None, ('wide', 'narrow')), may hold values from -0.125 to 0.125
- gains: bfloat16 [2560], P(('wide', 'narrow')), may hold values from 0.5 to 1.5
- biases: bfloat16 [14080], P(('wide', 'narrow')), may hold values from -1.25 to 1.25
- cotangent: bfloat16 [16384, 640], P(('wide', 'narrow')), may hold values from -6 to 6
Outputs:
- output: bfloat16 [16384, 640], P(('wide', 'narrow'))
- grad_tokens: bfloat16 [16384, 640], P(('wide', 'narrow'))
- grad_w_qkv: float32 [2, 1228800], P(None, ('wide', 'narrow'))
- grad_w_out: float32 [2, 409600], P(None, ('wide', 'narrow'))
- grad_w_up: float32 [2, 1638400], P(None, ('wide', 'narrow'))
- grad_w_down: float32 [2, 1638400], P(None, ('wide', 'narrow'))
- grad_gains: float32 [2560], P(('wide', 'narrow'))
- grad_biases: float32 [14080], P(('wide', 'narrow'))
Inputs may be any that keep to these rules, and one draw needn't show every extreme that they name: `lengths`: 1 slots, drawn from the seed, hold no crop (length 0); every other slot holds a crop of 128 to 512 residues, and at least one crop has exactly 512.
All inputs are finite; a program needn't handle non-finite values.
Results may differ from a plain program's by a relative error of at most 0.014.
Values may be sent and summed in bfloat16 or wider, within the bound.
No kernel may reach another device: no remote copies, remote signals or barrier semaphores. Data moves between devices by JAX's collectives and lax.ppermute only.
A program may use at most 256 MiB of HBM per device.

v0:
```python
import jax
import jax.numpy as jnp
from jax import lax
from jax.sharding import PartitionSpec as P

D = 640
HEADS = 20
HEAD_DIM = 32
FF = 2560
LAYERS = 2


EPSILON = 1e-05
MASKED = -1000000000.0
GROUP_HEADS = 4


def rotary_tables(length, head_dim):
    half_dim = head_dim // 2
    steps_up = jnp.arange(half_dim, dtype=jnp.float32) * (2.0 / head_dim)
    inverse = 1.0 / 10000.0**steps_up
    angles = jnp.arange(length, dtype=jnp.float32)[:, None] * inverse[None, :]
    cosine_table = jnp.concatenate([jnp.cos(angles), jnp.cos(angles)], 1)
    sine_table = jnp.concatenate([jnp.sin(angles), jnp.sin(angles)], 1)
    return (cosine_table, sine_table)


def rotate(tensor, cosine_table, sine_table):
    half_dim = tensor.shape[-1] // 2
    turned = jnp.concatenate([-tensor[..., half_dim:], tensor[..., :half_dim]], -1)
    return tensor * cosine_table[:, None, :] + turned * sine_table[:, None, :]


def rotate_back(grad_in, cosine_table, sine_table):
    half_dim = grad_in.shape[-1] // 2
    sined = grad_in * sine_table[:, None, :]
    return grad_in * cosine_table[:, None, :] + jnp.concatenate(
        [sined[..., half_dim:], -sined[..., :half_dim]], -1
    )


def rounded(value):
    return lax.optimization_barrier(value.astype(jnp.bfloat16)).astype(jnp.float32)


def gelu_value(hidden_pre):
    return 0.5 * hidden_pre * (1.0 + lax.erf(hidden_pre * 0.7071067811865476))


def gelu_slope(hidden_pre):
    return (
        0.5 * (1.0 + lax.erf(hidden_pre * 0.7071067811865476))
        + hidden_pre * jnp.exp(-0.5 * hidden_pre * hidden_pre) * 0.3989422804014327
    )


def norm_parts(stream, gain, shift):
    average = jnp.mean(stream, -1, keepdims=True)
    centered = stream - average
    variance = jnp.mean(centered * centered, -1, keepdims=True)
    inverse = lax.rsqrt(variance + EPSILON)
    unit = centered * inverse
    return (unit * gain + shift, unit, inverse)


def norm_back(grad_normed, unit, inverse, gain):
    grad_gain = jnp.sum(grad_normed * unit, axis=(0, 1))
    grad_shift = jnp.sum(grad_normed, axis=(0, 1))
    grad_unit = grad_normed * gain
    centered_grad = (
        grad_unit
        - jnp.mean(grad_unit, -1, keepdims=True)
        - unit * jnp.mean(grad_unit * unit, -1, keepdims=True)
    )
    return (grad_gain, grad_shift, inverse * centered_grad)


def outer_sum(left, right):
    return lax.dot_general(
        left, right, (((0,), (0,)), ((), ())), preferred_element_type=jnp.float32
    )


def back_dot(grad_rows, weight):
    return lax.dot_general(
        grad_rows, weight, (((1,), (1,)), ((), ())), preferred_element_type=jnp.float32
    )


def owner_rows(left, right, count, devices):
    width = right.shape[1]
    total = left.shape[1]
    piece_len = total * width // devices
    partial_term = outer_sum(left, right).reshape(-1)
    return partial_term.reshape(count, piece_len)


def term_builder(pairs, vectors, devices, count):
    members = [owner_rows(left, right, count, devices) for left, right in pairs]
    members = members + [vector.reshape(devices, -1) for vector in vectors]
    return jnp.concatenate(members, 1)


def split_columns(summed, pairs, vectors, devices):
    widths = [left.shape[1] * right.shape[1] // devices for left, right in pairs]
    widths = widths + [vector.shape[0] // devices for vector in vectors]
    pieces = []
    begin = 0
    for width in widths:
        pieces.append(summed[:, begin : begin + width])
        begin = begin + width
    return pieces


def grouped(tensor, group_count):
    array_shape = tensor.shape
    return jnp.moveaxis(
        tensor.reshape(array_shape[0], array_shape[1], group_count, GROUP_HEADS, array_shape[3]),
        2,
        0,
    )


def ungrouped(tensor):
    group_count, crop_count, length, heads_in, head_width = tensor.shape
    return jnp.moveaxis(tensor, 0, 2).reshape(
        crop_count, length, group_count * heads_in, head_width
    )


def scores_of(rotated_queries, rotated_keys, live):
    attention_scores = jnp.einsum(
        "clhd,cmhd->chlm", rotated_queries, rotated_keys, preferred_element_type=jnp.float32
    )
    return jnp.where(live[:, None, None, :], attention_scores, MASKED)


def attend(live):

    def run_group(pieces):
        rotated_queries, rotated_keys, value_rows = pieces
        attention_scores = scores_of(rotated_queries, rotated_keys, live)
        maximum = jnp.max(attention_scores, -1, keepdims=True)
        exponents = jnp.exp(attention_scores - maximum)
        totals = jnp.sum(exponents, -1, keepdims=True)
        attention_probs = (exponents / totals).astype(jnp.bfloat16)
        attention_mixture = jnp.einsum(
            "chlm,cmhd->clhd", attention_probs, value_rows, preferred_element_type=jnp.float32
        )
        return (attention_mixture, (maximum + jnp.log(totals))[..., 0])

    return run_group


def attend_back(live):

    def run_group(pieces):
        rotated_queries, rotated_keys, value_rows, log_totals, grad_mixed = pieces
        attention_scores = scores_of(rotated_queries, rotated_keys, live)
        probs_full = jnp.exp(attention_scores - log_totals[..., None])
        attention_probs = probs_full.astype(jnp.bfloat16)
        grad_probs = rounded(
            jnp.einsum(
                "clhd,cmhd->chlm", grad_mixed, value_rows, preferred_element_type=jnp.float32
            )
        )
        row_dot = jnp.sum(probs_full * grad_probs, -1, keepdims=True)
        grad_scores = (probs_full * (grad_probs - row_dot)).astype(jnp.bfloat16)
        grad_values = jnp.einsum(
            "chlm,clhd->cmhd", attention_probs, grad_mixed, preferred_element_type=jnp.float32
        )
        grad_queries = jnp.einsum(
            "chlm,cmhd->clhd", grad_scores, rotated_keys, preferred_element_type=jnp.float32
        ).astype(jnp.bfloat16)
        grad_keys = jnp.einsum(
            "chlm,clhd->cmhd", grad_scores, rotated_queries, preferred_element_type=jnp.float32
        ).astype(jnp.bfloat16)
        return (grad_queries, grad_keys, grad_values)

    return run_group


def weights_of(gathered, layer_index):
    qkv_one, out_one, up_one, down_one, gain_all, bias_all = gathered
    gain_rows = gain_all.astype(jnp.float32).reshape(LAYERS, 2, D)[layer_index]
    bias_row = bias_all.astype(jnp.float32).reshape(LAYERS, 7 * D + FF)[layer_index]
    return (
        qkv_one[0].reshape(D, 3 * D),
        out_one[0].reshape(D, D),
        up_one[0].reshape(D, FF),
        down_one[0].reshape(FF, D),
        gain_rows[0],
        gain_rows[1],
        bias_row[:D],
        bias_row[D : 4 * D],
        bias_row[4 * D : 5 * D],
        bias_row[5 * D : 6 * D],
        bias_row[6 * D : 6 * D + FF],
        bias_row[6 * D + FF :],
    )


def attention_inputs(stream, params, cosine_table, sine_table):
    w_qkv_full, gain_attn, shift_attn, bias_qkv = (params[0], params[4], params[6], params[7])
    crop_count, length, _ = stream.shape
    normed, unit_attn, scale_attn = norm_parts(stream, gain_attn, shift_attn)
    normed_attn = normed.astype(jnp.bfloat16).reshape(crop_count * length, D)
    projected = jnp.dot(normed_attn, w_qkv_full, preferred_element_type=jnp.float32) + bias_qkv
    queries = projected[:, :D].reshape(crop_count, length, HEADS, HEAD_DIM) * HEAD_DIM ** (-0.5)
    keys_plain = projected[:, D : 2 * D].reshape(crop_count, length, HEADS, HEAD_DIM)
    value_rows = (
        projected[:, 2 * D :].reshape(crop_count, length, HEADS, HEAD_DIM).astype(jnp.bfloat16)
    )
    rotated_queries = rotate(queries, cosine_table, sine_table).astype(jnp.bfloat16)
    rotated_keys = rotate(keys_plain, cosine_table, sine_table).astype(jnp.bfloat16)
    return (unit_attn, scale_attn, normed_attn, rotated_queries, rotated_keys, value_rows)


def after_attention(stream, attention_mixture, params):
    w_out_full, w_up_full, w_down_full = (params[1], params[2], params[3])
    gain_ffn, bias_out, shift_ffn, bias_up, bias_down = (
        params[5],
        params[8],
        params[9],
        params[10],
        params[11],
    )
    middle = stream + (
        jnp.dot(attention_mixture, w_out_full, preferred_element_type=jnp.float32) + bias_out
    ).reshape(stream.shape)
    normed, unit_ffn, scale_ffn = norm_parts(middle, gain_ffn, shift_ffn)
    normed_ffn = normed.astype(jnp.bfloat16).reshape(attention_mixture.shape[0], D)
    hidden_pre = jnp.dot(normed_ffn, w_up_full, preferred_element_type=jnp.float32) + bias_up
    hidden_act = gelu_value(hidden_pre).astype(jnp.bfloat16)
    result_stream = middle + (
        jnp.dot(hidden_act, w_down_full, preferred_element_type=jnp.float32) + bias_down
    ).reshape(stream.shape)
    return (result_stream, unit_ffn, scale_ffn, normed_ffn, hidden_pre, hidden_act)


def layer_backward(
    stream,
    attention_mixture,
    log_totals,
    live,
    params,
    cosine_table,
    sine_table,
    grad_stream,
    ffn_hook,
):
    w_qkv_full, w_out_full, w_up_full, w_down_full = (params[0], params[1], params[2], params[3])
    gain_attn, gain_ffn = (params[4], params[5])
    crop_count, length, _ = stream.shape
    row_count = crop_count * length
    group_count = HEADS // GROUP_HEADS
    unit_attn, scale_attn, normed_attn, rotated_queries, rotated_keys, value_rows = (
        attention_inputs(stream, params, cosine_table, sine_table)
    )
    _, unit_ffn, scale_ffn, normed_ffn, hidden_pre, hidden_act = after_attention(
        stream, attention_mixture, params
    )
    grad_branch = grad_stream.astype(jnp.bfloat16).reshape(row_count, D)
    grad_bias_down = jnp.sum(grad_branch, 0, dtype=jnp.float32)
    grad_act = rounded(back_dot(grad_branch, w_down_full))
    grad_pre = (grad_act * gelu_slope(hidden_pre)).astype(jnp.bfloat16)
    grad_bias_up = jnp.sum(grad_pre, 0, dtype=jnp.float32)
    ffn_result = ffn_hook(((normed_ffn, grad_pre), (hidden_act, grad_branch)))
    grad_normed_ffn = back_dot(grad_pre, w_up_full).reshape(stream.shape)
    grad_gain_ffn, grad_shift_ffn, grad_middle_norm = norm_back(
        grad_normed_ffn, unit_ffn, scale_ffn, gain_ffn
    )
    grad_middle = grad_stream + grad_middle_norm
    grad_attn_branch = grad_middle.astype(jnp.bfloat16).reshape(row_count, D)
    grad_bias_out = jnp.sum(grad_attn_branch, 0, dtype=jnp.float32)
    grad_mixed = (
        back_dot(grad_attn_branch, w_out_full)
        .astype(jnp.bfloat16)
        .reshape(crop_count, length, HEADS, HEAD_DIM)
    )
    grad_q_groups, grad_k_groups, grad_v_groups = lax.map(
        attend_back(live),
        (
            grouped(rotated_queries, group_count),
            grouped(rotated_keys, group_count),
            grouped(value_rows, group_count),
            log_totals,
            grouped(grad_mixed, group_count),
        ),
    )
    grad_queries = rotate_back(
        ungrouped(grad_q_groups).astype(jnp.float32), cosine_table, sine_table
    ) * HEAD_DIM ** (-0.5)
    grad_keys = rotate_back(ungrouped(grad_k_groups).astype(jnp.float32), cosine_table, sine_table)
    grad_values = ungrouped(grad_v_groups)
    grad_projected = jnp.concatenate(
        [
            grad_queries.reshape(row_count, D),
            grad_keys.reshape(row_count, D),
            grad_values.reshape(row_count, D),
        ],
        1,
    ).astype(jnp.bfloat16)
    grad_bias_qkv = jnp.sum(grad_projected, 0, dtype=jnp.float32)
    grad_normed_attn = back_dot(grad_projected, w_qkv_full).reshape(stream.shape)
    grad_gain_attn, grad_shift_attn, grad_input_norm = norm_back(
        grad_normed_attn, unit_attn, scale_attn, gain_attn
    )
    grad_input = grad_middle + grad_input_norm
    attn_pairs = ((normed_attn, grad_projected), (attention_mixture, grad_attn_branch))
    gain_grad = jnp.concatenate([grad_gain_attn, grad_gain_ffn])
    bias_grad = jnp.concatenate(
        [
            grad_shift_attn,
            grad_bias_qkv,
            grad_bias_out,
            grad_shift_ffn,
            grad_bias_up,
            grad_bias_down,
        ]
    )
    return (grad_input, attn_pairs, ffn_result, gain_grad, bias_grad)


def fetch_forward(w_qkv, w_out, w_up, w_down, gains, biases, layer_index):
    return (
        lax.all_gather(
            w_qkv[layer_index : layer_index + 1], ("wide", "narrow"), axis=1, tiled=True
        ),
        lax.all_gather(
            w_out[layer_index : layer_index + 1], ("wide", "narrow"), axis=1, tiled=True
        ),
        lax.all_gather(w_up[layer_index : layer_index + 1], ("wide", "narrow"), axis=1, tiled=True),
        lax.all_gather(
            w_down[layer_index : layer_index + 1], ("wide", "narrow"), axis=1, tiled=True
        ),
        lax.all_gather(gains, ("wide", "narrow"), axis=0, tiled=True),
        lax.all_gather(biases, ("wide", "narrow"), axis=0, tiled=True),
    )


def fetch_backward(w_qkv, w_out, w_up, w_down, gains, biases, layer_index):
    return (
        lax.all_gather(
            w_qkv[layer_index : layer_index + 1], ("wide", "narrow"), axis=1, tiled=True
        ),
        lax.all_gather(
            w_out[layer_index : layer_index + 1], ("wide", "narrow"), axis=1, tiled=True
        ),
        lax.all_gather(w_up[layer_index : layer_index + 1], ("wide", "narrow"), axis=1, tiled=True),
        lax.all_gather(
            w_down[layer_index : layer_index + 1], ("wide", "narrow"), axis=1, tiled=True
        ),
        lax.all_gather(gains, ("wide", "narrow"), axis=0, tiled=True),
        lax.all_gather(biases, ("wide", "narrow"), axis=0, tiled=True),
    )


def device_count():
    return lax.axis_size("wide") * lax.axis_size("narrow")


def keep_ffn(pairs):
    return pairs


def body(tokens, lengths, w_qkv, w_out, w_up, w_down, gains, biases, cotangent):
    crop_count = lengths.shape[0]
    length = tokens.shape[0] // crop_count
    devices = device_count()
    live = jnp.arange(length, dtype=jnp.int32)[None, :] < lengths[:, None]
    live_float = live.astype(jnp.float32)
    cosine_table, sine_table = rotary_tables(length, HEAD_DIM)
    group_count = HEADS // GROUP_HEADS
    stream = tokens.astype(jnp.float32).reshape(crop_count, length, D)
    layer_inputs = []
    layer_mixes = []
    layer_totals = []
    layer_weights = []
    for layer_index in range(LAYERS):
        gathered = fetch_forward(w_qkv, w_out, w_up, w_down, gains, biases, layer_index)
        layer_weights.append(gathered)
        params = weights_of(gathered, layer_index)
        _, _, _, rotated_queries, rotated_keys, value_rows = attention_inputs(
            stream, params, cosine_table, sine_table
        )
        mixed_groups, log_totals = lax.map(
            attend(live),
            (
                grouped(rotated_queries, group_count),
                grouped(rotated_keys, group_count),
                grouped(value_rows, group_count),
            ),
        )
        attention_mixture = (
            ungrouped(mixed_groups).reshape(crop_count * length, D).astype(jnp.bfloat16)
        )
        layer_inputs.append(stream)
        layer_mixes.append(attention_mixture)
        layer_totals.append(log_totals)
        stream = after_attention(stream, attention_mixture, params)[0]
    output = (stream * live_float[..., None]).reshape(crop_count * length, D).astype(jnp.bfloat16)
    layer_weights = [None] * LAYERS
    grad_stream = (
        cotangent.astype(jnp.float32).reshape(crop_count, length, D) * live_float[..., None]
    )
    matrix_parts = [None] * LAYERS
    gain_parts = [None] * LAYERS
    bias_parts = [None] * LAYERS
    for layer_index in reversed(range(LAYERS)):
        gathered = fetch_backward(w_qkv, w_out, w_up, w_down, gains, biases, layer_index)
        params = weights_of(gathered, layer_index)
        grad_stream, attn_pairs, ffn_result, gain_grad, bias_grad = layer_backward(
            layer_inputs[layer_index],
            layer_mixes[layer_index],
            layer_totals[layer_index],
            live,
            params,
            cosine_table,
            sine_table,
            grad_stream,
            keep_ffn,
        )
        gain_parts[layer_index] = gain_grad
        bias_parts[layer_index] = bias_grad
        all_pairs = attn_pairs + ffn_result
        if layer_index > 0:
            summed = lax.psum_scatter(
                term_builder(all_pairs, [], devices, 1 * lax.axis_size(("wide", "narrow"))),
                ("wide", "narrow"),
                scatter_dimension=0,
                tiled=True,
            )
            matrix_parts[layer_index] = split_columns(summed, all_pairs, [], devices)
        else:
            vectors = [jnp.concatenate(gain_parts), jnp.concatenate(bias_parts)]
            summed = lax.psum_scatter(
                term_builder(all_pairs, vectors, devices, 1 * lax.axis_size(("wide", "narrow"))),
                ("wide", "narrow"),
                scatter_dimension=0,
                tiled=True,
            )
            lower_sums = split_columns(summed, all_pairs, vectors, devices)
            matrix_parts[0] = lower_sums[:4]
            gain_out = lower_sums[4][0]
            bias_out = lower_sums[5][0]
    qkv_out = jnp.concatenate([member[0] for member in matrix_parts])
    out_out = jnp.concatenate([member[1] for member in matrix_parts])
    up_out = jnp.concatenate([member[2] for member in matrix_parts])
    down_out = jnp.concatenate([member[3] for member in matrix_parts])
    grad_tokens = grad_stream.reshape(crop_count * length, D).astype(jnp.bfloat16)
    return (output, grad_tokens, qkv_out, out_out, up_out, down_out, gain_out, bias_out)


def solution(mesh):
    return jax.shard_map(
        body,
        mesh=mesh,
        in_specs=(
            P(("wide", "narrow"), None),
            P(("wide", "narrow")),
            P(None, ("wide", "narrow")),
            P(None, ("wide", "narrow")),
            P(None, ("wide", "narrow")),
            P(None, ("wide", "narrow")),
            P(("wide", "narrow")),
            P(("wide", "narrow")),
            P(("wide", "narrow"), None),
        ),
        out_specs=(
            P(("wide", "narrow"), None),
            P(("wide", "narrow"), None),
            P(None, ("wide", "narrow")),
            P(None, ("wide", "narrow")),
            P(None, ("wide", "narrow")),
            P(None, ("wide", "narrow")),
            P(("wide", "narrow")),
            P(("wide", "narrow")),
        ),
        check_vma=False,
    )
```

profile of v0, /device:TPU:0, one launch (start us, length us, event | category | flops | bytes accessed | tf_op | source)
XLA Modules:
  0.0 1652.5 jit_solution(11529972729317461616)
XLA Ops:
  15.1 42.6 %all-reduce.5 = (bf16[14080]{0:T(1024)(128)(2,1)S(1)}, bf16[2560]{0:T(1024)(128)(2,1)S(1)}) all-reduce(bf16[14080]{0:T(1024)(128)(2,1)S(1)} %dynamic-update-slice.1, bf16[2560]{0:T(1024)(128)(2,1)S(1)} %dynamic-update-slice), channel_id=1, replica_groups=mesh['wide'=16,'narrow'=2] {'wide','narrow'}, use_global_device_ids=true, to_apply=%add.1 | all-reduce | flops 16640 | bytes 66560
  60.4 46.2 %all_gather.23 = bf16[1,409600]{1,0:T(2,128)(2,1)S(1)} all-gather(bf16[1,12800]{1,0:T(2,128)(2,1)S(1)} %get-tuple-element.503), channel_id=1, replica_groups=mesh['wide'=16,'narrow'=2] {'wide','narrow'}, dimensions={1}, use_global_device_ids=true | all-gather | bytes 844800 | tf_op jit(solution)/shard_map/all_gather | solution.py:330
  106.6 17.0 %reduce.63 = bf16[409600]{0:T(1024)(128)(2,1)S(1)} reduce(bf16[1,409600]{1,0:T(2,128)(2,1)S(1)} %all_gather.23, bf16[]{:T(256)} %constant.137), dimensions={0}, to_apply=%all_gather.23.reduce_sub_computation | reduce | bytes 1638402 | tf_op jit(solution)/shard_map/all_gather | solution.py:330
  125.1 44.1 %all_gather.51 = bf16[1,409600]{1,0:T(2,128)(2,1)S(1)} all-gather(bf16[1,12800]{1,0:T(2,128)(2,1)S(1)} %get-tuple-element.502), channel_id=1, replica_groups=mesh['wide'=16,'narrow'=2] {'wide','narrow'}, dimensions={1}, use_global_device_ids=true | all-gather | bytes 844800 | tf_op jit(solution)/shard_map/all_gather | solution.py:330
  169.2 17.0 %reduce.67 = bf16[409600]{0:T(1024)(128)(2,1)S(1)} reduce(bf16[1,409600]{1,0:T(2,128)(2,1)S(1)} %all_gather.51, bf16[]{:T(256)} %constant.137), dimensions={0}, to_apply=%all_gather.51.reduce_sub_computation | reduce | bytes 1638402 | tf_op jit(solution)/shard_map/all_gather | solution.py:330
  190.0 52.0 %reduce.62 = bf16[1228800]{0:T(1024)(128)(2,1)S(1)} reduce(bf16[1,1228800]{1,0:T(2,128)(2,1)} %all-gather.7.cloned.1.call-done, bf16[]{:T(256)} %constant.137), dimensions={0}, to_apply=%all_gather.22.reduce_sub_computation | reduce | bytes 4915202 | tf_op jit(solution)/shard_map/all_gather | solution.py:327
  268.8 29.4 %while.56 = (s32[]{:T(128)}, bf16[5,1,512,4,32]{2,4,3,1,0:T(8,128)(2,1)}, f32[5,1,4,512]{3,2,1,0:T(4,128)S(1)}, bf16[5,1,512,4,32]{2,4,3,1,0:T(8,128)(2,1)}, bf1...) while((s32[]{:T(128)}, ...), condition=%wide.region_5.6_spmd.clone, body=%wide.region_2.5_spmd.clone.sunk | while | flops 143653376 | bytes 13308005 | solution.py:387
  301.9 52.2 %reduce.66 = bf16[1228800]{0:T(1024)(128)(2,1)S(1)} reduce(bf16[1,1228800]{1,0:T(2,128)(2,1)} %all-gather.13.cloned.1.call-done, bf16[]{:T(256)} %constant.137), dimensions={0}, to_apply=%all_gather.50.reduce_sub_computation | reduce | bytes 4915202 | tf_op jit(solution)/shard_map/all_gather | solution.py:327
  357.8 69.2 %reduce.64 = bf16[1638400]{0:T(1024)(128)(2,1)S(1)} reduce(bf16[1,1638400]{1,0:T(2,128)(2,1)} %all-gather.9.cloned.1.call-done, bf16[]{:T(256)} %constant.137), dimensions={0}, to_apply=%all_gather.48.reduce_sub_computation | reduce | bytes 6553602 | tf_op jit(solution)/shard_map/all_gather | solution.py:333
  431.9 69.2 %reduce.65 = bf16[1638400]{0:T(1024)(128)(2,1)S(1)} reduce(bf16[1,1638400]{1,0:T(2,128)(2,1)} %all-gather.11.cloned.1.call-done, bf16[]{:T(256)} %constant.137), dimensions={0}, to_apply=%all_gather.49.reduce_sub_computation | reduce | bytes 6553602 | tf_op jit(solution)/shard_map/all_gather | solution.py:334
  505.1 6.9 multiply_convert_fusion.1
  530.9 70.9 %reduce.69 = bf16[1638400]{0:T(1024)(128)(2,1)} reduce(bf16[1,1638400]{1,0:T(2,128)(2,1)} %all-gather.17.cloned.1.call-done, bf16[]{:T(256)} %constant.137), dimensions={0}, to_apply=%all_gather.53.reduce_sub_computation | reduce | bytes 6553602 | tf_op jit(solution)/shard_map/all_gather | solution.py:334
  601.8 6.7 reshape_squeeze.39
  616.0 26.1 %while.57 = (s32[]{:T(128)}, bf16[5,1,512,4,32]{2,4,3,1,0:T(8,128)(2,1)S(1)}, f32[5,1,4,512]{3,2,1,0:T(4,128)S(1)}, bf16[5,1,512,4,32]{2,4,3,1,0:T(8,128)(2,1)},...) while((s32[]{:T(128)}, ...), condition=%wide.region_13.14_spmd.clone, body=%wide.region_10.13_spmd.clone.sunk | while | flops 143653376 | bytes 13308005 | solution.py:387
  643.0 70.9 %reduce.68 = bf16[1638400]{0:T(1024)(128)(2,1)} reduce(bf16[1,1638400]{1,0:T(2,128)(2,1)} %all-gather.15.cloned.1.call-done, bf16[]{:T(256)} %constant.137), dimensions={0}, to_apply=%all_gather.52.reduce_sub_computation | reduce | bytes 6553602 | tf_op jit(solution)/shard_map/all_gather | solution.py:333
  713.9 7.3 reshape_squeeze.38
  723.4 7.5 convert_reduce_fusion
  747.5 63.5 %while.58 = (s32[]{:T(128)}, bf16[5,1,512,4,32]{2,4,3,1,0:T(8,128)(2,1)}, bf16[5,1,512,4,32]{2,4,3,1,0:T(8,128)(2,1)}, bf16[5,1,512,4,32]{2,4,3,1,0:T(8,128)(2,1...) while((s32[]{:T(128)}, ...), condition=%wide.region_20.21_spmd.clone, body=%wide.region_18.20_spmd.clone.sunk | while | flops 351402496 | bytes 26672252 | solution.py:281
  856.5 68.2 %while.59 = (s32[]{:T(128)}, bf16[5,1,512,4,32]{2,4,3,1,0:T(8,128)(2,1)}, bf16[5,1,512,4,32]{2,4,3,1,0:T(8,128)(2,1)}, bf16[5,1,512,4,32]{2,4,3,1,0:T(8,128)(2,1...) while((s32[]{:T(128)}, ...), condition=%wide.region_27.28_spmd.clone, body=%wide.region_25.27_spmd.clone.sunk | while | flops 351402496 | bytes 26672252 | solution.py:281
  981.7 7.9 reshape_reshape.50
  1009.0 8.0 reshape_reshape.46
  1025.3 6.7 constant_dynamic-update-slice_fusion.2
  1038.3 14.6 pad_maximum_fusion
  1062.3 565.4 %all-reduce.8.cloned.1.call-done = (f32[32,153600]{1,0:T(8,128)}, f32[32,154120]{1,0:T(8,128)}) async-done(((f32[32,153600]{1,0:T(8,128)}, f32[32,154120]{1,0:T(8,128)}), (f32[32,153600]{1,0:T(8,128)}, f32[32,154120]{1,0:T(8,128)})) %all-reduce.8.cloned.1.call-update) | async-done | bytes 39388176
  (492 shorter events, 452.9 us)
Async XLA Ops:
  7.2 7.4 copy-start.78
  7.2 7.7 copy-start.79
  7.2 182.8 %all-gather.7.cloned.1.call-start = ((), (), s32[]{:S(2)}) async-start(), calls=%async_computation | async-start | bytes 5068800 | tf_op jit(solution)/shard_map/all_gather | solution.py:327
  9.3 50.3 %copy-start.24 = (bf16[512,640]{1,0:T(8,128)(2,1)S(1)}, bf16[512,640]{1,0:T(8,128)(2,1)}, u32[]{:S(2)}) copy-start(bf16[512,640]{1,0:T(8,128)(2,1)} %param.17) | copy-start | bytes 1966084
  9.3 292.6 %all-gather.13.cloned.1.call-start = ((), (), s32[]{:S(2)}) async-start(), calls=%async_computation.3 | async-start | bytes 5068800 | tf_op jit(solution)/shard_map/all_gather | solution.py:327
  10.0 347.8 %all-gather.9.cloned.1.call-start = ((), (), s32[]{:S(2)}) async-start(), calls=%async_computation.1 | async-start | bytes 6758400 | tf_op jit(solution)/shard_map/all_gather | solution.py:333
  12.2 48.1 %copy-start.56 = (bf16[2,12800]{1,0:T(2,128)(2,1)S(1)}, bf16[2,12800]{1,0:T(2,128)(2,1)}, u32[]{:S(2)}) copy-start(bf16[2,12800]{1,0:T(2,128)(2,1)} %param.20) | copy-start | bytes 153604
  12.2 419.7 %all-gather.11.cloned.1.call-start = ((), (), s32[]{:S(2)}) async-start(), calls=%async_computation.2 | async-start | bytes 6758400 | tf_op jit(solution)/shard_map/all_gather | solution.py:334
  13.4 517.5 %all-gather.17.cloned.1.call-start = ((), (), s32[]{:S(2)}) async-start(), calls=%async_computation.5 | async-start | bytes 6758400 | tf_op jit(solution)/shard_map/all_gather | solution.py:334
  13.9 628.3 %all-gather.15.cloned.1.call-start = ((), (), s32[]{:S(2)}) async-start(), calls=%async_computation.4 | async-start | bytes 6758400 | tf_op jit(solution)/shard_map/all_gather | solution.py:333
  14.5 1613.2 %all-reduce.8.cloned.1.call-start = ((), (), s32[]{:S(2)}) async-start(), calls=%async_computation.6 | async-start | bytes 78807040
  58.4 187.8 %copy-start.74 = (f32[640]{0:T(1024)}, f32[640]{0:T(1024)S(1)}, u32[]{:S(2)}) copy-start(f32[640]{0:T(1024)S(1)} %get-tuple-element.513) | copy-start | bytes 7684
  58.4 446.8 %copy-start.59 = (f32[640]{0:T(1024)}, f32[640]{0:T(1024)S(1)}, u32[]{:S(2)}) copy-start(f32[640]{0:T(1024)S(1)} %get-tuple-element.511) | copy-start | bytes 7684
  59.6 186.6 %copy-start.66 = (f32[640]{0:T(1024)}, f32[640]{0:T(1024)S(1)}, u32[]{:S(2)}) copy-start(f32[640]{0:T(1024)S(1)} %get-tuple-element.521) | copy-start | bytes 7684
  59.8 186.4 %copy-start.62 = (f32[512]{0:T(512)}, f32[512]{0:T(512)S(1)}, u32[]{:S(2)}) copy-start(f32[512]{0:T(512)S(1)} %broadcast_multiply_fusion.18) | copy-start | bytes 6148
  60.1 186.1 %copy-start.70 = (f32[512]{0:T(512)}, f32[512]{0:T(512)S(1)}, u32[]{:S(2)}) copy-start(f32[512]{0:T(512)S(1)} %add_rsqrt_fusion.3) | copy-start | bytes 6148
  268.8 29.5 %copy-start.38 = (bf16[640,640]{1,0:T(8,128)(2,1)S(1)}, bf16[640,640]{1,0:T(8,128)(2,1)}, u32[]{:S(2)}) copy-start(bf16[640,640]{1,0:T(8,128)(2,1)} %reshape_squeeze.33) | copy-start | bytes 2457604
  642.2 79.1 %copy-start.18 = (bf16[5,1,512,4,32]{2,4,3,1,0:T(8,128)(2,1)}, bf16[5,1,512,4,32]{2,4,3,1,0:T(8,128)(2,1)S(1)}, u32[]{:S(2)}) copy-start(bf16[5,1,512,4,32]{2,4,3,1,0:T(8,128)(2,1)S(1)} %get-tuple-element.193) | copy-start | bytes 1966084
  713.9 7.4 copy-start.13
  722.2 16.4 copy-start
  841.2 7.7 copy-start.2
  981.7 7.9 copy-start.14
  1017.0 7.0 copy-start.16
  1024.0 8.0 slice-start
  (67 other events, 239.4 us)
Sparse Core Ops, SparseCore 0:
  11.5 71.2 all-gather.6
  85.7 72.3 all-gather.12
  161.6 68.2 all-gather.8
  232.6 69.0 all-gather.10
  305.0 69.2 all-gather.16
  377.5 69.1 all-gather.14
  1053.0 574.6 all-reduce.7
where the time goes:
time: 1660 us; the launch traced here: 1650 us
  waiting for transfers between devices  567 us (34%)
  other arithmetic  517 us (31%)
  matrix products  229 us (14%)
  local copies, waits for them, and re-layouts  188 us (11%)
  blocking collectives  133 us (8%)
    unnamed x8, waiting for transfers between devices  567 us
    all_gather x2, other arithmetic, fetch_forward(): lax.all_gather(w_up[layer_index:layer_index + 1], ('wide', 'narrow'), axi...  140 us
    all_gather x2, other arithmetic, fetch_forward(): lax.all_gather(w_down[layer_index:layer_index + 1], ('wide', 'narrow'), a...  140 us
    all_gather x2, other arithmetic, fetch_forward(): lax.all_gather(w_qkv[layer_index:layer_index + 1], ('wide', 'narrow'), ax...  104 us
    all_gather x2, blocking collectives, fetch_forward(): lax.all_gather(w_out[layer_index:layer_index + 1], ('wide', 'narrow'), ax...  90.3 us
    another operation x8, local copies, waits for them, and re-layouts, owner_rows(): return partial_term.reshape(count, piece_len)  42.9 us
    unnamed x1, blocking collectives  42.6 us
    dot_general x20, matrix products, scores_of(): jnp.einsum('clhd,cmhd->chlm', rotated_queries, rotated_keys, preferred_el...  42.1 us
  transfers between devices with their start and end apart: 7, of which 1 were waited for; matrix products, arithmetic and copies ran while one was open for 30% of the time, Pallas kernels for 0%

commit v1 on v0

v1 whole, which is shorter than its diff:
```python
import functools

import jax
import jax.numpy as jnp
import numpy as np
from jax import lax
from jax.experimental import pallas as pl
from jax.experimental.pallas import tpu as pltpu
from jax.sharding import PartitionSpec as P

D = 640
HEADS = 20
HEAD_DIM = 32
FF = 2560
LAYERS = 2
EPSILON = 1e-05
MASKED = -1e9
LANES = 128
GROUPS = D // LANES
PER_GROUP = LANES // HEAD_DIM
BLOCKS = FF // D
PIECE = 80
VECS = 16
ROWS = 256
AXES = ("wide", "narrow")
VMEM_LIMIT = 56 * 1024 * 1024
f32, bf16 = jnp.float32, jnp.bfloat16

GAIN_A, GAIN_F, SHIFT_A, BIAS_QKV, BIAS_OUT, SHIFT_F, BIAS_UP, BIAS_DOWN = 0, 1, 2, 3, 6, 7, 8, 12


def rotary_tables(length):
    half = HEAD_DIM // 2
    inverse = 1.0 / 10000.0 ** (np.arange(half) * (2.0 / HEAD_DIM))
    angles = np.arange(length)[:, None] * inverse[None, :]
    cos = np.tile(np.cos(angles), (1, 2 * PER_GROUP))
    sine = np.sin(angles)
    none = np.zeros_like(sine)
    ahead = np.tile(np.concatenate([-sine, none], 1), (1, PER_GROUP))
    behind = np.tile(np.concatenate([none, sine], 1), (1, PER_GROUP))
    return np.stack([cos, ahead, behind]).astype(np.float32)


def dot(left, right):
    return jnp.dot(left, right, preferred_element_type=f32)


def dot_nt(left, right):
    return lax.dot_general(left, right, (((1,), (1,)), ((), ())), preferred_element_type=f32)


def dot_tn(left, right):
    return lax.dot_general(left, right, (((0,), (0,)), ((), ())), preferred_element_type=f32)


def rolled(value, table, rows, sign):
    half = HEAD_DIM // 2
    turned = pltpu.roll(value, LANES - half, 1) * table[1, rows, :] + pltpu.roll(value, half, 1) * table[2, rows, :]
    return value * table[0, rows, :] + (turned if sign > 0 else -turned)


def unit_of(value):
    centered = value - jnp.mean(value, -1, keepdims=True)
    inverse = lax.rsqrt(jnp.mean(centered * centered, -1, keepdims=True) + EPSILON)
    return centered * inverse, inverse


def norm_back(grad, unit, inverse, gain):
    scaled = grad * gain
    return inverse * (scaled - jnp.mean(scaled, -1, keepdims=True) - unit * jnp.mean(scaled * unit, -1, keepdims=True))


def column_sum(value):
    return jnp.sum(value, 0, keepdims=True)


def gelu_parts(value):
    scaled = jnp.abs(value) * 0.7071067811865476
    t = 1.0 / (1.0 + 0.3275911 * scaled)
    bell = jnp.exp(-scaled * scaled)
    series = t * (0.127414796 + t * (-0.142248368 + t * (0.7107068705 + t * (-0.7265760135 + t * 0.5307027145))))
    tail = series * bell
    return jnp.where(value >= 0.0, 1.0 - tail, tail), bell * 0.3989422804014327


def three_parts(value):
    first = value.astype(bf16)
    rest = value - first.astype(f32)
    second = rest.astype(bf16)
    third = (rest - second.astype(f32)).astype(bf16)
    return first, second, third


def spread(value):
    lane = lax.broadcasted_iota(jnp.int32, value.shape, 1) % HEAD_DIM
    first, second, third = three_parts(value)
    tail = jnp.where(lane == 3, 1.0, 0.0)
    out = jnp.where(lane == 2, third.astype(f32), tail)
    out = jnp.where(lane == 1, second.astype(f32), out)
    return jnp.where(lane == 0, first.astype(f32), out).astype(bf16)


def row_loop(length, step, body):
    def run(i, carry):
        body(pl.ds(pl.multiple_of(i * step, step), step), i)
        return carry

    lax.fori_loop(0, length // step, run, 0)


def place(coords, piece, kz):
    kx, kn, ky = piece // 4, piece // 2 % 2, piece % 2
    z, y, x, n = coords[0] ^ kz, coords[1] ^ ky, coords[2] ^ kx, coords[3] ^ kn
    return z, y, x, n


def quarter_copies(coords, pieces, whole, sems):
    copies = []
    for piece in range(8):
        for kz in range(4):
            z, y, x, n = place(coords, piece, kz)
            rows = pl.ds(pl.multiple_of((2 * z + y) * PIECE, PIECE), PIECE)
            columns = pl.ds(pl.multiple_of((2 * x + n) * D, D), D)
            copies.append(
                pltpu.make_async_copy(
                    pieces[piece].at[kz, pl.ds(0, PIECE)], whole.at[rows, columns], sems.at[4 * piece + kz]
                )
            )
    return copies


def row_copies(coords, pieces, whole, sems):
    copies = []
    for piece in range(8):
        for kz in range(4):
            z, y, x, n = place(coords, piece, kz)
            rows = pl.ds(pl.multiple_of((8 * z + 4 * y + 2 * x + n) * PIECE, PIECE), PIECE)
            copies.append(pltpu.make_async_copy(pieces[piece].at[kz], whole.at[rows], sems.at[4 * piece + kz]))
    return copies


def head_masks():
    lane = lax.broadcasted_iota(jnp.int32, (1, LANES), 1)
    return [(lane // HEAD_DIM == head).astype(f32).astype(bf16) for head in range(PER_GROUP)]


def key_tail(length, live, head):
    lane = lax.broadcasted_iota(jnp.int32, (length, LANES), 1)
    row = lax.broadcasted_iota(jnp.int32, (length, LANES), 0)
    base = head * HEAD_DIM
    ones = jnp.where((lane >= base) & (lane < base + 3), 1.0, 0.0)
    return jnp.where((lane == base + 3) & (row >= live), MASKED, ones).astype(bf16)


def attn_fwd_kernel(coords, x_ref, vec_ref, table_ref, *refs):
    pieces, refs = refs[:8], refs[8:]
    a_ref, qkv_ref, o_ref, lse_ref, m_ref, b_ref, w_ref, key_ref, val_ref, sems = refs
    length = x_ref.shape[0]
    copies = quarter_copies(coords, pieces, w_ref, sems)
    for copy in copies:
        copy.start()

    def norm(rows, _):
        unit, _ = unit_of(x_ref[rows, :].astype(f32))
        a_ref[rows, :] = (unit * vec_ref[GAIN_A : GAIN_A + 1, :] + vec_ref[SHIFT_A : SHIFT_A + 1, :]).astype(bf16)

    row_loop(length, 128, norm)
    for copy in copies:
        copy.wait()

    def project(rows, _):
        normed = a_ref[rows, :]
        for part in range(3):
            out = dot(normed, w_ref[:, part * D : (part + 1) * D]) + vec_ref[BIAS_QKV + part : BIAS_QKV + part + 1, :]
            if part == 0:
                out = out * HEAD_DIM**-0.5
            for group in range(GROUPS):
                piece = out[:, group * LANES : (group + 1) * LANES]
                if part < 2:
                    piece = rolled(piece, table_ref, rows, 1)
                qkv_ref[rows, part * D + group * LANES : part * D + (group + 1) * LANES] = piece.astype(bf16)

    row_loop(length, ROWS, project)
    live = coords[4]
    masks = head_masks()
    for head in range(PER_GROUP):
        key_ref[head, :, LANES:] = key_tail(length, live, head)
        val_ref[head, :, LANES:] = jnp.broadcast_to(masks[head], (length, LANES))

    def group_step(group, carry):
        at = [pl.ds(pl.multiple_of(part * D + group * LANES, LANES), LANES) for part in range(3)]
        for head in range(PER_GROUP):
            key_ref[head, :, :LANES] = qkv_ref[:, at[1]] * masks[head]
            val_ref[head, :, :LANES] = qkv_ref[:, at[2]] * masks[head]

        def rows_step(rows, _):
            lane = lax.broadcasted_iota(jnp.int32, (ROWS, LANES), 1)
            tail = jnp.where(lane % HEAD_DIM == 3, 1.0, 0.0).astype(bf16)
            query = jnp.concatenate([qkv_ref[rows, at[0]], tail], 1)
            total = jnp.zeros((ROWS, 2 * LANES), f32)
            tops = jnp.zeros((ROWS, LANES), f32)
            for head in range(PER_GROUP):
                scores = dot_nt(query, key_ref[head])
                top = jnp.max(scores, -1, keepdims=True)
                total = total + dot(jnp.exp(scores - top).astype(bf16), val_ref[head])
                tops = jnp.where(lane // HEAD_DIM == head, top, tops)
            o_ref[rows, at[0]] = (total[:, :LANES] / total[:, LANES:]).astype(bf16)
            lse_ref[rows, at[0]] = spread(-(tops + jnp.log(total[:, LANES:])))

        row_loop(length, ROWS, rows_step)
        return carry

    lax.fori_loop(0, GROUPS, group_step, 0)

    def after(rows, _):
        middle = x_ref[rows, :].astype(f32) + (dot(o_ref[rows, :], w_ref[:, 3 * D :]) + vec_ref[BIAS_OUT : BIAS_OUT + 1, :])
        m_ref[rows, :] = middle
        unit, _ = unit_of(middle)
        b_ref[rows, :] = (unit * vec_ref[GAIN_F : GAIN_F + 1, :] + vec_ref[SHIFT_F : SHIFT_F + 1, :]).astype(bf16)

    row_loop(length, ROWS, after)


def ffn_fwd_kernel(last, coords, m_ref, b_ref, vec_ref, *refs):
    up_pieces, down_pieces, refs = refs[:8], refs[8:16], refs[16:]
    y_ref, z_ref, slope_ref, up_ref, down_ref, up_sems, down_sems = refs
    length = m_ref.shape[0]
    copies = quarter_copies(coords, up_pieces, up_ref, up_sems)
    copies_down = row_copies(coords, down_pieces, down_ref, down_sems)
    for copy in copies + copies_down:
        copy.start()
    for copy in copies + copies_down:
        copy.wait()

    def step(rows, i):
        normed = b_ref[rows, :]
        for block in range(BLOCKS):
            columns = slice(block * D, (block + 1) * D)
            pre = dot(normed, up_ref[:, columns]) + vec_ref[BIAS_UP + block : BIAS_UP + block + 1, :]
            cdf, bell = gelu_parts(pre)
            z_ref[rows, columns] = (pre * cdf).astype(bf16)
            slope_ref[rows, columns] = (cdf + pre * bell).astype(bf16)
        out = m_ref[rows, :] + (dot(z_ref[rows, :], down_ref[...]) + vec_ref[BIAS_DOWN : BIAS_DOWN + 1, :])
        if last:
            row = lax.broadcasted_iota(jnp.int32, (ROWS, 1), 0) + i * ROWS
            out = jnp.where(row < coords[4], out, 0.0)
        y_ref[rows, :] = out.astype(y_ref.dtype)

    row_loop(length, ROWS, step)


def ffn_bwd_kernel(first, coords, g_ref, z_ref, slope_ref, m_ref, vec_ref, *refs):
    up_pieces, down_pieces, refs = refs[:8], refs[8:16], refs[16:]
    gb_ref, gu_ref, gm_ref, gmb_ref, sums_ref, up_ref, down_ref, up_sems, down_sems = refs
    length = m_ref.shape[0]
    copies = quarter_copies(coords, up_pieces, up_ref, up_sems)
    copies_down = row_copies(coords, down_pieces, down_ref, down_sems)
    for copy in copies_down + copies:
        copy.start()
    for copy in copies_down + copies:
        copy.wait()
    sums_ref[...] = jnp.zeros_like(sums_ref)

    def add(row, value):
        sums_ref[row : row + 1, :] += column_sum(value)

    def step(rows, i):
        grad = g_ref[rows, :].astype(f32)
        if first:
            row = lax.broadcasted_iota(jnp.int32, (ROWS, 1), 0) + i * ROWS
            grad = jnp.where(row < coords[4], grad, 0.0)
        low = grad.astype(bf16)
        gb_ref[rows, :] = low
        add(BIAS_DOWN, low.astype(f32))
        for block in range(BLOCKS):
            columns = slice(block * D, (block + 1) * D)
            back = dot_nt(low, down_ref[columns, :]) * slope_ref[rows, columns].astype(f32)
            part = back.astype(bf16)
            gu_ref[rows, columns] = part
            add(BIAS_UP + block, part.astype(f32))
        normed_grad = dot_nt(gu_ref[rows, :], up_ref[...])
        unit, inverse = unit_of(m_ref[rows, :])
        add(GAIN_F, normed_grad * unit)
        add(SHIFT_F, normed_grad)
        middle = grad + norm_back(normed_grad, unit, inverse, vec_ref[GAIN_F : GAIN_F + 1, :])
        gm_ref[rows, :] = middle
        low = middle.astype(bf16)
        gmb_ref[rows, :] = low
        add(BIAS_OUT, low.astype(f32))

    row_loop(length, ROWS, step)


def attn_bwd_kernel(coords, gm_ref, gmb_ref, qkv_ref, o_ref, lse_ref, x_ref, vec_ref, table_ref, *refs):
    pieces, refs = refs[:8], refs[8:]
    gpm_ref, gx_ref, sums_ref, w_ref, go_ref, key_ref, val_ref, q_ref, g_ref, dq_ref, sems = refs
    length = x_ref.shape[0]
    copies = quarter_copies(coords, pieces, w_ref, sems)
    for copy in copies:
        copy.start()
    for copy in copies:
        copy.wait()
    sums_ref[...] = jnp.zeros_like(sums_ref)

    def add(row, value):
        sums_ref[row : row + 1, :] += column_sum(value)

    def first(rows, _):
        low = gmb_ref[rows, :]
        gpm_ref[rows, 3 * D :] = low
        go_ref[rows, :] = dot_nt(low, w_ref[:, 3 * D :]).astype(bf16)

    row_loop(length, ROWS, first)
    live = coords[4]
    masks = head_masks()
    head_of = lax.broadcasted_iota(jnp.int32, (LANES, LANES), 0) // HEAD_DIM
    same = (head_of == lax.broadcasted_iota(jnp.int32, (LANES, LANES), 1) // HEAD_DIM).astype(f32).astype(bf16)
    for head in range(PER_GROUP):
        key_ref[head, :, LANES:] = key_tail(length, live, head)
        val_ref[head, :, LANES:] = key_tail(length, length, head)

    def group_step(group, carry):
        at = [pl.ds(pl.multiple_of(part * D + group * LANES, LANES), LANES) for part in range(3)]
        grad = go_ref[:, at[0]]
        query = qkv_ref[:, at[0]]
        product = grad.astype(f32) * o_ref[:, at[0]].astype(f32)
        high = product.astype(bf16)
        rest = (product - high.astype(f32)).astype(bf16)
        deltas = dot(high, same) + dot(rest, same)
        for head in range(PER_GROUP):
            key_ref[head, :, :LANES] = qkv_ref[:, at[1]] * masks[head]
            val_ref[head, :, :LANES] = qkv_ref[:, at[2]] * masks[head]
            q_ref[head] = query * masks[head]
            g_ref[head] = grad * masks[head]
        query_wide = jnp.concatenate([query, lse_ref[:, at[0]]], 1)
        grad_wide = jnp.concatenate([grad, spread(-deltas)], 1)
        dq_ref[...] = jnp.zeros_like(dq_ref)

        def rows_step(rows, _):
            dk = jnp.zeros((ROWS, LANES), f32)
            dv = jnp.zeros((ROWS, LANES), f32)
            for head in range(PER_GROUP):
                key = key_ref[head, rows, :]
                probs = jnp.exp(dot_nt(key, query_wide))
                scores = (probs * dot_nt(val_ref[head, rows, :], grad_wide)).astype(bf16)
                dv = dv + dot(probs.astype(bf16), g_ref[head])
                dk = dk + dot(scores, q_ref[head])
                dq_ref[...] += dot_tn(scores, key[:, :LANES])
            dk = rolled(dk.astype(bf16).astype(f32), table_ref, rows, -1)
            gpm_ref[rows, at[1]] = dk.astype(bf16)
            gpm_ref[rows, at[2]] = dv.astype(bf16)

        row_loop(length, ROWS, rows_step)

        def last_step(rows, _):
            dq = rolled(dq_ref[rows, :].astype(bf16).astype(f32), table_ref, rows, -1) * HEAD_DIM**-0.5
            gpm_ref[rows, at[0]] = dq.astype(bf16)

        row_loop(length, ROWS, last_step)
        return carry

    lax.fori_loop(0, GROUPS, group_step, 0)

    def after(rows, _):
        for part in range(3):
            add(BIAS_QKV + part, gpm_ref[rows, part * D : (part + 1) * D].astype(f32))
        normed_grad = dot_nt(gpm_ref[rows, : 3 * D], w_ref[:, : 3 * D])
        unit, inverse = unit_of(x_ref[rows, :].astype(f32))
        add(GAIN_A, normed_grad * unit)
        add(SHIFT_A, normed_grad)
        out = gm_ref[rows, :] + norm_back(normed_grad, unit, inverse, vec_ref[GAIN_A : GAIN_A + 1, :])
        gx_ref[rows, :] = out.astype(gx_ref.dtype)

    row_loop(length, ROWS, after)


def emit(coords, outs, second, kn, kx, ky, kz, value):
    core_ref, a_ref, b_ref, keep_ref = outs
    rows = slice(0, PIECE)
    ka, kb = (kx, ky) if second == "y" else (ky, kx)
    if kn:
        core_ref[ka, kb, kz, rows] = value
    elif ka:
        a_ref[kb, kz, rows] = value
    elif kb:
        b_ref[kz, rows] = value
    else:
        keep_ref[kz, rows] = value


def quarter_grad_kernel(second, coords, left_ref, right_ref, *refs):
    outs, (flip_ref, tmp_ref) = refs[-6:-2], refs[-2:]
    count = flip_ref.shape[0]
    for i in range(count):
        flip_ref[i] = (left_ref[i] if count > 1 else left_ref[...]).T
    for kn in (1, 0):
        for kx in (1, 0):
            quarter = 2 * (coords[2] ^ kx) + (coords[3] ^ kn)
            columns = pl.ds(pl.multiple_of(quarter * D, D), D)
            left = flip_ref[quarter // 3] if count > 1 else flip_ref[0]
            tmp_ref[...] = dot(left, right_ref[:, columns])
            for ky in range(2):
                for kz in range(4):
                    group = 2 * (coords[0] ^ kz) + (coords[1] ^ ky)
                    value = tmp_ref[pl.ds(pl.multiple_of(group * PIECE, PIECE), PIECE), :].astype(bf16)
                    emit(coords, outs, second, kn, kx, ky, kz, value)


def row_grad_kernel(second, coords, left_ref, right_ref, *refs):
    outs, (tmp_ref,) = refs[:4], refs[4:]
    for block in range(BLOCKS):
        columns = slice(block * D, (block + 1) * D)
        tmp_ref[columns, :] = dot(left_ref[:, columns].T, right_ref[...])
    for kn in (1, 0):
        for kx in (1, 0):
            for ky in range(2):
                for kz in range(4):
                    z, y, x, n = coords[0] ^ kz, coords[1] ^ ky, coords[2] ^ kx, coords[3] ^ kn
                    start = pl.multiple_of((8 * z + 4 * y + 2 * x + n) * PIECE, PIECE)
                    emit(coords, outs, second, kn, kx, ky, kz, tmp_ref[pl.ds(start, PIECE), :].astype(bf16))


def call(kernel, ins, outs, scratch, name, flops, exps=0):
    moved = sum(a.size * a.dtype.itemsize for a, _ in ins) + sum(int(np.prod(s)) * jnp.dtype(t).itemsize for s, t in outs)
    return pl.pallas_call(
        kernel,
        out_shape=[jax.ShapeDtypeStruct(s, t) for s, t in outs],
        in_specs=[pl.BlockSpec(memory_space=space) for _, space in ins],
        out_specs=[pl.BlockSpec(memory_space=pltpu.VMEM)] * len(outs),
        scratch_shapes=scratch,
        compiler_params=pltpu.CompilerParams(vmem_limit_bytes=VMEM_LIMIT),
        cost_estimate=pl.CostEstimate(flops=int(flops), bytes_accessed=int(moved), transcendentals=int(exps)),
        name=name,
    )(*[a for a, _ in ins])


V, S, H = pltpu.VMEM, pltpu.SMEM, pl.ANY
SEMS = pltpu.SemaphoreType.DMA


def attn_fwd(coords, x, vec, table, pieces):
    n = x.shape[0]
    ins = [(coords, S), (x, V), (vec, V), (table, V)] + [(p, H) for p in pieces]
    outs = [((n, D), bf16), ((n, 3 * D), bf16), ((n, D), bf16), ((n, D), bf16), ((n, D), f32), ((n, D), bf16)]
    scratch = [V((D, FF), bf16), V((PER_GROUP, n, 2 * LANES), bf16), V((PER_GROUP, n, 2 * LANES), bf16), SEMS((32,))]
    return call(attn_fwd_kernel, ins, outs, scratch, "attn_fwd", 2 * n * D * FF + 4 * n * n * D, HEADS * n * n)


def ffn_fwd(coords, m, b, vec, up, down, last):
    n = m.shape[0]
    ins = [(coords, S), (m, V), (b, V), (vec, V)] + [(p, H) for p in up + down]
    outs = [((n, D), bf16 if last else f32), ((n, FF), bf16), ((n, FF), bf16)]
    scratch = [V((D, FF), bf16), V((FF, D), bf16), SEMS((32,)), SEMS((32,))]
    return call(functools.partial(ffn_fwd_kernel, last), ins, outs, scratch, "ffn_fwd", 4 * n * D * FF, 2 * n * FF)


def ffn_bwd(coords, g, z, slope, m, vec, up, down, first):
    n = m.shape[0]
    ins = [(coords, S), (g, V), (z, V), (slope, V), (m, V), (vec, V)] + [(p, H) for p in up + down]
    outs = [((n, D), bf16), ((n, FF), bf16), ((n, D), f32), ((n, D), bf16), ((VECS, D), f32)]
    scratch = [V((D, FF), bf16), V((FF, D), bf16), SEMS((32,)), SEMS((32,))]
    return call(functools.partial(ffn_bwd_kernel, first), ins, outs, scratch, "ffn_bwd", 4 * n * D * FF, 0)


def attn_bwd(coords, gm, gmb, qkv, o, lse, x, vec, table, pieces, last):
    n = x.shape[0]
    ins = [(coords, S)] + [(a, V) for a in (gm, gmb, qkv, o, lse, x, vec, table)] + [(p, H) for p in pieces]
    outs = [((n, FF), bf16), ((n, D), bf16 if last else f32), ((VECS, D), f32)]
    wide, thin = V((PER_GROUP, n, 2 * LANES), bf16), V((PER_GROUP, n, LANES), bf16)
    scratch = [V((D, FF), bf16), V((n, D), bf16), wide, wide, thin, thin, V((n, LANES), f32), SEMS((32,))]
    return call(attn_bwd_kernel, ins, outs, scratch, "attn_bwd", 2 * n * D * FF + 10 * n * n * D, HEADS * n * n)


def grad_outs(rows):
    return [((2, 2, 4, rows, D), bf16), ((2, 4, rows, D), bf16), ((4, rows, D), bf16), ((4, rows, D), bf16)]


def quarter_grad(coords, left, right, second):
    count = left.shape[0] if left.ndim == 3 else 1
    n = right.shape[0]
    scratch = [V((count, D, n), bf16), V((D, D), f32)]
    ins = [(coords, S), (left, V), (right, V)]
    return call(functools.partial(quarter_grad_kernel, second), ins, grad_outs(PIECE), scratch, "quarter_grad", 2 * n * D * FF)


def row_grad(coords, left, right, second):
    n = right.shape[0]
    ins = [(coords, S), (left, V), (right, V)]
    return call(functools.partial(row_grad_kernel, second), ins, grad_outs(PIECE), [V((FF, D), f32)], "row_grad", 2 * n * D * FF)


def swap(axis_name, bit):
    size = lax.axis_size(axis_name)
    pairs = [(i, i ^ bit) for i in range(size)]
    return lambda value: lax.ppermute(value, axis_name, pairs)


NARROW = ("narrow", 1)
LINK = {"x": ("wide", 1), "y": ("wide", 2)}


def relative(values, bits):
    for place_of, bit in enumerate(reversed(bits)):
        step = 1 << place_of
        values = [jnp.where(bit > 0, values[i ^ step], values[i]) for i in range(len(values))]
    return values


def gather_blocks(block, first):
    second = "x" if first == "y" else "y"
    zs = jnp.stack([block] + [swap("wide", 4 * k)(block) for k in (1, 2, 3)])
    near = {0: zs, 1: swap(*LINK[first])(zs)}
    far = {k: swap(*LINK[second])(near[k]) for k in (0, 1)}
    pieces = [None] * 8
    for kx in range(2):
        for ky in range(2):
            ka, kb = (kx, ky) if first == "x" else (ky, kx)
            held = far[ka] if kb else near[ka]
            pieces[4 * kx + ky] = held
            pieces[4 * kx + 2 + ky] = swap(*NARROW)(held)
    return pieces


def add(*terms):
    return functools.reduce(lambda p, q: p + q, [t.astype(f32) for t in terms])


def scatter_blocks(sends, second):
    first = "x" if second == "y" else "y"
    core, a, b, keep = sends
    core = swap(*NARROW)(core)
    a = swap(*LINK[first])(add(a, core[1]).astype(bf16))
    b = swap(*LINK[second])(add(b, core[0, 1], a[1]).astype(bf16))
    total = add(keep, core[0, 0], a[0], b)
    return add(total[0], *[swap("wide", 4 * k)(total[k].astype(bf16)) for k in (1, 2, 3)])


def regroup(parts, bits):
    mine = relative(parts, bits)
    return relative([mine[0]] + [swap(AXES, k)(mine[k]) for k in (1, 2, 3)], bits)


def vector_tables(gains, biases):
    gains = gains.astype(f32).reshape(LAYERS, 2, D)
    biases = biases.astype(f32).reshape(LAYERS, 11, D)
    return jnp.concatenate([gains, biases, jnp.zeros((LAYERS, VECS - 13, D), f32)], 1)


def whole_pieces(matrix, by_rows):
    if by_rows:
        cut = matrix.reshape(4, 2, 2, 2, PIECE, D)
        return [cut[:, ky, kx, kn] for kx in range(2) for kn in range(2) for ky in range(2)]
    cut = matrix.reshape(4, 2, PIECE, 4, D)
    return [cut[:, ky, :, 2 * kx + kn] for kx in range(2) for kn in range(2) for ky in range(2)]


def whole_grad(sends, second, by_rows):
    core, a, b, keep = sends
    kept = jnp.stack([jnp.stack([keep, b]), a])
    cut = jnp.stack([kept, core])
    if second == "x":
        cut = jnp.swapaxes(cut, 1, 2)
    if by_rows:
        return jnp.transpose(cut, (3, 2, 1, 0, 4, 5)).reshape(FF, D)
    return jnp.transpose(cut, (3, 2, 4, 1, 0, 5)).reshape(D, FF)


FIRST = {("attn", 0): "y", ("up", 0): "x", ("down", 0): "y", ("attn", 1): "x", ("up", 1): "y", ("down", 1): "x"}
NAMES = ("attn", "up", "down")


def fetch(w_qkv, w_out, w_up, w_down, gains, biases, bits):
    rows = D // 32
    z1, z0, y, x, n = bits
    attn = [jnp.concatenate([w_qkv[l].reshape(rows, 3 * D), w_out[l].reshape(rows, D)], 1) for l in range(LAYERS)]
    ups = [w_up[l].reshape(rows, FF) for l in range(LAYERS)]
    cut = jnp.stack([attn[0], ups[0], attn[1], ups[1]])
    parts = [cut[:, :, s * D : (s + 1) * D] for s in range(4)]
    blocks = jnp.concatenate(regroup(parts, [x, n]), 1)
    mine = jnp.concatenate([gains, biases])
    width = mine.shape[0]
    tail = jnp.zeros((16, D), bf16).at[0, :width].set(mine)
    shards = {
        ("attn", 0): jnp.concatenate([blocks[0], tail]),
        ("up", 0): blocks[1],
        ("attn", 1): blocks[2],
        ("up", 1): blocks[3],
        ("down", 0): w_down[0].reshape(PIECE, D),
        ("down", 1): w_down[1].reshape(PIECE, D),
    }
    weights = {(name, l): gather_blocks(shards[name, l], FIRST[name, l]) for l in range(LAYERS) for name in NAMES}
    cut = jnp.stack([p[:, PIECE, :width] for p in weights["attn", 0]]).reshape(2, 2, 2, 2, 2, width)
    cut = jnp.transpose(cut, (3, 4, 2, 0, 1, 5))
    for axis, bit in enumerate(bits):
        cut = jnp.where(bit > 0, jnp.flip(cut, axis), cut)
    cut = cut.reshape(32, width)
    return weights, vector_tables(cut[:, : gains.shape[0]].reshape(-1), cut[:, gains.shape[0] :].reshape(-1))


def fetch_plain(w_qkv, w_out, w_up, w_down, gains, biases):
    def whole(value, rows):
        return lax.all_gather(value, AXES, axis=0, tiled=True).reshape(rows, -1)

    weights = {}
    for l in range(LAYERS):
        attn = jnp.concatenate([whole(w_qkv[l], D), whole(w_out[l], D)], 1)
        weights["attn", l] = whole_pieces(attn, False)
        weights["up", l] = whole_pieces(whole(w_up[l], D), False)
        weights["down", l] = whole_pieces(whole(w_down[l], FF), True)
    return weights, vector_tables(whole(gains, 1)[0], whole(biases, 1)[0])


def body(tokens, lengths, w_qkv, w_out, w_up, w_down, gains, biases, cotangent):
    length = tokens.shape[0] // lengths.shape[0]
    devices = lax.axis_size(AXES)
    fast = lax.axis_size("wide") == 16 and lax.axis_size("narrow") == 2
    wide, narrow = lax.axis_index("wide"), lax.axis_index("narrow")
    bits = [(wide >> 3) & 1, (wide >> 2) & 1, (wide >> 1) & 1, wide & 1, narrow]
    if fast:
        at = [wide >> 2, bits[2], bits[3], bits[4]]
        weights, vectors = fetch(w_qkv, w_out, w_up, w_down, gains, biases, bits)
    else:
        at = [jnp.int32(0)] * 4
        weights, vectors = fetch_plain(w_qkv, w_out, w_up, w_down, gains, biases)
    coords = jnp.stack([jnp.asarray(c, jnp.int32) for c in at + [lengths[0]]])
    table = jnp.asarray(rotary_tables(length))

    x = tokens
    kept = []
    for l in range(LAYERS):
        last = l == LAYERS - 1
        a, qkv, o, lse, m, b = attn_fwd(coords, x, vectors[l], table, weights["attn", l])
        y, z, slope = ffn_fwd(coords, m, b, vectors[l], weights["up", l], weights["down", l], last)
        kept.append((x, a, qkv, o, lse, m, b, z, slope))
        x = y
    output = x

    grad = cotangent
    sends, sums = {}, [None] * LAYERS
    for l in reversed(range(LAYERS)):
        x, a, qkv, o, lse, m, b, z, slope = kept[l]
        gb, gu, gm, gmb, sums_f = ffn_bwd(
            coords, grad, z, slope, m, vectors[l], weights["up", l], weights["down", l], l == LAYERS - 1
        )
        sends["down", l] = row_grad(coords, z, gb, FIRST["down", l])
        sends["up", l] = quarter_grad(coords, b, gu, FIRST["up", l])
        gpm, grad, sums_a = attn_bwd(coords, gm, gmb, qkv, o, lse, x, vectors[l], table, weights["attn", l], l == 0)
        sends["attn", l] = quarter_grad(coords, jnp.stack([a, o]), gpm, FIRST["attn", l])
        sums[l] = sums_f + sums_a
    sums = jnp.stack(sums)
    gain_sums, bias_sums = sums[:, :2].reshape(devices, -1), sums[:, 2:13].reshape(devices, -1)

    if not fast:
        outs = []
        for name, parts in (("attn", (3 * D, D)), ("up", (FF,)), ("down", (D,))):
            layers = [whole_grad(sends[name, l], FIRST[name, l], name == "down").astype(f32) for l in range(LAYERS)]
            start = 0
            for width in parts:
                cut = jnp.stack([g[:, start : start + width].reshape(-1) for g in layers])
                outs.append(lax.psum_scatter(cut, AXES, scatter_dimension=1, tiled=True))
                start += width
        small = [lax.psum_scatter(v.reshape(-1), AXES, scatter_dimension=0, tiled=True) for v in (gain_sums, bias_sums)]
        return (output, grad, *outs, *small)

    small = jnp.concatenate([gain_sums, bias_sums], 1)
    width = small.shape[1]
    small = small.reshape(2, 2, 2, 2, 2, width)
    for axis, bit in enumerate(bits):
        small = jnp.where(bit > 0, jnp.flip(small, axis), small)
    small = jnp.transpose(small, (4, 3, 2, 0, 1, 5)).reshape(2, 2, 2, 4, 1, width)
    if FIRST["attn", 0] == "x":
        small = jnp.swapaxes(small, 1, 2)
    small = jnp.pad(small, ((0, 0),) * 4 + ((0, 15), (0, D - width))).astype(bf16)
    ends = (small[1], small[0, 1], small[0, 0, 1], small[0, 0, 0])
    sends["attn", 0] = [jnp.concatenate([s, e], -2) for s, e in zip(sends["attn", 0], ends, strict=True)]
    sums = {key: scatter_blocks(value, FIRST[key]) for key, value in sends.items()}
    mine = sums["attn", 0][PIECE, :width]
    rows = D // 32
    shares = {}
    for keys in ((("up", 1), ("attn", 1), ("up", 0)), (("attn", 0),)):
        cut = jnp.stack([sums[key][:PIECE] for key in keys])
        parts = [cut[:, s * rows : (s + 1) * rows] for s in range(4)]
        whole = jnp.concatenate(regroup(parts, bits[3:]), 2)
        for i, key in enumerate(keys):
            shares[key] = whole[i]
    outs = (
        jnp.stack([shares["attn", l][:, : 3 * D].reshape(-1) for l in range(LAYERS)]),
        jnp.stack([shares["attn", l][:, 3 * D :].reshape(-1) for l in range(LAYERS)]),
        jnp.stack([shares["up", l].reshape(-1) for l in range(LAYERS)]),
        jnp.stack([sums["down", l].reshape(-1) for l in range(LAYERS)]),
    )
    return (output, grad, *outs, mine[: gains.shape[0]], mine[gains.shape[0] :])


def solution(mesh):
    both = P(AXES)
    flat = P(None, AXES)
    rows = P(AXES, None)
    return jax.shard_map(
        body,
        mesh=mesh,
        in_specs=(rows, both, flat, flat, flat, flat, both, both, rows),
        out_specs=(rows, rows, flat, flat, flat, flat, both, both),
        check_vma=False,
    )
```

time: 1660 us -> 542 us (0.33)
  other arithmetic: 517 us -> 22.1 us
  waiting for transfers between devices: 567 us -> 177 us
  matrix products: 229 us -> 0 us
  Pallas kernels: 0 us -> 204 us
  local copies, waits for them, and re-layouts: 188 us -> 14.9 us
  blocking collectives: 133 us -> 0 us
  starting transfers between devices: 0.28 us -> 113 us
    unnamed x8 -> x0, waiting for transfers between devices: 567 us -> none
    all_gather x8 -> x0, other arithmetic: 418 us -> none  [the longest x2 140 us: fetch_forward(): lax.all_gather(w_up[layer_index:layer_index + 1], ('wide', 'narrow'), axi...]
    dot_general x94 -> x0, matrix products: 229 us -> none  [the longest x20 42.1 us: scores_of(): jnp.einsum('clhd,cmhd->chlm', rotated_queries, rotated_keys, preferred_el...]
    pallas_call x0 -> x14, Pallas kernels: none -> 204 us  [call(): pl.pallas_call(kernel, out_shape=[jax.ShapeDtypeStruct(s, t) for s, t in...]
    ppermute x0 -> x105, waiting for transfers between devices: none -> 177 us  [swap(): return lambda value: lax.ppermute(value, axis_name, pairs)]
    ppermute x0 -> x105, starting transfers between devices: none -> 113 us  [swap(): return lambda value: lax.ppermute(value, axis_name, pairs)]
    all_gather x2 -> x0, blocking collectives: 90.3 us -> none  [fetch_forward(): lax.all_gather(w_out[layer_index:layer_index + 1], ('wide', 'narrow'), ax...]
    another operation x28 -> x14, local copies, waits for them, and re-layouts: 86.7 us -> 1.65 us  [the longest x1 0.68 us: body(): coords = jnp.stack([jnp.asarray(c, jnp.int32) for c in at + [lengths[0]]])]
  transfers between devices with their start and end apart: 7 -> 105, of which waited for: 1 -> 39; matrix products, arithmetic and copies ran while one was open for 30% -> 5% of each run, Pallas kernels for 0% -> 17%
where the time goes in v1:
time: 542 us; the launch traced here: 535 us
  Pallas kernels  204 us (38%)
  waiting for transfers between devices  177 us (33%)
  starting transfers between devices  113 us (21%)
  other arithmetic  22.1 us (4%)
  local copies, waits for them, and re-layouts  14.9 us (3%)
    pallas_call x14, Pallas kernels, call(): pl.pallas_call(kernel, out_shape=[jax.ShapeDtypeStruct(s, t) for s, t in...  204 us
    ppermute x105, waiting for transfers between devices, swap(): return lambda value: lax.ppermute(value, axis_name, pairs)  177 us
    ppermute x105, starting transfers between devices, swap(): return lambda value: lax.ppermute(value, axis_name, pairs)  113 us
  transfers between devices with their start and end apart: 105, of which 39 were waited for; matrix products, arithmetic and copies ran while one was open for 5% of the time, Pallas kernels for 17%

profile of v1, /device:TPU:0, one launch (start us, length us, event | category | flops | bytes accessed | tf_op | source)
XLA Modules:
  0.0 534.7 jit_solution(3878627762754255982)
XLA Ops:
  30.9 9.1 %collective-permute-start.53 = (bf16[80,640]{1,0:T(8,128)(2,1)S(1)}, bf16[80,640]{1,0:T(8,128)(2,1)S(1)}, u32[]{:S(2)}, u32[]{:S(2)}) collective-permute-start(bf16[80,640]{1,0:T(8,128)(2,1)S(1)} %reshape_squeeze.23), channel_id=1, source_target_pairs={{0,8},{2,10},{4,12},{6,14},{8,0},{10,2},{12,4},{14,6},{16,24},{18,... | collective-permute-start | bytes 307208 | tf_op jit(solution)/shard_map/ppermute | solution.py:495
  50.5 6.8 %collective-permute-done.14 = bf16[80,640]{1,0:T(8,128)(2,1)S(1)} collective-permute-done((bf16[80,640]{1,0:T(8,128)(2,1)S(1)}, bf16[80,640]{1,0:T(8,128)(2,1)S(1)}, u32[]{:S(2)}, u32[]{:S(2)}) %collective-permute-start.14) | collective-permute-done | bytes 102432 | tf_op jit(solution)/shard_map/ppermute | solution.py:495
  75.1 10.3 %collective-permute-done.10.refs_5_ = bf16[4,96,640]{2,1,0:T(8,128)(2,1)S(1)} collective-permute-done((bf16[4,96,640]{2,1,0:T(8,128)(2,1)S(1)}, bf16[4,96,640]{2,1,0:T(8,128)(2,1)S(1)}, u32[]{:S(2)}, u32[]{:S(2)}) %collective-permute-start.10) | collective-permute-done | bytes 491552 | tf_op jit(solution)/shard_map/ppermute | solution.py:495
  145.0 6.5 %collective-permute-done.20.refs_5_ = bf16[4,80,640]{2,1,0:T(8,128)(2,1)} collective-permute-done((bf16[4,80,640]{2,1,0:T(8,128)(2,1)}, bf16[4,80,640]{2,1,0:T(8,128)(2,1)}, u32[]{:S(2)}, u32[]{:S(2)}) %collective-permute-start.20) | collective-permute-done | bytes 409632 | tf_op jit(solution)/shard_map/ppermute | solution.py:495
  159.3 22.2 %attn_fwd.2 = (bf16[512,640]{1,0:T(8,128)(2,1)}, bf16[512,1920]{1,0:T(8,128)(2,1)}, bf16[512,640]{1,0:T(8,128)(2,1)}, bf16[512,640]{1,0:T(8,128)(2,1)}, f32[512,640]{1,0:T(8,128)}, /*index=5*/bf16[512,640]{1,0:T(8,128)(2,1)}) custom-call(s32[5]{0:T(128)} %stack.160.coords, bf16[512,640]{1,0:T(8,128)(2,1)} %x_ref.3, f32[16,640]{1,0:T(8,128)} %get-tuple-element.216.vec_ref, ...), custom_call_target="tpu_custom_call" | custom-call | flops 2348810240 | bytes 11313172 | tf_op jit(solution)/shard_map/attn_fwd/pallas_call | solution.py:425
  183.5 14.8 %ffn_fwd.2 = (f32[512,640]{1,0:T(8,128)}, bf16[512,2560]{1,0:T(8,128)(2,1)}, bf16[512,2560]{1,0:T(8,128)(2,1)}) custom-call(s32[5]{0:T(128)} %stack.160.coords, f32[512,640]{1,0:T(8,128)} %get-tuple-element.78.m_ref, bf16[512,640]{1,0:T(8,128)(2,1)} %get-tuple-element.79.b_ref.left_ref, f32[16,640]{1,0:T(8,128)} %get-tuple-element.216.vec_ref, ...), custom_call_target="tpu_custom_call" | custom-call | flops 3355443200 | bytes 15114260 | tf_op jit(solution)/shard_map/ffn_fwd/pallas_call | solution.py:425
  198.4 23.1 %attn_fwd.3 = (bf16[512,640]{1,0:T(8,128)(2,1)}, bf16[512,1920]{1,0:T(8,128)(2,1)}, bf16[512,640]{1,0:T(8,128)(2,1)}, bf16[512,640]{1,0:T(8,128)(2,1)}, f32[512,640]{1,0:T(8,128)}, /*index=5*/bf16[512,640]{1,0:T(8,128)(2,1)}) custom-call(s32[5]{0:T(128)} %stack.160.coords, f32[512,640]{1,0:T(8,128)} %get-tuple-element.80.x_ref, ...), custom_call_target="tpu_custom_call" | custom-call | flops 2348810240 | bytes 11313172 | tf_op jit(solution)/shard_map/attn_fwd/pallas_call | solution.py:425
  222.8 14.7 %ffn_fwd.3 = (bf16[512,640]{1,0:T(8,128)(2,1)}, bf16[512,2560]{1,0:T(8,128)(2,1)}, bf16[512,2560]{1,0:T(8,128)(2,1)}) custom-call(s32[5]{0:T(128)} %stack.160.coords, f32[512,640]{1,0:T(8,128)} %get-tuple-element.81.m_ref, bf16[512,640]{1,0:T(8,128)(2,1)} %get-tuple-element.82.b_ref.left_ref, f32[16,640]{1,0:T(8,128)} %get-tuple-element.215.vec_ref, ...), custom_call_target="tpu_custom_call" | custom-call | flops 3355443200 | bytes 14458900 | tf_op jit(solution)/shard_map/ffn_fwd/pallas_call | solution.py:425
  237.4 14.0 %ffn_bwd.2 = (bf16[512,640]{1,0:T(8,128)(2,1)}, bf16[512,2560]{1,0:T(8,128)(2,1)}, f32[512,640]{1,0:T(8,128)}, bf16[512,640]{1,0:T(8,128)(2,1)}, f32[16,640]{1,0:T(8,128)}) custom-call(s32[5]{0:T(128)} %stack.160.coords, bf16[512,640]{1,0:T(8,128)(2,1)} %g_ref.1, bf16[512,2560]{1,0:T(8,128)(2,1)} %get-tuple-element.84.z_ref.left_ref, ...), custom_call_target="tpu_custom_call" | custom-call | flops 3355443200 | bytes 19087380 | tf_op jit(solution)/shard_map/ffn_bwd/pallas_call | solution.py:425
  251.4 32.7 %attn_bwd.2 = (bf16[512,2560]{1,0:T(8,128)(2,1)}, f32[512,640]{1,0:T(8,128)}, f32[16,640]{1,0:T(8,128)}) custom-call(s32[5]{0:T(128)} %stack.160.coords, f32[512,640]{1,0:T(8,128)} %get-tuple-element.86.gm_ref, bf16[512,640]{1,0:T(8,128)(2,1)} %get-tuple-element.87.gmb_ref, bf16[512,1920]{1,0:T(8,128)(2,1)} %get-tuple-element.88.qkv_ref, ...), custom_call_target="tpu_custom_call" | custom-call | flops 3355443200 | bytes 14630932 | tf_op jit(solution)/shard_map/attn_bwd/pallas_call | solution.py:425
  284.9 13.7 %ffn_bwd.3 = (bf16[512,640]{1,0:T(8,128)(2,1)}, bf16[512,2560]{1,0:T(8,128)(2,1)}, f32[512,640]{1,0:T(8,128)}, bf16[512,640]{1,0:T(8,128)(2,1)}, f32[16,640]{1,0:T(8,128)}) custom-call(s32[5]{0:T(128)} %stack.160.coords, f32[512,640]{1,0:T(8,128)} %get-tuple-element.91.g_ref, bf16[512,2560]{1,0:T(8,128)(2,1)} %get-tuple-element.92.z_ref.left_ref, ...), custom_call_target="tpu_custom_call" | custom-call | flops 3355443200 | bytes 19742740 | tf_op jit(solution)/shard_map/ffn_bwd/pallas_call | solution.py:425
  298.6 32.0 %attn_bwd.3 = (bf16[512,2560]{1,0:T(8,128)(2,1)}, bf16[512,640]{1,0:T(8,128)(2,1)}, f32[16,640]{1,0:T(8,128)}) custom-call(s32[5]{0:T(128)} %stack.160.coords, f32[512,640]{1,0:T(8,128)} %get-tuple-element.94.gm_ref, bf16[512,640]{1,0:T(8,128)(2,1)} %get-tuple-element.95.gmb_ref, bf16[512,1920]{1,0:T(8,128)(2,1)} %get-tuple-element.96.qkv_ref, ...), custom_call_target="tpu_custom_call" | custom-call | flops 3355443200 | bytes 13975572 | tf_op jit(solution)/shard_map/attn_bwd/pallas_call | solution.py:425
  331.4 5.8 %quarter_grad.7 = (bf16[2,2,4,80,640]{4,3,2,1,0:T(8,128)(2,1)}, bf16[2,4,80,640]{3,2,1,0:T(8,128)(2,1)}, bf16[4,80,640]{2,1,0:T(8,128)(2,1)}, bf16[4,80,640]{2,1,0:T(8,128)(2,1)}) custom-call(s32[5]{0:T(128)} %stack.160.coords, bf16[512,640]{1,0:T(8,128)(2,1)} %get-tuple-element.79.b_ref.left_ref, bf16[512,2560]{1,0:T(8,128)(2,1)} %get-tuple-element.121.right_ref), custom_call_target="tpu_custom_call" | custom-call | flops 1677721600 | bytes 6553620 | tf_op jit(solution)/shard_map/quarter_grad/pallas_call | solution.py:425
  338.6 6.7 %quarter_grad.6 = (bf16[2,2,4,80,640]{4,3,2,1,0:T(8,128)(2,1)}, bf16[2,4,80,640]{3,2,1,0:T(8,128)(2,1)}, bf16[4,80,640]{2,1,0:T(8,128)(2,1)}, bf16[4,80,640]{2,1,0:T(8,128)(2,1)}) custom-call(s32[5]{0:T(128)} %stack.160.coords, bf16[2,512,640]{2,1,0:T(8,128)(2,1)} %pad_maximum_fusion.2.left_ref, bf16[512,2560]{1,0:T(8,128)(2,1)} %get-tuple-element.116.right_ref), custom_call_target="tpu_custom_call" | custom-call | flops 1677721600 | bytes 7208980 | tf_op jit(solution)/shard_map/quarter_grad/pallas_call | solution.py:425
  345.7 5.9 %quarter_grad.5 = (bf16[2,2,4,80,640]{4,3,2,1,0:T(8,128)(2,1)}, bf16[2,4,80,640]{3,2,1,0:T(8,128)(2,1)}, bf16[4,80,640]{2,1,0:T(8,128)(2,1)}, bf16[4,80,640]{2,1,0:T(8,128)(2,1)}) custom-call(s32[5]{0:T(128)} %stack.160.coords, bf16[512,640]{1,0:T(8,128)(2,1)} %get-tuple-element.82.b_ref.left_ref, bf16[512,2560]{1,0:T(8,128)(2,1)} %get-tuple-element.110.right_ref), custom_call_target="tpu_custom_call" | custom-call | flops 1677721600 | bytes 6553620 | tf_op jit(solution)/shard_map/quarter_grad/pallas_call | solution.py:425
  353.0 6.0 %row_grad.3 = (bf16[2,2,4,80,640]{4,3,2,1,0:T(8,128)(2,1)}, bf16[2,4,80,640]{3,2,1,0:T(8,128)(2,1)}, bf16[4,80,640]{2,1,0:T(8,128)(2,1)}, bf16[4,80,640]{2,1,0:T(8,128)(2,1)}) custom-call(s32[5]{0:T(128)} %stack.160.coords, bf16[512,2560]{1,0:T(8,128)(2,1)} %get-tuple-element.84.z_ref.left_ref, bf16[512,640]{1,0:T(8,128)(2,1)} %get-tuple-element.131.right_ref), custom_call_target="tpu_custom_call" | custom-call | flops 1677721600 | bytes 6553620 | tf_op jit(solution)/shard_map/row_grad/pallas_call | solution.py:425
  360.6 6.6 %quarter_grad.4 = (bf16[2,2,4,80,640]{4,3,2,1,0:T(8,128)(2,1)}, bf16[2,4,80,640]{3,2,1,0:T(8,128)(2,1)}, bf16[4,80,640]{2,1,0:T(8,128)(2,1)}, bf16[4,80,640]{2,1,0:T(8,128)(2,1)}) custom-call(s32[5]{0:T(128)} %stack.160.coords, bf16[2,512,640]{2,1,0:T(8,128)(2,1)} %pad_maximum_fusion.1.left_ref, bf16[512,2560]{1,0:T(8,128)(2,1)} %get-tuple-element.101.right_ref), custom_call_target="tpu_custom_call" | custom-call | flops 1677721600 | bytes 7208980 | tf_op jit(solution)/shard_map/quarter_grad/pallas_call | solution.py:425
  369.1 5.9 %row_grad.2 = (bf16[2,2,4,80,640]{4,3,2,1,0:T(8,128)(2,1)}, bf16[2,4,80,640]{3,2,1,0:T(8,128)(2,1)}, bf16[4,80,640]{2,1,0:T(8,128)(2,1)}, bf16[4,80,640]{2,1,0:T(8,128)(2,1)}) custom-call(s32[5]{0:T(128)} %stack.160.coords, bf16[512,2560]{1,0:T(8,128)(2,1)} %get-tuple-element.92.z_ref.left_ref, bf16[512,640]{1,0:T(8,128)(2,1)} %get-tuple-element.126.right_ref), custom_call_target="tpu_custom_call" | custom-call | flops 1677721600 | bytes 6553620 | tf_op jit(solution)/shard_map/row_grad/pallas_call | solution.py:425
  385.6 12.7 %collective-permute-done.85 = bf16[2,4,80,640]{3,2,1,0:T(8,128)(2,1)S(1)} collective-permute-done((bf16[2,4,80,640]{3,2,1,0:T(8,128)(2,1)S(1)}, bf16[2,4,80,640]{3,2,1,0:T(8,128)(2,1)S(1)}, u32[]{:S(2)}, u32[]{:S(2)}) %collective-permute-start.85) | collective-permute-done | bytes 819232 | tf_op jit(solution)/shard_map/ppermute | solution.py:495
  400.5 15.3 %collective-permute-done.79 = bf16[2,4,80,640]{3,2,1,0:T(8,128)(2,1)S(1)} collective-permute-done((bf16[2,4,80,640]{3,2,1,0:T(8,128)(2,1)S(1)}, bf16[2,4,80,640]{3,2,1,0:T(8,128)(2,1)S(1)}, u32[]{:S(2)}, u32[]{:S(2)}) %collective-permute-start.79) | collective-permute-done | bytes 819232 | tf_op jit(solution)/shard_map/ppermute | solution.py:495
  418.3 14.3 %collective-permute-done.100 = bf16[2,4,80,640]{3,2,1,0:T(8,128)(2,1)S(1)} collective-permute-done((bf16[2,4,80,640]{3,2,1,0:T(8,128)(2,1)S(1)}, bf16[2,4,80,640]{3,2,1,0:T(8,128)(2,1)S(1)}, u32[]{:S(2)}, u32[]{:S(2)}) %collective-permute-start.100) | collective-permute-done | bytes 819232 | tf_op jit(solution)/shard_map/ppermute | solution.py:495
  436.6 11.8 %collective-permute-done.86 = bf16[4,80,640]{2,1,0:T(8,128)(2,1)S(1)} collective-permute-done((bf16[4,80,640]{2,1,0:T(8,128)(2,1)S(1)}, bf16[4,80,640]{2,1,0:T(8,128)(2,1)S(1)}, u32[]{:S(2)}, u32[]{:S(2)}) %collective-permute-start.86) | collective-permute-done | bytes 409632 | tf_op jit(solution)/shard_map/ppermute | solution.py:495
  451.4 5.7 %collective-permute-done.80 = bf16[4,80,640]{2,1,0:T(8,128)(2,1)S(1)} collective-permute-done((bf16[4,80,640]{2,1,0:T(8,128)(2,1)S(1)}, bf16[4,80,640]{2,1,0:T(8,128)(2,1)S(1)}, u32[]{:S(2)}, u32[]{:S(2)}) %collective-permute-start.80) | collective-permute-done | bytes 409632 | tf_op jit(solution)/shard_map/ppermute | solution.py:495
  459.0 5.5 %collective-permute-done.101 = bf16[4,80,640]{2,1,0:T(8,128)(2,1)S(1)} collective-permute-done((bf16[4,80,640]{2,1,0:T(8,128)(2,1)S(1)}, bf16[4,80,640]{2,1,0:T(8,128)(2,1)S(1)}, u32[]{:S(2)}, u32[]{:S(2)}) %collective-permute-start.101) | collective-permute-done | bytes 409632 | tf_op jit(solution)/shard_map/ppermute | solution.py:495
  (452 shorter events, 229.3 us)
Async XLA Ops:
  20.6 23.8 %collective-permute-start.55 = (bf16[80,640]{1,0:T(8,128)(2,1)S(1)}, bf16[80,640]{1,0:T(8,128)(2,1)S(1)}, u32[]{:S(2)}, u32[]{:S(2)}) collective-permute-start(bf16[80,640]{1,0:T(8,128)(2,1)S(1)} %reshape_squeeze.23), channel_id=1, source_target_pairs={{0,24},{2,26},{4,28},{6,30},{8,16},{10,18},{12,20},{14,22},{16,8},... | collective-permute-start | bytes 307208 | tf_op jit(solution)/shard_map/ppermute | solution.py:495
  44.3 26.8 %collective-permute-start.6 = (bf16[4,96,640]{2,1,0:T(8,128)(2,1)S(1)}, bf16[4,96,640]{2,1,0:T(8,128)(2,1)S(1)}, u32[]{:S(2)}, u32[]{:S(2)}) collective-permute-start(bf16[4,96,640]{2,1,0:T(8,128)(2,1)S(1)} %pad_maximum_fusion.6.refs_0_), channel_id=1, source_target_pairs={{0,4},{2,6},{4,0},{6,2},{8,12},{10,14},{12,8},{14,10},{16,20},{18,... | collective-permute-start | bytes 1474568 | tf_op jit(solution)/shard_map/ppermute | solution.py:495
  144.9 36.7 %collective-permute-start.41 = (bf16[4,80,640]{2,1,0:T(8,128)(2,1)}, bf16[4,80,640]{2,1,0:T(8,128)(2,1)S(1)}, u32[]{:S(2)}, u32[]{:S(2)}) collective-permute-start(bf16[4,80,640]{2,1,0:T(8,128)(2,1)} %collective-permute-done.39.refs_4_), channel_id=1, source_target_pairs={{0,1},{1,0},{2,3},{3,2},{4,5},{5,4},{6,7},{7,6},{8,9},{9,8},{10,11... | collective-permute-start | bytes 1228808 | tf_op jit(solution)/shard_map/ppermute | solution.py:495
  151.5 30.8 %collective-permute-start.50 = (bf16[4,80,640]{2,1,0:T(8,128)(2,1)}, bf16[4,80,640]{2,1,0:T(8,128)(2,1)S(1)}, u32[]{:S(2)}, u32[]{:S(2)}) collective-permute-start(bf16[4,80,640]{2,1,0:T(8,128)(2,1)} %collective-permute-done.46.refs_1_), channel_id=1, source_target_pairs={{0,2},{2,0},{4,6},{6,4},{8,10},{10,8},{12,14},{14,12},{16,18},{18,... | collective-permute-start | bytes 1228808 | tf_op jit(solution)/shard_map/ppermute | solution.py:495
  152.8 29.5 %collective-permute-start.32 = (bf16[4,80,640]{2,1,0:T(8,128)(2,1)}, bf16[4,80,640]{2,1,0:T(8,128)(2,1)S(1)}, u32[]{:S(2)}, u32[]{:S(2)}) collective-permute-start(bf16[4,80,640]{2,1,0:T(8,128)(2,1)} %collective-permute-done.30.refs_13_), channel_id=1, source_target_pairs={{0,1},{1,0},{2,3},{3,2},{4,5},{5,4},{6,7},{7,6},{8,9},{9,8},{10,11... | collective-permute-start | bytes 1228808 | tf_op jit(solution)/shard_map/ppermute | solution.py:495
  152.8 29.9 %collective-permute-start.22 = (bf16[4,80,640]{2,1,0:T(8,128)(2,1)}, bf16[4,80,640]{2,1,0:T(8,128)(2,1)S(1)}, u32[]{:S(2)}, u32[]{:S(2)}) collective-permute-start(bf16[4,80,640]{2,1,0:T(8,128)(2,1)} %collective-permute-done.20.refs_5_), channel_id=1, source_target_pairs={{0,1},{1,0},{2,3},{3,2},{4,5},{5,4},{6,7},{7,6},{8,9},{9,8},{10,11... | collective-permute-start | bytes 1228808 | tf_op jit(solution)/shard_map/ppermute | solution.py:495
  158.7 24.1 %collective-permute-start.42 = (bf16[4,80,640]{2,1,0:T(8,128)(2,1)}, bf16[4,80,640]{2,1,0:T(8,128)(2,1)S(1)}, u32[]{:S(2)}, u32[]{:S(2)}) collective-permute-start(bf16[4,80,640]{2,1,0:T(8,128)(2,1)} %collective-permute-done.40.refs_5_), channel_id=1, source_target_pairs={{0,1},{1,0},{2,3},{3,2},{4,5},{5,4},{6,7},{7,6},{8,9},{9,8},{10,11... | collective-permute-start | bytes 1228808 | tf_op jit(solution)/shard_map/ppermute | solution.py:495
  181.7 39.8 %collective-permute-start.61 = (bf16[4,80,640]{2,1,0:T(8,128)(2,1)}, bf16[4,80,640]{2,1,0:T(8,128)(2,1)S(1)}, u32[]{:S(2)}, u32[]{:S(2)}) collective-permute-start(bf16[4,80,640]{2,1,0:T(8,128)(2,1)} %collective-permute-done.59.refs_12_), channel_id=1, source_target_pairs={{0,1},{1,0},{2,3},{3,2},{4,5},{5,4},{6,7},{7,6},{8,9},{9,8},{10,11... | collective-permute-start | bytes 1228808 | tf_op jit(solution)/shard_map/ppermute | solution.py:495
  182.2 39.2 %collective-permute-start.48 = (bf16[4,80,640]{2,1,0:T(8,128)(2,1)}, bf16[4,80,640]{2,1,0:T(8,128)(2,1)S(1)}, u32[]{:S(2)}, u32[]{:S(2)}) collective-permute-start(bf16[4,80,640]{2,1,0:T(8,128)(2,1)} %collective-permute-done.46.refs_1_), channel_id=1, source_target_pairs={{0,1},{1,0},{2,3},{3,2},{4,5},{5,4},{6,7},{7,6},{8,9},{9,8},{10,11... | collective-permute-start | bytes 1228808 | tf_op jit(solution)/shard_map/ppermute | solution.py:495
  182.3 39.1 %collective-permute-start.51 = (bf16[4,80,640]{2,1,0:T(8,128)(2,1)}, bf16[4,80,640]{2,1,0:T(8,128)(2,1)S(1)}, u32[]{:S(2)}, u32[]{:S(2)}) collective-permute-start(bf16[4,80,640]{2,1,0:T(8,128)(2,1)} %collective-permute-done.49.refs_4_), channel_id=1, source_target_pairs={{0,1},{1,0},{2,3},{3,2},{4,5},{5,4},{6,7},{7,6},{8,9},{9,8},{10,11... | collective-permute-start | bytes 1228808 | tf_op jit(solution)/shard_map/ppermute | solution.py:495
  182.7 38.7 %collective-permute-start.62 = (bf16[4,80,640]{2,1,0:T(8,128)(2,1)}, bf16[4,80,640]{2,1,0:T(8,128)(2,1)S(1)}, u32[]{:S(2)}, u32[]{:S(2)}) collective-permute-start(bf16[4,80,640]{2,1,0:T(8,128)(2,1)} %collective-permute-done.60.refs_13_), channel_id=1, source_target_pairs={{0,1},{1,0},{2,3},{3,2},{4,5},{5,4},{6,7},{7,6},{8,9},{9,8},{10,11... | collective-permute-start | bytes 1228808 | tf_op jit(solution)/shard_map/ppermute | solution.py:495
  182.8 38.7 %collective-permute-start.52 = (bf16[4,80,640]{2,1,0:T(8,128)(2,1)S(1)}, bf16[4,80,640]{2,1,0:T(8,128)(2,1)S(1)}, u32[]{:S(2)}, u32[]{:S(2)}) collective-permute-start(bf16[4,80,640]{2,1,0:T(8,128)(2,1)S(1)} %collective-permute-done.50.refs_5_), channel_id=1, source_target_pairs={{0,1},{1,0},{2,3},{3,2},{4,5},{5,4},{6,7},{7,6},{8,9},{9,8},{10,11... | collective-permute-start | bytes 1228808 | tf_op jit(solution)/shard_map/ppermute | solution.py:495
  337.3 37.8 %collective-permute-start.84 = (bf16[2,2,4,80,640]{4,3,2,1,0:T(8,128)(2,1)}, bf16[2,2,4,80,640]{4,3,2,1,0:T(8,128)(2,1)}, u32[]{:S(2)}, u32[]{:S(2)}) collective-permute-start(bf16[2,2,4,80,640]{4,3,2,1,0:T(8,128)(2,1)} %get-tuple-element.123), channel_id=1, source_target_pairs={{0,1},{1,0},{2,3},{3,2},{4,5},{5,4},{6,7},{7,6},{8,9},{9,8},{10,11... | collective-permute-start | bytes 4915208 | tf_op jit(solution)/shard_map/ppermute | solution.py:495
  345.4 31.7 %collective-permute-start.78 = (bf16[2,2,4,80,640]{4,3,2,1,0:T(8,128)(2,1)}, bf16[2,2,4,80,640]{4,3,2,1,0:T(8,128)(2,1)S(1)}, u32[]{:S(2)}, u32[]{:S(2)}) collective-permute-start(bf16[2,2,4,80,640]{4,3,2,1,0:T(8,128)(2,1)} %get-tuple-element.118), channel_id=1, source_target_pairs={{0,1},{1,0},{2,3},{3,2},{4,5},{5,4},{6,7},{7,6},{8,9},{9,8},{10,11... | collective-permute-start | bytes 4915208 | tf_op jit(solution)/shard_map/ppermute | solution.py:495
  351.6 27.5 %collective-permute-start.72 = (bf16[2,2,4,80,640]{4,3,2,1,0:T(8,128)(2,1)}, bf16[2,2,4,80,640]{4,3,2,1,0:T(8,128)(2,1)S(1)}, u32[]{:S(2)}, u32[]{:S(2)}) collective-permute-start(bf16[2,2,4,80,640]{4,3,2,1,0:T(8,128)(2,1)} %get-tuple-element.112), channel_id=1, source_target_pairs={{0,1},{1,0},{2,3},{3,2},{4,5},{5,4},{6,7},{7,6},{8,9},{9,8},{10,11... | collective-permute-start | bytes 4915208 | tf_op jit(solution)/shard_map/ppermute | solution.py:495
  379.2 36.6 %collective-permute-start.79 = (bf16[2,4,80,640]{3,2,1,0:T(8,128)(2,1)S(1)}, bf16[2,4,80,640]{3,2,1,0:T(8,128)(2,1)S(1)}, u32[]{:S(2)}, u32[]{:S(2)}) collective-permute-start(bf16[2,4,80,640]{3,2,1,0:T(8,128)(2,1)S(1)} %fusion.4), channel_id=1, source_target_pairs={{0,4},{2,6},{4,0},{6,2},{8,12},{10,14},{12,8},{14,10},{16,20},{18,... | collective-permute-start | bytes 2457608 | tf_op jit(solution)/shard_map/ppermute | solution.py:495
  379.7 37.3 %collective-permute-start.73 = (bf16[2,4,80,640]{3,2,1,0:T(8,128)(2,1)S(1)}, bf16[2,4,80,640]{3,2,1,0:T(8,128)(2,1)S(1)}, u32[]{:S(2)}, u32[]{:S(2)}) collective-permute-start(bf16[2,4,80,640]{3,2,1,0:T(8,128)(2,1)S(1)} %fusion.5), channel_id=1, source_target_pairs={{0,2},{2,0},{4,6},{6,4},{8,10},{10,8},{12,14},{14,12},{16,18},{18,... | collective-permute-start | bytes 2457608 | tf_op jit(solution)/shard_map/ppermute | solution.py:495
  382.2 50.4 %collective-permute-start.100 = (bf16[2,4,80,640]{3,2,1,0:T(8,128)(2,1)S(1)}, bf16[2,4,80,640]{3,2,1,0:T(8,128)(2,1)S(1)}, u32[]{:S(2)}, u32[]{:S(2)}) collective-permute-start(bf16[2,4,80,640]{3,2,1,0:T(8,128)(2,1)S(1)} %fusion.1), channel_id=1, source_target_pairs={{0,4},{2,6},{4,0},{6,2},{8,12},{10,14},{12,8},{14,10},{16,20},{18,... | collective-permute-start | bytes 2457608 | tf_op jit(solution)/shard_map/ppermute | solution.py:495
  384.0 51.6 %collective-permute-start.94 = (bf16[2,4,80,640]{3,2,1,0:T(8,128)(2,1)S(1)}, bf16[2,4,80,640]{3,2,1,0:T(8,128)(2,1)S(1)}, u32[]{:S(2)}, u32[]{:S(2)}) collective-permute-start(bf16[2,4,80,640]{3,2,1,0:T(8,128)(2,1)S(1)} %fusion.2), channel_id=1, source_target_pairs={{0,2},{2,0},{4,6},{6,4},{8,10},{10,8},{12,14},{14,12},{16,18},{18,... | collective-permute-start | bytes 2457608 | tf_op jit(solution)/shard_map/ppermute | solution.py:495
  398.3 68.7 %collective-permute-start.64 = (bf16[2,4,96,640]{3,2,1,0:T(8,128)(2,1)S(1)}, bf16[2,4,96,640]{3,2,1,0:T(8,128)(2,1)S(1)}, u32[]{:S(2)}, u32[]{:S(2)}) collective-permute-start(bf16[2,4,96,640]{3,2,1,0:T(8,128)(2,1)S(1)} %fusion), channel_id=1, source_target_pairs={{0,2},{2,0},{4,6},{6,4},{8,10},{10,8},{12,14},{14,12},{16,18},{18,... | collective-permute-start | bytes 2949128 | tf_op jit(solution)/shard_map/ppermute | solution.py:495
  415.8 32.5 %collective-permute-start.86 = (bf16[4,80,640]{2,1,0:T(8,128)(2,1)S(1)}, bf16[4,80,640]{2,1,0:T(8,128)(2,1)S(1)}, u32[]{:S(2)}, u32[]{:S(2)}) collective-permute-start(bf16[4,80,640]{2,1,0:T(8,128)(2,1)S(1)} %fusion.12), channel_id=1, source_target_pairs={{0,2},{2,0},{4,6},{6,4},{8,10},{10,8},{12,14},{14,12},{16,18},{18,... | collective-permute-start | bytes 1228808 | tf_op jit(solution)/shard_map/ppermute | solution.py:495
  417.0 40.1 %collective-permute-start.80 = (bf16[4,80,640]{2,1,0:T(8,128)(2,1)S(1)}, bf16[4,80,640]{2,1,0:T(8,128)(2,1)S(1)}, u32[]{:S(2)}, u32[]{:S(2)}) collective-permute-start(bf16[4,80,640]{2,1,0:T(8,128)(2,1)S(1)} %fusion.14), channel_id=1, source_target_pairs={{0,2},{2,0},{4,6},{6,4},{8,10},{10,8},{12,14},{14,12},{16,18},{18,... | collective-permute-start | bytes 1228808 | tf_op jit(solution)/shard_map/ppermute | solution.py:495
  432.6 25.4 %collective-permute-start.74 = (bf16[4,80,640]{2,1,0:T(8,128)(2,1)S(1)}, bf16[4,80,640]{2,1,0:T(8,128)(2,1)S(1)}, u32[]{:S(2)}, u32[]{:S(2)}) collective-permute-start(bf16[4,80,640]{2,1,0:T(8,128)(2,1)S(1)} %fusion.16), channel_id=1, source_target_pairs={{0,4},{2,6},{4,0},{6,2},{8,12},{10,14},{12,8},{14,10},{16,20},{18,... | collective-permute-start | bytes 1228808 | tf_op jit(solution)/shard_map/ppermute | solution.py:495
  435.6 29.0 %collective-permute-start.101 = (bf16[4,80,640]{2,1,0:T(8,128)(2,1)S(1)}, bf16[4,80,640]{2,1,0:T(8,128)(2,1)S(1)}, u32[]{:S(2)}, u32[]{:S(2)}) collective-permute-start(bf16[4,80,640]{2,1,0:T(8,128)(2,1)S(1)} %fusion.8), channel_id=1, source_target_pairs={{0,2},{2,0},{4,6},{6,4},{8,10},{10,8},{12,14},{14,12},{16,18},{18,... | collective-permute-start | bytes 1228808 | tf_op jit(solution)/shard_map/ppermute | solution.py:495
  (137 other events, 2279.4 us)

commit v2 on v1

v2 whole, which is shorter than its diff:
```python
import functools

import jax
import jax.numpy as jnp
import numpy as np
from jax import lax
from jax.experimental import pallas as pl
from jax.experimental.pallas import tpu as pltpu
from jax.sharding import PartitionSpec as P

D = 640
HEADS = 20
HEAD_DIM = 32
FF = 2560
LAYERS = 2
EPSILON = 1e-05
MASKED = -1e9
LANES = 128
GROUPS = D // LANES
PER_GROUP = LANES // HEAD_DIM
BLOCKS = FF // D
PIECE = 80
VECS = 16
ROWS = 256
AXES = ("wide", "narrow")
VMEM_LIMIT = 56 * 1024 * 1024
f32, bf16 = jnp.float32, jnp.bfloat16

GAIN_A, GAIN_F, SHIFT_A, BIAS_QKV, BIAS_OUT, SHIFT_F, BIAS_UP, BIAS_DOWN = 0, 1, 2, 3, 6, 7, 8, 12


def rotary_tables(length):
    half = HEAD_DIM // 2
    inverse = 1.0 / 10000.0 ** (np.arange(half) * (2.0 / HEAD_DIM))
    angles = np.arange(length)[:, None] * inverse[None, :]
    cos = np.tile(np.cos(angles), (1, 2 * PER_GROUP))
    sine = np.sin(angles)
    none = np.zeros_like(sine)
    ahead = np.tile(np.concatenate([-sine, none], 1), (1, PER_GROUP))
    behind = np.tile(np.concatenate([none, sine], 1), (1, PER_GROUP))
    return np.stack([cos, ahead, behind]).astype(np.float32)


def dot(left, right):
    return jnp.dot(left, right, preferred_element_type=f32)


def dot_nt(left, right):
    return lax.dot_general(left, right, (((1,), (1,)), ((), ())), preferred_element_type=f32)


def dot_tn(left, right):
    return lax.dot_general(left, right, (((0,), (0,)), ((), ())), preferred_element_type=f32)


def rolled(value, table, rows, sign):
    half = HEAD_DIM // 2
    turned = pltpu.roll(value, LANES - half, 1) * table[1, rows, :] + pltpu.roll(value, half, 1) * table[2, rows, :]
    return value * table[0, rows, :] + (turned if sign > 0 else -turned)


def unit_of(value):
    centered = value - jnp.mean(value, -1, keepdims=True)
    inverse = lax.rsqrt(jnp.mean(centered * centered, -1, keepdims=True) + EPSILON)
    return centered * inverse, inverse


def norm_back(grad, unit, inverse, gain):
    scaled = grad * gain
    return inverse * (scaled - jnp.mean(scaled, -1, keepdims=True) - unit * jnp.mean(scaled * unit, -1, keepdims=True))


def column_sum(value):
    return jnp.sum(value, 0, keepdims=True)


def gelu_parts(value):
    scaled = jnp.abs(value) * 0.7071067811865476
    t = 1.0 / (1.0 + 0.3275911 * scaled)
    bell = jnp.exp(-scaled * scaled)
    series = t * (0.127414796 + t * (-0.142248368 + t * (0.7107068705 + t * (-0.7265760135 + t * 0.5307027145))))
    tail = series * bell
    return jnp.where(value >= 0.0, 1.0 - tail, tail), bell * 0.3989422804014327


def three_parts(value):
    first = value.astype(bf16)
    rest = value - first.astype(f32)
    second = rest.astype(bf16)
    third = (rest - second.astype(f32)).astype(bf16)
    return first, second, third


def spread(value):
    lane = lax.broadcasted_iota(jnp.int32, value.shape, 1) % HEAD_DIM
    first, second, third = three_parts(value)
    tail = jnp.where(lane == 3, 1.0, 0.0)
    out = jnp.where(lane == 2, third.astype(f32), tail)
    out = jnp.where(lane == 1, second.astype(f32), out)
    return jnp.where(lane == 0, first.astype(f32), out).astype(bf16)


def row_loop(length, step, body):
    def run(i, carry):
        body(pl.ds(pl.multiple_of(i * step, step), step), i)
        return carry

    lax.fori_loop(0, length // step, run, 0)


def blocks_of(coords, first):
    for kb in range(2):
        for kn in range(2):
            for ka in range(2):
                for kz in range(4):
                    kx, ky = (ka, kb) if first == "x" else (kb, ka)
                    yield 2 * kb + kn, 4 * ka + kz, coords[0] ^ kz, coords[1] ^ ky, coords[2] ^ kx, coords[3] ^ kn


def quarter_copies(coords, first, pieces, whole, sems):
    copies = []
    for piece, block, z, y, x, n in blocks_of(coords, first):
        rows = pl.ds(pl.multiple_of((2 * z + y) * PIECE, PIECE), PIECE)
        columns = pl.ds(pl.multiple_of((2 * x + n) * D, D), D)
        copies.append(
            pltpu.make_async_copy(
                pieces[piece].at[block, pl.ds(0, PIECE)], whole.at[rows, columns], sems.at[8 * piece + block]
            )
        )
    return copies


def row_copies(coords, first, pieces, whole, sems):
    copies = []
    for piece, block, z, y, x, n in blocks_of(coords, first):
        rows = pl.ds(pl.multiple_of((8 * z + 4 * y + 2 * x + n) * PIECE, PIECE), PIECE)
        copies.append(pltpu.make_async_copy(pieces[piece].at[block], whole.at[rows], sems.at[8 * piece + block]))
    return copies


def head_masks():
    lane = lax.broadcasted_iota(jnp.int32, (1, LANES), 1)
    return [(lane // HEAD_DIM == head).astype(f32).astype(bf16) for head in range(PER_GROUP)]


def key_tail(length, live, head):
    lane = lax.broadcasted_iota(jnp.int32, (length, LANES), 1)
    row = lax.broadcasted_iota(jnp.int32, (length, LANES), 0)
    base = head * HEAD_DIM
    ones = jnp.where((lane >= base) & (lane < base + 3), 1.0, 0.0)
    return jnp.where((lane == base + 3) & (row >= live), MASKED, ones).astype(bf16)


def attn_fwd_kernel(first, coords, x_ref, vec_ref, table_ref, *refs):
    pieces, refs = refs[:4], refs[4:]
    at_ref, qkv_ref, o_ref, ot_ref, lse_ref, m_ref, b_ref, bt_ref, a_ref, w_ref, key_ref, val_ref, sems = refs
    length = x_ref.shape[0]
    copies = quarter_copies(coords, first, pieces, w_ref, sems)
    for copy in copies:
        copy.start()

    def norm(rows, _):
        unit, _ = unit_of(x_ref[rows, :].astype(f32))
        a_ref[rows, :] = (unit * vec_ref[GAIN_A : GAIN_A + 1, :] + vec_ref[SHIFT_A : SHIFT_A + 1, :]).astype(bf16)

    row_loop(length, 128, norm)
    for copy in copies:
        copy.wait()

    def project(rows, _):
        normed = a_ref[rows, :]
        for part in range(3):
            out = dot(normed, w_ref[:, part * D : (part + 1) * D]) + vec_ref[BIAS_QKV + part : BIAS_QKV + part + 1, :]
            if part == 0:
                out = out * HEAD_DIM**-0.5
            for group in range(GROUPS):
                piece = out[:, group * LANES : (group + 1) * LANES]
                if part < 2:
                    piece = rolled(piece, table_ref, rows, 1)
                qkv_ref[rows, part * D + group * LANES : part * D + (group + 1) * LANES] = piece.astype(bf16)

    row_loop(length, ROWS, project)
    live = coords[4]
    masks = head_masks()
    for head in range(PER_GROUP):
        key_ref[head, :, LANES:] = key_tail(length, live, head)
        val_ref[head, :, LANES:] = jnp.broadcast_to(masks[head], (length, LANES))

    def group_step(group, carry):
        at = [pl.ds(pl.multiple_of(part * D + group * LANES, LANES), LANES) for part in range(3)]
        for head in range(PER_GROUP):
            key_ref[head, :, :LANES] = qkv_ref[:, at[1]] * masks[head]
            val_ref[head, :, :LANES] = qkv_ref[:, at[2]] * masks[head]

        def rows_step(rows, _):
            lane = lax.broadcasted_iota(jnp.int32, (ROWS, LANES), 1)
            tail = jnp.where(lane % HEAD_DIM == 3, 1.0, 0.0).astype(bf16)
            query = jnp.concatenate([qkv_ref[rows, at[0]], tail], 1)
            total = jnp.zeros((ROWS, 2 * LANES), f32)
            tops = jnp.zeros((ROWS, LANES), f32)
            for head in range(PER_GROUP):
                scores = dot_nt(query, key_ref[head])
                top = jnp.max(scores, -1, keepdims=True)
                total = total + dot(jnp.exp(scores - top).astype(bf16), val_ref[head])
                tops = jnp.where(lane // HEAD_DIM == head, top, tops)
            o_ref[rows, at[0]] = (total[:, :LANES] / total[:, LANES:]).astype(bf16)
            lse_ref[rows, at[0]] = spread(-(tops + jnp.log(total[:, LANES:])))

        row_loop(length, ROWS, rows_step)
        return carry

    lax.fori_loop(0, GROUPS, group_step, 0)

    def after(rows, _):
        middle = x_ref[rows, :].astype(f32) + (dot(o_ref[rows, :], w_ref[:, 3 * D :]) + vec_ref[BIAS_OUT : BIAS_OUT + 1, :])
        m_ref[rows, :] = middle
        unit, _ = unit_of(middle)
        b_ref[rows, :] = (unit * vec_ref[GAIN_F : GAIN_F + 1, :] + vec_ref[SHIFT_F : SHIFT_F + 1, :]).astype(bf16)

    row_loop(length, ROWS, after)
    at_ref[...] = a_ref[...].T
    ot_ref[...] = o_ref[...].T
    bt_ref[...] = b_ref[...].T


def ffn_fwd_kernel(first, last, coords, m_ref, b_ref, vec_ref, *refs):
    up_pieces, down_pieces, refs = refs[:4], refs[4:8], refs[8:]
    y_ref, zt_ref, slope_ref, z_ref, up_ref, down_ref, up_sems, down_sems = refs
    length = m_ref.shape[0]
    copies = quarter_copies(coords, first[0], up_pieces, up_ref, up_sems)
    copies_down = row_copies(coords, first[1], down_pieces, down_ref, down_sems)
    for copy in copies + copies_down:
        copy.start()
    for copy in copies + copies_down:
        copy.wait()

    def step(rows, i):
        normed = b_ref[rows, :]
        for block in range(BLOCKS):
            columns = slice(block * D, (block + 1) * D)
            pre = dot(normed, up_ref[:, columns]) + vec_ref[BIAS_UP + block : BIAS_UP + block + 1, :]
            cdf, bell = gelu_parts(pre)
            z_ref[rows, columns] = (pre * cdf).astype(bf16)
            slope_ref[rows, columns] = (cdf + pre * bell).astype(bf16)
        out = m_ref[rows, :] + (dot(z_ref[rows, :], down_ref[...]) + vec_ref[BIAS_DOWN : BIAS_DOWN + 1, :])
        if last:
            row = lax.broadcasted_iota(jnp.int32, (ROWS, 1), 0) + i * ROWS
            out = jnp.where(row < coords[4], out, 0.0)
        y_ref[rows, :] = out.astype(y_ref.dtype)

    row_loop(length, ROWS, step)
    for block in range(BLOCKS):
        columns = slice(block * D, (block + 1) * D)
        zt_ref[columns, :] = z_ref[:, columns].T


def ffn_bwd_kernel(first, top, coords, g_ref, slope_ref, m_ref, vec_ref, *refs):
    up_pieces, down_pieces, refs = refs[:4], refs[4:8], refs[8:]
    gb_ref, gu_ref, gm_ref, gmb_ref, sums_ref, up_ref, down_ref, up_sems, down_sems = refs
    length = m_ref.shape[0]
    copies = quarter_copies(coords, first[0], up_pieces, up_ref, up_sems)
    copies_down = row_copies(coords, first[1], down_pieces, down_ref, down_sems)
    for copy in copies_down + copies:
        copy.start()
    for copy in copies_down + copies:
        copy.wait()
    sums_ref[...] = jnp.zeros_like(sums_ref)

    def add(row, value):
        sums_ref[row : row + 1, :] += column_sum(value)

    def step(rows, i):
        grad = g_ref[rows, :].astype(f32)
        if top:
            row = lax.broadcasted_iota(jnp.int32, (ROWS, 1), 0) + i * ROWS
            grad = jnp.where(row < coords[4], grad, 0.0)
        low = grad.astype(bf16)
        gb_ref[rows, :] = low
        add(BIAS_DOWN, low.astype(f32))
        for block in range(BLOCKS):
            columns = slice(block * D, (block + 1) * D)
            back = dot_nt(low, down_ref[columns, :]) * slope_ref[rows, columns].astype(f32)
            part = back.astype(bf16)
            gu_ref[rows, columns] = part
            add(BIAS_UP + block, part.astype(f32))
        normed_grad = dot_nt(gu_ref[rows, :], up_ref[...])
        unit, inverse = unit_of(m_ref[rows, :])
        add(GAIN_F, normed_grad * unit)
        add(SHIFT_F, normed_grad)
        middle = grad + norm_back(normed_grad, unit, inverse, vec_ref[GAIN_F : GAIN_F + 1, :])
        gm_ref[rows, :] = middle
        low = middle.astype(bf16)
        gmb_ref[rows, :] = low
        add(BIAS_OUT, low.astype(f32))

    row_loop(length, ROWS, step)


def attn_bwd_kernel(first, coords, gmb_ref, qkv_ref, o_ref, lse_ref, table_ref, *refs):
    pieces, refs = refs[:4], refs[4:]
    gpm_ref, w_ref, go_ref, key_ref, val_ref, q_ref, g_ref, dq_ref, sems = refs
    length = gmb_ref.shape[0]
    copies = quarter_copies(coords, first, pieces, w_ref, sems)
    for copy in copies:
        copy.start()
    for copy in copies:
        copy.wait()

    def back(rows, _):
        low = gmb_ref[rows, :]
        gpm_ref[rows, 3 * D :] = low
        go_ref[rows, :] = dot_nt(low, w_ref[:, 3 * D :]).astype(bf16)

    row_loop(length, ROWS, back)
    live = coords[4]
    masks = head_masks()
    head_of = lax.broadcasted_iota(jnp.int32, (LANES, LANES), 0) // HEAD_DIM
    same = (head_of == lax.broadcasted_iota(jnp.int32, (LANES, LANES), 1) // HEAD_DIM).astype(f32).astype(bf16)
    for head in range(PER_GROUP):
        key_ref[head, :, LANES:] = key_tail(length, live, head)
        val_ref[head, :, LANES:] = key_tail(length, length, head)

    def group_step(group, carry):
        at = [pl.ds(pl.multiple_of(part * D + group * LANES, LANES), LANES) for part in range(3)]
        grad = go_ref[:, at[0]]
        query = qkv_ref[:, at[0]]
        product = grad.astype(f32) * o_ref[:, at[0]].astype(f32)
        high = product.astype(bf16)
        rest = (product - high.astype(f32)).astype(bf16)
        deltas = dot(high, same) + dot(rest, same)
        for head in range(PER_GROUP):
            key_ref[head, :, :LANES] = qkv_ref[:, at[1]] * masks[head]
            val_ref[head, :, :LANES] = qkv_ref[:, at[2]] * masks[head]
            q_ref[head] = query * masks[head]
            g_ref[head] = grad * masks[head]
        query_wide = jnp.concatenate([query, lse_ref[:, at[0]]], 1)
        grad_wide = jnp.concatenate([grad, spread(-deltas)], 1)
        dq_ref[...] = jnp.zeros_like(dq_ref)

        def rows_step(rows, _):
            dk = jnp.zeros((ROWS, LANES), f32)
            dv = jnp.zeros((ROWS, LANES), f32)
            for head in range(PER_GROUP):
                key = key_ref[head, rows, :]
                probs = jnp.exp(dot_nt(key, query_wide))
                scores = (probs * dot_nt(val_ref[head, rows, :], grad_wide)).astype(bf16)
                dv = dv + dot(probs.astype(bf16), g_ref[head])
                dk = dk + dot(scores, q_ref[head])
                dq_ref[...] += dot_tn(scores, key[:, :LANES])
            dk = rolled(dk.astype(bf16).astype(f32), table_ref, rows, -1)
            gpm_ref[rows, at[1]] = dk.astype(bf16)
            gpm_ref[rows, at[2]] = dv.astype(bf16)

        row_loop(length, ROWS, rows_step)

        def last_step(rows, _):
            dq = rolled(dq_ref[rows, :].astype(bf16).astype(f32), table_ref, rows, -1) * HEAD_DIM**-0.5
            gpm_ref[rows, at[0]] = dq.astype(bf16)

        row_loop(length, ROWS, last_step)
        return carry

    lax.fori_loop(0, GROUPS, group_step, 0)


def attn_after_kernel(first, coords, gpm_ref, gm_ref, x_ref, vec_ref, *refs):
    pieces, refs = refs[:4], refs[4:]
    gx_ref, sums_ref, w_ref, sems = refs
    length = x_ref.shape[0]
    copies = quarter_copies(coords, first, pieces, w_ref, sems)
    for copy in copies:
        copy.start()
    for copy in copies:
        copy.wait()
    sums_ref[...] = jnp.zeros_like(sums_ref)

    def add(row, value):
        sums_ref[row : row + 1, :] += column_sum(value)

    def after(rows, _):
        for part in range(3):
            add(BIAS_QKV + part, gpm_ref[rows, part * D : (part + 1) * D].astype(f32))
        normed_grad = dot_nt(gpm_ref[rows, : 3 * D], w_ref[:, : 3 * D])
        unit, inverse = unit_of(x_ref[rows, :].astype(f32))
        add(GAIN_A, normed_grad * unit)
        add(SHIFT_A, normed_grad)
        out = gm_ref[rows, :] + norm_back(normed_grad, unit, inverse, vec_ref[GAIN_A : GAIN_A + 1, :])
        gx_ref[rows, :] = out.astype(gx_ref.dtype)

    row_loop(length, ROWS, after)


def grads_kernel(plan, phase, coords, *refs):
    items, inputs, halves = plan
    offset = halves[0]
    ins, rest = refs[:inputs], refs[inputs:]
    left_ref, rest = rest[-1], rest[:-1]
    for kind, lefts, right, cuts in items:
        if kind == "rest":
            block = ins[right]

            def value_of(kx, ky, kz, block=block):
                return block[phase, kx, ky, kz]

            put(rest, phase, offset, value_of, cuts)
            continue
        if kind == "down":
            for kx in range(2):
                for ky in range(2):
                    for kz in range(4):
                        z, y, x, n = coords[0] ^ kz, coords[1] ^ ky, coords[2] ^ kx, coords[3] ^ phase
                        start = pl.multiple_of((8 * z + 4 * y + 2 * x + n) * PIECE, PIECE)
                        to = (8 * kx + 4 * ky + kz) * PIECE
                        left_ref[to : to + PIECE, :] = ins[lefts[0]][pl.ds(start, PIECE), :]
            for kx in range(2):
                whole = dot(left_ref[kx * D : (kx + 1) * D, :], ins[right][...]).astype(bf16)
                put(rest, phase, offset, functools.partial(block_of, whole), cuts, kx)
            continue
        for i, left in enumerate(lefts):
            for ky in range(2):
                for kz in range(4):
                    start = pl.multiple_of((2 * (coords[0] ^ kz) + (coords[1] ^ ky)) * PIECE, PIECE)
                    to = i * D + (4 * ky + kz) * PIECE
                    left_ref[to : to + PIECE, :] = ins[left][pl.ds(start, PIECE), :]
        for kx in range(2):
            quarter = 2 * (coords[2] ^ kx) + (coords[3] ^ phase)
            columns = pl.ds(pl.multiple_of(quarter * D, D), D)
            if len(lefts) > 1:
                left = left_ref[pl.ds(pl.multiple_of(quarter // 3 * D, D), D), :]
            else:
                left = left_ref[:D, :]
            whole = dot(left, ins[right][:, columns]).astype(bf16)
            put(rest, phase, offset, functools.partial(block_of, whole), cuts, kx)


def block_of(whole, kx, ky, kz):
    start = (4 * ky + kz) * PIECE
    return whole[start : start + PIECE]


def put(outs, phase, offset, value_of, cuts, only=None):
    for kx in range(2) if only is None else (only,):
        for ky in range(2):
            for kz in range(4):
                value = value_of(kx, ky, kz)
                for half, to, start, rows in cuts:
                    ka, kb = (ky, kx) if half else (kx, ky)
                    begin = to + (offset if phase and half else 0)
                    part, at = value[start : start + rows], slice(begin, begin + rows)
                    if phase:
                        outs[0][ka, kb, kz, at] = part
                    elif ka:
                        outs[3 * half][kb, kz, at] = part
                    elif kb:
                        outs[3 * half + 1][kz, at] = part
                    else:
                        outs[3 * half + 2][kz, at] = part


def call(kernel, ins, outs, scratch, name, flops, exps=0):
    moved = sum(a.size * a.dtype.itemsize for a, _ in ins) + sum(int(np.prod(s)) * jnp.dtype(t).itemsize for s, t in outs)
    return pl.pallas_call(
        kernel,
        out_shape=[jax.ShapeDtypeStruct(s, t) for s, t in outs],
        in_specs=[pl.BlockSpec(memory_space=space) for _, space in ins],
        out_specs=[pl.BlockSpec(memory_space=pltpu.VMEM)] * len(outs),
        scratch_shapes=scratch,
        compiler_params=pltpu.CompilerParams(vmem_limit_bytes=VMEM_LIMIT),
        cost_estimate=pl.CostEstimate(flops=int(flops), bytes_accessed=int(moved), transcendentals=int(exps)),
        name=name,
    )(*[a for a, _ in ins])


V, S, H = pltpu.VMEM, pltpu.SMEM, pl.ANY
SEMS = pltpu.SemaphoreType.DMA


def attn_fwd(coords, x, vec, table, weight):
    pieces, first = weight
    n = x.shape[0]
    ins = [(coords, S), (x, V), (vec, V), (table, V)] + [(p, H) for p in pieces]
    outs = [((D, n), bf16), ((n, 3 * D), bf16), ((n, D), bf16), ((D, n), bf16), ((n, D), bf16)]
    outs += [((n, D), f32), ((n, D), bf16), ((D, n), bf16)]
    wide = V((PER_GROUP, n, 2 * LANES), bf16)
    scratch = [V((n, D), bf16), V((D, FF), bf16), wide, wide, SEMS((32,))]
    kernel = functools.partial(attn_fwd_kernel, first)
    out = call(kernel, ins, outs, scratch, "attn_fwd", 2 * n * D * FF + 4 * n * n * D, HEADS * n * n)
    return dict(zip(("at", "qkv", "o", "ot", "lse", "m", "b", "bt"), out, strict=True)) | {"x": x}


def ffn_fwd(coords, kept, vec, up, down, last):
    m, b = kept["m"], kept["b"]
    n = m.shape[0]
    ins = [(coords, S), (m, V), (b, V), (vec, V)] + [(p, H) for p in up[0] + down[0]]
    outs = [((n, D), bf16 if last else f32), ((FF, n), bf16), ((n, FF), bf16)]
    scratch = [V((n, FF), bf16), V((D, FF), bf16), V((FF, D), bf16), SEMS((32,)), SEMS((32,))]
    kernel = functools.partial(ffn_fwd_kernel, (up[1], down[1]), last)
    y, zt, slope = call(kernel, ins, outs, scratch, "ffn_fwd", 4 * n * D * FF, 2 * n * FF)
    return y, {"zt": zt, "slope": slope}


def ffn_bwd(coords, g, kept, vec, up, down, top):
    slope, m = kept["slope"], kept["m"]
    n = m.shape[0]
    ins = [(coords, S), (g, V), (slope, V), (m, V), (vec, V)] + [(p, H) for p in up[0] + down[0]]
    outs = [((n, D), bf16), ((n, FF), bf16), ((n, D), f32), ((n, D), bf16), ((VECS, D), f32)]
    scratch = [V((D, FF), bf16), V((FF, D), bf16), SEMS((32,)), SEMS((32,))]
    kernel = functools.partial(ffn_bwd_kernel, (up[1], down[1]), top)
    out = call(kernel, ins, outs, scratch, "ffn_bwd", 4 * n * D * FF, 0)
    return dict(zip(("gb", "gu", "gm", "gmb", "sums"), out, strict=True))


def attn_bwd(coords, gmb, kept, table, weight):
    pieces, first = weight
    n = gmb.shape[0]
    ins = [(coords, S)] + [(a, V) for a in (gmb, kept["qkv"], kept["o"], kept["lse"], table)] + [(p, H) for p in pieces]
    wide, thin = V((PER_GROUP, n, 2 * LANES), bf16), V((PER_GROUP, n, LANES), bf16)
    scratch = [V((D, FF), bf16), V((n, D), bf16), wide, wide, thin, thin, V((n, LANES), f32), SEMS((32,))]
    kernel = functools.partial(attn_bwd_kernel, first)
    return call(kernel, ins, [((n, FF), bf16)], scratch, "attn_bwd", 2 * n * D * D + 10 * n * n * D, HEADS * n * n)[0]


def attn_after(coords, back, kept, vec, weight, last):
    gpm, gm, x = back["gpm"], back["gm"], kept["x"]
    pieces, first = weight
    n = x.shape[0]
    ins = [(coords, S)] + [(a, V) for a in (gpm, gm, x, vec)] + [(p, H) for p in pieces]
    outs = [((n, D), bf16 if last else f32), ((VECS, D), f32)]
    kernel = functools.partial(attn_after_kernel, first)
    return call(kernel, ins, outs, [V((D, FF), bf16), SEMS((32,))], "attn_after", 6 * n * D * D, 0)


def grads(coords, items, halves, phase):
    arrays, plan, flops = [], [], 0
    for kind, lefts, right, cuts in items:
        index = list(range(len(arrays), len(arrays) + len(lefts)))
        arrays += [*lefts, right]
        plan.append((kind, index, index[-1] + 1 if lefts else len(arrays) - 1, cuts))
        if lefts:
            flops += right.shape[0] * D * FF
    if phase:
        outs = [((2, 2, 4, sum(halves), D), bf16)]
    else:
        outs = [((*lead, rows, D), bf16) for rows in halves for lead in ((2, 4), (4,), (4,))]
    n = arrays[0].shape[1]
    kernel = functools.partial(grads_kernel, (plan, len(arrays), halves), phase)
    ins = [(coords, S)] + [(a, V) for a in arrays]
    return call(kernel, ins, outs, [V((2 * D, n), bf16)], "grads", flops, 0)


def swap(axis_name, bit):
    size = lax.axis_size(axis_name)
    pairs = [(i, i ^ bit) for i in range(size)]
    return lambda value: lax.ppermute(value, axis_name, pairs)


def mate(value):
    return swap("narrow", 1)(value)


def along(axis, value):
    return swap("wide", {"x": 1, "y": 2, "z0": 4, "z1": 8}[axis])(value)


def other(axis):
    return "x" if axis == "y" else "y"


def together(*values):
    return lax.optimization_barrier(values)


def relative(values, bits):
    for place_of, bit in enumerate(reversed(bits)):
        step = 1 << place_of
        values = [jnp.where(bit > 0, values[i ^ step], values[i]) for i in range(len(values))]
    return values


def add(*terms):
    return functools.reduce(lambda p, q: p + q, [t.astype(f32) for t in terms])


def regroup(parts, bits):
    mine = relative(parts, bits)
    return relative([mine[0]] + [swap(AXES, k)(mine[k]) for k in (1, 2, 3)], bits)


def vector_tables(gains, biases):
    gains = gains.astype(f32).reshape(LAYERS, 2, D)
    biases = biases.astype(f32).reshape(LAYERS, 11, D)
    return jnp.concatenate([gains, biases, jnp.zeros((LAYERS, VECS - 13, D), f32)], 1)


FIRST = {("attn", 0): "y", ("down", 0): "x", ("up", 0): "y", ("attn", 1): "x", ("up", 1): "y", ("down", 1): "x"}
LOTS = (
    ((80, 80), {("down", 1): ((0, 0, 0, 80),), ("up", 1): ((1, 0, 0, 80),)}),
    (
        (128, 112),
        {("attn", 1): ((0, 0, 0, 80),), ("down", 0): ((1, 0, 0, 80),), ("up", 0): ((0, 80, 0, 48), (1, 80, 48, 32))},
    ),
    ((48, 48), {("attn", 0): ((0, 0, 0, 48), (1, 0, 48, 32)), ("rest", 0): ((1, 32, 0, 16),)}),
)


def whole_pieces(matrix, by_rows, first):
    if by_rows:
        cut = jnp.transpose(matrix.reshape(4, 2, 2, 2, PIECE, D), (3, 2, 1, 0, 4, 5))
    else:
        cut = jnp.transpose(matrix.reshape(4, 2, PIECE, 2, 2, D), (4, 3, 1, 0, 2, 5))
    if first == "x":
        cut = jnp.swapaxes(cut, 1, 2)
    return [cut[kn, kb].reshape(8, PIECE, D) for kb in range(2) for kn in range(2)]


def whole_block(kept, core, halves, cuts):
    parts = {}
    for half in range(2):
        a, b, k = kept[3 * half : 3 * half + 3]
        rows = slice(halves[0], None) if half else slice(0, halves[0])
        cut = jnp.stack([jnp.stack([jnp.stack([k, b]), a]), core[:, :, :, rows]])
        parts[half] = jnp.swapaxes(cut, 1, 2) if half else cut
    return jnp.concatenate([parts[half][..., to : to + rows, :] for half, to, _, rows in cuts], -2)


def fetch_plain(w_qkv, w_out, w_up, w_down, gains, biases):
    def whole(value, rows):
        return lax.all_gather(value, AXES, axis=0, tiled=True).reshape(rows, -1)

    weights = {}
    for l in range(LAYERS):
        attn = jnp.concatenate([whole(w_qkv[l], D), whole(w_out[l], D)], 1)
        for name, matrix in (("attn", attn), ("up", whole(w_up[l], D)), ("down", whole(w_down[l], FF))):
            first = FIRST[name, l]
            weights[name, l] = (whole_pieces(matrix, name == "down", first), first)
    return weights, vector_tables(whole(gains, 1)[0], whole(biases, 1)[0])


class Lot:
    def __init__(self, halves):
        self.halves = halves

    def cut(self, core, half):
        return core[..., self.halves[0] :, :] if half else core[..., : self.halves[0], :]

    def first(self, core, kept):
        self.kept = kept
        self.core = [self.cut(core, half) for half in range(2)]
        return [add(kept[3 * half], self.core[half][1]).astype(bf16) for half in range(2)]

    def send_first(self, values):
        return along("x", values[0]), along("y", values[1])

    def second(self, got):
        self.got = got
        return [add(self.kept[3 * h + 1], self.core[h][0, 1], got[h][1]).astype(bf16) for h in range(2)]

    def send_second(self, values):
        return along("y", values[0]), along("x", values[1])

    def third(self, got):
        total = [add(self.kept[3 * h + 2], self.core[h][0, 0], self.got[h][0], got[h]) for h in range(2)]
        self.total = jnp.concatenate([t[:2] for t in total], 1)
        return jnp.concatenate([t[2:].astype(bf16) for t in total], 1)

    def fourth(self, got):
        total = add(self.total, got)
        self.total = total[0]
        return total[1].astype(bf16)

    def last(self, got):
        return add(self.total, got)


def stage(*groups):
    flat, tree = jax.tree.flatten(groups)
    return jax.tree.unflatten(tree, lax.optimization_barrier(flat))


def device_bits():
    wide = lax.axis_index("wide")
    return [(wide >> 3) & 1, (wide >> 2) & 1, (wide >> 1) & 1, wide & 1, lax.axis_index("narrow")]


def coordinates(values):
    return jnp.stack([jnp.asarray(v, jnp.int32) for v in values])


def layer_grads(sums):
    both = jnp.stack(sums)
    return both[:, :2].reshape(-1), both[:, 2:13].reshape(-1)


def gradient_blocks(coords, lot, kept, back, phase):
    items = []
    for (name, l), cuts in LOTS[lot][1].items():
        if name == "attn":
            items.append(("attn", [kept[l]["at"], kept[l]["ot"]], back[l]["gpm"], cuts))
        elif name == "up":
            items.append(("up", [kept[l]["bt"]], back[l]["gu"], cuts))
        elif name == "down":
            items.append(("down", [kept[l]["zt"]], back[l]["gb"], cuts))
        elif "rest" in back[l]:
            items.append(("rest", [], back[l]["rest"], cuts))
    halves = LOTS[lot][0]
    outs = grads(coords, items, halves if "rest" in back[0] or lot < 2 else (48, 32), phase)
    return outs[0] if phase else outs


def shares_of(parts, bits):
    rows = D // 32
    cut = jnp.stack(parts)
    whole = jnp.concatenate(regroup([cut[:, s * rows : (s + 1) * rows] for s in range(4)], bits[3:]), 2)
    return [whole[i] for i in range(len(parts))]


def body(tokens, lengths, w_qkv, w_out, w_up, w_down, gains, biases, cotangent):
    args = (tokens, lengths, w_qkv, w_out, w_up, w_down, gains, biases, cotangent)
    if lax.axis_size("wide") == 16 and lax.axis_size("narrow") == 2:
        return staged(*args)
    return plain(*args)


def plain(tokens, lengths, w_qkv, w_out, w_up, w_down, gains, biases, cotangent):
    length = tokens.shape[0] // lengths.shape[0]
    coords = coordinates([0, 0, 0, 0, lengths[0]])
    table = jnp.asarray(rotary_tables(length))
    weights, vectors = fetch_plain(w_qkv, w_out, w_up, w_down, gains, biases)
    kept, back, x = [], [{}, {}], tokens
    for l in range(LAYERS):
        held = attn_fwd(coords, x, vectors[l], table, weights["attn", l])
        x, more = ffn_fwd(coords, held, vectors[l], weights["up", l], weights["down", l], l == LAYERS - 1)
        kept.append(held | more)
    output, grad, sums = x, cotangent, [None] * LAYERS
    for l in reversed(range(LAYERS)):
        last = l == 0
        back[l] = ffn_bwd(coords, grad, kept[l], vectors[l], weights["up", l], weights["down", l], not last)
        back[l]["gpm"] = attn_bwd(coords, back[l]["gmb"], kept[l], table, weights["attn", l])
        grad, more = attn_after(coords, back[l], kept[l], vectors[l], weights["attn", l], last)
        sums[l] = back[l]["sums"] + more
    matrices = {}
    for lot, (halves, cuts) in enumerate(LOTS):
        core, rest = [gradient_blocks(coords, lot, kept, back, phase) for phase in (1, 0)]
        for key, where in cuts.items():
            if key[0] != "rest":
                cut = whole_block(rest, core, halves, where)
                order = (3, 2, 1, 0, 4, 5) if key[0] == "down" else (3, 2, 4, 1, 0, 5)
                matrices[key] = jnp.transpose(cut, order).reshape((FF, D) if key[0] == "down" else (D, FF)).astype(f32)
    outs = []
    for name, begin, end in (("attn", 0, 3 * D), ("attn", 3 * D, FF), ("up", 0, FF), ("down", 0, D)):
        cut = jnp.stack([matrices[name, l][:, begin:end].reshape(-1) for l in range(LAYERS)])
        outs.append(lax.psum_scatter(cut, AXES, scatter_dimension=1, tiled=True))
    outs += [lax.psum_scatter(v, AXES, scatter_dimension=0, tiled=True) for v in layer_grads(sums)]
    return (output, grad, *outs)


def staged(tokens, lengths, w_qkv, w_out, w_up, w_down, gains, biases, cotangent):
    length = tokens.shape[0] // lengths.shape[0]
    bits = device_bits()
    coords = coordinates([lax.axis_index("wide") >> 2, *bits[2:], lengths[0]])
    table = jnp.asarray(rotary_tables(length))
    rows = D // 32
    kept, back = [{}, {}], [{}, {}]

    flat = []
    for l in range(LAYERS):
        flat.append(jnp.concatenate([w_qkv[l].reshape(rows, 3 * D), w_out[l].reshape(rows, D)], 1))
        flat.append(w_up[l].reshape(rows, FF))
    flat = jnp.stack(flat)
    down0, down1 = [w_down[l].reshape(PIECE, D) for l in range(LAYERS)]
    down_t = jnp.stack([down0, along("z0", down0)])
    down_u = along("z1", down_t)
    attn0, up0, attn1, up1 = jnp.concatenate(regroup([flat[:, :, s * D : (s + 1) * D] for s in range(4)], bits[3:]), 1)
    small = jnp.concatenate([gains, biases])
    width = small.shape[0]
    attn0 = jnp.concatenate([attn0, jnp.zeros((16, D), bf16).at[0, :width].set(small)])
    attn_z = jnp.stack([attn0] + [swap("wide", k)(attn0) for k in (4, 8, 12)])
    down_z = jnp.concatenate([down_t, down_u])

    names = ((("attn", 0), ("down", 0)), (("up", 0), ("attn", 1)), (("up", 1), ("down", 1)))
    pairs = [None, jnp.stack([up0, attn1]), jnp.stack([up1, down1])]

    def hop(p, zs):
        return [along(FIRST[key], z) for key, z in zip(names[p], zs)]

    def jump(p, near):
        return [along(other(FIRST[key]), n) for key, n in zip(names[p], near)]

    def joined(left, right):
        return [jnp.concatenate([a, b]) for a, b in zip(left, right)]

    def z_blocks(near, far):
        return [jnp.concatenate([near[:, i], far[:, i]]) for i in range(2)]

    def mates(values):
        return [mate(v) for v in values]

    weights = {}

    def arrived(p, near, far, near_mate, far_mate):
        for i, key in enumerate(names[p]):
            weights[key] = ([near[i], near_mate[i], far[i], far_mate[i]], FIRST[key])

    zs0, pairs[1] = stage([attn_z, down_z], pairs[1])
    hop0, got1 = hop(0, zs0), along("z0", pairs[1])
    near0, t1 = stage(joined(zs0, hop0), jnp.stack([pairs[1], got1]))
    far0, mate0, u1 = jump(0, near0), mates(near0), along("z1", t1)
    far0, mate0, zs1, near0, pairs[2] = stage(far0, mate0, z_blocks(t1, u1), near0, pairs[2])
    far_mate0, hop1, got2 = mates(far0), hop(1, zs1), along("z0", pairs[2])
    far_mate0, near1, t2, near0, far0, mate0 = stage(
        far_mate0, joined(zs1, hop1), jnp.stack([pairs[2], got2]), near0, far0, mate0
    )
    arrived(0, near0, far0, mate0, far_mate0)
    cut = jnp.stack([p[:, PIECE, :width] for p in weights["attn", 0][0]]).reshape(2, 2, 2, 2, 2, width)
    cut = jnp.transpose(cut, (3, 4, 2, 0, 1, 5) if FIRST["attn", 0] == "y" else (3, 4, 0, 2, 1, 5))
    for axis, bit in enumerate(bits):
        cut = jnp.where(bit > 0, jnp.flip(cut, axis), cut)
    cut = cut.reshape(32, width)
    vectors = vector_tables(cut[:, : gains.shape[0]].reshape(-1), cut[:, gains.shape[0] :].reshape(-1))
    far1, mate1, u2 = jump(1, near1), mates(near1), along("z1", t2)
    kept[0] = attn_fwd(coords, tokens, vectors[0], table, weights["attn", 0])
    far1, mate1, zs2, near1, kept[0] = stage(far1, mate1, z_blocks(t2, u2), near1, kept[0])
    far_mate1, hop2 = mates(far1), hop(2, zs2)
    arrived(1, near1, far1, mate1, far_mate1)
    x, more = ffn_fwd(coords, kept[0], vectors[0], weights["up", 0], weights["down", 0], False)
    kept[0] |= more
    near2, x = stage(joined(zs2, hop2), x)
    far2, mate2 = jump(2, near2), mates(near2)
    kept[1] = attn_fwd(coords, x, vectors[1], table, weights["attn", 1])
    far2, mate2, kept[1] = stage(far2, mate2, kept[1])
    far_mate2 = mates(far2)
    arrived(2, near2, far2, mate2, far_mate2)
    output, more = ffn_fwd(coords, kept[1], vectors[1], weights["up", 1], weights["down", 1], True)
    kept[1] |= more

    lots = [Lot(halves) for halves, _ in LOTS]
    back[1] = ffn_bwd(coords, cotangent, kept[1], vectors[1], weights["up", 1], weights["down", 1], True)
    core = gradient_blocks(coords, 0, kept, back, 1)
    core, back[1]["gu"] = stage(core, back[1]["gu"])
    first = lots[0].first(mate(core), gradient_blocks(coords, 0, kept, back, 0))
    first, back[1] = stage(first, back[1])
    got = lots[0].send_first(first)
    gpm = attn_bwd(coords, back[1]["gmb"], kept[1], table, weights["attn", 1])
    got, back[1]["gpm"] = stage(got, gpm)
    second, back[1] = stage(lots[0].second(got), back[1])
    got = lots[0].send_second(second)
    grad, more = attn_after(coords, back[1], kept[1], vectors[1], weights["attn", 1], False)
    back[0] = ffn_bwd(coords, grad, kept[0], vectors[0], weights["up", 0], weights["down", 0], False)
    sums = [None, back[1]["sums"] + more]
    got, back[0] = stage(got, back[0])
    third, back[0] = stage(lots[0].third(got), back[0])
    got, core = stage(along("z1", third), gradient_blocks(coords, 1, kept, back, 1))
    fourth, core, back[1]["gpm"] = stage(lots[0].fourth(got), core, back[1]["gpm"])
    got, core = along("z0", fourth), mate(core)
    first = lots[1].first(core, gradient_blocks(coords, 1, kept, back, 0))
    first, back[0], done0 = stage(first, back[0], lots[0].last(got))
    got = lots[1].send_first(first)
    gpm = attn_bwd(coords, back[0]["gmb"], kept[0], table, weights["attn", 0])
    got, back[0]["gpm"] = stage(got, gpm)
    second, back[0] = stage(lots[1].second(got), back[0])
    got = lots[1].send_second(second)
    grad, more = attn_after(coords, back[0], kept[0], vectors[0], weights["attn", 0], True)
    sums[0] = back[0]["sums"] + more
    small = jnp.concatenate([v.reshape(32, -1) for v in layer_grads(sums)], 1).reshape(2, 2, 2, 2, 2, width)
    for axis, bit in enumerate(bits):
        small = jnp.where(bit > 0, jnp.flip(small, axis), small)
    small = jnp.transpose(small, (4, 3, 2, 0, 1, 5)).reshape(2, 2, 2, 4, 1, width)
    back[0]["rest"] = jnp.pad(small, ((0, 0),) * 4 + ((0, 15), (0, D - width))).astype(bf16)
    core = gradient_blocks(coords, 2, kept, back, 1)
    got, core, back[0]["gpm"] = stage(got, core, back[0]["gpm"])
    third, core = stage(lots[1].third(got), core)
    got, core = along("z1", third), mate(core)
    first = lots[2].first(core, gradient_blocks(coords, 2, kept, back, 0))
    got, first = stage(got, first)
    fourth, first = stage(lots[1].fourth(got), first)
    got, got2 = along("z0", fourth), lots[2].send_first(first)
    second, done1 = stage(lots[2].second(got2), lots[1].last(got))
    got2 = lots[2].send_second(second)
    up0 = jnp.concatenate([done1[80:128], done1[208:240]])
    up1, attn1, up0 = shares_of([done0[80:160], done1[:80], up0], bits)
    fourth = lots[2].fourth(along("z1", lots[2].third(got2)))
    done2 = lots[2].last(along("z0", fourth))
    (attn0,) = shares_of([done2[:80]], bits)
    mine = done2[80, :width]
    return (
        output,
        grad,
        jnp.stack([v[:, : 3 * D].reshape(-1) for v in (attn0, attn1)]),
        jnp.stack([v[:, 3 * D :].reshape(-1) for v in (attn0, attn1)]),
        jnp.stack([up0.reshape(-1), up1.reshape(-1)]),
        jnp.stack([done1[128:208].reshape(-1), done0[:80].reshape(-1)]),
        mine[: gains.shape[0]],
        mine[gains.shape[0] :],
    )


def solution(mesh):
    both, flat, rows = P(AXES), P(None, AXES), P(AXES, None)
    return jax.shard_map(
        body,
        mesh=mesh,
        in_specs=(rows, both, flat, flat, flat, flat, both, both, rows),
        out_specs=(rows, rows, flat, flat, flat, flat, both, both),
        check_vma=False,
    )
```

time: 542 us -> 482 us (0.89)
  starting transfers between devices: 113 us -> 52.3 us
  waiting for transfers between devices: 177 us -> 151 us
  Pallas kernels: 204 us -> 221 us
  other arithmetic: 22.1 us -> 28 us
    ppermute x105 -> x63, starting transfers between devices: 113 us -> 52.3 us  [swap(): return lambda value: lax.ppermute(value, axis_name, pairs)]
    ppermute x105 -> x63, waiting for transfers between devices: 177 us -> 151 us  [swap(): return lambda value: lax.ppermute(value, axis_name, pairs)]
    pallas_call x14 -> x16, Pallas kernels: 204 us -> 221 us  [call(): pl.pallas_call(kernel, out_shape=[jax.ShapeDtypeStruct(s, t) for s, t in...]
    another operation x29 -> x20, other arithmetic: 12.2 us -> 6.25 us  [the longest x1 1.12 us: staged(): jnp.stack([up0.reshape(-1), up1.reshape(-1)])]
    convert_element_type x12 -> x8, other arithmetic: 6.89 us -> 12 us  [the longest x4 8.2 us: first(): add(kept[3 * half], self.core[half][1]).astype(bf16)]
  transfers between devices with their start and end apart: 105 -> 63, of which waited for: 39 -> 29; matrix products, arithmetic and copies ran while one was open for 5% -> 3% of each run, Pallas kernels for 17% -> 37%
where the time goes in v2:
time: 482 us; the launch traced here: 475 us
  Pallas kernels  221 us (46%)
  waiting for transfers between devices  151 us (31%)
  starting transfers between devices  52.3 us (11%)
  other arithmetic  28 us (6%)
  local copies, waits for them, and re-layouts  19.5 us (4%)
    pallas_call x16, Pallas kernels, call(): pl.pallas_call(kernel, out_shape=[jax.ShapeDtypeStruct(s, t) for s, t in...  221 us
    ppermute x63, waiting for transfers between devices, swap(): return lambda value: lax.ppermute(value, axis_name, pairs)  151 us
    ppermute x63, starting transfers between devices, swap(): return lambda value: lax.ppermute(value, axis_name, pairs)  52.3 us
  transfers between devices with their start and end apart: 63, of which 29 were waited for; matrix products, arithmetic and copies ran while one was open for 3% of the time, Pallas kernels for 37%

profile of v2, /device:TPU:0, one launch (start us, length us, event | category | flops | bytes accessed | tf_op | source)
XLA Modules:
  0.0 475.0 jit_solution(4614019335444115850)
XLA Ops:
  28.1 9.9 %collective-permute-done.7 = bf16[2,80,640]{2,1,0:T(8,128)(2,1)S(1)} collective-permute-done((bf16[2,80,640]{2,1,0:T(8,128)(2,1)S(1)}, bf16[2,80,640]{2,1,0:T(8,128)(2,1)S(1)}, u32[]{:S(2)}, u32[]{:S(2)}) %collective-permute-start.7) | collective-permute-done | bytes 204832 | tf_op jit(solution)/shard_map/ppermute | solution.py:554
  41.5 5.6 %collective-permute-done.10 = bf16[2,80,640]{2,1,0:T(8,128)(2,1)S(1)} collective-permute-done((bf16[2,80,640]{2,1,0:T(8,128)(2,1)S(1)}, bf16[2,80,640]{2,1,0:T(8,128)(2,1)S(1)}, u32[]{:S(2)}, u32[]{:S(2)}) %collective-permute-start.10) | collective-permute-done | bytes 204832 | tf_op jit(solution)/shard_map/ppermute | solution.py:554
  55.1 21.0 %collective-permute-done.15 = bf16[2,2,80,640]{3,2,0,1:T(8,128)(2,1)S(1)} collective-permute-done((bf16[2,2,80,640]{3,2,0,1:T(8,128)(2,1)S(1)}, bf16[2,2,80,640]{3,2,0,1:T(8,128)(2,1)S(1)}, u32[]{:S(2)}, u32[]{:S(2)}) %collective-permute-start.15) | collective-permute-done | bytes 409632 | tf_op jit(solution)/shard_map/ppermute | solution.py:554
  101.3 22.6 %attn_fwd.2 = (bf16[640,512]{1,0:T(8,128)(2,1)}, bf16[512,1920]{1,0:T(8,128)(2,1)}, bf16[512,640]{1,0:T(8,128)(2,1)}, bf16[640,512]{1,0:T(8,128)(2,1)}, bf16[512...) custom-call(s32[5]{0:T(128)} %stack.112.coords, ...), custom_call_target="tpu_custom_call" | custom-call | flops 2348810240 | bytes 12623892 | tf_op jit(solution)/shard_map/attn_fwd/pallas_call | solution.py:462
  127.0 9.1 %collective-permute-done.26 = bf16[4,80,640]{2,1,0:T(8,128)(2,1)S(1)} collective-permute-done((bf16[4,80,640]{2,1,0:T(8,128)(2,1)S(1)}, bf16[4,80,640]{2,1,0:T(8,128)(2,1)S(1)}, u32[]{:S(2)}, u32[]{:S(2)}) %collective-permute-start.26) | collective-permute-done | bytes 409632 | tf_op jit(solution)/shard_map/ppermute | solution.py:554
  138.5 15.9 %ffn_fwd.2 = (f32[512,640]{1,0:T(8,128)}, bf16[2560,512]{1,0:T(8,128)(2,1)}, bf16[512,2560]{1,0:T(8,128)(2,1)}) custom-call(s32[5]{0:T(128)} %stack.112.coords, f32[512,640]{1,0:T(8,128)} %get-tuple-element.227.m_ref, bf16[512,640]{1,0:T(8,128)(2,1)} %get-tuple-element.228.b_ref, f32[16,640]{1,0:T(8,128)} %get-tuple-element.431.vec_ref, ...), custom_call_target="tpu_custom_call" | custom-call | flops 3355443200 | bytes 15114260 | tf_op jit(solution)/shard_map/ffn_fwd/pallas_call | solution.py:462
  157.3 23.2 %attn_fwd.3 = (bf16[640,512]{1,0:T(8,128)(2,1)}, bf16[512,1920]{1,0:T(8,128)(2,1)}, bf16[512,640]{1,0:T(8,128)(2,1)}, bf16[640,512]{1,0:T(8,128)(2,1)}, bf16[512...) custom-call(s32[5]{0:T(128)} %stack.112.coords, ...), custom_call_target="tpu_custom_call" | custom-call | flops 2348810240 | bytes 12623892 | tf_op jit(solution)/shard_map/attn_fwd/pallas_call | solution.py:462
  185.2 16.0 %ffn_fwd.3 = (bf16[512,640]{1,0:T(8,128)(2,1)}, bf16[2560,512]{1,0:T(8,128)(2,1)}, bf16[512,2560]{1,0:T(8,128)(2,1)}) custom-call(s32[5]{0:T(128)} %stack.112.coords, f32[512,640]{1,0:T(8,128)} %get-tuple-element.251.m_ref, bf16[512,640]{1,0:T(8,128)(2,1)} %get-tuple-element.252.b_ref, f32[16,640]{1,0:T(8,128)} %get-tuple-element.430.vec_ref, ...), custom_call_target="tpu_custom_call" | custom-call | flops 3355443200 | bytes 14458900 | tf_op jit(solution)/shard_map/ffn_fwd/pallas_call | solution.py:462
  201.2 13.2 %ffn_bwd.2 = (bf16[512,640]{1,0:T(8,128)(2,1)}, bf16[512,2560]{1,0:T(8,128)(2,1)}, f32[512,640]{1,0:T(8,128)}, bf16[512,640]{1,0:T(8,128)(2,1)}, f32[16,640]{1,0:T(8,128)}) custom-call(s32[5]{0:T(128)} %stack.112.coords, bf16[512,640]{1,0:T(8,128)(2,1)} %g_ref.1, bf16[512,2560]{1,0:T(8,128)(2,1)} %get-tuple-element.261.slope_ref, ...), custom_call_target="tpu_custom_call" | custom-call | flops 3355443200 | bytes 16465940 | tf_op jit(solution)/shard_map/ffn_bwd/pallas_call | solution.py:462
  214.4 6.9 %grads.6 = bf16[2,2,4,160,640]{4,3,2,1,0:T(8,128)(2,1)} custom-call(s32[5]{0:T(128)} %stack.112.coords, bf16[2560,512]{1,0:T(8,128)(2,1)} %get-tuple-element.260.refs_0_, bf16[512,640]{1,0:T(8,128)(2,1)} %get-tuple-element.262.refs_1_, bf16[640,512]{1,0:T(8,128)(2,1)} %get-tuple-element.263.refs_2_, bf16[512,2560]{1,0:T(8,128)(2,1)} %get-tuple-element.265.refs_3_), custom_call_target="tpu_custom_call" | custom-call | flops 1677721600 | bytes 9830420 | tf_op jit(solution)/shard_map/grads/pallas_call | solution.py:462
  221.5 6.5 %grads.7 = (bf16[2,4,80,640]{3,2,1,0:T(8,128)(2,1)}, bf16[4,80,640]{2,1,0:T(8,128)(2,1)}, bf16[4,80,640]{2,1,0:T(8,128)(2,1)}, bf16[2,4,80,640]{3,2,1,0:T(8,128)...) custom-call(s32[5]{0:T(128)} %stack.112.coords, bf16[2560,512]{1,0:T(8,128)(2,1)} %get-tuple-element.260.refs_0_, ...), custom_call_target="tpu_custom_call" | custom-call | flops 1677721600 | bytes 9830420 | tf_op jit(solution)/shard_map/grads/pallas_call | solution.py:462
  232.3 29.3 %attn_bwd.2.gpm_ref.refs_2_ = bf16[512,2560]{1,0:T(8,128)(2,1)} custom-call(s32[5]{0:T(128)} %stack.112.coords, bf16[512,640]{1,0:T(8,128)(2,1)} %get-tuple-element.275.gmb_ref, bf16[512,1920]{1,0:T(8,128)(2,1)} %get-tuple-element.276.qkv_ref, bf16[512,640]{1,0:T(8,128)(2,1)} %get-tuple-element.277.o_ref, bf16[512,640]{1,0:T(8,128)(2,1)} %get-tuple-element.278.lse_ref, ...), custom_call_target="tpu_custom_call" | custom-call | flops 2097152000 | bytes 10616852 | tf_op jit(solution)/shard_map/attn_bwd/pallas_call | solution.py:462
  263.7 8.5 %attn_after.2 = (f32[512,640]{1,0:T(8,128)}, f32[16,640]{1,0:T(8,128)}) custom-call(s32[5]{0:T(128)} %stack.112.coords, bf16[512,2560]{1,0:T(8,128)(2,1)} %attn_bwd.2.gpm_ref.refs_2_, f32[512,640]{1,0:T(8,128)} %get-tuple-element.289.gm_ref, f32[512,640]{1,0:T(8,128)} %get-tuple-element.290.x_ref, f32[16,640]{1,0:T(8,128)} %get-tuple-element.430.vec_ref, ...), custom_call_target="tpu_custom_call" | custom-call | flops 1258291200 | bytes 9912340 | tf_op jit(solution)/shard_map/attn_after/pallas_call | solution.py:462
  272.2 13.1 %ffn_bwd.3 = (bf16[512,640]{1,0:T(8,128)(2,1)}, bf16[512,2560]{1,0:T(8,128)(2,1)}, f32[512,640]{1,0:T(8,128)}, bf16[512,640]{1,0:T(8,128)(2,1)}, f32[16,640]{1,0:T(8,128)}) custom-call(s32[5]{0:T(128)} %stack.112.coords, f32[512,640]{1,0:T(8,128)} %get-tuple-element.291.g_ref, bf16[512,2560]{1,0:T(8,128)(2,1)} %get-tuple-element.292.slope_ref, ...), custom_call_target="tpu_custom_call" | custom-call | flops 3355443200 | bytes 17121300 | tf_op jit(solution)/shard_map/ffn_bwd/pallas_call | solution.py:462
  286.7 9.6 %grads.8 = bf16[2,2,4,240,640]{4,3,2,1,0:T(8,128)(2,1)} custom-call(s32[5]{0:T(128)} %stack.112.coords, bf16[640,512]{1,0:T(8,128)(2,1)} %get-tuple-element.258.refs_0_, bf16[640,512]{1,0:T(8,128)(2,1)} %get-tuple-element.259.refs_1_, bf16[512,2560]{1,0:T(8,128)(2,1)} %attn_bwd.2.gpm_ref.refs_2_, bf16[2560,512]{1,0:T(8,128)(2,1)} %get-tuple-element.307.refs_3_, ...), custom_call_target="tpu_custom_call" | custom-call | flops 2516582400 | bytes 15400980 | tf_op jit(solution)/shard_map/grads/pallas_call | solution.py:462
  296.3 9.9 %collective-permute-done.41 = bf16[2,160,640]{2,1,0:T(8,128)(2,1)S(1)} collective-permute-done((bf16[2,160,640]{2,1,0:T(8,128)(2,1)S(1)}, bf16[2,160,640]{2,1,0:T(8,128)(2,1)S(1)}, u32[]{:S(2)}, u32[]{:S(2)}) %collective-permute-start.41) | collective-permute-done | bytes 409632 | tf_op jit(solution)/shard_map/ppermute | solution.py:554
  306.5 9.3 %grads.9 = (bf16[2,4,128,640]{3,2,1,0:T(8,128)(2,1)}, bf16[4,128,640]{2,1,0:T(8,128)(2,1)}, bf16[4,128,640]{2,1,0:T(8,128)(2,1)}, bf16[2,4,112,640]{3,2,1,0:T(8,...) custom-call(s32[5]{0:T(128)} %stack.112.coords, bf16[640,512]{1,0:T(8,128)(2,1)} %get-tuple-element.258.refs_0_, ...), custom_call_target="tpu_custom_call" | custom-call | flops 2516582400 | bytes 15400980 | tf_op jit(solution)/shard_map/grads/pallas_call | solution.py:462
  323.2 29.3 %attn_bwd.3.gpm_ref.refs_2_ = bf16[512,2560]{1,0:T(8,128)(2,1)} custom-call(s32[5]{0:T(128)} %stack.112.coords, bf16[512,640]{1,0:T(8,128)(2,1)} %get-tuple-element.324.gmb_ref, bf16[512,1920]{1,0:T(8,128)(2,1)} %get-tuple-element.325.qkv_ref, bf16[512,640]{1,0:T(8,128)(2,1)} %get-tuple-element.326.o_ref, bf16[512,640]{1,0:T(8,128)(2,1)} %get-tuple-element.327.lse_ref, ...), custom_call_target="tpu_custom_call" | custom-call | flops 2097152000 | bytes 11272212 | tf_op jit(solution)/shard_map/attn_bwd/pallas_call | solution.py:462
  355.8 8.3 %attn_after.3 = (bf16[512,640]{1,0:T(8,128)(2,1)}, f32[16,640]{1,0:T(8,128)}) custom-call(s32[5]{0:T(128)} %stack.112.coords, bf16[512,2560]{1,0:T(8,128)(2,1)} %attn_bwd.3.gpm_ref.refs_2_, f32[512,640]{1,0:T(8,128)} %get-tuple-element.335.gm_ref, bf16[512,640]{1,0:T(8,128)(2,1)} %x_ref.2, f32[16,640]{1,0:T(8,128)} %get-tuple-element.431.vec_ref, ...), custom_call_target="tpu_custom_call" | custom-call | flops 1258291200 | bytes 9256980 | tf_op jit(solution)/shard_map/attn_after/pallas_call | solution.py:462
  373.8 6.7 %collective-permute-done.47 = bf16[4,112,640]{2,1,0:T(8,128)(2,1)} collective-permute-done((bf16[4,112,640]{2,1,0:T(8,128)(2,1)}, bf16[4,112,640]{2,1,0:T(8,128)(2,1)}, u32[]{:S(2)}, u32[]{:S(2)}) %collective-permute-start.47) | collective-permute-done | bytes 573472 | tf_op jit(solution)/shard_map/ppermute | solution.py:554
  394.3 23.1 %collective-permute-done.49 = bf16[2,240,640]{2,1,0:T(8,128)(2,1)S(1)} collective-permute-done((bf16[2,240,640]{2,1,0:T(8,128)(2,1)S(1)}, bf16[2,240,640]{2,1,0:T(8,128)(2,1)S(1)}, u32[]{:S(2)}, u32[]{:S(2)}) %collective-permute-start.49) | collective-permute-done | bytes 614432 | tf_op jit(solution)/shard_map/ppermute | solution.py:554
  419.8 6.8 %collective-permute-done.52 = bf16[240,640]{1,0:T(8,128)(2,1)S(1)} collective-permute-done((bf16[240,640]{1,0:T(8,128)(2,1)S(1)}, bf16[240,640]{1,0:T(8,128)(2,1)S(1)}, u32[]{:S(2)}, u32[]{:S(2)}) %collective-permute-start.52) | collective-permute-done | bytes 307232 | tf_op jit(solution)/shard_map/ppermute | solution.py:554
  437.0 7.7 %collective-permute-done.61 = f32[3,20,640]{2,1,0:T(8,128)S(1)} collective-permute-done((f32[3,20,640]{2,1,0:T(8,128)S(1)}, f32[3,20,640]{2,1,0:T(8,128)S(1)}, u32[]{:S(2)}, u32[]{:S(2)}) %collective-permute-start.61) | collective-permute-done | bytes 153632 | tf_op jit(solution)/shard_map/ppermute | solution.py:554
  449.1 12.8 %collective-permute-done.55 = bf16[2,96,640]{2,1,0:T(8,128)(2,1)S(1)} collective-permute-done((bf16[2,96,640]{2,1,0:T(8,128)(2,1)S(1)}, bf16[2,96,640]{2,1,0:T(8,128)(2,1)S(1)}, u32[]{:S(2)}, u32[]{:S(2)}) %collective-permute-start.55) | collective-permute-done | bytes 245792 | tf_op jit(solution)/shard_map/ppermute | solution.py:554
  (361 shorter events, 147.3 us)
Async XLA Ops:
  18.9 19.0 %collective-permute-start.7 = (bf16[2,80,640]{2,1,0:T(8,128)(2,1)S(1)}, bf16[2,80,640]{2,1,0:T(8,128)(2,1)S(1)}, u32[]{:S(2)}, u32[]{:S(2)}) collective-permute-start(bf16[2,80,640]{2,1,0:T(8,128)(2,1)S(1)} %pad_maximum_fusion.27), channel_id=1, source_target_pairs={{0,16},{2,18},{4,20},{6,22},{8,24},{10,26},{12,28},{14,30},{16,0},... | collective-permute-start | bytes 614408 | tf_op jit(solution)/shard_map/ppermute | solution.py:554
  52.1 24.2 %collective-permute-start.13 = (bf16[8,96,640]{2,1,0:T(8,128)(2,1)S(1)}, bf16[8,96,640]{2,1,0:T(8,128)(2,1)S(1)}, u32[]{:S(2)}, u32[]{:S(2)}) collective-permute-start(bf16[8,96,640]{2,1,0:T(8,128)(2,1)S(1)} %pad_maximum_fusion.refs_0_), channel_id=1, source_target_pairs={{0,1},{1,0},{2,3},{3,2},{4,5},{5,4},{6,7},{7,6},{8,9},{9,8},{10,11... | collective-permute-start | bytes 2949128 | tf_op jit(solution)/shard_map/ppermute | solution.py:554
  52.2 24.3 %collective-permute-start.11 = (bf16[8,96,640]{2,1,0:T(8,128)(2,1)S(1)}, bf16[8,96,640]{2,1,0:T(8,128)(2,1)}, u32[]{:S(2)}, u32[]{:S(2)}) collective-permute-start(bf16[8,96,640]{2,1,0:T(8,128)(2,1)S(1)} %pad_maximum_fusion.refs_0_), channel_id=1, source_target_pairs={{0,2},{2,0},{4,6},{6,4},{8,10},{10,8},{12,14},{14,12},{16,18},{18,... | collective-permute-start | bytes 2949128 | tf_op jit(solution)/shard_map/ppermute | solution.py:554
  53.0 23.3 %collective-permute-start.14 = (bf16[8,80,640]{2,1,0:T(8,128)(2,1)S(1)}, bf16[8,80,640]{2,1,0:T(8,128)(2,1)S(1)}, u32[]{:S(2)}, u32[]{:S(2)}) collective-permute-start(bf16[8,80,640]{2,1,0:T(8,128)(2,1)S(1)} %pad_maximum_fusion.1.refs_4_), channel_id=1, source_target_pairs={{0,1},{1,0},{2,3},{3,2},{4,5},{5,4},{6,7},{7,6},{8,9},{9,8},{10,11... | collective-permute-start | bytes 2457608 | tf_op jit(solution)/shard_map/ppermute | solution.py:554
  53.2 23.1 %collective-permute-start.12 = (bf16[8,80,640]{2,1,0:T(8,128)(2,1)S(1)}, bf16[8,80,640]{2,1,0:T(8,128)(2,1)}, u32[]{:S(2)}, u32[]{:S(2)}) collective-permute-start(bf16[8,80,640]{2,1,0:T(8,128)(2,1)S(1)} %pad_maximum_fusion.1.refs_4_), channel_id=1, source_target_pairs={{0,4},{2,6},{4,0},{6,2},{8,12},{10,14},{12,8},{14,10},{16,20},{18,... | collective-permute-start | bytes 2457608 | tf_op jit(solution)/shard_map/ppermute | solution.py:554
  54.9 21.2 %collective-permute-start.15 = (bf16[2,2,80,640]{3,2,0,1:T(8,128)(2,1)S(1)}, bf16[2,2,80,640]{3,2,0,1:T(8,128)(2,1)S(1)}, u32[]{:S(2)}, u32[]{:S(2)}) collective-permute-start(bf16[2,2,80,640]{3,2,0,1:T(8,128)(2,1)S(1)} %copy.73), channel_id=1, source_target_pairs={{0,16},{2,18},{4,20},{6,22},{8,24},{10,26},{12,28},{14,30},{16,0},... | collective-permute-start | bytes 1228808 | tf_op jit(solution)/shard_map/ppermute | solution.py:554
  95.6 28.5 %collective-permute-start.23 = (bf16[8,80,640]{2,1,0:T(8,128)(2,1)}, bf16[8,80,640]{2,1,0:T(8,128)(2,1)}, u32[]{:S(2)}, u32[]{:S(2)}) collective-permute-start(bf16[8,80,640]{2,1,0:T(8,128)(2,1)} %pad_maximum_fusion.2.refs_0_), channel_id=1, source_target_pairs={{0,1},{1,0},{2,3},{3,2},{4,5},{5,4},{6,7},{7,6},{8,9},{9,8},{10,11... | collective-permute-start | bytes 2457608 | tf_op jit(solution)/shard_map/ppermute | solution.py:554
  95.6 28.5 %collective-permute-start.21 = (bf16[8,80,640]{2,1,0:T(8,128)(2,1)}, bf16[8,80,640]{2,1,0:T(8,128)(2,1)}, u32[]{:S(2)}, u32[]{:S(2)}) collective-permute-start(bf16[8,80,640]{2,1,0:T(8,128)(2,1)} %pad_maximum_fusion.2.refs_0_), channel_id=1, source_target_pairs={{0,2},{2,0},{4,6},{6,4},{8,10},{10,8},{12,14},{14,12},{16,18},{18,... | collective-permute-start | bytes 2457608 | tf_op jit(solution)/shard_map/ppermute | solution.py:554
  96.8 27.4 %collective-permute-start.24 = (bf16[8,80,640]{2,1,0:T(8,128)(2,1)S(1)}, bf16[8,80,640]{2,1,0:T(8,128)(2,1)S(1)}, u32[]{:S(2)}, u32[]{:S(2)}) collective-permute-start(bf16[8,80,640]{2,1,0:T(8,128)(2,1)S(1)} %pad_maximum_fusion.3.refs_0_), channel_id=1, source_target_pairs={{0,1},{1,0},{2,3},{3,2},{4,5},{5,4},{6,7},{7,6},{8,9},{9,8},{10,11... | collective-permute-start | bytes 2457608 | tf_op jit(solution)/shard_map/ppermute | solution.py:554
  97.0 27.2 %collective-permute-start.22 = (bf16[8,80,640]{2,1,0:T(8,128)(2,1)S(1)}, bf16[8,80,640]{2,1,0:T(8,128)(2,1)S(1)}, u32[]{:S(2)}, u32[]{:S(2)}) collective-permute-start(bf16[8,80,640]{2,1,0:T(8,128)(2,1)S(1)} %pad_maximum_fusion.3.refs_0_), channel_id=1, source_target_pairs={{0,4},{2,6},{4,0},{6,2},{8,12},{10,14},{12,8},{14,10},{16,20},{18,... | collective-permute-start | bytes 2457608 | tf_op jit(solution)/shard_map/ppermute | solution.py:554
  99.1 24.8 %collective-permute-start.25 = (bf16[2,2,80,640]{3,2,0,1:T(8,128)(2,1)}, bf16[2,2,80,640]{3,2,0,1:T(8,128)(2,1)S(1)}, u32[]{:S(2)}, u32[]{:S(2)}) collective-permute-start(bf16[2,2,80,640]{3,2,0,1:T(8,128)(2,1)} %copy.75), channel_id=1, source_target_pairs={{0,16},{2,18},{4,20},{6,22},{8,24},{10,26},{12,28},{14,30},{16,0},... | collective-permute-start | bytes 1228808 | tf_op jit(solution)/shard_map/ppermute | solution.py:554
  127.0 29.4 %collective-permute-start.33 = (bf16[8,80,640]{2,1,0:T(8,128)(2,1)S(1)}, bf16[8,80,640]{2,1,0:T(8,128)(2,1)S(1)}, u32[]{:S(2)}, u32[]{:S(2)}) collective-permute-start(bf16[8,80,640]{2,1,0:T(8,128)(2,1)S(1)} %collective-permute-done.22.refs_2_), channel_id=1, source_target_pairs={{0,1},{1,0},{2,3},{3,2},{4,5},{5,4},{6,7},{7,6},{8,9},{9,8},{10,11... | collective-permute-start | bytes 2457608 | tf_op jit(solution)/shard_map/ppermute | solution.py:554
  154.4 26.2 %collective-permute-start.31 = (bf16[8,80,640]{2,1,0:T(8,128)(2,1)S(1)}, bf16[8,80,640]{2,1,0:T(8,128)(2,1)S(1)}, u32[]{:S(2)}, u32[]{:S(2)}) collective-permute-start(bf16[8,80,640]{2,1,0:T(8,128)(2,1)S(1)} %pad_maximum_fusion.4.refs_0_), channel_id=1, source_target_pairs={{0,1},{1,0},{2,3},{3,2},{4,5},{5,4},{6,7},{7,6},{8,9},{9,8},{10,11... | collective-permute-start | bytes 2457608 | tf_op jit(solution)/shard_map/ppermute | solution.py:554
  154.5 26.1 %collective-permute-start.29 = (bf16[8,80,640]{2,1,0:T(8,128)(2,1)S(1)}, bf16[8,80,640]{2,1,0:T(8,128)(2,1)S(1)}, u32[]{:S(2)}, u32[]{:S(2)}) collective-permute-start(bf16[8,80,640]{2,1,0:T(8,128)(2,1)S(1)} %pad_maximum_fusion.4.refs_0_), channel_id=1, source_target_pairs={{0,2},{2,0},{4,6},{6,4},{8,10},{10,8},{12,14},{14,12},{16,18},{18,... | collective-permute-start | bytes 2457608 | tf_op jit(solution)/shard_map/ppermute | solution.py:554
  155.7 24.9 %collective-permute-start.32 = (bf16[8,80,640]{2,1,0:T(8,128)(2,1)S(1)}, bf16[8,80,640]{2,1,0:T(8,128)(2,1)S(1)}, u32[]{:S(2)}, u32[]{:S(2)}) collective-permute-start(bf16[8,80,640]{2,1,0:T(8,128)(2,1)S(1)} %pad_maximum_fusion.5.refs_4_), channel_id=1, source_target_pairs={{0,1},{1,0},{2,3},{3,2},{4,5},{5,4},{6,7},{7,6},{8,9},{9,8},{10,11... | collective-permute-start | bytes 2457608 | tf_op jit(solution)/shard_map/ppermute | solution.py:554
  155.9 24.7 %collective-permute-start.30 = (bf16[8,80,640]{2,1,0:T(8,128)(2,1)S(1)}, bf16[8,80,640]{2,1,0:T(8,128)(2,1)S(1)}, u32[]{:S(2)}, u32[]{:S(2)}) collective-permute-start(bf16[8,80,640]{2,1,0:T(8,128)(2,1)S(1)} %pad_maximum_fusion.5.refs_4_), channel_id=1, source_target_pairs={{0,4},{2,6},{4,0},{6,2},{8,12},{10,14},{12,8},{14,10},{16,20},{18,... | collective-permute-start | bytes 2457608 | tf_op jit(solution)/shard_map/ppermute | solution.py:554
  229.8 31.7 %collective-permute-start.37 = (bf16[2,4,80,640]{3,2,1,0:T(8,128)(2,1)S(1)}, bf16[2,4,80,640]{3,2,1,0:T(8,128)(2,1)S(1)}, u32[]{:S(2)}, u32[]{:S(2)}) collective-permute-start(bf16[2,4,80,640]{3,2,1,0:T(8,128)(2,1)S(1)} %get-tuple-element.273), channel_id=1, source_target_pairs={{0,2},{2,0},{4,6},{6,4},{8,10},{10,8},{12,14},{14,12},{16,18},{18,... | collective-permute-start | bytes 2457608 | tf_op jit(solution)/shard_map/ppermute | solution.py:554
  230.8 30.8 %collective-permute-start.38 = (bf16[2,4,80,640]{3,2,1,0:T(8,128)(2,1)S(1)}, bf16[2,4,80,640]{3,2,1,0:T(8,128)(2,1)S(1)}, u32[]{:S(2)}, u32[]{:S(2)}) collective-permute-start(bf16[2,4,80,640]{3,2,1,0:T(8,128)(2,1)S(1)} %get-tuple-element.274), channel_id=1, source_target_pairs={{0,4},{2,6},{4,0},{6,2},{8,12},{10,14},{12,8},{14,10},{16,20},{18,... | collective-permute-start | bytes 2457608 | tf_op jit(solution)/shard_map/ppermute | solution.py:554
  261.9 23.4 %collective-permute-start.39 = (bf16[4,80,640]{2,1,0:T(8,128)(2,1)S(1)}, bf16[4,80,640]{2,1,0:T(8,128)(2,1)S(1)}, u32[]{:S(2)}, u32[]{:S(2)}) collective-permute-start(bf16[4,80,640]{2,1,0:T(8,128)(2,1)S(1)} %get-tuple-element.286), channel_id=1, source_target_pairs={{0,4},{2,6},{4,0},{6,2},{8,12},{10,14},{12,8},{14,10},{16,20},{18,... | collective-permute-start | bytes 1228808 | tf_op jit(solution)/shard_map/ppermute | solution.py:554
  262.5 22.8 %collective-permute-start.40 = (bf16[4,80,640]{2,1,0:T(8,128)(2,1)S(1)}, bf16[4,80,640]{2,1,0:T(8,128)(2,1)S(1)}, u32[]{:S(2)}, u32[]{:S(2)}) collective-permute-start(bf16[4,80,640]{2,1,0:T(8,128)(2,1)S(1)} %get-tuple-element.287), channel_id=1, source_target_pairs={{0,2},{2,0},{4,6},{6,4},{8,10},{10,8},{12,14},{14,12},{16,18},{18,... | collective-permute-start | bytes 1228808 | tf_op jit(solution)/shard_map/ppermute | solution.py:554
  285.8 20.4 %collective-permute-start.41 = (bf16[2,160,640]{2,1,0:T(8,128)(2,1)S(1)}, bf16[2,160,640]{2,1,0:T(8,128)(2,1)S(1)}, u32[]{:S(2)}, u32[]{:S(2)}) collective-permute-start(bf16[2,160,640]{2,1,0:T(8,128)(2,1)S(1)} %pad_maximum_fusion.19), channel_id=1, source_target_pairs={{0,16},{2,18},{4,20},{6,22},{8,24},{10,26},{12,28},{14,30},{16,0},... | collective-permute-start | bytes 1228808 | tf_op jit(solution)/shard_map/ppermute | solution.py:554
  320.8 31.7 %collective-permute-start.44 = (bf16[2,4,128,640]{3,2,1,0:T(8,128)(2,1)}, bf16[2,4,128,640]{3,2,1,0:T(8,128)(2,1)S(1)}, u32[]{:S(2)}, u32[]{:S(2)}) collective-permute-start(bf16[2,4,128,640]{3,2,1,0:T(8,128)(2,1)} %fusion), channel_id=1, source_target_pairs={{0,2},{2,0},{4,6},{6,4},{8,10},{10,8},{12,14},{14,12},{16,18},{18,... | collective-permute-start | bytes 3932168 | tf_op jit(solution)/shard_map/ppermute | solution.py:554
  321.6 30.8 %collective-permute-start.45 = (bf16[2,4,112,640]{3,2,1,0:T(8,128)(2,1)}, bf16[2,4,112,640]{3,2,1,0:T(8,128)(2,1)S(1)}, u32[]{:S(2)}, u32[]{:S(2)}) collective-permute-start(bf16[2,4,112,640]{3,2,1,0:T(8,128)(2,1)} %fusion.1), channel_id=1, source_target_pairs={{0,4},{2,6},{4,0},{6,2},{8,12},{10,14},{12,8},{14,10},{16,20},{18,... | collective-permute-start | bytes 3440648 | tf_op jit(solution)/shard_map/ppermute | solution.py:554
  387.1 30.3 %collective-permute-start.49 = (bf16[2,240,640]{2,1,0:T(8,128)(2,1)S(1)}, bf16[2,240,640]{2,1,0:T(8,128)(2,1)S(1)}, u32[]{:S(2)}, u32[]{:S(2)}) collective-permute-start(bf16[2,240,640]{2,1,0:T(8,128)(2,1)S(1)} %pad_maximum_fusion.7), channel_id=1, source_target_pairs={{0,16},{2,18},{4,20},{6,22},{8,24},{10,26},{12,28},{14,30},{16,0},... | collective-permute-start | bytes 1843208 | tf_op jit(solution)/shard_map/ppermute | solution.py:554
  (83 other events, 810.9 us)

commit v3 on v2

v3 whole, which is shorter than its diff:
```python
import functools

import jax
import jax.numpy as jnp
import numpy as np
from jax import lax
from jax.experimental import pallas as pl
from jax.experimental.pallas import tpu as pltpu
from jax.sharding import PartitionSpec as P

D = 640
HEADS = 20
HEAD_DIM = 32
FF = 2560
LAYERS = 2
EPSILON = 1e-05
MASKED = -1e9
LANES = 128
GROUPS = D // LANES
PER_GROUP = LANES // HEAD_DIM
BLOCKS = FF // D
EARLY, LATE = (0, 3), (3, 2)
PIECE = 80
VECS = 16
AXES = ("wide", "narrow")
WHOLE, WHOLE_ROWS = (4, 2, PIECE, FF), (4, 2, 2, 2, PIECE, D)
SLACK = 8 * 1024 * 1024
f32, bf16 = jnp.float32, jnp.bfloat16

GAIN_A, GAIN_F, SHIFT_A, BIAS_QKV, BIAS_OUT, SHIFT_F, BIAS_UP, BIAS_DOWN = 0, 1, 2, 3, 6, 7, 8, 12


def rotary_tables(length):
    half = HEAD_DIM // 2
    inverse = 1.0 / 10000.0 ** (np.arange(half) * (2.0 / HEAD_DIM))
    angles = np.arange(length)[:, None] * inverse[None, :]
    cos, sine = np.cos(angles), np.sin(angles)
    none = np.zeros_like(sine)
    ahead = np.tile(np.concatenate([-sine, none], 1), (1, PER_GROUP))
    behind = np.tile(np.concatenate([none, sine], 1), (1, PER_GROUP))
    wide = np.stack([np.tile(cos, (1, 2 * PER_GROUP)), ahead, behind]).astype(np.float32)
    return jnp.asarray(wide), jnp.asarray(np.stack([cos.T, sine.T]).astype(np.float32))


def dot(left, right):
    return jnp.dot(left, right, preferred_element_type=f32)


def dot_nt(left, right):
    return lax.dot_general(left, right, (((1,), (1,)), ((), ())), preferred_element_type=f32)


def dot_tn(left, right):
    return lax.dot_general(left, right, (((0,), (0,)), ((), ())), preferred_element_type=f32)


def rotated(value, table):
    half = HEAD_DIM // 2
    return value * table[0] + pltpu.roll(value, LANES - half, 1) * table[1] + pltpu.roll(value, half, 1) * table[2]


def rotated_back(value, table):
    half = HEAD_DIM // 2
    first, second = value[:half], value[half:]
    return jnp.concatenate([first * table[0] + second * table[1], second * table[0] - first * table[1]], 0)


def unit_of(value):
    centered = value - jnp.mean(value, -1, keepdims=True)
    inverse = lax.rsqrt(jnp.mean(centered * centered, -1, keepdims=True) + EPSILON)
    return centered * inverse, inverse


def norm_back(grad, unit, inverse, gain):
    scaled = grad * gain
    return inverse * (scaled - jnp.mean(scaled, -1, keepdims=True) - unit * jnp.mean(scaled * unit, -1, keepdims=True))


def column_sum(value):
    return jnp.sum(value, 0, keepdims=True)


def gelu_parts(value):
    scaled = jnp.abs(value) * 0.7071067811865476
    t = 1.0 / (1.0 + 0.3275911 * scaled)
    bell = jnp.exp(-scaled * scaled)
    series = t * (0.127414796 + t * (-0.142248368 + t * (0.7107068705 + t * (-0.7265760135 + t * 0.5307027145))))
    tail = series * bell
    return jnp.where(value >= 0.0, 1.0 - tail, tail), bell * 0.3989422804014327


def row_loop(length, step, body):
    def run(i, carry):
        body(pl.ds(pl.multiple_of(i * step, step), step), i)
        return carry

    lax.fori_loop(0, length // step, run, 0)


def owner_of(coords, kn, kb, ka, k2, k1):
    n = coords[3] ^ kn
    z = coords[0] ^ (2 * k1 + k2 + n * (k2 - k1))
    return z, coords[1] ^ (kb + n * (ka - kb)), coords[2] ^ (ka + n * (kb - ka)), n


PLACES = [(ka, k2, k1) for ka in range(2) for k2 in range(2) for k1 in range(2)]


class Assembly:
    def __init__(self, coords, by_rows, pieces, offset, whole, sems):
        self.by_rows, self.whole, self.sems = by_rows, whole, sems
        self.any = pieces[0].at[0, :, pl.ds(offset, PIECE)]
        for kb in range(2):
            for kn in range(2):
                n = coords[3] ^ kn
                b = (coords[1] + n * (coords[2] - coords[1])) ^ kb
                for a in range(2):
                    target = self.target(a + n * (b - a), b + n * (a - b), n)
                    pltpu.make_async_copy(pieces[2 * kb + kn].at[a, :, pl.ds(offset, PIECE)], *target).start()

    def target(self, x, y, n):
        to = (y, x, n) if self.by_rows else (y, slice(None), pl.ds(pl.multiple_of((2 * x + n) * D, D), D))
        return self.whole.at[(slice(None), *to)], self.sems.at[4 * x + 2 * n + y]

    def wait(self, quarters=(0, 1, 2, 3)):
        for quarter in quarters:
            for y in range(2):
                pltpu.make_async_copy(self.any, *self.target(quarter // 2, y, quarter % 2)).wait()


def head_masks():
    lane = lax.broadcasted_iota(jnp.int32, (1, LANES), 1)
    return [(lane // HEAD_DIM == head).astype(f32).astype(bf16) for head in range(PER_GROUP)]


def masked_tail(length, live):
    row = lax.broadcasted_iota(jnp.int32, (length, LANES), 0)
    lane = lax.broadcasted_iota(jnp.int32, (length, LANES), 1)
    keys = jnp.where((lane == 0) & (row >= live), MASKED, 0.0).astype(bf16)
    row = lax.broadcasted_iota(jnp.int32, (LANES, length), 0)
    return keys, jnp.where(row == 0, 1.0, 0.0).astype(bf16)


def attn_fwd_kernel(plan, coords, x_ref, vec_ref, table_ref, *refs):
    count = len(plan)
    pieces, refs = refs[: 4 * count], refs[4 * count :]
    at_ref, qt_ref, kv_ref, ot_ref, lse_ref, m_ref, b_ref, bt_ref, *refs = refs
    wholes, refs = refs[:count], refs[count:]
    a_ref, q_ref, key_ref, query_ref, sems = refs
    length = x_ref.shape[0]
    jobs = [
        Assembly(coords, by_rows, pieces[4 * i : 4 * i + 4], offset, wholes[i], sems.at[i])
        for i, (offset, by_rows) in enumerate(plan)
    ]
    w_ref = wholes[0]

    def norm(rows, _):
        unit, _ = unit_of(x_ref[rows, :].astype(f32))
        a_ref[rows, :] = (unit * vec_ref[GAIN_A : GAIN_A + 1, :] + vec_ref[SHIFT_A : SHIFT_A + 1, :]).astype(bf16)

    row_loop(length, 128, norm)
    normed = a_ref[...]
    at_ref[...] = normed.T
    for part in range(3):
        jobs[0].wait([part])
        out = dot(normed, w_ref[:, :, :, part * D : (part + 1) * D].reshape(D, D)) + vec_ref[BIAS_QKV + part : BIAS_QKV + part + 1, :]
        if part == 0:
            out = out * HEAD_DIM**-0.5
        for group in range(GROUPS):
            lanes = slice(group * LANES, (group + 1) * LANES)
            piece = out[:, lanes]
            if part < 2:
                piece = rotated(piece, table_ref)
            if part == 0:
                qt_ref[lanes, :] = piece.astype(bf16).T
            else:
                kv_ref[:, (part - 1) * D + group * LANES : (part - 1) * D + (group + 1) * LANES] = piece.astype(bf16)
    masks = head_masks()
    tail, query_ref[LANES:, :] = masked_tail(length, coords[4])
    for head in range(PER_GROUP):
        key_ref[head, :, LANES:] = tail
    ones = jnp.ones((16, length), bf16)

    def group_step(group, carry):
        rows = pl.ds(pl.multiple_of(group * LANES, LANES), LANES)
        query_ref[:LANES, :] = qt_ref[rows, :]
        values = kv_ref[:, pl.ds(pl.multiple_of(D + group * LANES, LANES), LANES)].T
        for head in range(PER_GROUP):
            key_ref[head, :, :LANES] = kv_ref[:, rows] * masks[head]
        for head in range(PER_GROUP):
            scores = dot(key_ref[head], query_ref[...])
            top = jnp.max(scores, 0, keepdims=True)
            probs = jnp.exp(scores - top).astype(bf16)
            wide = jnp.concatenate([values[head * HEAD_DIM : (head + 1) * HEAD_DIM], ones], 0)
            out = dot(wide, probs)
            total = out[HEAD_DIM : HEAD_DIM + 1]
            to = pl.ds(pl.multiple_of(group * LANES + head * HEAD_DIM, HEAD_DIM), HEAD_DIM)
            ot_ref[to, :] = (out[:HEAD_DIM] / total).astype(bf16)
            lse_ref[pl.ds(group * PER_GROUP + head, 1), :] = top + jnp.log(total)
        return carry

    lax.fori_loop(0, GROUPS, group_step, 0)
    jobs[0].wait([3])
    q_ref[...] = ot_ref[...].T
    m_ref[...] = x_ref[...].astype(f32) + (dot(q_ref[...], w_ref[:, :, :, 3 * D :].reshape(D, D)) + vec_ref[BIAS_OUT : BIAS_OUT + 1, :])

    def after(rows, _):
        unit, _ = unit_of(m_ref[rows, :])
        b_ref[rows, :] = (unit * vec_ref[GAIN_F : GAIN_F + 1, :] + vec_ref[SHIFT_F : SHIFT_F + 1, :]).astype(bf16)

    row_loop(length, 128, after)
    bt_ref[...] = b_ref[...].T
    for job in jobs[1:]:
        job.wait()


def assemble_kernel(offset, by_rows, coords, *refs):
    Assembly(coords, by_rows, refs[:4], offset, refs[4], refs[5]).wait()


def ffn_fwd_kernel(offsets, last, coords, m_ref, b_ref, vec_ref, *refs):
    offset, offset_down = offsets
    if offset is None:
        up_ref, down_ref, y_ref, zt_ref, slope_ref, z_ref = refs
    elif offset_down is None:
        down_ref, *pieces, y_ref, zt_ref, slope_ref, up_ref, z_ref, sems = refs
    else:
        *pieces, y_ref, zt_ref, slope_ref, up_ref, down_ref, z_ref, sems = refs
    if offset is not None:
        job = Assembly(coords, False, pieces, offset, up_ref, sems.at[0])
    if offset_down is not None:
        job_down = Assembly(coords, True, pieces, offset_down, down_ref, sems.at[1])
    length = m_ref.shape[0]
    normed = b_ref[...]
    for block in range(BLOCKS):
        if offset is not None:
            job.wait([block])
        columns = slice(block * D, (block + 1) * D)
        part = up_ref[:, columns] if offset is None else up_ref[:, :, :, columns].reshape(D, D)
        pre = dot(normed, part) + vec_ref[BIAS_UP + block : BIAS_UP + block + 1, :]
        cdf, bell = gelu_parts(pre)
        z_ref[:, columns] = (pre * cdf).astype(bf16)
        slope_ref[:, columns] = (cdf + pre * bell).astype(bf16)
        zt_ref[columns, :] = z_ref[:, columns].T
    if offset_down is not None:
        job_down.wait()
    out = m_ref[...] + (dot(z_ref[...], down_ref[...].reshape(FF, D)) + vec_ref[BIAS_DOWN : BIAS_DOWN + 1, :])
    if last:
        row = lax.broadcasted_iota(jnp.int32, (length, 1), 0)
        out = jnp.where(row < coords[4], out, 0.0)
    y_ref[...] = out.astype(y_ref.dtype)


def ffn_bwd_kernel(top, coords, g_ref, slope_ref, m_ref, vec_ref, up_ref, down_ref, *refs):
    gb_ref, gu_ref, gm_ref, gmb_ref, sums_ref = refs
    length = m_ref.shape[0]
    sums_ref[...] = jnp.zeros_like(sums_ref)

    def add(row, value):
        sums_ref[row : row + 1, :] += column_sum(value)

    grad = g_ref[...].astype(f32)
    if top:
        row = lax.broadcasted_iota(jnp.int32, (length, 1), 0)
        grad = jnp.where(row < coords[4], grad, 0.0)
    low = grad.astype(bf16)
    gb_ref[...] = low
    add(BIAS_DOWN, low.astype(f32))
    for block in range(BLOCKS):
        columns = slice(block * D, (block + 1) * D)
        part = (dot_nt(low, down_ref[columns, :]) * slope_ref[:, columns].astype(f32)).astype(bf16)
        gu_ref[:, columns] = part
        add(BIAS_UP + block, part.astype(f32))
    gm_ref[...] = dot_nt(gu_ref[...], up_ref[...])

    def after(rows, i):
        normed_grad = gm_ref[rows, :]
        unit, inverse = unit_of(m_ref[rows, :])
        add(GAIN_F, normed_grad * unit)
        add(SHIFT_F, normed_grad)
        grad = g_ref[rows, :].astype(f32)
        if top:
            row = lax.broadcasted_iota(jnp.int32, (128, 1), 0) + i * 128
            grad = jnp.where(row < coords[4], grad, 0.0)
        middle = grad + norm_back(normed_grad, unit, inverse, vec_ref[GAIN_F : GAIN_F + 1, :])
        gm_ref[rows, :] = middle
        low = middle.astype(bf16)
        gmb_ref[rows, :] = low
        add(BIAS_OUT, low.astype(f32))

    row_loop(length, 128, after)


def attn_bwd_kernel(groups, coords, gmb_ref, qt_ref, kv_ref, ot_ref, lse_ref, table_ref, w_ref, *refs):
    start, count = groups
    gp_ref, *flip_ref, go_ref, key_ref, query_ref = refs
    length = gmb_ref.shape[0]
    low = gmb_ref[...]
    if flip_ref:
        flip_ref[0][...] = low.T
    go_ref[...] = dot_nt(w_ref[start * LANES : (start + count) * LANES, 3 * D :], low).astype(bf16)
    masks = head_masks()
    tail, query_ref[LANES:, :] = masked_tail(length, coords[4])
    for head in range(PER_GROUP):
        key_ref[head, :, LANES:] = tail

    def group_step(i, carry):
        group = i + start
        rows = pl.ds(pl.multiple_of(group * LANES, LANES), LANES)
        query, grad = qt_ref[rows, :], go_ref[pl.ds(pl.multiple_of(i * LANES, LANES), LANES), :]
        query_ref[:LANES, :] = query
        keys = kv_ref[:, rows]
        values = kv_ref[:, pl.ds(pl.multiple_of(D + group * LANES, LANES), LANES)]
        flipped = keys.T
        products = grad.astype(f32) * ot_ref[rows, :].astype(f32)
        for head in range(PER_GROUP):
            key_ref[head, :, :LANES] = keys * masks[head]
        for head in range(PER_GROUP):
            part = slice(head * HEAD_DIM, (head + 1) * HEAD_DIM)
            delta = column_sum(products[part])
            probs = jnp.exp(dot(key_ref[head], query_ref[...]) - lse_ref[pl.ds(group * PER_GROUP + head, 1), :])
            scores = (probs * (dot(values * masks[head], grad) - delta)).astype(bf16)
            dv = dot_nt(grad[part], probs.astype(bf16))
            dk = dot_nt(query[part], scores)
            dq = dot(flipped[part], scores)
            to = pl.ds(pl.multiple_of(i * LANES + head * HEAD_DIM, HEAD_DIM), HEAD_DIM)
            dq = rotated_back(dq.astype(bf16).astype(f32), table_ref) * HEAD_DIM**-0.5
            dk = rotated_back(dk.astype(bf16).astype(f32), table_ref)
            for part, value in enumerate((dq, dk, dv)):
                gp_ref[part, to, :] = value.astype(bf16)
        return carry

    lax.fori_loop(0, count, group_step, 0)


def attn_after_kernel(early_ref, late_ref, gm_ref, x_ref, vec_ref, w_ref, *refs):
    gx_ref, sums_ref, ga_ref = refs
    length = x_ref.shape[0]
    sums_ref[...] = jnp.zeros_like(sums_ref)

    def add(row, value):
        sums_ref[row : row + 1, :] += column_sum(value)

    ones = jnp.ones((16, length), bf16)
    total = 0.0
    for part in range(3):
        for ref, (start, count) in ((early_ref, EARLY), (late_ref, LATE)):
            columns = slice(start * LANES, (start + count) * LANES)
            sums_ref[BIAS_QKV + part : BIAS_QKV + part + 1, columns] = dot_nt(ones, ref[part])[:1]
            total = total + dot(w_ref[:, part * D + start * LANES : part * D + (start + count) * LANES], ref[part])
    ga_ref[...] = total.T

    def after(rows, _):
        normed_grad = ga_ref[rows, :]
        unit, inverse = unit_of(x_ref[rows, :].astype(f32))
        add(GAIN_A, normed_grad * unit)
        add(SHIFT_A, normed_grad)
        out = gm_ref[rows, :] + norm_back(normed_grad, unit, inverse, vec_ref[GAIN_A : GAIN_A + 1, :])
        gx_ref[rows, :] = out.astype(gx_ref.dtype)

    row_loop(length, 128, after)


def grads_kernel(items, inputs, phase, coords, *refs):
    ins, outs, (left_ref, whole_ref) = refs[:inputs], refs[inputs:-2], refs[-2:]

    def put(value, kb, ka, k2, k1, to):
        to = slice(to, to + value.shape[0])
        if phase:
            outs[0][kb, ka, k2, k1, to] = value
        elif kb:
            outs[0][ka, k2, k1, to] = value
        elif ka:
            outs[1][k2, k1, to] = value
        else:
            outs[2][k2, k1, to] = value

    for kind, lefts, right, to in items:
        if kind == "down":
            for kb in range(2):
                for place, (ka, k2, k1) in enumerate(PLACES):
                    z, y, x, n = owner_of(coords, phase, kb, ka, k2, k1)
                    start = pl.multiple_of((8 * z + 4 * y + 2 * x + n) * PIECE, PIECE)
                    left_ref[place * PIECE : (place + 1) * PIECE, :] = ins[lefts[0]][pl.ds(start, PIECE), :]
                whole = dot(left_ref[...], ins[right][...]).astype(bf16)
                for place, (ka, k2, k1) in enumerate(PLACES):
                    put(whole[place * PIECE : (place + 1) * PIECE], kb, ka, k2, k1, to)
        else:
            for kx in range(2):
                quarter = 2 * (coords[2] ^ kx) + (coords[3] ^ phase)
                n = coords[3] ^ phase
                for ky in range(2):
                    for kz in range(4):
                        k2, k1 = kz // 2, kz % 2
                        z = coords[0] ^ (2 * k1 + k2 + n * (k2 - k1))
                        start = pl.multiple_of((2 * z + (coords[1] ^ ky)) * PIECE, PIECE)
                        to_row = (4 * ky + kz) * PIECE
                        if kind == "up":
                            part = ins[lefts[0]][pl.ds(start, PIECE), :]
                        else:
                            part = jnp.where(quarter == 3, ins[lefts[1]][pl.ds(start, PIECE), :], ins[lefts[0]][pl.ds(start, PIECE), :])
                        left_ref[to_row : to_row + PIECE, :] = part
                if kind == "attn":

                    @pl.when(quarter == 3)
                    def _(right=right):
                        whole_ref[...] = dot_nt(left_ref[...], ins[right][...]).astype(bf16)

                    @pl.when(quarter < 3)
                    def _(right=right, quarter=quarter):
                        part = jnp.minimum(quarter, 2)
                        for i, (start, count) in ((2, EARLY), (1, LATE)):
                            columns = slice(start * LANES, (start + count) * LANES)
                            whole_ref[:, columns] = dot_nt(left_ref[...], ins[right - i][part]).astype(bf16)

                else:
                    columns = pl.ds(pl.multiple_of(quarter * D, D), D)
                    whole_ref[...] = dot(left_ref[...], ins[right][:, columns]).astype(bf16)

                def write(swapped, kx=kx, to=to):
                    for ky in range(2):
                        for kz in range(4):
                            start = (4 * ky + kz) * PIECE
                            ka, kb = (ky, kx) if swapped else (kx, ky)
                            put(whole_ref[start : start + PIECE, :], kb, ka, kz // 2, kz % 2, to)

                pl.when(n == 0)(functools.partial(write, False))
                pl.when(n == 1)(functools.partial(write, True))


def call(kernel, ins, outs, scratch, name, flops, exps=0):
    moved = sum(a.size * a.dtype.itemsize for a, _ in ins) + sum(int(np.prod(s)) * jnp.dtype(t).itemsize for s, t in outs)
    limit = SLACK + sum(int(np.prod(t.shape)) * t.dtype.itemsize for t in scratch if t.memory_space == V)
    return pl.pallas_call(
        kernel,
        out_shape=[jax.ShapeDtypeStruct(s, t) for s, t in outs],
        in_specs=[pl.BlockSpec(memory_space=space) for _, space in ins],
        out_specs=[pl.BlockSpec(memory_space=pltpu.VMEM)] * len(outs),
        scratch_shapes=scratch,
        compiler_params=pltpu.CompilerParams(vmem_limit_bytes=limit),
        cost_estimate=pl.CostEstimate(flops=int(flops), bytes_accessed=int(moved), transcendentals=int(exps)),
        name=name,
    )(*[a for a, _ in ins])


V, S, H = pltpu.VMEM, pltpu.SMEM, pl.ANY
SEMS = pltpu.SemaphoreType.DMA


def attn_fwd(coords, x, vec, table, weights):
    n = x.shape[0]
    ins = [(coords, S), (x, V), (vec, V), (table[0], V)] + [(p, H) for w in weights for p in w[0]]
    outs = [((D, n), bf16), ((D, n), bf16), ((n, 2 * D), bf16), ((D, n), bf16), ((24, n), f32)]
    outs += [((n, D), f32), ((n, D), bf16), ((D, n), bf16)]
    outs += [(WHOLE_ROWS if w[2] else WHOLE, bf16) for w in weights]
    scratch = [V((n, D), bf16), V((n, D), bf16), V((PER_GROUP, n, 2 * LANES), bf16), V((2 * LANES, n), bf16)]
    scratch.append(SEMS((len(weights), 8)))
    kernel = functools.partial(attn_fwd_kernel, [w[1:] for w in weights])
    out = call(kernel, ins, outs, scratch, "attn_fwd", 2 * n * D * FF + 4 * n * n * D, HEADS * n * n)
    return dict(zip(("at", "qt", "kv", "ot", "lse", "m", "b", "bt"), out[:8], strict=True)) | {"x": x}, [w.reshape((FF, D) if w.ndim == 6 else (D, FF)) for w in out[8:]]


def assemble(coords, weight):
    pieces, offset, by_rows = weight
    outs = [(WHOLE_ROWS if by_rows else WHOLE, bf16)]
    ins = [(coords, S)] + [(p, H) for p in pieces]
    out = call(functools.partial(assemble_kernel, offset, by_rows), ins, outs, [SEMS((8,))], "assemble", 0)[0]
    return out.reshape((FF, D) if by_rows else (D, FF))


def ffn_fwd(coords, kept, vec, up, down, last):
    n = kept["m"].shape[0]
    parts = [isinstance(w, tuple) for w in (up, down)]
    ins = [(coords, S), (kept["m"], V), (kept["b"], V), (vec, V)]
    ins += [(w, V) for w, part in zip((up, down), parts) if not part]
    ins += [(p, H) for p in up[0]] if parts[0] else []
    outs = [((n, D), bf16 if last else f32), ((FF, n), bf16), ((n, FF), bf16)]
    outs += [(shape, bf16) for shape, part in zip((WHOLE, WHOLE_ROWS), parts) if part]
    scratch = [V((n, FF), bf16)] + ([SEMS((2, 8))] if parts[0] else [])
    offsets = [w[1] if part else None for w, part in zip((up, down), parts)]
    kernel = functools.partial(ffn_fwd_kernel, offsets, last)
    y, zt, slope, *more = call(kernel, ins, outs, scratch, "ffn_fwd", 4 * n * D * FF, 2 * n * FF)
    up = more[0].reshape(D, FF) if parts[0] else up
    down = more[1].reshape(FF, D) if parts[1] else down
    return y, {"zt": zt, "slope": slope}, up, down


def ffn_bwd(coords, g, kept, vec, up, down, top):
    n = g.shape[0]
    ins = [(coords, S)] + [(a, V) for a in (g, kept["slope"], kept["m"], vec, up, down)]
    outs = [((n, D), bf16), ((n, FF), bf16), ((n, D), f32), ((n, D), bf16), ((VECS, D), f32)]
    out = call(functools.partial(ffn_bwd_kernel, top), ins, outs, [], "ffn_bwd", 4 * n * D * FF, 0)
    return dict(zip(("gb", "gu", "gm", "gmb", "sums"), out, strict=True))


def attn_bwd(coords, gmb, kept, table, weight, groups):
    n = gmb.shape[0]
    ins = [(coords, S)] + [(a, V) for a in (gmb, kept["qt"], kept["kv"], kept["ot"], kept["lse"], table[1], weight)]
    rows = groups[1] * LANES
    scratch = [V((rows, n), bf16), V((PER_GROUP, n, 2 * LANES), bf16), V((2 * LANES, n), bf16)]
    outs = [((3, rows, n), bf16)] + ([((D, n), bf16)] if groups == LATE else [])
    flops = 2 * n * D * rows + 10 * n * n * rows
    kernel = functools.partial(attn_bwd_kernel, groups)
    return call(kernel, ins, outs, scratch, "attn_bwd", flops, HEADS * n * n)


def attn_after(back, kept, vec, weight, last):
    n = back["gm"].shape[0]
    ins = [(a, V) for a in (back["early"], back["late"], back["gm"], kept["x"], vec, weight)]
    outs = [((n, D), bf16 if last else f32), ((VECS, D), f32)]
    return call(attn_after_kernel, ins, outs, [V((n, D), f32)], "attn_after", 6 * n * D * D, 0)


def grads(coords, items, phase):
    arrays, plan, flops, rows = [], [], 0, 0
    for kind, lefts, right, height in items:
        index = list(range(len(arrays), len(arrays) + len(lefts)))
        arrays += [*lefts, right]
        plan.append((kind, index, len(arrays) - 1, rows))
        rows += height
        flops += 2 * arrays[0].shape[1] * D * D * 2
    leads = [(2, 2, 2, 2)] if phase else [(2, 2, 2), (2, 2), (2, 2)]
    outs = [((*lead, rows, D), bf16) for lead in leads]
    kernel = functools.partial(grads_kernel, plan, len(arrays), phase)
    ins = [(coords, S)] + [(a, V) for a in arrays]
    return call(kernel, ins, outs, [V((D, arrays[0].shape[1]), bf16), V((D, D), bf16)], "grads", flops, 0)


def mate(value):
    return lax.ppermute(value, "narrow", [(0, 1), (1, 0)])


def step(link, value):
    masks = ((8, 4, 1, 2)[link], (4, 8, 2, 1)[link])
    pairs = [(2 * w + n, 2 * (w ^ masks[n]) + n) for w in range(16) for n in range(2)]
    return lax.ppermute(value, AXES, pairs)


def relative(values, bits):
    for place_of, bit in enumerate(reversed(bits)):
        flip = 1 << place_of
        values = [jnp.where(bit > 0, values[i ^ flip], values[i]) for i in range(len(values))]
    return values


def add(*terms):
    return functools.reduce(lambda p, q: p + q, [t.astype(f32) for t in terms])


def regroup(parts, bits):
    mine = relative(parts, bits)
    return relative([mine[0]] + [lax.ppermute(mine[k], AXES, [(i, i ^ k) for i in range(32)]) for k in (1, 2, 3)], bits)


def vector_tables(gains, biases):
    gains = gains.astype(f32).reshape(LAYERS, 2, D)
    biases = biases.astype(f32).reshape(LAYERS, 11, D)
    return jnp.concatenate([gains, biases, jnp.zeros((LAYERS, VECS - 13, D), f32)], 1)


NAMES = ("down", "up", "attn")
LOTS = tuple(((name, l),) for l in (1, 0) for name in NAMES)


def whole_weight(matrix, by_rows):
    if by_rows:
        cut = jnp.transpose(matrix.reshape(4, 2, 2, 2, PIECE, D), (3, 1, 2, 0, 4, 5))
    else:
        cut = jnp.transpose(matrix.reshape(4, 2, PIECE, 2, 2, D), (4, 1, 3, 0, 2, 5))
    cut = [cut[0], jnp.swapaxes(cut[1], 0, 1)]
    return [cut[kn][kb] for kb in range(2) for kn in range(2)], 0, by_rows


def whole_grad(core, rest, rows, by_rows):
    near = jnp.stack([jnp.stack([rest[2], rest[1]]), rest[0]])
    cut = jnp.stack([jnp.transpose(near, (1, 0, 3, 2, 4, 5)), core])[..., rows, :]
    if by_rows:
        return jnp.transpose(cut, (3, 4, 2, 1, 0, 5, 6)).reshape(FF, D)
    return jnp.transpose(cut, (3, 4, 2, 5, 1, 0, 6)).reshape(D, FF)


def fetch_plain(w_qkv, w_out, w_up, w_down, gains, biases):
    def whole(value, rows):
        return lax.all_gather(value, AXES, axis=0, tiled=True).reshape(rows, -1)

    weights = {}
    for l in range(LAYERS):
        attn = jnp.concatenate([whole(w_qkv[l], D), whole(w_out[l], D)], 1)
        weights["attn", l] = whole_weight(attn, False)
        weights["up", l] = whole_weight(whole(w_up[l], D), False)
        weights["down", l] = whole_weight(whole(w_down[l], FF), True)
    return weights, vector_tables(whole(gains, 1)[0], whole(biases, 1)[0])


class Lot:
    def first(self, core, rest):
        self.core, self.rest = core, rest
        return add(rest[0], core[1]).astype(bf16)

    def second(self, got):
        self.got = got
        return add(self.rest[1], self.core[0, 1], got[1]).astype(bf16)

    def third(self, got):
        total = add(self.rest[2], self.core[0, 0], self.got[0], got)
        self.total = total[0]
        return total[1].astype(bf16)

    def fourth(self, got):
        total = add(self.total, got)
        self.total = total[0]
        return total[1].astype(bf16)

    def last(self, got):
        return add(self.total, got)


def stage(*groups):
    flat, tree = jax.tree.flatten(groups)
    return jax.tree.unflatten(tree, lax.optimization_barrier(flat))


def device_bits():
    wide = lax.axis_index("wide")
    return [(wide >> 3) & 1, (wide >> 2) & 1, (wide >> 1) & 1, wide & 1, lax.axis_index("narrow")]


def coordinates(values):
    return jnp.stack([jnp.asarray(v, jnp.int32) for v in values])


def layer_grads(sums):
    both = jnp.stack(sums)
    return both[:, :2].reshape(-1), both[:, 2:13].reshape(-1)


def gradient_blocks(coords, lot, kept, back, phase):
    items = []
    for name, l in LOTS[lot]:
        if name == "attn":
            items.append((name, [kept[l]["at"], kept[l]["ot"], back[l]["early"], back[l]["late"]], back[l]["flip"], PIECE))
        elif name == "up":
            items.append((name, [kept[l]["bt"]], back[l]["gu"], PIECE))
        else:
            items.append((name, [kept[l]["zt"]], back[l]["gb"], PIECE))
    outs = grads(coords, items, phase)
    return outs[0] if phase else outs


def shares_of(parts, bits):
    rows = D // 32
    cut = jnp.stack(parts)
    whole = jnp.concatenate(regroup([cut[:, s * rows : (s + 1) * rows] for s in range(4)], bits[3:]), 2)
    return [whole[i] for i in range(len(parts))]


def body(tokens, lengths, w_qkv, w_out, w_up, w_down, gains, biases, cotangent):
    args = (tokens, lengths, w_qkv, w_out, w_up, w_down, gains, biases, cotangent)
    if lax.axis_size("wide") == 16 and lax.axis_size("narrow") == 2:
        return staged(*args)
    return plain(*args)


def plain(tokens, lengths, w_qkv, w_out, w_up, w_down, gains, biases, cotangent):
    length = tokens.shape[0] // lengths.shape[0]
    coords = coordinates([0, 0, 0, 0, lengths[0]])
    table = rotary_tables(length)
    weights, vectors = fetch_plain(w_qkv, w_out, w_up, w_down, gains, biases)
    kept, back, wholes, x = [], [{}, {}], [], tokens
    for l in range(LAYERS):
        held, whole = attn_fwd(coords, x, vectors[l], table, [weights[name, l] for name in ("attn", "up", "down")])
        x, more, *_ = ffn_fwd(coords, held, vectors[l], whole[1], whole[2], l == LAYERS - 1)
        kept.append(held | more)
        wholes.append(whole)
    output, grad, sums = x, cotangent, [None] * LAYERS
    for l in reversed(range(LAYERS)):
        last = l == 0
        back[l] = ffn_bwd(coords, grad, kept[l], vectors[l], wholes[l][1], wholes[l][2], not last)
        (back[l]["early"],) = attn_bwd(coords, back[l]["gmb"], kept[l], table, wholes[l][0], EARLY)
        back[l]["late"], back[l]["flip"] = attn_bwd(coords, back[l]["gmb"], kept[l], table, wholes[l][0], LATE)
        grad, more = attn_after(back[l], kept[l], vectors[l], wholes[l][0], last)
        sums[l] = back[l]["sums"] + more
    matrices = {}
    for lot, keys in enumerate(LOTS):
        core, rest = [gradient_blocks(coords, lot, kept, back, phase) for phase in (1, 0)]
        for i, key in enumerate(keys):
            rows = slice(i * PIECE, (i + 1) * PIECE)
            matrices[key] = whole_grad(core, rest, rows, key[0] == "down").astype(f32)
    outs = []
    for name, begin, end in (("attn", 0, 3 * D), ("attn", 3 * D, FF), ("up", 0, FF), ("down", 0, D)):
        cut = jnp.stack([matrices[name, l][:, begin:end].reshape(-1) for l in range(LAYERS)])
        outs.append(lax.psum_scatter(cut, AXES, scatter_dimension=1, tiled=True))
    outs += [lax.psum_scatter(v, AXES, scatter_dimension=0, tiled=True) for v in layer_grads(sums)]
    return (output, grad, *outs)


def turned(value, bits):
    value = value.reshape(2, 2, 2, 2, 2, -1)
    for axis, bit in enumerate(bits):
        value = jnp.where(bit > 0, jnp.flip(value, axis), value)
    cores = [jnp.transpose(value, order) for order in ((4, 2, 3, 1, 0, 5), (4, 3, 2, 0, 1, 5))]
    own = jnp.where(bits[4] > 0, cores[1][0], cores[0][0])
    other = jnp.where(bits[4] > 0, cores[0][1], cores[1][1])
    return jnp.stack([own, other])


def ordered(bit, own, got):
    return jnp.stack([jnp.where(bit > 0, got, own), jnp.where(bit > 0, own, got)])


def staged(tokens, lengths, w_qkv, w_out, w_up, w_down, gains, biases, cotangent):
    length = tokens.shape[0] // lengths.shape[0]
    bits = device_bits()
    coords = coordinates([lax.axis_index("wide") >> 2, *bits[2:], lengths[0]])
    table = rotary_tables(length)
    rows = D // 32
    weights, whole = {}, {}

    z1, z0, y, x, n = bits
    third, fourth = jnp.where(n > 0, y, x), jnp.where(n > 0, x, y)

    def link0(value):
        return ordered(jnp.where(n > 0, z0, z1), value, step(0, value))

    def link1(value):
        return value, step(1, value)

    def by_z(pair):
        own, got = pair
        blocks = []
        for high in range(2):
            for low in range(2):
                core0 = jnp.where(z0 == low, own[high], got[high])
                blocks.append(jnp.where(n > 0, jnp.where(z1 == high, own[low], got[low]), core0))
        return jnp.stack(blocks)

    def link2(value):
        return ordered(third, value, step(2, value))

    def arrived(keys, *pieces):
        offset = 0
        for key, height in keys:
            weights[key] = (list(pieces), offset, key[0] == "down")
            offset += height

    small = jnp.concatenate([gains, biases])
    width = small.shape[0]
    c0 = jnp.concatenate([w_down[0].reshape(PIECE, D), jnp.zeros((16, D), bf16).at[0, :width].set(small)])
    c0, w_qkv, w_out, w_up = stage(c0, w_qkv, w_out, w_up)
    t0 = link0(c0)
    flat = []
    for l in range(LAYERS):
        flat.append(jnp.concatenate([w_qkv[l].reshape(rows, 3 * D), w_out[l].reshape(rows, D)], 1))
        flat.append(w_up[l].reshape(rows, FF))
    flat = jnp.stack(flat)
    parts = [flat[:, :, s * D : (s + 1) * D] for s in range(4)]
    t0, parts = stage(t0, parts)
    u0 = link1(t0)
    c1, up0, attn1, up1 = jnp.concatenate(regroup(parts, bits[3:]), 1)
    c2, c3 = jnp.concatenate([up0, attn1]), jnp.concatenate([w_down[1].reshape(PIECE, D), up1])
    zz0, c1, c2, c3 = stage(by_z(u0), c1, c2, c3)
    near0, t1 = stage(link2(zz0), link0(c1))
    far0, mate0, u1, t2 = step(3, near0), mate(near0), link1(t1), link0(c2)
    far0, mate0, zz1, t2 = stage(far0, mate0, by_z(u1), t2)
    near1, far_mate0, u2, t3 = link2(zz1), mate(far0), link1(t2), link0(c3)
    near1, far_mate0, zz2, t3 = stage(near1, far_mate0, by_z(u2), t3)
    arrived(((("down", 0), PIECE),), near0, mate0, far0, far_mate0)
    far1, mate1, near2, u3 = step(3, near1), mate(near1), link2(zz2), link1(t3)
    whole["down", 0] = assemble(coords, weights["down", 0])
    own, other = [], []
    for first, second, to in ((near0, far0, own), (mate0, far_mate0, other)):
        turn = n if to is own else 1 - n
        both = ordered(jnp.where(turn > 0, x, y), first[:, :, PIECE, :width], second[:, :, PIECE, :width])
        to.append(jnp.where(turn > 0, jnp.transpose(both, (2, 1, 0, 3)), jnp.transpose(both, (2, 0, 1, 3))))
    both = ordered(n, own[0], other[0])
    both = jnp.transpose(both, (1, 2, 3, 0, 4)).reshape(32, width)
    vectors = vector_tables(both[:, : gains.shape[0]].reshape(-1), both[:, gains.shape[0] :].reshape(-1))
    far1, mate1, near2, zz3, vectors, whole = stage(far1, mate1, near2, by_z(u3), vectors, whole)
    far_mate1, near2, zz3 = stage(mate(far1), near2, zz3)
    arrived(((("attn", 0), PIECE),), near1, mate1, far1, far_mate1)
    kept, back = [None, None], [None, None]
    far2, mate2 = step(3, near2), mate(near2)
    kept[0], got = attn_fwd(coords, tokens, vectors[0], table, [weights["attn", 0]])
    whole["attn", 0] = got[0]
    far2, mate2, kept[0] = stage(far2, mate2, kept[0])
    far_mate2, kept[0], zz3 = stage(mate(far2), kept[0], zz3)
    arrived(((("up", 0), PIECE), (("attn", 1), PIECE)), near2, mate2, far2, far_mate2)
    got3 = step(2, zz3)
    h, more, whole["up", 0], _ = ffn_fwd(coords, kept[0], vectors[0], weights["up", 0], whole["down", 0], False)
    kept[0] |= more
    got3, h = stage(got3, h)
    near3, h = stage(ordered(third, zz3, got3), h)
    far3, mate3 = step(3, near3), mate(near3)
    kept[1], got = attn_fwd(coords, h, vectors[1], table, [weights["attn", 1]])
    whole["attn", 1] = got[0]
    far3, mate3, kept[1] = stage(far3, mate3, kept[1])
    arrived(((("down", 1), PIECE), (("up", 1), PIECE)), near3, mate3, far3, mate(far3))
    output, more, whole["up", 1], whole["down", 1] = ffn_fwd(
        coords, kept[1], vectors[1], weights["up", 1], weights["down", 1], True
    )
    kept[1] |= more

    d1, u1, a1, d0, u0, a0 = [Lot() for _ in LOTS]

    def blocks(lot, phase):
        return gradient_blocks(coords, lot, kept, back, phase)

    live = jnp.arange(length, dtype=jnp.int32)[:, None] < lengths[0]
    back[1] = {"gb": jnp.where(live, cotangent, jnp.zeros((), bf16))}
    core, back[1] = stage(blocks(0, 1), back[1])
    first, cotangent = stage(d1.first(mate(core), blocks(0, 0)), cotangent)

    got_d1 = step(3, first)
    back[1] |= ffn_bwd(coords, cotangent, kept[1], vectors[1], whole["up", 1], whole["down", 1], True)
    got_d1, core, back[1] = stage(got_d1, blocks(1, 1), back[1])
    second, core, back[1] = stage(d1.second(got_d1), core, back[1])

    got_d1, core, rest = stage(step(2, second), mate(core), blocks(1, 0))
    first, third, back[1] = stage(u1.first(core, rest), d1.third(got_d1), back[1])

    got_u1, got_d1 = step(3, first), step(1, third)
    (back[1]["early"],) = attn_bwd(coords, back[1]["gmb"], kept[1], table, whole["attn", 1], EARLY)
    got_u1, got_d1, back[1] = stage(got_u1, got_d1, back[1])
    second, fourth, back[1] = stage(u1.second(got_u1), d1.fourth(got_d1), back[1])

    got_u1, got_d1 = step(2, second), step(0, fourth)
    back[1]["late"], back[1]["flip"] = attn_bwd(coords, back[1]["gmb"], kept[1], table, whole["attn", 1], LATE)
    got_u1, got_d1, core, back[1] = stage(got_u1, got_d1, blocks(2, 1), back[1])
    third, core, back[1] = stage(u1.third(got_u1), core, back[1])

    got_u1, core, rest = stage(step(1, third), mate(core), blocks(2, 0))
    first, fourth, back[1] = stage(a1.first(core, rest), u1.fourth(got_u1), back[1])

    got_a1, got_u1 = step(3, first), step(0, fourth)
    grad, more = attn_after(back[1], kept[1], vectors[1], whole["attn", 1], False)
    sums = [None, back[1]["sums"] + more]
    back[0] = {"gb": grad.astype(bf16)}
    got_a1, got_u1, core, grad, back[0] = stage(got_a1, got_u1, blocks(3, 1), grad, back[0])
    second, core, grad, back[0] = stage(a1.second(got_a1), core, grad, back[0])

    got_a1, core, rest = stage(step(2, second), mate(core), blocks(3, 0))
    first, third, grad, back[0] = stage(d0.first(core, rest), a1.third(got_a1), grad, back[0])

    got_d0, got_a1 = step(3, first), step(1, third)
    back[0] |= ffn_bwd(coords, grad, kept[0], vectors[0], whole["up", 0], whole["down", 0], False)
    got_d0, got_a1, core, back[0] = stage(got_d0, got_a1, blocks(4, 1), back[0])
    second, fourth, core, back[0] = stage(d0.second(got_d0), a1.fourth(got_a1), core, back[0])

    got_d0, got_a1, core, rest = stage(step(2, second), step(0, fourth), mate(core), blocks(4, 0))
    first, third, back[0] = stage(u0.first(core, rest), d0.third(got_d0), back[0])

    got_u0, got_d0 = step(3, first), step(1, third)
    (back[0]["early"],) = attn_bwd(coords, back[0]["gmb"], kept[0], table, whole["attn", 0], EARLY)
    got_u0, got_d0, back[0] = stage(got_u0, got_d0, back[0])
    second, fourth, back[0] = stage(u0.second(got_u0), d0.fourth(got_d0), back[0])

    got_u0, got_d0 = step(2, second), step(0, fourth)
    back[0]["late"], back[0]["flip"] = attn_bwd(coords, back[0]["gmb"], kept[0], table, whole["attn", 0], LATE)
    got_u0, got_d0, core, back[0] = stage(got_u0, got_d0, blocks(5, 1), back[0])
    third, core, back[0] = stage(u0.third(got_u0), core, back[0])

    got_u0, core, rest = stage(step(1, third), mate(core), blocks(5, 0))
    first, fourth, back[0] = stage(a0.first(core, rest), u0.fourth(got_u0), back[0])

    got_a0, got_u0 = step(3, first), step(0, fourth)
    grad, more = attn_after(back[0], kept[0], vectors[0], whole["attn", 0], True)
    sums[0] = back[0]["sums"] + more
    got_a0, got_u0, grad, sums = stage(got_a0, got_u0, grad, sums)
    small = turned(jnp.concatenate([v.reshape(32, -1) for v in layer_grads(sums)], 1), bits)[..., None, :]
    small = jnp.pad(small, ((0, 0),) * 5 + ((0, 15), (0, D - width))).astype(bf16)
    extra = Lot()
    first_x = extra.first(mate(small[1]), [small[0, 1], small[0, 0, 1], small[0, 0, 0]])
    second, first_x = stage(a0.second(got_a0), first_x)

    got_a0, got_x = step(2, second), step(3, first_x)
    up1, attn1, up0 = shares_of([u1.last(got_u1), a1.last(got_a1), u0.last(got_u0)], bits)
    got_x = step(2, extra.second(got_x))
    got_a0, got_x, up1, attn1, up0 = stage(got_a0, got_x, up1, attn1, up0)
    third = jnp.concatenate([a0.third(got_a0), extra.third(got_x)], -2)
    a0.total = jnp.concatenate([a0.total, extra.total], -2)
    got_a0 = step(1, third)
    fourth = a0.fourth(got_a0)
    done_a0 = a0.last(step(0, fourth))
    (attn0,) = shares_of([done_a0[:PIECE]], bits)
    mine = done_a0[PIECE, :width]
    return (
        output,
        grad,
        jnp.stack([v[:, : 3 * D].reshape(-1) for v in (attn0, attn1)]),
        jnp.stack([v[:, 3 * D :].reshape(-1) for v in (attn0, attn1)]),
        jnp.stack([up0.reshape(-1), up1.reshape(-1)]),
        jnp.stack([d0.last(got_d0).reshape(-1), d1.last(got_d1).reshape(-1)]),
        mine[: gains.shape[0]],
        mine[gains.shape[0] :],
    )


def solution(mesh):
    both, flat, rows = P(AXES), P(None, AXES), P(AXES, None)
    return jax.shard_map(
        body,
        mesh=mesh,
        in_specs=(rows, both, flat, flat, flat, flat, both, both, rows),
        out_specs=(rows, rows, flat, flat, flat, flat, both, both),
        check_vma=False,
    )
```

time: 482 us -> 372 us (0.77)
  Pallas kernels: 221 us -> 143 us
  waiting for transfers between devices: 151 us -> 118 us
  starting transfers between devices: 52.3 us -> 62 us
  local copies, waits for them, and re-layouts: 19.5 us -> 14.4 us
    pallas_call x16 -> x25, Pallas kernels: 221 us -> 143 us  [call(): pl.pallas_call(kernel, out_shape=[jax.ShapeDtypeStruct(s, t) for s, t in...]
    ppermute x63 -> x66, waiting for transfers between devices: 151 us -> 118 us  [the longest x42 94.1 us: step(): return lax.ppermute(value, AXES, pairs)]
    ppermute x63 -> x66, starting transfers between devices: 52.3 us -> 62 us  [the longest x42 53.4 us: step(): return lax.ppermute(value, AXES, pairs)]
    convert_element_type x8 -> x15, other arithmetic: 12 us -> 4.77 us  [the longest x7 2.59 us: first(): return add(rest[0], core[1]).astype(bf16)]
  transfers between devices with their start and end apart: 63 -> 66, of which waited for: 29 -> 37; matrix products, arithmetic and copies ran while one was open for 3% -> 6% of each run, Pallas kernels for 37% -> 35%
where the time goes in v3:
time: 372 us; the launch traced here: 365 us
  Pallas kernels  143 us (38%)
  waiting for transfers between devices  118 us (32%)
  starting transfers between devices  62 us (17%)
  other arithmetic  24.2 us (7%)
  local copies, waits for them, and re-layouts  14.4 us (4%)
    pallas_call x25, Pallas kernels, call(): pl.pallas_call(kernel, out_shape=[jax.ShapeDtypeStruct(s, t) for s, t in...  143 us
    ppermute x42, waiting for transfers between devices, step(): return lax.ppermute(value, AXES, pairs)  94.1 us
    ppermute x42, starting transfers between devices, step(): return lax.ppermute(value, AXES, pairs)  53.4 us
    ppermute x9, waiting for transfers between devices, regroup(): lax.ppermute(mine[k], AXES, [(i, i ^ k) for i in range(32)])  13.4 us
    ppermute x15, waiting for transfers between devices, mate(): return lax.ppermute(value, 'narrow', [(0, 1), (1, 0)])  10.7 us
  transfers between devices with their start and end apart: 66, of which 37 were waited for; matrix products, arithmetic and copies ran while one was open for 6% of the time, Pallas kernels for 35%

profile of v3, /device:TPU:0, one launch (start us, length us, event | category | flops | bytes accessed | tf_op | source)
XLA Modules:
  0.0 365.4 jit_solution(693145991337635175)
XLA Ops:
  3.8 4.1 %collective-permute-start = (bf16[96,640]{1,0:T(8,128)(2,1)S(1)}, bf16[96,640]{1,0:T(8,128)(2,1)S(1)}, u32[]{:S(2)}, u32[]{:S(2)}) collective-permute-start(bf16[96,640]{1,0:T(8,128)(2,1)S(1)} %fusion.46), channel_id=1, source_target_pairs={{0,16},{1,9},{2,18},{3,11},{4,20},{5,13},{6,22},{7,15},{8,24},{9,1... | collective-permute-start | bytes 368648 | tf_op jit(solution)/shard_map/ppermute | solution.py:536
  43.9 5.4 %collective-permute-done.9 = bf16[2,80,640]{2,1,0:T(8,128)(2,1)S(1)} collective-permute-done((bf16[2,80,640]{2,1,0:T(8,128)(2,1)}, bf16[2,80,640]{2,1,0:T(8,128)(2,1)S(1)}, u32[]{:S(2)}, u32[]{:S(2)}) %collective-permute-start.9) | collective-permute-done | bytes 204832 | tf_op jit(solution)/shard_map/ppermute | solution.py:536
  53.0 4.5 %collective-permute-done.11 = bf16[4,80,640]{2,1,0:T(8,128)(2,1)S(1)} collective-permute-done((bf16[4,80,640]{2,1,0:T(8,128)(2,1)S(1)}, bf16[4,80,640]{2,1,0:T(8,128)(2,1)S(1)}, u32[]{:S(2)}, u32[]{:S(2)}) %collective-permute-start.11) | collective-permute-done | bytes 409632 | tf_op jit(solution)/shard_map/ppermute | solution.py:536
  58.6 4.3 %collective-permute-done.13 = bf16[2,160,640]{2,1,0:T(8,128)(2,1)S(1)} collective-permute-done((bf16[2,160,640]{2,1,0:T(8,128)(2,1)S(1)}, bf16[2,160,640]{2,1,0:T(8,128)(2,1)S(1)}, u32[]{:S(2)}, u32[]{:S(2)}) %collective-permute-start.13) | collective-permute-done | bytes 409632 | tf_op jit(solution)/shard_map/ppermute | solution.py:536
  71.0 9.9 %collective-permute-done.18 = bf16[2,160,640]{2,1,0:T(8,128)(2,1)S(1)} collective-permute-done((bf16[2,160,640]{2,1,0:T(8,128)(2,1)S(1)}, bf16[2,160,640]{2,1,0:T(8,128)(2,1)S(1)}, u32[]{:S(2)}, u32[]{:S(2)}) %collective-permute-start.18) | collective-permute-done | bytes 409632 | tf_op jit(solution)/shard_map/ppermute | solution.py:536
  89.4 18.5 %attn_fwd.2 = (bf16[640,512]{1,0:T(8,128)(2,1)S(1)}, bf16[640,512]{1,0:T(8,128)(2,1)S(1)}, bf16[512,1280]{1,0:T(8,128)(2,1)S(1)}, bf16[640,512]{1,0:T(8,128)(2,1...) custom-call(s32[5]{0:T(128)S(1)} %stack.189.coords, ...), custom_call_target="tpu_custom_call" | custom-call | flops 2348810240 | bytes 13983764 | tf_op jit(solution)/shard_map/attn_fwd/pallas_call | solution.py:434
  113.9 10.9 %ffn_fwd.2 = (f32[512,640]{1,0:T(8,128)S(1)}, bf16[2560,512]{1,0:T(8,128)(2,1)S(1)}, bf16[512,2560]{1,0:T(8,128)(2,1)S(1)}, bf16[4,2,80,2560]{3,2,1,0:T(8,128)(2,1)S(1)}) custom-call(s32[5]{0:T(128)S(1)} %stack.189.coords, f32[512,640]{1,0:T(8,128)S(1)} %get-tuple-element.356.m_ref, bf16[512,640]{1,0:T(8,128)(2,1)S(1)} %get-tuple-element.357.b_ref, ...), custom_call_target="tpu_custom_call" | custom-call | flops 3355443200 | bytes 21667860 | tf_op jit(solution)/shard_map/ffn_fwd/pallas_call | solution.py:434
  126.4 18.2 %attn_fwd.3 = (bf16[640,512]{1,0:T(8,128)(2,1)S(1)}, bf16[640,512]{1,0:T(8,128)(2,1)S(1)}, bf16[512,1280]{1,0:T(8,128)(2,1)S(1)}, bf16[640,512]{1,0:T(8,128)(2,1...) custom-call(s32[5]{0:T(128)S(1)} %stack.189.coords, ...), custom_call_target="tpu_custom_call" | custom-call | flops 2348810240 | bytes 17915924 | tf_op jit(solution)/shard_map/attn_fwd/pallas_call | solution.py:434
  149.9 12.4 %ffn_fwd.3 = (bf16[512,640]{1,0:T(8,128)(2,1)}, bf16[2560,512]{1,0:T(8,128)(2,1)S(1)}, bf16[512,2560]{1,0:T(8,128)(2,1)S(1)}, bf16[4,2,80,2560]{3,2,1,0:T(8,128)(2,1)S(1)}, bf16[4,2,2,2,80,640]{5,4,3,2,1,0:T(8,128)(2,1)S(1)}) custom-call(s32[5]{0:T(128)S(1)} %stack.189.coords, f32[512,640]{1,0:T(8,128)S(1)} %get-tuple-element.374.m_ref, ...), custom_call_target="tpu_custom_call" | custom-call | flops 3355443200 | bytes 21012500 | tf_op jit(solution)/shard_map/ffn_fwd/pallas_call | solution.py:434
  169.0 7.7 %ffn_bwd.2 = (bf16[512,640]{1,0:T(8,128)(2,1)}, bf16[512,2560]{1,0:T(8,128)(2,1)S(1)}, f32[512,640]{1,0:T(8,128)S(1)}, bf16[512,640]{1,0:T(8,128)(2,1)S(1)}, f32[16,640]{1,0:T(8,128)S(1)}) custom-call(s32[5]{0:T(128)S(1)} %stack.189.coords, bf16[512,640]{1,0:T(8,128)(2,1)S(1)} %copy-done.8, bf16[512,2560]{1,0:T(8,128)(2,1)S(1)} %get-tuple-element.387.slope_ref, ...), custom_call_target="tpu_custom_call" | custom-call | flops 3355443200 | bytes 16465940 | tf_op jit(solution)/shard_map/ffn_bwd/pallas_call | solution.py:434
  184.3 4.3 %collective-permute-done.29 = bf16[2,2,80,640]{3,2,1,0:T(8,128)(2,1)S(1)} collective-permute-done((bf16[2,2,80,640]{3,2,1,0:T(8,128)(2,1)S(1)}, bf16[2,2,80,640]{3,2,1,0:T(8,128)(2,1)S(1)}, u32[]{:S(2)}, u32[]{:S(2)}) %collective-permute-start.29) | collective-permute-done | bytes 409632 | tf_op jit(solution)/shard_map/ppermute | solution.py:536
  192.3 9.4 %attn_bwd.4.refs_2_.early_ref = bf16[3,384,512]{2,1,0:T(8,128)(2,1)S(1)} custom-call(s32[5]{0:T(128)S(1)} %stack.189.coords, bf16[512,640]{1,0:T(8,128)(2,1)S(1)} %get-tuple-element.435.gmb_ref, bf16[640,512]{1,0:T(8,128)(2,1)S(1)} %get-tuple-element.417.qt_ref, bf16[512,1280]{1,0:T(8,128)(2,1)S(1)} %copy-done.18, ...), custom_call_target="tpu_custom_call" | custom-call | flops 1258291200 | bytes 7847956 | tf_op jit(solution)/shard_map/attn_bwd/pallas_call | solution.py:434
  205.9 6.6 %attn_bwd.5 = (bf16[3,256,512]{2,1,0:T(8,128)(2,1)S(1)}, bf16[640,512]{1,0:T(8,128)(2,1)S(1)}) custom-call(s32[5]{0:T(128)S(1)} %stack.189.coords, bf16[512,640]{1,0:T(8,128)(2,1)S(1)} %get-tuple-element.435.gmb_ref, bf16[640,512]{1,0:T(8,128)(2,1)S(1)} %get-tuple-element.417.qt_ref, bf16[512,1280]{1,0:T(8,128)(2,1)S(1)} %copy-done.18, ...), custom_call_target="tpu_custom_call" | custom-call | flops 838860800 | bytes 8110100 | tf_op jit(solution)/shard_map/attn_bwd/pallas_call | solution.py:434
  230.5 4.9 %collective-permute-done.37 = bf16[2,2,2,80,640]{4,3,2,1,0:T(8,128)(2,1)S(1)} collective-permute-done((bf16[2,2,2,80,640]{4,3,2,1,0:T(8,128)(2,1)S(1)}, bf16[2,2,2,80,640]{4,3,2,1,0:T(8,128)(2,1)S(1)}, u32[]{:S(2)}, u32[]{:S(2)}) %collective-permute-start.37) | collective-permute-done | bytes 819232 | tf_op jit(solution)/shard_map/ppermute | solution.py:536
  238.2 5.5 %collective-permute-done.39 = bf16[2,2,80,640]{3,2,1,0:T(8,128)(2,1)S(1)} collective-permute-done((bf16[2,2,80,640]{3,2,1,0:T(8,128)(2,1)S(1)}, bf16[2,2,80,640]{3,2,1,0:T(8,128)(2,1)S(1)}, u32[]{:S(2)}, u32[]{:S(2)}) %collective-permute-start.39) | collective-permute-done | bytes 409632 | tf_op jit(solution)/shard_map/ppermute | solution.py:536
  245.6 7.2 %ffn_bwd.3 = (bf16[512,640]{1,0:T(8,128)(2,1)}, bf16[512,2560]{1,0:T(8,128)(2,1)S(1)}, f32[512,640]{1,0:T(8,128)S(1)}, bf16[512,640]{1,0:T(8,128)(2,1)S(1)}, f32[16,640]{1,0:T(8,128)S(1)}) custom-call(s32[5]{0:T(128)S(1)} %stack.189.coords, f32[512,640]{1,0:T(8,128)S(1)} %get-tuple-element.488.g_ref, bf16[512,2560]{1,0:T(8,128)(2,1)S(1)} %get-tuple-element.489.slope_ref, ...), custom_call_target="tpu_custom_call" | custom-call | flops 3355443200 | bytes 17121300 | tf_op jit(solution)/shard_map/ffn_bwd/pallas_call | solution.py:434
  266.8 9.4 %attn_bwd.6.refs_2_.early_ref = bf16[3,384,512]{2,1,0:T(8,128)(2,1)S(1)} custom-call(s32[5]{0:T(128)S(1)} %stack.189.coords, bf16[512,640]{1,0:T(8,128)(2,1)S(1)} %get-tuple-element.538.gmb_ref, bf16[640,512]{1,0:T(8,128)(2,1)S(1)} %copy-done.22, bf16[512,1280]{1,0:T(8,128)(2,1)S(1)} %copy-done.20, bf16[640,512]{1,0:T(8,128)(2,1)S(1)} %get-tuple-element.522.ot_ref.refs_1_, ...), custom_call_target="tpu_custom_call" | custom-call | flops 1258291200 | bytes 7847956 | tf_op jit(solution)/shard_map/attn_bwd/pallas_call | solution.py:434
  279.1 6.6 %attn_bwd.7 = (bf16[3,256,512]{2,1,0:T(8,128)(2,1)S(1)}, bf16[640,512]{1,0:T(8,128)(2,1)S(1)}) custom-call(s32[5]{0:T(128)S(1)} %stack.189.coords, bf16[512,640]{1,0:T(8,128)(2,1)S(1)} %get-tuple-element.538.gmb_ref, bf16[640,512]{1,0:T(8,128)(2,1)S(1)} %copy-done.22, bf16[512,1280]{1,0:T(8,128)(2,1)S(1)} %copy-done.20, ...), custom_call_target="tpu_custom_call" | custom-call | flops 838860800 | bytes 8110100 | tf_op jit(solution)/shard_map/attn_bwd/pallas_call | solution.py:434
  309.3 4.5 %attn_after.3 = (bf16[512,640]{1,0:T(8,128)(2,1)}, f32[16,640]{1,0:T(8,128)S(1)}) custom-call(bf16[3,384,512]{2,1,0:T(8,128)(2,1)S(1)} %attn_bwd.6.refs_2_.early_ref, bf16[3,256,512]{2,1,0:T(8,128)(2,1)S(1)} %get-tuple-element.566.refs_3_.late_ref, f32[512,640]{1,0:T(8,128)S(1)} %copy-done.7, bf16[512,640]{1,0:T(8,128)(2,1)S(1)} %copy-done.10, ...), custom_call_target="tpu_custom_call" | custom-call | flops 1258291200 | bytes 7946240 | tf_op jit(solution)/shard_map/attn_after/pallas_call | solution.py:434
  324.8 4.3 %collective-permute-done.59 = f32[3,20,640]{2,1,0:T(8,128)S(1)} collective-permute-done((f32[3,20,640]{2,1,0:T(8,128)S(1)}, f32[3,20,640]{2,1,0:T(8,128)S(1)}, u32[]{:S(2)}, u32[]{:S(2)}) %collective-permute-start.59) | collective-permute-done | bytes 153632 | tf_op jit(solution)/shard_map/ppermute | solution.py:552
  331.0 5.3 %collective-permute-done.56 = bf16[2,2,2,16,640]{4,3,2,1,0:T(8,128)(2,1)S(1)} collective-permute-done((bf16[2,2,2,16,640]{4,3,2,1,0:T(8,128)(2,1)S(1)}, bf16[2,2,2,16,640]{4,3,2,1,0:T(8,128)(2,1)S(1)}, u32[]{:S(2)}, u32[]{:S(2)}) %collective-permute-start.56) | collective-permute-done | bytes 163872 | tf_op jit(solution)/shard_map/ppermute | solution.py:536
  336.5 4.3 %collective-permute-done.57 = bf16[2,2,16,640]{3,2,1,0:T(8,128)(2,1)S(1)} collective-permute-done((bf16[2,2,16,640]{3,2,1,0:T(8,128)(2,1)S(1)}, bf16[2,2,16,640]{3,2,1,0:T(8,128)(2,1)S(1)}, u32[]{:S(2)}, u32[]{:S(2)}) %collective-permute-start.57) | collective-permute-done | bytes 81952 | tf_op jit(solution)/shard_map/ppermute | solution.py:536
  344.3 6.3 %collective-permute-done.61 = bf16[2,96,640]{2,1,0:T(8,128)(2,1)S(1)} collective-permute-done((bf16[2,96,640]{2,1,0:T(8,128)(2,1)S(1)}, bf16[2,96,640]{2,1,0:T(8,128)(2,1)S(1)}, u32[]{:S(2)}, u32[]{:S(2)}) %collective-permute-start.61) | collective-permute-done | bytes 245792 | tf_op jit(solution)/shard_map/ppermute | solution.py:536
  352.6 5.2 %collective-permute-done.62 = bf16[96,640]{1,0:T(8,128)(2,1)S(1)} collective-permute-done((bf16[96,640]{1,0:T(8,128)(2,1)S(1)}, bf16[96,640]{1,0:T(8,128)(2,1)S(1)}, u32[]{:S(2)}, u32[]{:S(2)}) %collective-permute-start.62) | collective-permute-done | bytes 122912 | tf_op jit(solution)/shard_map/ppermute | solution.py:536
  (383 shorter events, 182.3 us)
Async XLA Ops:
  32.3 17.2 %collective-permute-start.7 = (bf16[2,4,96,640]{3,2,1,0:T(8,128)(2,1)S(1)}, bf16[2,4,96,640]{3,2,1,0:T(8,128)(2,1)S(1)}, u32[]{:S(2)}, u32[]{:S(2)}) collective-permute-start(bf16[2,4,96,640]{3,2,1,0:T(8,128)(2,1)S(1)} %pad_maximum_fusion.2.refs_0_), channel_id=1, source_target_pairs={{0,4},{1,3},{2,6},{3,1},{4,0},{5,7},{6,2},{7,5},{8,12},{9,11},{10,... | collective-permute-start | bytes 2949128 | tf_op jit(solution)/shard_map/ppermute | solution.py:536
  33.8 15.7 %collective-permute-start.8 = (bf16[2,4,96,640]{3,2,1,0:T(8,128)(2,1)S(1)}, bf16[2,4,96,640]{3,2,1,0:T(8,128)(2,1)S(1)}, u32[]{:S(2)}, u32[]{:S(2)}) collective-permute-start(bf16[2,4,96,640]{3,2,1,0:T(8,128)(2,1)S(1)} %pad_maximum_fusion.2.refs_0_), channel_id=1, source_target_pairs={{0,1},{1,0},{2,3},{3,2},{4,5},{5,4},{6,7},{7,6},{8,9},{9,8},{10,11... | collective-permute-start | bytes 2949128 | tf_op jit(solution)/shard_map/ppermute | solution.py:530
  36.8 14.3 %collective-permute-start.14 = (bf16[160,640]{1,0:T(8,128)(2,1)S(1)}, bf16[160,640]{1,0:T(8,128)(2,1)S(1)}, u32[]{:S(2)}, u32[]{:S(2)}) collective-permute-start(bf16[160,640]{1,0:T(8,128)(2,1)S(1)} %pad_maximum_fusion.20), channel_id=1, source_target_pairs={{0,16},{1,9},{2,18},{3,11},{4,20},{5,13},{6,22},{7,15},{8,24},{9,1... | collective-permute-start | bytes 614408 | tf_op jit(solution)/shard_map/ppermute | solution.py:536
  37.6 11.7 %collective-permute-start.9 = (bf16[2,80,640]{2,1,0:T(8,128)(2,1)}, bf16[2,80,640]{2,1,0:T(8,128)(2,1)S(1)}, u32[]{:S(2)}, u32[]{:S(2)}) collective-permute-start(bf16[2,80,640]{2,1,0:T(8,128)(2,1)} %pad_maximum_fusion.21), channel_id=1, source_target_pairs={{0,8},{1,17},{2,10},{3,19},{4,12},{5,21},{6,14},{7,23},{8,0},{9,25... | collective-permute-start | bytes 614408 | tf_op jit(solution)/shard_map/ppermute | solution.py:536
  51.1 11.7 %collective-permute-start.13 = (bf16[2,160,640]{2,1,0:T(8,128)(2,1)S(1)}, bf16[2,160,640]{2,1,0:T(8,128)(2,1)S(1)}, u32[]{:S(2)}, u32[]{:S(2)}) collective-permute-start(bf16[2,160,640]{2,1,0:T(8,128)(2,1)S(1)} %pad_maximum_fusion.12), channel_id=1, source_target_pairs={{0,8},{1,17},{2,10},{3,19},{4,12},{5,21},{6,14},{7,23},{8,0},{9,25... | collective-permute-start | bytes 1228808 | tf_op jit(solution)/shard_map/ppermute | solution.py:536
  64.0 20.2 %collective-permute-start.15 = (bf16[2,4,80,640]{3,2,1,0:T(8,128)(2,1)}, bf16[2,4,80,640]{3,2,1,0:T(8,128)(2,1)}, u32[]{:S(2)}, u32[]{:S(2)}) collective-permute-start(bf16[2,4,80,640]{3,2,1,0:T(8,128)(2,1)} %pad_maximum_fusion.3.refs_0_), channel_id=1, source_target_pairs={{0,4},{1,3},{2,6},{3,1},{4,0},{5,7},{6,2},{7,5},{8,12},{9,11},{10,... | collective-permute-start | bytes 2457608 | tf_op jit(solution)/shard_map/ppermute | solution.py:536
  65.2 19.1 %collective-permute-start.16 = (bf16[2,4,80,640]{3,2,1,0:T(8,128)(2,1)}, bf16[2,4,80,640]{3,2,1,0:T(8,128)(2,1)}, u32[]{:S(2)}, u32[]{:S(2)}) collective-permute-start(bf16[2,4,80,640]{3,2,1,0:T(8,128)(2,1)} %pad_maximum_fusion.3.refs_0_), channel_id=1, source_target_pairs={{0,1},{1,0},{2,3},{3,2},{4,5},{5,4},{6,7},{7,6},{8,9},{9,8},{10,11... | collective-permute-start | bytes 2457608 | tf_op jit(solution)/shard_map/ppermute | solution.py:530
  68.8 12.1 %collective-permute-start.18 = (bf16[2,160,640]{2,1,0:T(8,128)(2,1)S(1)}, bf16[2,160,640]{2,1,0:T(8,128)(2,1)S(1)}, u32[]{:S(2)}, u32[]{:S(2)}) collective-permute-start(bf16[2,160,640]{2,1,0:T(8,128)(2,1)S(1)} %pad_maximum_fusion.13), channel_id=1, source_target_pairs={{0,8},{1,17},{2,10},{3,19},{4,12},{5,21},{6,14},{7,23},{8,0},{9,25... | collective-permute-start | bytes 1228808 | tf_op jit(solution)/shard_map/ppermute | solution.py:536
  70.5 13.3 %collective-permute-start.17 = (bf16[4,160,640]{2,1,0:T(8,128)(2,1)}, bf16[4,160,640]{2,1,0:T(8,128)(2,1)S(1)}, u32[]{:S(2)}, u32[]{:S(2)}) collective-permute-start(bf16[4,160,640]{2,1,0:T(8,128)(2,1)} %pad_maximum_fusion.4), channel_id=1, source_target_pairs={{0,2},{1,5},{2,0},{3,7},{4,6},{5,1},{6,4},{7,3},{8,10},{9,13},{10,... | collective-permute-start | bytes 2457608 | tf_op jit(solution)/shard_map/ppermute | solution.py:536
  87.8 21.1 %collective-permute-start.20 = (bf16[2,4,160,640]{3,2,1,0:T(8,128)(2,1)S(1)}, bf16[2,4,160,640]{3,2,1,0:T(8,128)(2,1)S(1)}, u32[]{:S(2)}, u32[]{:S(2)}) collective-permute-start(bf16[2,4,160,640]{3,2,1,0:T(8,128)(2,1)S(1)} %pad_maximum_fusion.refs_1_.refs_0_), channel_id=1, source_target_pairs={{0,4},{1,3},{2,6},{3,1},{4,0},{5,7},{6,2},{7,5},{8,12},{9,11},{10,... | collective-permute-start | bytes 4915208 | tf_op jit(solution)/shard_map/ppermute | solution.py:536
  89.0 19.9 %collective-permute-start.21 = (bf16[2,4,160,640]{3,2,1,0:T(8,128)(2,1)S(1)}, bf16[2,4,160,640]{3,2,1,0:T(8,128)(2,1)S(1)}, u32[]{:S(2)}, u32[]{:S(2)}) collective-permute-start(bf16[2,4,160,640]{3,2,1,0:T(8,128)(2,1)S(1)} %pad_maximum_fusion.refs_1_.refs_0_), channel_id=1, source_target_pairs={{0,1},{1,0},{2,3},{3,2},{4,5},{5,4},{6,7},{7,6},{8,9},{9,8},{10,11... | collective-permute-start | bytes 4915208 | tf_op jit(solution)/shard_map/ppermute | solution.py:530
  112.5 12.4 %collective-permute-start.23 = (bf16[4,160,640]{2,1,0:T(8,128)(2,1)S(1)}, bf16[4,160,640]{2,1,0:T(8,128)(2,1)S(1)}, u32[]{:S(2)}, u32[]{:S(2)}) collective-permute-start(bf16[4,160,640]{2,1,0:T(8,128)(2,1)S(1)} %pad_maximum_fusion.5), channel_id=1, source_target_pairs={{0,2},{1,5},{2,0},{3,7},{4,6},{5,1},{6,4},{7,3},{8,10},{9,13},{10,... | collective-permute-start | bytes 2457608 | tf_op jit(solution)/shard_map/ppermute | solution.py:536
  125.2 21.2 %collective-permute-start.24 = (bf16[2,4,160,640]{3,2,1,0:T(8,128)(2,1)S(1)}, bf16[2,4,160,640]{3,2,1,0:T(8,128)(2,1)S(1)}, u32[]{:S(2)}, u32[]{:S(2)}) collective-permute-start(bf16[2,4,160,640]{3,2,1,0:T(8,128)(2,1)S(1)} %pad_maximum_fusion.1.refs_0_), channel_id=1, source_target_pairs={{0,4},{1,3},{2,6},{3,1},{4,0},{5,7},{6,2},{7,5},{8,12},{9,11},{10,... | collective-permute-start | bytes 4915208 | tf_op jit(solution)/shard_map/ppermute | solution.py:536
  126.4 20.0 %collective-permute-start.25 = (bf16[2,4,160,640]{3,2,1,0:T(8,128)(2,1)S(1)}, bf16[2,4,160,640]{3,2,1,0:T(8,128)(2,1)S(1)}, u32[]{:S(2)}, u32[]{:S(2)}) collective-permute-start(bf16[2,4,160,640]{3,2,1,0:T(8,128)(2,1)S(1)} %pad_maximum_fusion.1.refs_0_), channel_id=1, source_target_pairs={{0,1},{1,0},{2,3},{3,2},{4,5},{5,4},{6,7},{7,6},{8,9},{9,8},{10,11... | collective-permute-start | bytes 4915208 | tf_op jit(solution)/shard_map/ppermute | solution.py:530
  167.9 12.4 %collective-permute-start.28 = (bf16[2,2,2,80,640]{4,3,2,1,0:T(8,128)(2,1)S(1)}, bf16[2,2,2,80,640]{4,3,2,1,0:T(8,128)(2,1)S(1)}, u32[]{:S(2)}, u32[]{:S(2)}) collective-permute-start(bf16[2,2,2,80,640]{4,3,2,1,0:T(8,128)(2,1)S(1)} %fusion.5), channel_id=1, source_target_pairs={{0,4},{1,3},{2,6},{3,1},{4,0},{5,7},{6,2},{7,5},{8,12},{9,11},{10,... | collective-permute-start | bytes 2457608 | tf_op jit(solution)/shard_map/ppermute | solution.py:536
  189.0 12.8 %collective-permute-start.31 = (bf16[2,2,2,80,640]{4,3,2,1,0:T(8,128)(2,1)S(1)}, bf16[2,2,2,80,640]{4,3,2,1,0:T(8,128)(2,1)S(1)}, u32[]{:S(2)}, u32[]{:S(2)}) collective-permute-start(bf16[2,2,2,80,640]{4,3,2,1,0:T(8,128)(2,1)S(1)} %fusion.4), channel_id=1, source_target_pairs={{0,4},{1,3},{2,6},{3,1},{4,0},{5,7},{6,2},{7,5},{8,12},{9,11},{10,... | collective-permute-start | bytes 2457608 | tf_op jit(solution)/shard_map/ppermute | solution.py:536
  190.2 11.6 %collective-permute-start.32 = (bf16[2,80,640]{2,1,0:T(8,128)(2,1)S(1)}, bf16[2,80,640]{2,1,0:T(8,128)(2,1)S(1)}, u32[]{:S(2)}, u32[]{:S(2)}) collective-permute-start(bf16[2,80,640]{2,1,0:T(8,128)(2,1)S(1)} %fusion.27), channel_id=1, source_target_pairs={{0,8},{1,17},{2,10},{3,19},{4,12},{5,21},{6,14},{7,23},{8,0},{9,25... | collective-permute-start | bytes 614408 | tf_op jit(solution)/shard_map/ppermute | solution.py:536
  202.1 12.7 %collective-permute-start.33 = (bf16[2,2,80,640]{3,2,1,0:T(8,128)(2,1)S(1)}, bf16[2,2,80,640]{3,2,1,0:T(8,128)(2,1)S(1)}, u32[]{:S(2)}, u32[]{:S(2)}) collective-permute-start(bf16[2,2,80,640]{3,2,1,0:T(8,128)(2,1)S(1)} %fusion.14), channel_id=1, source_target_pairs={{0,2},{1,5},{2,0},{3,7},{4,6},{5,1},{6,4},{7,3},{8,10},{9,13},{10,... | collective-permute-start | bytes 1228808 | tf_op jit(solution)/shard_map/ppermute | solution.py:536
  203.5 11.3 %collective-permute-start.34 = (bf16[80,640]{1,0:T(8,128)(2,1)S(1)}, bf16[80,640]{1,0:T(8,128)(2,1)S(1)}, u32[]{:S(2)}, u32[]{:S(2)}) collective-permute-start(bf16[80,640]{1,0:T(8,128)(2,1)S(1)} %fusion.48), channel_id=1, source_target_pairs={{0,16},{1,9},{2,18},{3,11},{4,20},{5,13},{6,22},{7,15},{8,24},{9,1... | collective-permute-start | bytes 307208 | tf_op jit(solution)/shard_map/ppermute | solution.py:536
  223.1 12.4 %collective-permute-start.37 = (bf16[2,2,2,80,640]{4,3,2,1,0:T(8,128)(2,1)S(1)}, bf16[2,2,2,80,640]{4,3,2,1,0:T(8,128)(2,1)S(1)}, u32[]{:S(2)}, u32[]{:S(2)}) collective-permute-start(bf16[2,2,2,80,640]{4,3,2,1,0:T(8,128)(2,1)S(1)} %fusion.3), channel_id=1, source_target_pairs={{0,4},{1,3},{2,6},{3,1},{4,0},{5,7},{6,2},{7,5},{8,12},{9,11},{10,... | collective-permute-start | bytes 2457608 | tf_op jit(solution)/shard_map/ppermute | solution.py:536
  244.2 12.4 %collective-permute-start.41 = (bf16[2,2,2,80,640]{4,3,2,1,0:T(8,128)(2,1)S(1)}, bf16[2,2,2,80,640]{4,3,2,1,0:T(8,128)(2,1)S(1)}, u32[]{:S(2)}, u32[]{:S(2)}) collective-permute-start(bf16[2,2,2,80,640]{4,3,2,1,0:T(8,128)(2,1)S(1)} %fusion.2), channel_id=1, source_target_pairs={{0,4},{1,3},{2,6},{3,1},{4,0},{5,7},{6,2},{7,5},{8,12},{9,11},{10,... | collective-permute-start | bytes 2457608 | tf_op jit(solution)/shard_map/ppermute | solution.py:536
  265.4 12.4 %collective-permute-start.46 = (bf16[2,2,2,80,640]{4,3,2,1,0:T(8,128)(2,1)S(1)}, bf16[2,2,2,80,640]{4,3,2,1,0:T(8,128)(2,1)S(1)}, u32[]{:S(2)}, u32[]{:S(2)}) collective-permute-start(bf16[2,2,2,80,640]{4,3,2,1,0:T(8,128)(2,1)S(1)} %fusion.1), channel_id=1, source_target_pairs={{0,4},{1,3},{2,6},{3,1},{4,0},{5,7},{6,2},{7,5},{8,12},{9,11},{10,... | collective-permute-start | bytes 2457608 | tf_op jit(solution)/shard_map/ppermute | solution.py:536
  291.0 11.7 %collective-permute-start.51 = (bf16[2,2,2,2,80,640]{5,4,3,2,1,0:T(8,128)(2,1)}, bf16[2,2,2,2,80,640]{5,4,3,2,1,0:T(8,128)(2,1)}, u32[]{:S(2)}, u32[]{:S(2)}) collective-permute-start(bf16[2,2,2,2,80,640]{5,4,3,2,1,0:T(8,128)(2,1)} %grads.22), channel_id=1, source_target_pairs={{0,1},{1,0},{2,3},{3,2},{4,5},{5,4},{6,7},{7,6},{8,9},{9,8},{10,11... | collective-permute-start | bytes 4915208 | tf_op jit(solution)/shard_map/ppermute | solution.py:530
  304.3 12.5 %collective-permute-start.52 = (bf16[2,2,2,80,640]{4,3,2,1,0:T(8,128)(2,1)S(1)}, bf16[2,2,2,80,640]{4,3,2,1,0:T(8,128)(2,1)}, u32[]{:S(2)}, u32[]{:S(2)}) collective-permute-start(bf16[2,2,2,80,640]{4,3,2,1,0:T(8,128)(2,1)S(1)} %fusion), channel_id=1, source_target_pairs={{0,4},{1,3},{2,6},{3,1},{4,0},{5,7},{6,2},{7,5},{8,12},{9,11},{10,... | collective-permute-start | bytes 2457608 | tf_op jit(solution)/shard_map/ppermute | solution.py:536
  (84 other events, 762.7 us)

commit v4 on v3

--- a/solution.py
+++ b/solution.py
@@ -187,8 +187,9 @@
         values = kv_ref[:, pl.ds(pl.multiple_of(D + group * LANES, LANES), LANES)].T
         for head in range(PER_GROUP):
             key_ref[head, :, :LANES] = kv_ref[:, rows] * masks[head]
+        every = dot(key_ref[...].reshape(PER_GROUP * length, 2 * LANES), query_ref[...])
         for head in range(PER_GROUP):
-            scores = dot(key_ref[head], query_ref[...])
+            scores = every[head * length : (head + 1) * length]
             top = jnp.max(scores, 0, keepdims=True)
             probs = jnp.exp(scores - top).astype(bf16)
             wide = jnp.concatenate([values[head * HEAD_DIM : (head + 1) * HEAD_DIM], ones], 0)
@@ -199,7 +200,8 @@
             lse_ref[pl.ds(group * PER_GROUP + head, 1), :] = top + jnp.log(total)
         return carry
 
-    lax.fori_loop(0, GROUPS, group_step, 0)
+    for group in range(GROUPS):
+        group_step(group, 0)
     jobs[0].wait([3])
     q_ref[...] = ot_ref[...].T
     m_ref[...] = x_ref[...].astype(f32) + (dot(q_ref[...], w_ref[:, :, :, 3 * D :].reshape(D, D)) + vec_ref[BIAS_OUT : BIAS_OUT + 1, :])
@@ -559,7 +561,7 @@
 
 
 NAMES = ("down", "up", "attn")
-LOTS = tuple(((name, l),) for l in (1, 0) for name in NAMES)
+LOTS = ((("down", 1),), (("up", 1),), (("attn", 1),), (("down", 0), ("up", 0)), (("attn", 0),))
 
 
 def whole_weight(matrix, by_rows):
@@ -759,8 +761,9 @@
     c1, up0, attn1, up1 = jnp.concatenate(regroup(parts, bits[3:]), 1)
     c2, c3 = jnp.concatenate([up0, attn1]), jnp.concatenate([w_down[1].reshape(PIECE, D), up1])
     zz0, c1, c2, c3 = stage(by_z(u0), c1, c2, c3)
-    near0, t1 = stage(link2(zz0), link0(c1))
-    far0, mate0, u1, t2 = step(3, near0), mate(near0), link1(t1), link0(c2)
+    near0, t12 = stage(link2(zz0), link0(jnp.concatenate([c1, c2])))
+    t1, t2 = t12[:, :PIECE], t12[:, PIECE:]
+    far0, mate0, u1 = step(3, near0), mate(near0), link1(t1)
     far0, mate0, zz1, t2 = stage(far0, mate0, by_z(u1), t2)
     near1, far_mate0, u2, t3 = link2(zz1), mate(far0), link1(t2), link0(c3)
     near1, far_mate0, zz2, t3 = stage(near1, far_mate0, by_z(u2), t3)
@@ -800,7 +803,7 @@
     )
     kept[1] |= more
 
-    d1, u1, a1, d0, u0, a0 = [Lot() for _ in LOTS]
+    d1, u1, a1, du0, a0, extra = [Lot() for _ in range(6)]
 
     def blocks(lot, phase):
         return gradient_blocks(coords, lot, kept, back, phase)
@@ -834,62 +837,60 @@
     got_a1, got_u1 = step(3, first), step(0, fourth)
     grad, more = attn_after(back[1], kept[1], vectors[1], whole["attn", 1], False)
     sums = [None, back[1]["sums"] + more]
-    back[0] = {"gb": grad.astype(bf16)}
-    got_a1, got_u1, core, grad, back[0] = stage(got_a1, got_u1, blocks(3, 1), grad, back[0])
-    second, core, grad, back[0] = stage(a1.second(got_a1), core, grad, back[0])
+    back[0] = ffn_bwd(coords, grad, kept[0], vectors[0], whole["up", 0], whole["down", 0], False)
+    got_a1, got_u1, core, back[0] = stage(got_a1, got_u1, blocks(3, 1), back[0])
+    second, core, back[0] = stage(a1.second(got_a1), core, back[0])
 
     got_a1, core, rest = stage(step(2, second), mate(core), blocks(3, 0))
-    first, third, grad, back[0] = stage(d0.first(core, rest), a1.third(got_a1), grad, back[0])
-
-    got_d0, got_a1 = step(3, first), step(1, third)
-    back[0] |= ffn_bwd(coords, grad, kept[0], vectors[0], whole["up", 0], whole["down", 0], False)
-    got_d0, got_a1, core, back[0] = stage(got_d0, got_a1, blocks(4, 1), back[0])
-    second, fourth, core, back[0] = stage(d0.second(got_d0), a1.fourth(got_a1), core, back[0])
-
-    got_d0, got_a1, core, rest = stage(step(2, second), step(0, fourth), mate(core), blocks(4, 0))
-    first, third, back[0] = stage(u0.first(core, rest), d0.third(got_d0), back[0])
-
-    got_u0, got_d0 = step(3, first), step(1, third)
+    first, third, back[0] = stage(du0.first(core, rest), a1.third(got_a1), back[0])
+
+    got_du0, got_a1 = step(3, first), step(1, third)
     (back[0]["early"],) = attn_bwd(coords, back[0]["gmb"], kept[0], table, whole["attn", 0], EARLY)
-    got_u0, got_d0, back[0] = stage(got_u0, got_d0, back[0])
-    second, fourth, back[0] = stage(u0.second(got_u0), d0.fourth(got_d0), back[0])
-
-    got_u0, got_d0 = step(2, second), step(0, fourth)
     back[0]["late"], back[0]["flip"] = attn_bwd(coords, back[0]["gmb"], kept[0], table, whole["attn", 0], LATE)
-    got_u0, got_d0, core, back[0] = stage(got_u0, got_d0, blocks(5, 1), back[0])
-    third, core, back[0] = stage(u0.third(got_u0), core, back[0])
-
-    got_u0, core, rest = stage(step(1, third), mate(core), blocks(5, 0))
-    first, fourth, back[0] = stage(a0.first(core, rest), u0.fourth(got_u0), back[0])
-
-    got_a0, got_u0 = step(3, first), step(0, fourth)
+    got_du0, got_a1, back[0] = stage(got_du0, got_a1, back[0])
+    second, fourth, back[0] = stage(du0.second(got_du0), a1.fourth(got_a1), back[0])
+
+    got_du0, got_a1 = step(2, second), step(0, fourth)
+    core = blocks(4, 1)
     grad, more = attn_after(back[0], kept[0], vectors[0], whole["attn", 0], True)
     sums[0] = back[0]["sums"] + more
-    got_a0, got_u0, grad, sums = stage(got_a0, got_u0, grad, sums)
-    small = turned(jnp.concatenate([v.reshape(32, -1) for v in layer_grads(sums)], 1), bits)[..., None, :]
-    small = jnp.pad(small, ((0, 0),) * 5 + ((0, 15), (0, D - width))).astype(bf16)
-    extra = Lot()
-    first_x = extra.first(mate(small[1]), [small[0, 1], small[0, 0, 1], small[0, 0, 0]])
-    second, first_x = stage(a0.second(got_a0), first_x)
-
-    got_a0, got_x = step(2, second), step(3, first_x)
-    up1, attn1, up0 = shares_of([u1.last(got_u1), a1.last(got_a1), u0.last(got_u0)], bits)
-    got_x = step(2, extra.second(got_x))
-    got_a0, got_x, up1, attn1, up0 = stage(got_a0, got_x, up1, attn1, up0)
-    third = jnp.concatenate([a0.third(got_a0), extra.third(got_x)], -2)
-    a0.total = jnp.concatenate([a0.total, extra.total], -2)
-    got_a0 = step(1, third)
-    fourth = a0.fourth(got_a0)
-    done_a0 = a0.last(step(0, fourth))
-    (attn0,) = shares_of([done_a0[:PIECE]], bits)
-    mine = done_a0[PIECE, :width]
+    got_du0, got_a1, core, grad, sums, back[0] = stage(got_du0, got_a1, core, grad, sums, back[0])
+    third, core, back[0] = stage(du0.third(got_du0), core, back[0])
+
+    got_du0 = step(1, third)
+    core, rest = stage(mate(core), blocks(4, 0))
+    first, sums = stage(a0.first(core, rest), sums)
+
+    got_a0 = step(3, first)
+    small = turned(jnp.concatenate([v.reshape(32, -1) for v in layer_grads(sums)], 1), bits)
+    first = extra.first(mate(small[1]), [small[0, 1], small[0, 0, 1], small[0, 0, 0]])
+    got_a0, got_du0, first, got_d1, got_u1, got_a1, grad = stage(got_a0, got_du0, first, got_d1, got_u1, got_a1, grad)
+    second, first, fourth = stage(a0.second(got_a0), first, du0.fourth(got_du0))
+
+    got_a0, got_x, got_du0 = step(2, second), step(3, first), step(0, fourth)
+    shares = [u1.last(got_u1), a1.last(got_a1)]
+    got_a0, got_x, got_du0, shares = stage(got_a0, got_x, got_du0, shares)
+    third, second, got_du0 = stage(a0.third(got_a0), extra.second(got_x), got_du0)
+
+    got_a0, got_x = step(1, third), step(2, second)
+    done = du0.last(got_du0)
+    downs = jnp.stack([done[:PIECE].reshape(-1), d1.last(got_d1).reshape(-1)])
+    up1, attn1, up0 = shares_of([*shares, done[PIECE:]], bits)
+    got_a0, got_x, up1, attn1, up0, downs = stage(got_a0, got_x, up1, attn1, up0, downs)
+    fourth, third = stage(a0.fourth(got_a0), extra.third(got_x))
+
+    got_a0, got_x = step(0, fourth), step(1, third)
+    ups = jnp.stack([up0.reshape(-1), up1.reshape(-1)])
+    got_a0, got_x, ups = stage(got_a0, got_x, ups)
+    (attn0,) = shares_of([a0.last(got_a0)], bits)
+    mine = extra.last(step(0, extra.fourth(got_x)))
     return (
         output,
         grad,
         jnp.stack([v[:, : 3 * D].reshape(-1) for v in (attn0, attn1)]),
         jnp.stack([v[:, 3 * D :].reshape(-1) for v in (attn0, attn1)]),
-        jnp.stack([up0.reshape(-1), up1.reshape(-1)]),
-        jnp.stack([d0.last(got_d0).reshape(-1), d1.last(got_d1).reshape(-1)]),
+        ups,
+        downs,
         mine[: gains.shape[0]],
         mine[gains.shape[0] :],
     )

time: 372 us -> 352 us (0.946)
  waiting for transfers between devices: 118 us -> 103 us
  Pallas kernels: 143 us -> 133 us
  local copies, waits for them, and re-layouts: 14.4 us -> 20.8 us
  other arithmetic: 24.2 us -> 19.6 us
    ppermute x42 -> x39, waiting for transfers between devices: 94.1 us -> 81.1 us  [step(): return lax.ppermute(value, AXES, pairs)]
    pallas_call x25 -> x23, Pallas kernels: 143 us -> 133 us  [call(): pl.pallas_call(kernel, out_shape=[jax.ShapeDtypeStruct(s, t) for s, t in...]
    unnamed x100 -> x96, local copies, waits for them, and re-layouts: 4.87 us -> 9.44 us
    ppermute x42 -> x39, starting transfers between devices: 53.4 us -> 54.7 us  [step(): return lax.ppermute(value, AXES, pairs)]
    ppermute x15 -> x14, waiting for transfers between devices: 10.7 us -> 11.5 us  [mate(): return lax.ppermute(value, 'narrow', [(0, 1), (1, 0)])]
  transfers between devices with their start and end apart: 66 -> 62, of which waited for: 37 -> 34; matrix products, arithmetic and copies ran while one was open for 6% -> 5% of each run, Pallas kernels for 35% -> 34%
where the time goes in v4:
time: 352 us; the launch traced here: 345 us
  Pallas kernels  133 us (38%)
  waiting for transfers between devices  103 us (29%)
  starting transfers between devices  65.4 us (19%)
  local copies, waits for them, and re-layouts  20.8 us (6%)
  other arithmetic  19.6 us (6%)
    pallas_call x23, Pallas kernels, call(): pl.pallas_call(kernel, out_shape=[jax.ShapeDtypeStruct(s, t) for s, t in...  133 us
    ppermute x39, waiting for transfers between devices, step(): return lax.ppermute(value, AXES, pairs)  81.1 us
    ppermute x39, starting transfers between devices, step(): return lax.ppermute(value, AXES, pairs)  54.7 us
    ppermute x14, waiting for transfers between devices, mate(): return lax.ppermute(value, 'narrow', [(0, 1), (1, 0)])  11.5 us
    ppermute x9, waiting for transfers between devices, regroup(): lax.ppermute(mine[k], AXES, [(i, i ^ k) for i in range(32)])  10.7 us
    unnamed x96, local copies, waits for them, and re-layouts  9.44 us
  transfers between devices with their start and end apart: 62, of which 34 were waited for; matrix products, arithmetic and copies ran while one was open for 5% of the time, Pallas kernels for 34%

profile of v4, /device:TPU:0, one launch (start us, length us, event | category | flops | bytes accessed | tf_op | source)
XLA Modules:
  0.0 345.4 jit_solution(16457763403800637234)
XLA Ops:
  3.8 4.1 %collective-permute-start = (bf16[96,640]{1,0:T(8,128)(2,1)S(1)}, bf16[96,640]{1,0:T(8,128)(2,1)S(1)}, u32[]{:S(2)}, u32[]{:S(2)}) collective-permute-start(bf16[96,640]{1,0:T(8,128)(2,1)S(1)} %fusion.34), channel_id=1, source_target_pairs={{0,16},{1,9},{2,18},{3,11},{4,20},{5,13},{6,22},{7,15},{8,24},{9,1... | collective-permute-start | bytes 368648 | tf_op jit(solution)/shard_map/ppermute | solution.py:538
  26.8 7.6 %collective-permute-done.6 = bf16[240,640]{1,0:T(8,128)(2,1)S(1)} collective-permute-done((bf16[240,640]{1,0:T(8,128)(2,1)S(1)}, bf16[240,640]{1,0:T(8,128)(2,1)S(1)}, u32[]{:S(2)}, u32[]{:S(2)}) %collective-permute-start.6) | collective-permute-done | bytes 307232 | tf_op jit(solution)/shard_map/ppermute | solution.py:538
  42.9 4.9 %collective-permute-done.9 = bf16[2,80,640]{2,1,0:T(8,128)(2,1)S(1)} collective-permute-done((bf16[2,80,640]{2,1,0:T(8,128)(2,1)}, bf16[2,80,640]{2,1,0:T(8,128)(2,1)S(1)}, u32[]{:S(2)}, u32[]{:S(2)}) %collective-permute-start.9) | collective-permute-done | bytes 204832 | tf_op jit(solution)/shard_map/ppermute | solution.py:538
  58.3 4.5 %collective-permute-done.12 = bf16[2,160,640]{2,1,0:T(8,128)(2,1)S(1)} collective-permute-done((bf16[2,160,640]{2,1,0:T(8,128)(2,1)S(1)}, bf16[2,160,640]{2,1,0:T(8,128)(2,1)S(1)}, u32[]{:S(2)}, u32[]{:S(2)}) %collective-permute-start.12) | collective-permute-done | bytes 409632 | tf_op jit(solution)/shard_map/ppermute | solution.py:538
  70.4 11.5 %collective-permute-done.17 = bf16[2,160,640]{2,1,0:T(8,128)(2,1)S(1)} collective-permute-done((bf16[2,160,640]{2,1,0:T(8,128)(2,1)S(1)}, bf16[2,160,640]{2,1,0:T(8,128)(2,1)S(1)}, u32[]{:S(2)}, u32[]{:S(2)}) %collective-permute-start.17) | collective-permute-done | bytes 409632 | tf_op jit(solution)/shard_map/ppermute | solution.py:538
  89.6 14.2 %attn_fwd.2 = (bf16[640,512]{1,0:T(8,128)(2,1)S(1)}, bf16[640,512]{1,0:T(8,128)(2,1)S(1)}, bf16[512,1280]{1,0:T(8,128)(2,1)S(1)}, bf16[640,512]{1,0:T(8,128)(2,1...) custom-call(s32[5]{0:T(128)S(1)} %stack.175.coords, ...), custom_call_target="tpu_custom_call" | custom-call | flops 2348810240 | bytes 13983764 | tf_op jit(solution)/shard_map/attn_fwd/pallas_call | solution.py:436
  103.8 5.1 %collective-permute-done.19.refs_3_.refs_2_ = bf16[2,4,160,640]{3,2,1,0:T(8,128)(2,1)S(1)} collective-permute-done((bf16[2,4,160,640]{3,2,1,0:T(8,128)(2,1)S(1)}, bf16[2,4,160,640]{3,2,1,0:T(8,128)(2,1)S(1)}, u32[]{:S(2)}, u32[]{:S(2)}) %collective-permute-start.19) | collective-permute-done | bytes 1638432 | tf_op jit(solution)/shard_map/ppermute | solution.py:538
  113.4 10.9 %ffn_fwd.2 = (f32[512,640]{1,0:T(8,128)S(1)}, bf16[2560,512]{1,0:T(8,128)(2,1)S(1)}, bf16[512,2560]{1,0:T(8,128)(2,1)S(1)}, bf16[4,2,80,2560]{3,2,1,0:T(8,128)(2,1)S(1)}) custom-call(s32[5]{0:T(128)S(1)} %stack.175.coords, f32[512,640]{1,0:T(8,128)S(1)} %get-tuple-element.351.m_ref, bf16[512,640]{1,0:T(8,128)(2,1)S(1)} %get-tuple-element.352.b_ref, ...), custom_call_target="tpu_custom_call" | custom-call | flops 3355443200 | bytes 21667860 | tf_op jit(solution)/shard_map/ffn_fwd/pallas_call | solution.py:436
  127.0 13.9 %attn_fwd.3 = (bf16[640,512]{1,0:T(8,128)(2,1)S(1)}, bf16[640,512]{1,0:T(8,128)(2,1)S(1)}, bf16[512,1280]{1,0:T(8,128)(2,1)S(1)}, bf16[640,512]{1,0:T(8,128)(2,1...) custom-call(s32[5]{0:T(128)S(1)} %stack.175.coords, ...), custom_call_target="tpu_custom_call" | custom-call | flops 2348810240 | bytes 17915924 | tf_op jit(solution)/shard_map/attn_fwd/pallas_call | solution.py:436
  149.8 12.5 %ffn_fwd.3 = (bf16[512,640]{1,0:T(8,128)(2,1)}, bf16[2560,512]{1,0:T(8,128)(2,1)S(1)}, bf16[512,2560]{1,0:T(8,128)(2,1)S(1)}, bf16[4,2,80,2560]{3,2,1,0:T(8,128)(2,1)S(1)}, bf16[4,2,2,2,80,640]{5,4,3,2,1,0:T(8,128)(2,1)S(1)}) custom-call(s32[5]{0:T(128)S(1)} %stack.175.coords, f32[512,640]{1,0:T(8,128)S(1)} %get-tuple-element.369.m_ref, ...), custom_call_target="tpu_custom_call" | custom-call | flops 3355443200 | bytes 21012500 | tf_op jit(solution)/shard_map/ffn_fwd/pallas_call | solution.py:436
  169.6 7.7 %ffn_bwd.2 = (bf16[512,640]{1,0:T(8,128)(2,1)}, bf16[512,2560]{1,0:T(8,128)(2,1)S(1)}, f32[512,640]{1,0:T(8,128)S(1)}, bf16[512,640]{1,0:T(8,128)(2,1)S(1)}, f32[16,640]{1,0:T(8,128)S(1)}) custom-call(s32[5]{0:T(128)S(1)} %stack.175.coords, bf16[512,640]{1,0:T(8,128)(2,1)S(1)} %copy-done.4, bf16[512,2560]{1,0:T(8,128)(2,1)S(1)} %get-tuple-element.382.slope_ref, ...), custom_call_target="tpu_custom_call" | custom-call | flops 3355443200 | bytes 16465940 | tf_op jit(solution)/shard_map/ffn_bwd/pallas_call | solution.py:436
  183.8 4.7 %collective-permute-done.28 = bf16[2,2,80,640]{3,2,1,0:T(8,128)(2,1)S(1)} collective-permute-done((bf16[2,2,80,640]{3,2,1,0:T(8,128)(2,1)S(1)}, bf16[2,2,80,640]{3,2,1,0:T(8,128)(2,1)S(1)}, u32[]{:S(2)}, u32[]{:S(2)}) %collective-permute-start.28) | collective-permute-done | bytes 409632 | tf_op jit(solution)/shard_map/ppermute | solution.py:538
  190.8 9.5 %attn_bwd.4.refs_2_.early_ref = bf16[3,384,512]{2,1,0:T(8,128)(2,1)S(1)} custom-call(s32[5]{0:T(128)S(1)} %stack.175.coords, bf16[512,640]{1,0:T(8,128)(2,1)S(1)} %get-tuple-element.430.gmb_ref, bf16[640,512]{1,0:T(8,128)(2,1)S(1)} %copy-done.17, bf16[512,1280]{1,0:T(8,128)(2,1)S(1)} %copy-done.15, bf16[640,512]{1,0:T(8,128)(2,1)S(1)} %get-tuple-element.414.ot_ref.refs_1_, ...), custom_call_target="tpu_custom_call" | custom-call | flops 1258291200 | bytes 7847956 | tf_op jit(solution)/shard_map/attn_bwd/pallas_call | solution.py:436
  206.1 6.6 %attn_bwd.5 = (bf16[3,256,512]{2,1,0:T(8,128)(2,1)S(1)}, bf16[640,512]{1,0:T(8,128)(2,1)S(1)}) custom-call(s32[5]{0:T(128)S(1)} %stack.175.coords, bf16[512,640]{1,0:T(8,128)(2,1)S(1)} %get-tuple-element.430.gmb_ref, bf16[640,512]{1,0:T(8,128)(2,1)S(1)} %copy-done.17, bf16[512,1280]{1,0:T(8,128)(2,1)S(1)} %copy-done.15, ...), custom_call_target="tpu_custom_call" | custom-call | flops 838860800 | bytes 8110100 | tf_op jit(solution)/shard_map/attn_bwd/pallas_call | solution.py:436
  219.1 3.9 %collective-permute-done.34 = bf16[2,80,640]{2,1,0:T(8,128)(2,1)S(1)} collective-permute-done((bf16[2,80,640]{2,1,0:T(8,128)(2,1)S(1)}, bf16[2,80,640]{2,1,0:T(8,128)(2,1)S(1)}, u32[]{:S(2)}, u32[]{:S(2)}) %collective-permute-start.34) | collective-permute-done | bytes 204832 | tf_op jit(solution)/shard_map/ppermute | solution.py:538
  224.3 3.7 %attn_after.2 = (f32[512,640]{1,0:T(8,128)S(1)}, f32[16,640]{1,0:T(8,128)S(1)}) custom-call(bf16[3,384,512]{2,1,0:T(8,128)(2,1)S(1)} %attn_bwd.4.refs_2_.early_ref, bf16[3,256,512]{2,1,0:T(8,128)(2,1)S(1)} %get-tuple-element.460.refs_3_.late_ref, f32[512,640]{1,0:T(8,128)S(1)} %get-tuple-element.461.gm_ref, f32[512,640]{1,0:T(8,128)S(1)} %get-tuple-element.462.x_ref, ...), custom_call_target="tpu_custom_call" | custom-call | flops 1258291200 | bytes 9256960 | tf_op jit(solution)/shard_map/attn_after/pallas_call | solution.py:436
  228.0 6.7 %ffn_bwd.3 = (bf16[512,640]{1,0:T(8,128)(2,1)S(1)}, bf16[512,2560]{1,0:T(8,128)(2,1)S(1)}, f32[512,640]{1,0:T(8,128)S(1)}, bf16[512,640]{1,0:T(8,128)(2,1)S(1)}, f32[16,640]{1,0:T(8,128)S(1)}) custom-call(s32[5]{0:T(128)S(1)} %stack.175.coords, f32[512,640]{1,0:T(8,128)S(1)} %get-tuple-element.463.g_ref, bf16[512,2560]{1,0:T(8,128)(2,1)S(1)} %get-tuple-element.464.slope_ref, ...), custom_call_target="tpu_custom_call" | custom-call | flops 3355443200 | bytes 17121300 | tf_op jit(solution)/shard_map/ffn_bwd/pallas_call | solution.py:436
  243.3 4.0 %collective-permute-done.38 = bf16[2,2,80,640]{3,2,1,0:T(8,128)(2,1)S(1)} collective-permute-done((bf16[2,2,80,640]{3,2,1,0:T(8,128)(2,1)S(1)}, bf16[2,2,80,640]{3,2,1,0:T(8,128)(2,1)S(1)}, u32[]{:S(2)}, u32[]{:S(2)}) %collective-permute-start.38) | collective-permute-done | bytes 409632 | tf_op jit(solution)/shard_map/ppermute | solution.py:538
  250.4 6.6 %attn_bwd.7 = (bf16[3,256,512]{2,1,0:T(8,128)(2,1)S(1)}, bf16[640,512]{1,0:T(8,128)(2,1)S(1)}) custom-call(s32[5]{0:T(128)S(1)} %stack.175.coords, bf16[512,640]{1,0:T(8,128)(2,1)S(1)} %get-tuple-element.496.gmb_ref, bf16[640,512]{1,0:T(8,128)(2,1)S(1)} %copy-done.21, bf16[512,1280]{1,0:T(8,128)(2,1)S(1)} %copy-done.19, ...), custom_call_target="tpu_custom_call" | custom-call | flops 838860800 | bytes 8110100 | tf_op jit(solution)/shard_map/attn_bwd/pallas_call | solution.py:436
  257.0 9.4 %attn_bwd.6.refs_2_.early_ref = bf16[3,384,512]{2,1,0:T(8,128)(2,1)S(1)} custom-call(s32[5]{0:T(128)S(1)} %stack.175.coords, bf16[512,640]{1,0:T(8,128)(2,1)S(1)} %get-tuple-element.496.gmb_ref, bf16[640,512]{1,0:T(8,128)(2,1)S(1)} %copy-done.21, bf16[512,1280]{1,0:T(8,128)(2,1)S(1)} %copy-done.19, bf16[640,512]{1,0:T(8,128)(2,1)S(1)} %get-tuple-element.499.ot_ref.refs_1_, ...), custom_call_target="tpu_custom_call" | custom-call | flops 1258291200 | bytes 7847956 | tf_op jit(solution)/shard_map/attn_bwd/pallas_call | solution.py:436
  273.6 4.6 %attn_after.3 = (bf16[512,640]{1,0:T(8,128)(2,1)}, f32[16,640]{1,0:T(8,128)S(1)}) custom-call(bf16[3,384,512]{2,1,0:T(8,128)(2,1)S(1)} %attn_bwd.6.refs_2_.early_ref, bf16[3,256,512]{2,1,0:T(8,128)(2,1)S(1)} %get-tuple-element.534.refs_3_.late_ref, f32[512,640]{1,0:T(8,128)S(1)} %get-tuple-element.520.gm_ref, bf16[512,640]{1,0:T(8,128)(2,1)S(1)} %copy-done.5, ...), custom_call_target="tpu_custom_call" | custom-call | flops 1258291200 | bytes 7946240 | tf_op jit(solution)/shard_map/attn_after/pallas_call | solution.py:436
  278.2 3.7 %grads.18 = bf16[2,2,2,2,80,640]{5,4,3,2,1,0:T(8,128)(2,1)} custom-call(s32[5]{0:T(128)S(1)} %stack.175.coords, bf16[640,512]{1,0:T(8,128)(2,1)S(1)} %get-tuple-element.516.refs_0_, bf16[640,512]{1,0:T(8,128)(2,1)S(1)} %get-tuple-element.499.ot_ref.refs_1_, bf16[3,384,512]{2,1,0:T(8,128)(2,1)S(1)} %attn_bwd.6.refs_2_.early_ref, ...), custom_call_target="tpu_custom_call" | custom-call | flops 838860800 | bytes 5570580 | tf_op jit(solution)/shard_map/grads/pallas_call | solution.py:436
  297.4 8.8 %collective-permute-done.45 = bf16[2,2,2,80,640]{4,3,2,1,0:T(8,128)(2,1)S(1)} collective-permute-done((bf16[2,2,2,80,640]{4,3,2,1,0:T(8,128)(2,1)S(1)}, bf16[2,2,2,80,640]{4,3,2,1,0:T(8,128)(2,1)S(1)}, u32[]{:S(2)}, u32[]{:S(2)}) %collective-permute-start.45) | collective-permute-done | bytes 819232 | tf_op jit(solution)/shard_map/ppermute | solution.py:538
  314.6 3.7 %collective-permute-done.50 = bf16[160,640]{1,0:T(8,128)(2,1)S(1)} collective-permute-done((bf16[160,640]{1,0:T(8,128)(2,1)S(1)}, bf16[160,640]{1,0:T(8,128)(2,1)S(1)}, u32[]{:S(2)}, u32[]{:S(2)}) %collective-permute-start.50) | collective-permute-done | bytes 204832 | tf_op jit(solution)/shard_map/ppermute | solution.py:538
  (364 shorter events, 169.6 us)
Async XLA Ops:
  34.8 14.5 %collective-permute-start.7 = (bf16[2,4,96,640]{3,2,1,0:T(8,128)(2,1)S(1)}, bf16[2,4,96,640]{3,2,1,0:T(8,128)(2,1)S(1)}, u32[]{:S(2)}, u32[]{:S(2)}) collective-permute-start(bf16[2,4,96,640]{3,2,1,0:T(8,128)(2,1)S(1)} %pad_maximum_fusion.2.refs_0_), channel_id=1, source_target_pairs={{0,4},{1,3},{2,6},{3,1},{4,0},{5,7},{6,2},{7,5},{8,12},{9,11},{10,... | collective-permute-start | bytes 2949128 | tf_op jit(solution)/shard_map/ppermute | solution.py:538
  36.3 12.9 %collective-permute-start.8 = (bf16[2,4,96,640]{3,2,1,0:T(8,128)(2,1)S(1)}, bf16[2,4,96,640]{3,2,1,0:T(8,128)(2,1)S(1)}, u32[]{:S(2)}, u32[]{:S(2)}) collective-permute-start(bf16[2,4,96,640]{3,2,1,0:T(8,128)(2,1)S(1)} %pad_maximum_fusion.2.refs_0_), channel_id=1, source_target_pairs={{0,1},{1,0},{2,3},{3,2},{4,5},{5,4},{6,7},{7,6},{8,9},{9,8},{10,11... | collective-permute-start | bytes 2949128 | tf_op jit(solution)/shard_map/ppermute | solution.py:532
  51.2 11.6 %collective-permute-start.12 = (bf16[2,160,640]{2,1,0:T(8,128)(2,1)S(1)}, bf16[2,160,640]{2,1,0:T(8,128)(2,1)S(1)}, u32[]{:S(2)}, u32[]{:S(2)}) collective-permute-start(bf16[2,160,640]{2,1,0:T(8,128)(2,1)S(1)} %slice.465), channel_id=1, source_target_pairs={{0,8},{1,17},{2,10},{3,19},{4,12},{5,21},{6,14},{7,23},{8,0},{9,25... | collective-permute-start | bytes 1228808 | tf_op jit(solution)/shard_map/ppermute | solution.py:538
  64.0 19.2 %collective-permute-start.14 = (bf16[2,4,80,640]{3,2,1,0:T(8,128)(2,1)}, bf16[2,4,80,640]{3,2,1,0:T(8,128)(2,1)}, u32[]{:S(2)}, u32[]{:S(2)}) collective-permute-start(bf16[2,4,80,640]{3,2,1,0:T(8,128)(2,1)} %pad_maximum_fusion.3.refs_0_), channel_id=1, source_target_pairs={{0,4},{1,3},{2,6},{3,1},{4,0},{5,7},{6,2},{7,5},{8,12},{9,11},{10,... | collective-permute-start | bytes 2457608 | tf_op jit(solution)/shard_map/ppermute | solution.py:538
  65.8 17.4 %collective-permute-start.15 = (bf16[2,4,80,640]{3,2,1,0:T(8,128)(2,1)}, bf16[2,4,80,640]{3,2,1,0:T(8,128)(2,1)}, u32[]{:S(2)}, u32[]{:S(2)}) collective-permute-start(bf16[2,4,80,640]{3,2,1,0:T(8,128)(2,1)} %pad_maximum_fusion.3.refs_0_), channel_id=1, source_target_pairs={{0,1},{1,0},{2,3},{3,2},{4,5},{5,4},{6,7},{7,6},{8,9},{9,8},{10,11... | collective-permute-start | bytes 2457608 | tf_op jit(solution)/shard_map/ppermute | solution.py:532
  69.4 12.4 %collective-permute-start.17 = (bf16[2,160,640]{2,1,0:T(8,128)(2,1)S(1)}, bf16[2,160,640]{2,1,0:T(8,128)(2,1)S(1)}, u32[]{:S(2)}, u32[]{:S(2)}) collective-permute-start(bf16[2,160,640]{2,1,0:T(8,128)(2,1)S(1)} %pad_maximum_fusion.13), channel_id=1, source_target_pairs={{0,8},{1,17},{2,10},{3,19},{4,12},{5,21},{6,14},{7,23},{8,0},{9,25... | collective-permute-start | bytes 1228808 | tf_op jit(solution)/shard_map/ppermute | solution.py:538
  69.5 13.3 %collective-permute-start.16 = (bf16[4,160,640]{2,1,0:T(8,128)(2,1)}, bf16[4,160,640]{2,1,0:T(8,128)(2,1)S(1)}, u32[]{:S(2)}, u32[]{:S(2)}) collective-permute-start(bf16[4,160,640]{2,1,0:T(8,128)(2,1)} %pad_maximum_fusion.4), channel_id=1, source_target_pairs={{0,2},{1,5},{2,0},{3,7},{4,6},{5,1},{6,4},{7,3},{8,10},{9,13},{10,... | collective-permute-start | bytes 2457608 | tf_op jit(solution)/shard_map/ppermute | solution.py:538
  87.8 21.1 %collective-permute-start.19 = (bf16[2,4,160,640]{3,2,1,0:T(8,128)(2,1)S(1)}, bf16[2,4,160,640]{3,2,1,0:T(8,128)(2,1)S(1)}, u32[]{:S(2)}, u32[]{:S(2)}) collective-permute-start(bf16[2,4,160,640]{3,2,1,0:T(8,128)(2,1)S(1)} %pad_maximum_fusion.refs_1_.refs_0_), channel_id=1, source_target_pairs={{0,4},{1,3},{2,6},{3,1},{4,0},{5,7},{6,2},{7,5},{8,12},{9,11},{10,... | collective-permute-start | bytes 4915208 | tf_op jit(solution)/shard_map/ppermute | solution.py:538
  89.6 19.3 %collective-permute-start.20 = (bf16[2,4,160,640]{3,2,1,0:T(8,128)(2,1)S(1)}, bf16[2,4,160,640]{3,2,1,0:T(8,128)(2,1)S(1)}, u32[]{:S(2)}, u32[]{:S(2)}) collective-permute-start(bf16[2,4,160,640]{3,2,1,0:T(8,128)(2,1)S(1)} %pad_maximum_fusion.refs_1_.refs_0_), channel_id=1, source_target_pairs={{0,1},{1,0},{2,3},{3,2},{4,5},{5,4},{6,7},{7,6},{8,9},{9,8},{10,11... | collective-permute-start | bytes 4915208 | tf_op jit(solution)/shard_map/ppermute | solution.py:532
  112.4 12.3 %collective-permute-start.22 = (bf16[4,160,640]{2,1,0:T(8,128)(2,1)S(1)}, bf16[4,160,640]{2,1,0:T(8,128)(2,1)S(1)}, u32[]{:S(2)}, u32[]{:S(2)}) collective-permute-start(bf16[4,160,640]{2,1,0:T(8,128)(2,1)S(1)} %pad_maximum_fusion.5), channel_id=1, source_target_pairs={{0,2},{1,5},{2,0},{3,7},{4,6},{5,1},{6,4},{7,3},{8,10},{9,13},{10,... | collective-permute-start | bytes 2457608 | tf_op jit(solution)/shard_map/ppermute | solution.py:538
  125.1 21.2 %collective-permute-start.23 = (bf16[2,4,160,640]{3,2,1,0:T(8,128)(2,1)S(1)}, bf16[2,4,160,640]{3,2,1,0:T(8,128)(2,1)S(1)}, u32[]{:S(2)}, u32[]{:S(2)}) collective-permute-start(bf16[2,4,160,640]{3,2,1,0:T(8,128)(2,1)S(1)} %pad_maximum_fusion.1.refs_0_), channel_id=1, source_target_pairs={{0,4},{1,3},{2,6},{3,1},{4,0},{5,7},{6,2},{7,5},{8,12},{9,11},{10,... | collective-permute-start | bytes 4915208 | tf_op jit(solution)/shard_map/ppermute | solution.py:538
  126.9 19.3 %collective-permute-start.24 = (bf16[2,4,160,640]{3,2,1,0:T(8,128)(2,1)S(1)}, bf16[2,4,160,640]{3,2,1,0:T(8,128)(2,1)S(1)}, u32[]{:S(2)}, u32[]{:S(2)}) collective-permute-start(bf16[2,4,160,640]{3,2,1,0:T(8,128)(2,1)S(1)} %pad_maximum_fusion.1.refs_0_), channel_id=1, source_target_pairs={{0,1},{1,0},{2,3},{3,2},{4,5},{5,4},{6,7},{7,6},{8,9},{9,8},{10,11... | collective-permute-start | bytes 4915208 | tf_op jit(solution)/shard_map/ppermute | solution.py:532
  167.8 12.4 %collective-permute-start.27 = (bf16[2,2,2,80,640]{4,3,2,1,0:T(8,128)(2,1)S(1)}, bf16[2,2,2,80,640]{4,3,2,1,0:T(8,128)(2,1)S(1)}, u32[]{:S(2)}, u32[]{:S(2)}) collective-permute-start(bf16[2,2,2,80,640]{4,3,2,1,0:T(8,128)(2,1)S(1)} %fusion.6), channel_id=1, source_target_pairs={{0,4},{1,3},{2,6},{3,1},{4,0},{5,7},{6,2},{7,5},{8,12},{9,11},{10,... | collective-permute-start | bytes 2457608 | tf_op jit(solution)/shard_map/ppermute | solution.py:538
  188.9 12.4 %collective-permute-start.30 = (bf16[2,2,2,80,640]{4,3,2,1,0:T(8,128)(2,1)S(1)}, bf16[2,2,2,80,640]{4,3,2,1,0:T(8,128)(2,1)S(1)}, u32[]{:S(2)}, u32[]{:S(2)}) collective-permute-start(bf16[2,2,2,80,640]{4,3,2,1,0:T(8,128)(2,1)S(1)} %fusion.5), channel_id=1, source_target_pairs={{0,4},{1,3},{2,6},{3,1},{4,0},{5,7},{6,2},{7,5},{8,12},{9,11},{10,... | collective-permute-start | bytes 2457608 | tf_op jit(solution)/shard_map/ppermute | solution.py:538
  201.5 13.6 %collective-permute-start.32 = (bf16[2,2,80,640]{3,2,1,0:T(8,128)(2,1)S(1)}, bf16[2,2,80,640]{3,2,1,0:T(8,128)(2,1)S(1)}, u32[]{:S(2)}, u32[]{:S(2)}) collective-permute-start(bf16[2,2,80,640]{3,2,1,0:T(8,128)(2,1)S(1)} %fusion.12), channel_id=1, source_target_pairs={{0,2},{1,5},{2,0},{3,7},{4,6},{5,1},{6,4},{7,3},{8,10},{9,13},{10,... | collective-permute-start | bytes 1228808 | tf_op jit(solution)/shard_map/ppermute | solution.py:538
  202.6 12.6 %collective-permute-start.33 = (bf16[80,640]{1,0:T(8,128)(2,1)S(1)}, bf16[80,640]{1,0:T(8,128)(2,1)S(1)}, u32[]{:S(2)}, u32[]{:S(2)}) collective-permute-start(bf16[80,640]{1,0:T(8,128)(2,1)S(1)} %fusion.35), channel_id=1, source_target_pairs={{0,16},{1,9},{2,18},{3,11},{4,20},{5,13},{6,22},{7,15},{8,24},{9,1... | collective-permute-start | bytes 307208 | tf_op jit(solution)/shard_map/ppermute | solution.py:538
  223.2 15.1 %collective-permute-start.36 = (bf16[2,2,2,80,640]{4,3,2,1,0:T(8,128)(2,1)S(1)}, bf16[2,2,2,80,640]{4,3,2,1,0:T(8,128)(2,1)S(1)}, u32[]{:S(2)}, u32[]{:S(2)}) collective-permute-start(bf16[2,2,2,80,640]{4,3,2,1,0:T(8,128)(2,1)S(1)} %fusion.4), channel_id=1, source_target_pairs={{0,4},{1,3},{2,6},{3,1},{4,0},{5,7},{6,2},{7,5},{8,12},{9,11},{10,... | collective-permute-start | bytes 2457608 | tf_op jit(solution)/shard_map/ppermute | solution.py:538
  224.3 14.0 %collective-permute-start.37 = (bf16[80,640]{1,0:T(8,128)(2,1)S(1)}, bf16[80,640]{1,0:T(8,128)(2,1)S(1)}, u32[]{:S(2)}, u32[]{:S(2)}) collective-permute-start(bf16[80,640]{1,0:T(8,128)(2,1)S(1)} %fusion.36), channel_id=1, source_target_pairs={{0,16},{1,9},{2,18},{3,11},{4,20},{5,13},{6,22},{7,15},{8,24},{9,1... | collective-permute-start | bytes 307208 | tf_op jit(solution)/shard_map/ppermute | solution.py:538
  248.0 21.2 %collective-permute-start.40 = (bf16[2,2,2,160,640]{4,3,2,1,0:T(8,128)(2,1)S(1)}, bf16[2,2,2,160,640]{4,3,2,1,0:T(8,128)(2,1)S(1)}, u32[]{:S(2)}, u32[]{:S(2)}) collective-permute-start(bf16[2,2,2,160,640]{4,3,2,1,0:T(8,128)(2,1)S(1)} %fusion), channel_id=1, source_target_pairs={{0,4},{1,3},{2,6},{3,1},{4,0},{5,7},{6,2},{7,5},{8,12},{9,11},{10,... | collective-permute-start | bytes 4915208 | tf_op jit(solution)/shard_map/ppermute | solution.py:538
  248.6 17.8 %collective-permute-start.41 = (bf16[2,80,640]{2,1,0:T(8,128)(2,1)S(1)}, bf16[2,80,640]{2,1,0:T(8,128)(2,1)S(1)}, u32[]{:S(2)}, u32[]{:S(2)}) collective-permute-start(bf16[2,80,640]{2,1,0:T(8,128)(2,1)S(1)} %fusion.25), channel_id=1, source_target_pairs={{0,8},{1,17},{2,10},{3,19},{4,12},{5,21},{6,14},{7,23},{8,0},{9,25... | collective-permute-start | bytes 614408 | tf_op jit(solution)/shard_map/ppermute | solution.py:538
  270.0 12.3 %collective-permute-start.42 = (bf16[2,2,160,640]{3,2,1,0:T(8,128)(2,1)S(1)}, bf16[2,2,160,640]{3,2,1,0:T(8,128)(2,1)S(1)}, u32[]{:S(2)}, u32[]{:S(2)}) collective-permute-start(bf16[2,2,160,640]{3,2,1,0:T(8,128)(2,1)S(1)} %fusion.2), channel_id=1, source_target_pairs={{0,2},{1,5},{2,0},{3,7},{4,6},{5,1},{6,4},{7,3},{8,10},{9,13},{10,... | collective-permute-start | bytes 2457608 | tf_op jit(solution)/shard_map/ppermute | solution.py:538
  270.6 11.2 %collective-permute-start.43 = (bf16[80,640]{1,0:T(8,128)(2,1)S(1)}, bf16[80,640]{1,0:T(8,128)(2,1)S(1)}, u32[]{:S(2)}, u32[]{:S(2)}) collective-permute-start(bf16[80,640]{1,0:T(8,128)(2,1)S(1)} %fusion.37), channel_id=1, source_target_pairs={{0,16},{1,9},{2,18},{3,11},{4,20},{5,13},{6,22},{7,15},{8,24},{9,1... | collective-permute-start | bytes 307208 | tf_op jit(solution)/shard_map/ppermute | solution.py:538
  284.7 12.7 %collective-permute-start.46 = (bf16[2,160,640]{2,1,0:T(8,128)(2,1)}, bf16[2,160,640]{2,1,0:T(8,128)(2,1)}, u32[]{:S(2)}, u32[]{:S(2)}) collective-permute-start(bf16[2,160,640]{2,1,0:T(8,128)(2,1)} %fusion.16), channel_id=1, source_target_pairs={{0,8},{1,17},{2,10},{3,19},{4,12},{5,21},{6,14},{7,23},{8,0},{9,25... | collective-permute-start | bytes 1228808 | tf_op jit(solution)/shard_map/ppermute | solution.py:538
  293.7 12.4 %collective-permute-start.45 = (bf16[2,2,2,80,640]{4,3,2,1,0:T(8,128)(2,1)S(1)}, bf16[2,2,2,80,640]{4,3,2,1,0:T(8,128)(2,1)S(1)}, u32[]{:S(2)}, u32[]{:S(2)}) collective-permute-start(bf16[2,2,2,80,640]{4,3,2,1,0:T(8,128)(2,1)S(1)} %fusion.1), channel_id=1, source_target_pairs={{0,4},{1,3},{2,6},{3,1},{4,0},{5,7},{6,2},{7,5},{8,12},{9,11},{10,... | collective-permute-start | bytes 2457608 | tf_op jit(solution)/shard_map/ppermute | solution.py:538
  (76 other events, 561.1 us)

commit v5 on v4

--- a/solution.py
+++ b/solution.py
@@ -223,16 +223,19 @@
 def ffn_fwd_kernel(offsets, last, coords, m_ref, b_ref, vec_ref, *refs):
     offset, offset_down = offsets
     if offset is None:
-        up_ref, down_ref, y_ref, zt_ref, slope_ref, z_ref = refs
+        up_ref, down_ref, y_ref, zt_ref, slope_ref, *rest = refs
     elif offset_down is None:
-        down_ref, *pieces, y_ref, zt_ref, slope_ref, up_ref, z_ref, sems = refs
+        down_ref, *pieces, y_ref, zt_ref, slope_ref, up_ref = refs[:9]
+        rest = refs[9:]
     else:
-        *pieces, y_ref, zt_ref, slope_ref, up_ref, down_ref, z_ref, sems = refs
+        *pieces, y_ref, zt_ref, slope_ref, up_ref, down_ref = refs[:9]
+        rest = refs[9:]
+    z_ref = y_ref if last else rest[0]
+    sems = rest[-1] if rest else None
     if offset is not None:
         job = Assembly(coords, False, pieces, offset, up_ref, sems.at[0])
     if offset_down is not None:
         job_down = Assembly(coords, True, pieces, offset_down, down_ref, sems.at[1])
-    length = m_ref.shape[0]
     normed = b_ref[...]
     for block in range(BLOCKS):
         if offset is not None:
@@ -246,11 +249,14 @@
         zt_ref[columns, :] = z_ref[:, columns].T
     if offset_down is not None:
         job_down.wait()
-    out = m_ref[...] + (dot(z_ref[...], down_ref[...].reshape(FF, D)) + vec_ref[BIAS_DOWN : BIAS_DOWN + 1, :])
-    if last:
-        row = lax.broadcasted_iota(jnp.int32, (length, 1), 0)
-        out = jnp.where(row < coords[4], out, 0.0)
-    y_ref[...] = out.astype(y_ref.dtype)
+    if not last:
+        y_ref[...] = m_ref[...] + (dot(z_ref[...], down_ref[...].reshape(FF, D)) + vec_ref[BIAS_DOWN : BIAS_DOWN + 1, :])
+
+
+def ffn_out_kernel(coords, m_ref, z_ref, vec_ref, down_ref, y_ref):
+    out = m_ref[...] + (dot(z_ref[...], down_ref[...]) + vec_ref[BIAS_DOWN : BIAS_DOWN + 1, :])
+    row = lax.broadcasted_iota(jnp.int32, (m_ref.shape[0], 1), 0)
+    y_ref[...] = jnp.where(row < coords[4], out, 0.0).astype(bf16)
 
 
 def ffn_bwd_kernel(top, coords, g_ref, slope_ref, m_ref, vec_ref, up_ref, down_ref, *refs):
@@ -476,15 +482,20 @@
     ins = [(coords, S), (kept["m"], V), (kept["b"], V), (vec, V)]
     ins += [(w, V) for w, part in zip((up, down), parts) if not part]
     ins += [(p, H) for p in up[0]] if parts[0] else []
-    outs = [((n, D), bf16 if last else f32), ((FF, n), bf16), ((n, FF), bf16)]
+    outs = [((n, FF), bf16) if last else ((n, D), f32), ((FF, n), bf16), ((n, FF), bf16)]
     outs += [(shape, bf16) for shape, part in zip((WHOLE, WHOLE_ROWS), parts) if part]
-    scratch = [V((n, FF), bf16)] + ([SEMS((2, 8))] if parts[0] else [])
+    scratch = ([] if last else [V((n, FF), bf16)]) + ([SEMS((2, 8))] if parts[0] else [])
     offsets = [w[1] if part else None for w, part in zip((up, down), parts)]
     kernel = functools.partial(ffn_fwd_kernel, offsets, last)
     y, zt, slope, *more = call(kernel, ins, outs, scratch, "ffn_fwd", 4 * n * D * FF, 2 * n * FF)
     up = more[0].reshape(D, FF) if parts[0] else up
     down = more[1].reshape(FF, D) if parts[1] else down
     return y, {"zt": zt, "slope": slope}, up, down
+
+
+def ffn_out(coords, kept, hidden, vec, down):
+    ins = [(coords, S)] + [(a, V) for a in (kept["m"], hidden, vec, down)]
+    return call(ffn_out_kernel, ins, [(kept["m"].shape, bf16)], [], "ffn_out", 2 * hidden.size * D)[0]
 
 
 def ffn_bwd(coords, g, kept, vec, up, down, top):
@@ -674,7 +685,8 @@
         x, more, *_ = ffn_fwd(coords, held, vectors[l], whole[1], whole[2], l == LAYERS - 1)
         kept.append(held | more)
         wholes.append(whole)
-    output, grad, sums = x, cotangent, [None] * LAYERS
+    output = ffn_out(coords, kept[-1], x, vectors[-1], wholes[-1][2])
+    grad, sums = cotangent, [None] * LAYERS
     for l in reversed(range(LAYERS)):
         last = l == 0
         back[l] = ffn_bwd(coords, grad, kept[l], vectors[l], wholes[l][1], wholes[l][2], not last)
@@ -766,7 +778,8 @@
     far0, mate0, u1 = step(3, near0), mate(near0), link1(t1)
     far0, mate0, zz1, t2 = stage(far0, mate0, by_z(u1), t2)
     near1, far_mate0, u2, t3 = link2(zz1), mate(far0), link1(t2), link0(c3)
-    near1, far_mate0, zz2, t3 = stage(near1, far_mate0, by_z(u2), t3)
+    near1, far_mate0, t3 = stage(near1, far_mate0, t3)
+    zz2 = by_z(u2)
     arrived(((("down", 0), PIECE),), near0, mate0, far0, far_mate0)
     far1, mate1, near2, u3 = step(3, near1), mate(near1), link2(zz2), link1(t3)
     whole["down", 0] = assemble(coords, weights["down", 0])
@@ -798,7 +811,7 @@
     whole["attn", 1] = got[0]
     far3, mate3, kept[1] = stage(far3, mate3, kept[1])
     arrived(((("down", 1), PIECE), (("up", 1), PIECE)), near3, mate3, far3, mate(far3))
-    output, more, whole["up", 1], whole["down", 1] = ffn_fwd(
+    hidden, more, whole["up", 1], whole["down", 1] = ffn_fwd(
         coords, kept[1], vectors[1], weights["up", 1], weights["down", 1], True
     )
     kept[1] |= more
@@ -818,43 +831,46 @@
     got_d1, core, back[1] = stage(got_d1, blocks(1, 1), back[1])
     second, core, back[1] = stage(d1.second(got_d1), core, back[1])
 
-    got_d1, core, rest = stage(step(2, second), mate(core), blocks(1, 0))
-    first, third, back[1] = stage(u1.first(core, rest), d1.third(got_d1), back[1])
-
-    got_u1, got_d1 = step(3, first), step(1, third)
+    got_d1 = step(2, second)
+    core, rest = stage(mate(core), blocks(1, 0))
+    first, back[1] = stage(u1.first(core, rest), back[1])
+
+    got_u1 = step(3, first)
     (back[1]["early"],) = attn_bwd(coords, back[1]["gmb"], kept[1], table, whole["attn", 1], EARLY)
     got_u1, got_d1, back[1] = stage(got_u1, got_d1, back[1])
-    second, fourth, back[1] = stage(u1.second(got_u1), d1.fourth(got_d1), back[1])
-
-    got_u1, got_d1 = step(2, second), step(0, fourth)
+    second, third, back[1] = stage(u1.second(got_u1), d1.third(got_d1), back[1])
+
+    got_u1, got_d1 = step(2, second), step(1, third)
     back[1]["late"], back[1]["flip"] = attn_bwd(coords, back[1]["gmb"], kept[1], table, whole["attn", 1], LATE)
     got_u1, got_d1, core, back[1] = stage(got_u1, got_d1, blocks(2, 1), back[1])
-    third, core, back[1] = stage(u1.third(got_u1), core, back[1])
-
-    got_u1, core, rest = stage(step(1, third), mate(core), blocks(2, 0))
-    first, fourth, back[1] = stage(a1.first(core, rest), u1.fourth(got_u1), back[1])
-
-    got_a1, got_u1 = step(3, first), step(0, fourth)
+    third, fourth, core, back[1] = stage(u1.third(got_u1), d1.fourth(got_d1), core, back[1])
+
+    got_u1, got_d1 = step(1, third), step(0, fourth)
+    core, rest = stage(mate(core), blocks(2, 0))
+    first, back[1] = stage(a1.first(core, rest), back[1])
+
+    got_a1 = step(3, first)
     grad, more = attn_after(back[1], kept[1], vectors[1], whole["attn", 1], False)
     sums = [None, back[1]["sums"] + more]
     back[0] = ffn_bwd(coords, grad, kept[0], vectors[0], whole["up", 0], whole["down", 0], False)
-    got_a1, got_u1, core, back[0] = stage(got_a1, got_u1, blocks(3, 1), back[0])
-    second, core, back[0] = stage(a1.second(got_a1), core, back[0])
-
-    got_a1, core, rest = stage(step(2, second), mate(core), blocks(3, 0))
+    got_a1, got_u1, got_d1, core, back[0] = stage(got_a1, got_u1, got_d1, blocks(3, 1), back[0])
+    second, fourth, core, back[0] = stage(a1.second(got_a1), u1.fourth(got_u1), core, back[0])
+
+    got_a1, got_u1, core, rest = stage(step(2, second), step(0, fourth), mate(core), blocks(3, 0))
     first, third, back[0] = stage(du0.first(core, rest), a1.third(got_a1), back[0])
 
     got_du0, got_a1 = step(3, first), step(1, third)
     (back[0]["early"],) = attn_bwd(coords, back[0]["gmb"], kept[0], table, whole["attn", 0], EARLY)
     back[0]["late"], back[0]["flip"] = attn_bwd(coords, back[0]["gmb"], kept[0], table, whole["attn", 0], LATE)
     got_du0, got_a1, back[0] = stage(got_du0, got_a1, back[0])
-    second, fourth, back[0] = stage(du0.second(got_du0), a1.fourth(got_a1), back[0])
+    second, fourth, back[0], hidden = stage(du0.second(got_du0), a1.fourth(got_a1), back[0], hidden)
 
     got_du0, got_a1 = step(2, second), step(0, fourth)
     core = blocks(4, 1)
     grad, more = attn_after(back[0], kept[0], vectors[0], whole["attn", 0], True)
     sums[0] = back[0]["sums"] + more
-    got_du0, got_a1, core, grad, sums, back[0] = stage(got_du0, got_a1, core, grad, sums, back[0])
+    output = ffn_out(coords, kept[1], hidden, vectors[1], whole["down", 1])
+    got_du0, got_a1, core, grad, sums, back[0], output = stage(got_du0, got_a1, core, grad, sums, back[0], output)
     third, core, back[0] = stage(du0.third(got_du0), core, back[0])
 
     got_du0 = step(1, third)

time: 352 us -> 347 us (0.986)
  waiting for transfers between devices: 103 us -> 96.7 us
    ppermute x39, waiting for transfers between devices: 81.1 us -> 71.9 us  [step(): return lax.ppermute(value, AXES, pairs)]
    ppermute x14, starting transfers between devices: 4.94 us -> 1.34 us  [mate(): return lax.ppermute(value, 'narrow', [(0, 1), (1, 0)])]
    unnamed x96 -> x104, local copies, waits for them, and re-layouts: 9.44 us -> 11.1 us
    pallas_call x23 -> x24, Pallas kernels: 133 us -> 134 us  [call(): pl.pallas_call(kernel, out_shape=[jax.ShapeDtypeStruct(s, t) for s, t in...]
  transfers between devices with their start and end apart: 62 -> 62, of which waited for: 34 -> 31; matrix products, arithmetic and copies ran while one was open for 5% -> 6% of each run, Pallas kernels for 34% -> 36%
where the time goes in v5:
time: 347 us; the launch traced here: 340 us
  Pallas kernels  134 us (39%)
  waiting for transfers between devices  96.7 us (28%)
  starting transfers between devices  62.5 us (18%)
  local copies, waits for them, and re-layouts  22.5 us (6%)
  other arithmetic  21.7 us (6%)
    pallas_call x24, Pallas kernels, call(): pl.pallas_call(kernel, out_shape=[jax.ShapeDtypeStruct(s, t) for s, t in...  134 us
    ppermute x39, waiting for transfers between devices, step(): return lax.ppermute(value, AXES, pairs)  71.9 us
    ppermute x39, starting transfers between devices, step(): return lax.ppermute(value, AXES, pairs)  55.4 us
    ppermute x14, waiting for transfers between devices, mate(): return lax.ppermute(value, 'narrow', [(0, 1), (1, 0)])  14.3 us
    unnamed x104, local copies, waits for them, and re-layouts  11.1 us
    ppermute x9, waiting for transfers between devices, regroup(): lax.ppermute(mine[k], AXES, [(i, i ^ k) for i in range(32)])  10.5 us
  transfers between devices with their start and end apart: 62, of which 31 were waited for; matrix products, arithmetic and copies ran while one was open for 6% of the time, Pallas kernels for 36%

profile of v5, /device:TPU:0, one launch (start us, length us, event | category | flops | bytes accessed | tf_op | source)
XLA Modules:
  0.0 340.5 jit_solution(14728396927005066041)
XLA Ops:
  3.8 4.1 %collective-permute-start = (bf16[96,640]{1,0:T(8,128)(2,1)S(1)}, bf16[96,640]{1,0:T(8,128)(2,1)S(1)}, u32[]{:S(2)}, u32[]{:S(2)}) collective-permute-start(bf16[96,640]{1,0:T(8,128)(2,1)S(1)} %fusion.34), channel_id=1, source_target_pairs={{0,16},{1,9},{2,18},{3,11},{4,20},{5,13},{6,22},{7,15},{8,24},{9,1... | collective-permute-start | bytes 368648 | tf_op jit(solution)/shard_map/ppermute | solution.py:549
  26.8 7.6 %collective-permute-done.6 = bf16[240,640]{1,0:T(8,128)(2,1)S(1)} collective-permute-done((bf16[240,640]{1,0:T(8,128)(2,1)S(1)}, bf16[240,640]{1,0:T(8,128)(2,1)S(1)}, u32[]{:S(2)}, u32[]{:S(2)}) %collective-permute-start.6) | collective-permute-done | bytes 307232 | tf_op jit(solution)/shard_map/ppermute | solution.py:549
  42.9 4.9 %collective-permute-done.9 = bf16[2,80,640]{2,1,0:T(8,128)(2,1)S(1)} collective-permute-done((bf16[2,80,640]{2,1,0:T(8,128)(2,1)}, bf16[2,80,640]{2,1,0:T(8,128)(2,1)S(1)}, u32[]{:S(2)}, u32[]{:S(2)}) %collective-permute-start.9) | collective-permute-done | bytes 204832 | tf_op jit(solution)/shard_map/ppermute | solution.py:549
  55.0 5.2 %collective-permute-done.15 = bf16[2,160,640]{2,1,0:T(8,128)(2,1)S(1)} collective-permute-done((bf16[2,160,640]{2,1,0:T(8,128)(2,1)S(1)}, bf16[2,160,640]{2,1,0:T(8,128)(2,1)S(1)}, u32[]{:S(2)}, u32[]{:S(2)}) %collective-permute-start.15) | collective-permute-done | bytes 409632 | tf_op jit(solution)/shard_map/ppermute | solution.py:549
  69.9 12.9 %collective-permute-done.16 = bf16[4,160,640]{2,1,0:T(8,128)(2,1)} collective-permute-done((bf16[4,160,640]{2,1,0:T(8,128)(2,1)}, bf16[4,160,640]{2,1,0:T(8,128)(2,1)}, u32[]{:S(2)}, u32[]{:S(2)}) %collective-permute-start.16) | collective-permute-done | bytes 819232 | tf_op jit(solution)/shard_map/ppermute | solution.py:549
  89.8 14.2 %attn_fwd.2 = (bf16[640,512]{1,0:T(8,128)(2,1)S(1)}, bf16[640,512]{1,0:T(8,128)(2,1)S(1)}, bf16[512,1280]{1,0:T(8,128)(2,1)S(1)}, bf16[640,512]{1,0:T(8,128)(2,1...) custom-call(s32[5]{0:T(128)S(1)} %stack.175.coords, ...), custom_call_target="tpu_custom_call" | custom-call | flops 2348810240 | bytes 13983764 | tf_op jit(solution)/shard_map/attn_fwd/pallas_call | solution.py:442
  104.0 5.4 %collective-permute-done.19.refs_3_.refs_2_ = bf16[2,4,160,640]{3,2,1,0:T(8,128)(2,1)S(1)} collective-permute-done((bf16[2,4,160,640]{3,2,1,0:T(8,128)(2,1)S(1)}, bf16[2,4,160,640]{3,2,1,0:T(8,128)(2,1)S(1)}, u32[]{:S(2)}, u32[]{:S(2)}) %collective-permute-start.19) | collective-permute-done | bytes 1638432 | tf_op jit(solution)/shard_map/ppermute | solution.py:549
  109.4 3.5 %collective-permute-done.21.refs_4_.refs_3_ = bf16[2,4,160,640]{3,2,1,0:T(8,128)(2,1)S(1)} collective-permute-done((bf16[2,4,160,640]{3,2,1,0:T(8,128)(2,1)S(1)}, bf16[2,4,160,640]{3,2,1,0:T(8,128)(2,1)S(1)}, u32[]{:S(2)}, u32[]{:S(2)}) %collective-permute-start.21) | collective-permute-done | bytes 1638432 | tf_op jit(solution)/shard_map/ppermute | solution.py:543
  114.3 10.9 %ffn_fwd.2 = (f32[512,640]{1,0:T(8,128)S(1)}, bf16[2560,512]{1,0:T(8,128)(2,1)S(1)}, bf16[512,2560]{1,0:T(8,128)(2,1)S(1)}, bf16[4,2,80,2560]{3,2,1,0:T(8,128)(2,1)S(1)}) custom-call(s32[5]{0:T(128)S(1)} %stack.175.coords, f32[512,640]{1,0:T(8,128)S(1)} %get-tuple-element.351.m_ref, bf16[512,640]{1,0:T(8,128)(2,1)S(1)} %get-tuple-element.352.b_ref, ...), custom_call_target="tpu_custom_call" | custom-call | flops 3355443200 | bytes 21667860 | tf_op jit(solution)/shard_map/ffn_fwd/pallas_call | solution.py:442
  128.5 14.0 %attn_fwd.3 = (bf16[640,512]{1,0:T(8,128)(2,1)S(1)}, bf16[640,512]{1,0:T(8,128)(2,1)S(1)}, bf16[512,1280]{1,0:T(8,128)(2,1)S(1)}, bf16[640,512]{1,0:T(8,128)(2,1...) custom-call(s32[5]{0:T(128)S(1)} %stack.175.coords, ...), custom_call_target="tpu_custom_call" | custom-call | flops 2348810240 | bytes 17915924 | tf_op jit(solution)/shard_map/attn_fwd/pallas_call | solution.py:442
  143.3 4.8 %collective-permute-done.23.refs_2_ = bf16[2,4,160,640]{3,2,1,0:T(8,128)(2,1)S(1)} collective-permute-done((bf16[2,4,160,640]{3,2,1,0:T(8,128)(2,1)S(1)}, bf16[2,4,160,640]{3,2,1,0:T(8,128)(2,1)S(1)}, u32[]{:S(2)}, u32[]{:S(2)}) %collective-permute-start.23) | collective-permute-done | bytes 1638432 | tf_op jit(solution)/shard_map/ppermute | solution.py:549
  151.6 9.4 %ffn_fwd.3 = (bf16[512,2560]{1,0:T(8,128)(2,1)S(1)}, bf16[2560,512]{1,0:T(8,128)(2,1)S(1)}, bf16[512,2560]{1,0:T(8,128)(2,1)S(1)}, bf16[4,2,80,2560]{3,2,1,0:T(8...) custom-call(s32[5]{0:T(128)S(1)} %stack.175.coords, f32[512,640]{1,0:T(8,128)S(1)} %get-tuple-element.369.m_ref, ...), custom_call_target="tpu_custom_call" | custom-call | flops 3355443200 | bytes 22978580 | tf_op jit(solution)/shard_map/ffn_fwd/pallas_call | solution.py:442
  168.1 7.8 %ffn_bwd.2 = (bf16[512,640]{1,0:T(8,128)(2,1)}, bf16[512,2560]{1,0:T(8,128)(2,1)S(1)}, f32[512,640]{1,0:T(8,128)S(1)}, bf16[512,640]{1,0:T(8,128)(2,1)S(1)}, f32[16,640]{1,0:T(8,128)S(1)}) custom-call(s32[5]{0:T(128)S(1)} %stack.175.coords, bf16[512,640]{1,0:T(8,128)(2,1)S(1)} %copy-done.4, bf16[512,2560]{1,0:T(8,128)(2,1)S(1)} %copy-done.15, ...), custom_call_target="tpu_custom_call" | custom-call | flops 3355443200 | bytes 16465940 | tf_op jit(solution)/shard_map/ffn_bwd/pallas_call | solution.py:442
  185.0 9.4 %attn_bwd.4.refs_2_.early_ref = bf16[3,384,512]{2,1,0:T(8,128)(2,1)S(1)} custom-call(s32[5]{0:T(128)S(1)} %stack.175.coords, bf16[512,640]{1,0:T(8,128)(2,1)S(1)} %get-tuple-element.427.gmb_ref, bf16[640,512]{1,0:T(8,128)(2,1)S(1)} %copy-done.19, bf16[512,1280]{1,0:T(8,128)(2,1)S(1)} %copy-done.17, bf16[640,512]{1,0:T(8,128)(2,1)S(1)} %get-tuple-element.410.ot_ref.refs_1_, ...), custom_call_target="tpu_custom_call" | custom-call | flops 1258291200 | bytes 7847956 | tf_op jit(solution)/shard_map/attn_bwd/pallas_call | solution.py:442
  200.7 6.6 %attn_bwd.5 = (bf16[3,256,512]{2,1,0:T(8,128)(2,1)S(1)}, bf16[640,512]{1,0:T(8,128)(2,1)S(1)}) custom-call(s32[5]{0:T(128)S(1)} %stack.175.coords, bf16[512,640]{1,0:T(8,128)(2,1)S(1)} %get-tuple-element.427.gmb_ref, bf16[640,512]{1,0:T(8,128)(2,1)S(1)} %copy-done.19, bf16[512,1280]{1,0:T(8,128)(2,1)S(1)} %copy-done.17, ...), custom_call_target="tpu_custom_call" | custom-call | flops 838860800 | bytes 8110100 | tf_op jit(solution)/shard_map/attn_bwd/pallas_call | solution.py:442
  218.0 3.7 %attn_after.2 = (f32[512,640]{1,0:T(8,128)S(1)}, f32[16,640]{1,0:T(8,128)S(1)}) custom-call(bf16[3,384,512]{2,1,0:T(8,128)(2,1)S(1)} %attn_bwd.4.refs_2_.early_ref, bf16[3,256,512]{2,1,0:T(8,128)(2,1)S(1)} %get-tuple-element.457.refs_3_.late_ref, f32[512,640]{1,0:T(8,128)S(1)} %get-tuple-element.458.gm_ref, f32[512,640]{1,0:T(8,128)S(1)} %get-tuple-element.459.x_ref, ...), custom_call_target="tpu_custom_call" | custom-call | flops 1258291200 | bytes 9256960 | tf_op jit(solution)/shard_map/attn_after/pallas_call | solution.py:442
  221.7 6.7 %ffn_bwd.3 = (bf16[512,640]{1,0:T(8,128)(2,1)S(1)}, bf16[512,2560]{1,0:T(8,128)(2,1)S(1)}, f32[512,640]{1,0:T(8,128)S(1)}, bf16[512,640]{1,0:T(8,128)(2,1)S(1)}, f32[16,640]{1,0:T(8,128)S(1)}) custom-call(s32[5]{0:T(128)S(1)} %stack.175.coords, f32[512,640]{1,0:T(8,128)S(1)} %get-tuple-element.460.g_ref, bf16[512,2560]{1,0:T(8,128)(2,1)S(1)} %copy-done.13, ...), custom_call_target="tpu_custom_call" | custom-call | flops 3355443200 | bytes 17121300 | tf_op jit(solution)/shard_map/ffn_bwd/pallas_call | solution.py:442
  235.9 3.5 %grads.17 = (bf16[2,2,2,160,640]{4,3,2,1,0:T(8,128)(2,1)S(1)}, bf16[2,2,160,640]{3,2,1,0:T(8,128)(2,1)S(1)}, bf16[2,2,160,640]{3,2,1,0:T(8,128)(2,1)S(1)}) custom-call(s32[5]{0:T(128)S(1)} %stack.175.coords, bf16[2560,512]{1,0:T(8,128)(2,1)S(1)} %get-tuple-element.455.refs_0_, bf16[512,640]{1,0:T(8,128)(2,1)S(1)} %get-tuple-element.480.refs_1_, ...), custom_call_target="tpu_custom_call" | custom-call | flops 1677721600 | bytes 9830420 | tf_op jit(solution)/shard_map/grads/pallas_call | solution.py:442
  244.1 6.6 %attn_bwd.7 = (bf16[3,256,512]{2,1,0:T(8,128)(2,1)S(1)}, bf16[640,512]{1,0:T(8,128)(2,1)S(1)}) custom-call(s32[5]{0:T(128)S(1)} %stack.175.coords, bf16[512,640]{1,0:T(8,128)(2,1)S(1)} %get-tuple-element.495.gmb_ref, bf16[640,512]{1,0:T(8,128)(2,1)S(1)} %copy-done.23, bf16[512,1280]{1,0:T(8,128)(2,1)S(1)} %copy-done.21, ...), custom_call_target="tpu_custom_call" | custom-call | flops 838860800 | bytes 8110100 | tf_op jit(solution)/shard_map/attn_bwd/pallas_call | solution.py:442
  250.7 9.5 %attn_bwd.6.refs_2_.early_ref = bf16[3,384,512]{2,1,0:T(8,128)(2,1)S(1)} custom-call(s32[5]{0:T(128)S(1)} %stack.175.coords, bf16[512,640]{1,0:T(8,128)(2,1)S(1)} %get-tuple-element.495.gmb_ref, bf16[640,512]{1,0:T(8,128)(2,1)S(1)} %copy-done.23, bf16[512,1280]{1,0:T(8,128)(2,1)S(1)} %copy-done.21, bf16[640,512]{1,0:T(8,128)(2,1)S(1)} %get-tuple-element.498.ot_ref.refs_1_, ...), custom_call_target="tpu_custom_call" | custom-call | flops 1258291200 | bytes 7847956 | tf_op jit(solution)/shard_map/attn_bwd/pallas_call | solution.py:442
  266.5 3.6 %ffn_out.1 = bf16[512,640]{1,0:T(8,128)(2,1)} custom-call(s32[5]{0:T(128)S(1)} %stack.175.coords, f32[512,640]{1,0:T(8,128)S(1)} %get-tuple-element.369.m_ref, bf16[512,2560]{1,0:T(8,128)(2,1)S(1)} %get-tuple-element.526.z_ref, f32[16,640]{1,0:T(8,128)S(1)} %get-tuple-element.670.vec_ref, bf16[2560,640]{1,0:T(8,128)(2,1)S(1)} %bitcast.342), custom_call_target="tpu_custom_call" | custom-call | flops 1677721600 | bytes 7905300 | tf_op jit(solution)/shard_map/ffn_out/pallas_call | solution.py:442
  270.1 4.6 %attn_after.3 = (bf16[512,640]{1,0:T(8,128)(2,1)}, f32[16,640]{1,0:T(8,128)S(1)}) custom-call(bf16[3,384,512]{2,1,0:T(8,128)(2,1)S(1)} %attn_bwd.6.refs_2_.early_ref, bf16[3,256,512]{2,1,0:T(8,128)(2,1)S(1)} %get-tuple-element.536.refs_3_.late_ref, f32[512,640]{1,0:T(8,128)S(1)} %get-tuple-element.519.gm_ref, bf16[512,640]{1,0:T(8,128)(2,1)S(1)} %copy-done.5, ...), custom_call_target="tpu_custom_call" | custom-call | flops 1258291200 | bytes 7946240 | tf_op jit(solution)/shard_map/attn_after/pallas_call | solution.py:442
  274.7 3.7 %grads.18 = bf16[2,2,2,2,80,640]{5,4,3,2,1,0:T(8,128)(2,1)} custom-call(s32[5]{0:T(128)S(1)} %stack.175.coords, bf16[640,512]{1,0:T(8,128)(2,1)S(1)} %get-tuple-element.515.refs_0_, bf16[640,512]{1,0:T(8,128)(2,1)S(1)} %get-tuple-element.498.ot_ref.refs_1_, bf16[3,384,512]{2,1,0:T(8,128)(2,1)S(1)} %attn_bwd.6.refs_2_.early_ref, ...), custom_call_target="tpu_custom_call" | custom-call | flops 838860800 | bytes 5570580 | tf_op jit(solution)/shard_map/grads/pallas_call | solution.py:442
  293.2 7.5 %collective-permute-done.45 = bf16[2,2,2,80,640]{4,3,2,1,0:T(8,128)(2,1)S(1)} collective-permute-done((bf16[2,2,2,80,640]{4,3,2,1,0:T(8,128)(2,1)S(1)}, bf16[2,2,2,80,640]{4,3,2,1,0:T(8,128)(2,1)S(1)}, u32[]{:S(2)}, u32[]{:S(2)}) %collective-permute-start.45) | collective-permute-done | bytes 819232 | tf_op jit(solution)/shard_map/ppermute | solution.py:549
  (373 shorter events, 167.2 us)
Async XLA Ops:
  34.8 14.2 %collective-permute-start.7 = (bf16[2,4,96,640]{3,2,1,0:T(8,128)(2,1)S(1)}, bf16[2,4,96,640]{3,2,1,0:T(8,128)(2,1)S(1)}, u32[]{:S(2)}, u32[]{:S(2)}) collective-permute-start(bf16[2,4,96,640]{3,2,1,0:T(8,128)(2,1)S(1)} %pad_maximum_fusion.2.refs_0_), channel_id=1, source_target_pairs={{0,4},{1,3},{2,6},{3,1},{4,0},{5,7},{6,2},{7,5},{8,12},{9,11},{10,... | collective-permute-start | bytes 2949128 | tf_op jit(solution)/shard_map/ppermute | solution.py:549
  36.3 12.6 %collective-permute-start.8 = (bf16[2,4,96,640]{3,2,1,0:T(8,128)(2,1)S(1)}, bf16[2,4,96,640]{3,2,1,0:T(8,128)(2,1)S(1)}, u32[]{:S(2)}, u32[]{:S(2)}) collective-permute-start(bf16[2,4,96,640]{3,2,1,0:T(8,128)(2,1)S(1)} %pad_maximum_fusion.2.refs_0_), channel_id=1, source_target_pairs={{0,1},{1,0},{2,3},{3,2},{4,5},{5,4},{6,7},{7,6},{8,9},{9,8},{10,11... | collective-permute-start | bytes 2949128 | tf_op jit(solution)/shard_map/ppermute | solution.py:543
  40.9 11.6 %collective-permute-start.12 = (bf16[160,640]{1,0:T(8,128)(2,1)S(1)}, bf16[160,640]{1,0:T(8,128)(2,1)S(1)}, u32[]{:S(2)}, u32[]{:S(2)}) collective-permute-start(bf16[160,640]{1,0:T(8,128)(2,1)S(1)} %pad_maximum_fusion.19), channel_id=1, source_target_pairs={{0,16},{1,9},{2,18},{3,11},{4,20},{5,13},{6,22},{7,15},{8,24},{9,1... | collective-permute-start | bytes 614408 | tf_op jit(solution)/shard_map/ppermute | solution.py:549
  61.5 21.4 %collective-permute-start.16 = (bf16[4,160,640]{2,1,0:T(8,128)(2,1)}, bf16[4,160,640]{2,1,0:T(8,128)(2,1)}, u32[]{:S(2)}, u32[]{:S(2)}) collective-permute-start(bf16[4,160,640]{2,1,0:T(8,128)(2,1)} %pad_maximum_fusion.4), channel_id=1, source_target_pairs={{0,2},{1,5},{2,0},{3,7},{4,6},{5,1},{6,4},{7,3},{8,10},{9,13},{10,... | collective-permute-start | bytes 2457608 | tf_op jit(solution)/shard_map/ppermute | solution.py:549
  64.6 21.1 %collective-permute-start.13 = (bf16[2,4,80,640]{3,2,1,0:T(8,128)(2,1)}, bf16[2,4,80,640]{3,2,1,0:T(8,128)(2,1)}, u32[]{:S(2)}, u32[]{:S(2)}) collective-permute-start(bf16[2,4,80,640]{3,2,1,0:T(8,128)(2,1)} %pad_maximum_fusion.3.refs_0_), channel_id=1, source_target_pairs={{0,4},{1,3},{2,6},{3,1},{4,0},{5,7},{6,2},{7,5},{8,12},{9,11},{10,... | collective-permute-start | bytes 2457608 | tf_op jit(solution)/shard_map/ppermute | solution.py:549
  66.1 19.6 %collective-permute-start.14 = (bf16[2,4,80,640]{3,2,1,0:T(8,128)(2,1)}, bf16[2,4,80,640]{3,2,1,0:T(8,128)(2,1)}, u32[]{:S(2)}, u32[]{:S(2)}) collective-permute-start(bf16[2,4,80,640]{3,2,1,0:T(8,128)(2,1)} %pad_maximum_fusion.3.refs_0_), channel_id=1, source_target_pairs={{0,1},{1,0},{2,3},{3,2},{4,5},{5,4},{6,7},{7,6},{8,9},{9,8},{10,11... | collective-permute-start | bytes 2457608 | tf_op jit(solution)/shard_map/ppermute | solution.py:543
  69.8 14.8 %collective-permute-start.17 = (bf16[2,160,640]{2,1,0:T(8,128)(2,1)}, bf16[2,160,640]{2,1,0:T(8,128)(2,1)S(1)}, u32[]{:S(2)}, u32[]{:S(2)}) collective-permute-start(bf16[2,160,640]{2,1,0:T(8,128)(2,1)} %pad_maximum_fusion.13), channel_id=1, source_target_pairs={{0,8},{1,17},{2,10},{3,19},{4,12},{5,21},{6,14},{7,23},{8,0},{9,25... | collective-permute-start | bytes 1228808 | tf_op jit(solution)/shard_map/ppermute | solution.py:549
  88.2 21.1 %collective-permute-start.19 = (bf16[2,4,160,640]{3,2,1,0:T(8,128)(2,1)S(1)}, bf16[2,4,160,640]{3,2,1,0:T(8,128)(2,1)S(1)}, u32[]{:S(2)}, u32[]{:S(2)}) collective-permute-start(bf16[2,4,160,640]{3,2,1,0:T(8,128)(2,1)S(1)} %pad_maximum_fusion.refs_1_.refs_0_), channel_id=1, source_target_pairs={{0,4},{1,3},{2,6},{3,1},{4,0},{5,7},{6,2},{7,5},{8,12},{9,11},{10,... | collective-permute-start | bytes 4915208 | tf_op jit(solution)/shard_map/ppermute | solution.py:549
  89.8 19.6 %collective-permute-start.20 = (bf16[2,4,160,640]{3,2,1,0:T(8,128)(2,1)S(1)}, bf16[2,4,160,640]{3,2,1,0:T(8,128)(2,1)S(1)}, u32[]{:S(2)}, u32[]{:S(2)}) collective-permute-start(bf16[2,4,160,640]{3,2,1,0:T(8,128)(2,1)S(1)} %pad_maximum_fusion.refs_1_.refs_0_), channel_id=1, source_target_pairs={{0,1},{1,0},{2,3},{3,2},{4,5},{5,4},{6,7},{7,6},{8,9},{9,8},{10,11... | collective-permute-start | bytes 4915208 | tf_op jit(solution)/shard_map/ppermute | solution.py:543
  112.9 12.4 %collective-permute-start.22 = (bf16[4,160,640]{2,1,0:T(8,128)(2,1)S(1)}, bf16[4,160,640]{2,1,0:T(8,128)(2,1)S(1)}, u32[]{:S(2)}, u32[]{:S(2)}) collective-permute-start(bf16[4,160,640]{2,1,0:T(8,128)(2,1)S(1)} %pad_maximum_fusion.5), channel_id=1, source_target_pairs={{0,2},{1,5},{2,0},{3,7},{4,6},{5,1},{6,4},{7,3},{8,10},{9,13},{10,... | collective-permute-start | bytes 2457608 | tf_op jit(solution)/shard_map/ppermute | solution.py:549
  126.9 21.2 %collective-permute-start.23 = (bf16[2,4,160,640]{3,2,1,0:T(8,128)(2,1)S(1)}, bf16[2,4,160,640]{3,2,1,0:T(8,128)(2,1)S(1)}, u32[]{:S(2)}, u32[]{:S(2)}) collective-permute-start(bf16[2,4,160,640]{3,2,1,0:T(8,128)(2,1)S(1)} %pad_maximum_fusion.1.refs_0_), channel_id=1, source_target_pairs={{0,4},{1,3},{2,6},{3,1},{4,0},{5,7},{6,2},{7,5},{8,12},{9,11},{10,... | collective-permute-start | bytes 4915208 | tf_op jit(solution)/shard_map/ppermute | solution.py:549
  128.5 19.6 %collective-permute-start.24 = (bf16[2,4,160,640]{3,2,1,0:T(8,128)(2,1)S(1)}, bf16[2,4,160,640]{3,2,1,0:T(8,128)(2,1)S(1)}, u32[]{:S(2)}, u32[]{:S(2)}) collective-permute-start(bf16[2,4,160,640]{3,2,1,0:T(8,128)(2,1)S(1)} %pad_maximum_fusion.1.refs_0_), channel_id=1, source_target_pairs={{0,1},{1,0},{2,3},{3,2},{4,5},{5,4},{6,7},{7,6},{8,9},{9,8},{10,11... | collective-permute-start | bytes 4915208 | tf_op jit(solution)/shard_map/ppermute | solution.py:543
  166.5 12.4 %collective-permute-start.27 = (bf16[2,2,2,80,640]{4,3,2,1,0:T(8,128)(2,1)S(1)}, bf16[2,2,2,80,640]{4,3,2,1,0:T(8,128)(2,1)S(1)}, u32[]{:S(2)}, u32[]{:S(2)}) collective-permute-start(bf16[2,2,2,80,640]{4,3,2,1,0:T(8,128)(2,1)S(1)} %fusion.6), channel_id=1, source_target_pairs={{0,4},{1,3},{2,6},{3,1},{4,0},{5,7},{6,2},{7,5},{8,12},{9,11},{10,... | collective-permute-start | bytes 2457608 | tf_op jit(solution)/shard_map/ppermute | solution.py:549
  182.8 16.3 %collective-permute-start.29 = (bf16[2,2,2,80,640]{4,3,2,1,0:T(8,128)(2,1)S(1)}, bf16[2,2,2,80,640]{4,3,2,1,0:T(8,128)(2,1)S(1)}, u32[]{:S(2)}, u32[]{:S(2)}) collective-permute-start(bf16[2,2,2,80,640]{4,3,2,1,0:T(8,128)(2,1)S(1)} %fusion.5), channel_id=1, source_target_pairs={{0,4},{1,3},{2,6},{3,1},{4,0},{5,7},{6,2},{7,5},{8,12},{9,11},{10,... | collective-permute-start | bytes 2457608 | tf_op jit(solution)/shard_map/ppermute | solution.py:549
  184.4 12.4 %collective-permute-start.30 = (bf16[2,2,80,640]{3,2,1,0:T(8,128)(2,1)S(1)}, bf16[2,2,80,640]{3,2,1,0:T(8,128)(2,1)S(1)}, u32[]{:S(2)}, u32[]{:S(2)}) collective-permute-start(bf16[2,2,80,640]{3,2,1,0:T(8,128)(2,1)S(1)} %fusion.15), channel_id=1, source_target_pairs={{0,2},{1,5},{2,0},{3,7},{4,6},{5,1},{6,4},{7,3},{8,10},{9,13},{10,... | collective-permute-start | bytes 1228808 | tf_op jit(solution)/shard_map/ppermute | solution.py:549
  214.2 17.6 %collective-permute-start.34 = (bf16[2,2,2,80,640]{4,3,2,1,0:T(8,128)(2,1)S(1)}, bf16[2,2,2,80,640]{4,3,2,1,0:T(8,128)(2,1)S(1)}, u32[]{:S(2)}, u32[]{:S(2)}) collective-permute-start(bf16[2,2,2,80,640]{4,3,2,1,0:T(8,128)(2,1)S(1)} %fusion.4), channel_id=1, source_target_pairs={{0,4},{1,3},{2,6},{3,1},{4,0},{5,7},{6,2},{7,5},{8,12},{9,11},{10,... | collective-permute-start | bytes 2457608 | tf_op jit(solution)/shard_map/ppermute | solution.py:549
  215.8 16.0 %collective-permute-start.35 = (bf16[2,80,640]{2,1,0:T(8,128)(2,1)S(1)}, bf16[2,80,640]{2,1,0:T(8,128)(2,1)S(1)}, u32[]{:S(2)}, u32[]{:S(2)}) collective-permute-start(bf16[2,80,640]{2,1,0:T(8,128)(2,1)S(1)} %fusion.24), channel_id=1, source_target_pairs={{0,8},{1,17},{2,10},{3,19},{4,12},{5,21},{6,14},{7,23},{8,0},{9,25... | collective-permute-start | bytes 614408 | tf_op jit(solution)/shard_map/ppermute | solution.py:549
  217.9 13.9 %collective-permute-start.36 = (bf16[80,640]{1,0:T(8,128)(2,1)S(1)}, bf16[80,640]{1,0:T(8,128)(2,1)S(1)}, u32[]{:S(2)}, u32[]{:S(2)}) collective-permute-start(bf16[80,640]{1,0:T(8,128)(2,1)S(1)} %fusion.35), channel_id=1, source_target_pairs={{0,16},{1,9},{2,18},{3,11},{4,20},{5,13},{6,22},{7,15},{8,24},{9,1... | collective-permute-start | bytes 307208 | tf_op jit(solution)/shard_map/ppermute | solution.py:549
  240.9 21.2 %collective-permute-start.40 = (bf16[2,2,2,160,640]{4,3,2,1,0:T(8,128)(2,1)S(1)}, bf16[2,2,2,160,640]{4,3,2,1,0:T(8,128)(2,1)S(1)}, u32[]{:S(2)}, u32[]{:S(2)}) collective-permute-start(bf16[2,2,2,160,640]{4,3,2,1,0:T(8,128)(2,1)S(1)} %fusion), channel_id=1, source_target_pairs={{0,4},{1,3},{2,6},{3,1},{4,0},{5,7},{6,2},{7,5},{8,12},{9,11},{10,... | collective-permute-start | bytes 4915208 | tf_op jit(solution)/shard_map/ppermute | solution.py:549
  242.0 18.1 %collective-permute-start.41 = (bf16[2,80,640]{2,1,0:T(8,128)(2,1)S(1)}, bf16[2,80,640]{2,1,0:T(8,128)(2,1)S(1)}, u32[]{:S(2)}, u32[]{:S(2)}) collective-permute-start(bf16[2,80,640]{2,1,0:T(8,128)(2,1)S(1)} %fusion.25), channel_id=1, source_target_pairs={{0,8},{1,17},{2,10},{3,19},{4,12},{5,21},{6,14},{7,23},{8,0},{9,25... | collective-permute-start | bytes 614408 | tf_op jit(solution)/shard_map/ppermute | solution.py:549
  262.9 15.6 %collective-permute-start.42 = (bf16[2,2,160,640]{3,2,1,0:T(8,128)(2,1)S(1)}, bf16[2,2,160,640]{3,2,1,0:T(8,128)(2,1)S(1)}, u32[]{:S(2)}, u32[]{:S(2)}) collective-permute-start(bf16[2,2,160,640]{3,2,1,0:T(8,128)(2,1)S(1)} %fusion.3), channel_id=1, source_target_pairs={{0,2},{1,5},{2,0},{3,7},{4,6},{5,1},{6,4},{7,3},{8,10},{9,13},{10,... | collective-permute-start | bytes 2457608 | tf_op jit(solution)/shard_map/ppermute | solution.py:549
  263.8 14.6 %collective-permute-start.43 = (bf16[80,640]{1,0:T(8,128)(2,1)S(1)}, bf16[80,640]{1,0:T(8,128)(2,1)S(1)}, u32[]{:S(2)}, u32[]{:S(2)}) collective-permute-start(bf16[80,640]{1,0:T(8,128)(2,1)S(1)} %fusion.37), channel_id=1, source_target_pairs={{0,16},{1,9},{2,18},{3,11},{4,20},{5,13},{6,22},{7,15},{8,24},{9,1... | collective-permute-start | bytes 307208 | tf_op jit(solution)/shard_map/ppermute | solution.py:549
  281.1 12.1 %collective-permute-start.46 = (bf16[2,160,640]{2,1,0:T(8,128)(2,1)}, bf16[2,160,640]{2,1,0:T(8,128)(2,1)}, u32[]{:S(2)}, u32[]{:S(2)}) collective-permute-start(bf16[2,160,640]{2,1,0:T(8,128)(2,1)} %fusion.16), channel_id=1, source_target_pairs={{0,8},{1,17},{2,10},{3,19},{4,12},{5,21},{6,14},{7,23},{8,0},{9,25... | collective-permute-start | bytes 1228808 | tf_op jit(solution)/shard_map/ppermute | solution.py:549
  288.3 12.4 %collective-permute-start.45 = (bf16[2,2,2,80,640]{4,3,2,1,0:T(8,128)(2,1)S(1)}, bf16[2,2,2,80,640]{4,3,2,1,0:T(8,128)(2,1)S(1)}, u32[]{:S(2)}, u32[]{:S(2)}) collective-permute-start(bf16[2,2,2,80,640]{4,3,2,1,0:T(8,128)(2,1)S(1)} %fusion.1), channel_id=1, source_target_pairs={{0,4},{1,3},{2,6},{3,1},{4,0},{5,7},{6,2},{7,5},{8,12},{9,11},{10,... | collective-permute-start | bytes 2457608 | tf_op jit(solution)/shard_map/ppermute | solution.py:549
  (80 other events, 544.4 us)

commit v6 on v5

--- a/solution.py
+++ b/solution.py
@@ -594,7 +594,7 @@
 
 def fetch_plain(w_qkv, w_out, w_up, w_down, gains, biases):
     def whole(value, rows):
-        return lax.all_gather(value, AXES, axis=0, tiled=True).reshape(rows, -1)
+        return lax.all_gather(value[None], AXES, axis=1, tiled=True).reshape(rows, -1)
 
     weights = {}
     for l in range(LAYERS):
@@ -700,11 +700,15 @@
         for i, key in enumerate(keys):
             rows = slice(i * PIECE, (i + 1) * PIECE)
             matrices[key] = whole_grad(core, rest, rows, key[0] == "down").astype(f32)
-    outs = []
+    devices = lax.axis_size(AXES)
+    parts = []
     for name, begin, end in (("attn", 0, 3 * D), ("attn", 3 * D, FF), ("up", 0, FF), ("down", 0, D)):
-        cut = jnp.stack([matrices[name, l][:, begin:end].reshape(-1) for l in range(LAYERS)])
-        outs.append(lax.psum_scatter(cut, AXES, scatter_dimension=1, tiled=True))
-    outs += [lax.psum_scatter(v, AXES, scatter_dimension=0, tiled=True) for v in layer_grads(sums)]
+        parts += [matrices[name, l][:, begin:end].reshape(devices, -1) for l in range(LAYERS)]
+    parts += [v.reshape(devices, -1) for v in layer_grads(sums)]
+    summed = lax.psum_scatter(jnp.concatenate(parts, 1), AXES, scatter_dimension=0, tiled=True)[0]
+    ends = np.cumsum([p.shape[1] for p in parts])
+    cut = [summed[end - p.shape[1] : end] for end, p in zip(ends, parts, strict=True)]
+    outs = [jnp.stack(cut[i : i + LAYERS]) for i in range(0, 4 * LAYERS, LAYERS)] + cut[4 * LAYERS :]
     return (output, grad, *outs)
 
 

time: 347 us -> 347 us (level)
  no operation moved by 1% of the time
where the time goes in v6:
time: 347 us; the launch traced here: 340 us
  Pallas kernels  134 us (39%)
  waiting for transfers between devices  96.7 us (28%)
  starting transfers between devices  62.5 us (18%)
  local copies, waits for them, and re-layouts  22.5 us (6%)
  other arithmetic  21.7 us (6%)
    pallas_call x24, Pallas kernels, call(): pl.pallas_call(kernel, out_shape=[jax.ShapeDtypeStruct(s, t) for s, t in...  134 us
    ppermute x39, waiting for transfers between devices, step(): return lax.ppermute(value, AXES, pairs)  71.9 us
    ppermute x39, starting transfers between devices, step(): return lax.ppermute(value, AXES, pairs)  55.4 us
    ppermute x14, waiting for transfers between devices, mate(): return lax.ppermute(value, 'narrow', [(0, 1), (1, 0)])  14.3 us
    unnamed x104, local copies, waits for them, and re-layouts  11.1 us
    ppermute x9, waiting for transfers between devices, regroup(): lax.ppermute(mine[k], AXES, [(i, i ^ k) for i in range(32)])  10.5 us
  transfers between devices with their start and end apart: 62, of which 31 were waited for; matrix products, arithmetic and copies ran while one was open for 6% of the time, Pallas kernels for 36%

profile of v6, /device:TPU:0, one launch (start us, length us, event | category | flops | bytes accessed | tf_op | source)
XLA Modules:
  0.0 340.5 jit_solution(14728396927005066041)
XLA Ops:
  3.8 4.1 %collective-permute-start = (bf16[96,640]{1,0:T(8,128)(2,1)S(1)}, bf16[96,640]{1,0:T(8,128)(2,1)S(1)}, u32[]{:S(2)}, u32[]{:S(2)}) collective-permute-start(bf16[96,640]{1,0:T(8,128)(2,1)S(1)} %fusion.34), channel_id=1, source_target_pairs={{0,16},{1,9},{2,18},{3,11},{4,20},{5,13},{6,22},{7,15},{8,24},{9,1... | collective-permute-start | bytes 368648 | tf_op jit(solution)/shard_map/ppermute | solution.py:549
  26.8 7.6 %collective-permute-done.6 = bf16[240,640]{1,0:T(8,128)(2,1)S(1)} collective-permute-done((bf16[240,640]{1,0:T(8,128)(2,1)S(1)}, bf16[240,640]{1,0:T(8,128)(2,1)S(1)}, u32[]{:S(2)}, u32[]{:S(2)}) %collective-permute-start.6) | collective-permute-done | bytes 307232 | tf_op jit(solution)/shard_map/ppermute | solution.py:549
  42.9 4.9 %collective-permute-done.9 = bf16[2,80,640]{2,1,0:T(8,128)(2,1)S(1)} collective-permute-done((bf16[2,80,640]{2,1,0:T(8,128)(2,1)}, bf16[2,80,640]{2,1,0:T(8,128)(2,1)S(1)}, u32[]{:S(2)}, u32[]{:S(2)}) %collective-permute-start.9) | collective-permute-done | bytes 204832 | tf_op jit(solution)/shard_map/ppermute | solution.py:549
  55.0 5.2 %collective-permute-done.15 = bf16[2,160,640]{2,1,0:T(8,128)(2,1)S(1)} collective-permute-done((bf16[2,160,640]{2,1,0:T(8,128)(2,1)S(1)}, bf16[2,160,640]{2,1,0:T(8,128)(2,1)S(1)}, u32[]{:S(2)}, u32[]{:S(2)}) %collective-permute-start.15) | collective-permute-done | bytes 409632 | tf_op jit(solution)/shard_map/ppermute | solution.py:549
  69.9 12.9 %collective-permute-done.16 = bf16[4,160,640]{2,1,0:T(8,128)(2,1)} collective-permute-done((bf16[4,160,640]{2,1,0:T(8,128)(2,1)}, bf16[4,160,640]{2,1,0:T(8,128)(2,1)}, u32[]{:S(2)}, u32[]{:S(2)}) %collective-permute-start.16) | collective-permute-done | bytes 819232 | tf_op jit(solution)/shard_map/ppermute | solution.py:549
  89.8 14.2 %attn_fwd.2 = (bf16[640,512]{1,0:T(8,128)(2,1)S(1)}, bf16[640,512]{1,0:T(8,128)(2,1)S(1)}, bf16[512,1280]{1,0:T(8,128)(2,1)S(1)}, bf16[640,512]{1,0:T(8,128)(2,1...) custom-call(s32[5]{0:T(128)S(1)} %stack.175.coords, ...), custom_call_target="tpu_custom_call" | custom-call | flops 2348810240 | bytes 13983764 | tf_op jit(solution)/shard_map/attn_fwd/pallas_call | solution.py:442
  104.0 5.4 %collective-permute-done.19.refs_3_.refs_2_ = bf16[2,4,160,640]{3,2,1,0:T(8,128)(2,1)S(1)} collective-permute-done((bf16[2,4,160,640]{3,2,1,0:T(8,128)(2,1)S(1)}, bf16[2,4,160,640]{3,2,1,0:T(8,128)(2,1)S(1)}, u32[]{:S(2)}, u32[]{:S(2)}) %collective-permute-start.19) | collective-permute-done | bytes 1638432 | tf_op jit(solution)/shard_map/ppermute | solution.py:549
  109.4 3.5 %collective-permute-done.21.refs_4_.refs_3_ = bf16[2,4,160,640]{3,2,1,0:T(8,128)(2,1)S(1)} collective-permute-done((bf16[2,4,160,640]{3,2,1,0:T(8,128)(2,1)S(1)}, bf16[2,4,160,640]{3,2,1,0:T(8,128)(2,1)S(1)}, u32[]{:S(2)}, u32[]{:S(2)}) %collective-permute-start.21) | collective-permute-done | bytes 1638432 | tf_op jit(solution)/shard_map/ppermute | solution.py:543
  114.3 10.9 %ffn_fwd.2 = (f32[512,640]{1,0:T(8,128)S(1)}, bf16[2560,512]{1,0:T(8,128)(2,1)S(1)}, bf16[512,2560]{1,0:T(8,128)(2,1)S(1)}, bf16[4,2,80,2560]{3,2,1,0:T(8,128)(2,1)S(1)}) custom-call(s32[5]{0:T(128)S(1)} %stack.175.coords, f32[512,640]{1,0:T(8,128)S(1)} %get-tuple-element.351.m_ref, bf16[512,640]{1,0:T(8,128)(2,1)S(1)} %get-tuple-element.352.b_ref, ...), custom_call_target="tpu_custom_call" | custom-call | flops 3355443200 | bytes 21667860 | tf_op jit(solution)/shard_map/ffn_fwd/pallas_call | solution.py:442
  128.5 14.0 %attn_fwd.3 = (bf16[640,512]{1,0:T(8,128)(2,1)S(1)}, bf16[640,512]{1,0:T(8,128)(2,1)S(1)}, bf16[512,1280]{1,0:T(8,128)(2,1)S(1)}, bf16[640,512]{1,0:T(8,128)(2,1...) custom-call(s32[5]{0:T(128)S(1)} %stack.175.coords, ...), custom_call_target="tpu_custom_call" | custom-call | flops 2348810240 | bytes 17915924 | tf_op jit(solution)/shard_map/attn_fwd/pallas_call | solution.py:442
  143.3 4.8 %collective-permute-done.23.refs_2_ = bf16[2,4,160,640]{3,2,1,0:T(8,128)(2,1)S(1)} collective-permute-done((bf16[2,4,160,640]{3,2,1,0:T(8,128)(2,1)S(1)}, bf16[2,4,160,640]{3,2,1,0:T(8,128)(2,1)S(1)}, u32[]{:S(2)}, u32[]{:S(2)}) %collective-permute-start.23) | collective-permute-done | bytes 1638432 | tf_op jit(solution)/shard_map/ppermute | solution.py:549
  151.6 9.4 %ffn_fwd.3 = (bf16[512,2560]{1,0:T(8,128)(2,1)S(1)}, bf16[2560,512]{1,0:T(8,128)(2,1)S(1)}, bf16[512,2560]{1,0:T(8,128)(2,1)S(1)}, bf16[4,2,80,2560]{3,2,1,0:T(8...) custom-call(s32[5]{0:T(128)S(1)} %stack.175.coords, f32[512,640]{1,0:T(8,128)S(1)} %get-tuple-element.369.m_ref, ...), custom_call_target="tpu_custom_call" | custom-call | flops 3355443200 | bytes 22978580 | tf_op jit(solution)/shard_map/ffn_fwd/pallas_call | solution.py:442
  168.1 7.8 %ffn_bwd.2 = (bf16[512,640]{1,0:T(8,128)(2,1)}, bf16[512,2560]{1,0:T(8,128)(2,1)S(1)}, f32[512,640]{1,0:T(8,128)S(1)}, bf16[512,640]{1,0:T(8,128)(2,1)S(1)}, f32[16,640]{1,0:T(8,128)S(1)}) custom-call(s32[5]{0:T(128)S(1)} %stack.175.coords, bf16[512,640]{1,0:T(8,128)(2,1)S(1)} %copy-done.4, bf16[512,2560]{1,0:T(8,128)(2,1)S(1)} %copy-done.15, ...), custom_call_target="tpu_custom_call" | custom-call | flops 3355443200 | bytes 16465940 | tf_op jit(solution)/shard_map/ffn_bwd/pallas_call | solution.py:442
  185.0 9.4 %attn_bwd.4.refs_2_.early_ref = bf16[3,384,512]{2,1,0:T(8,128)(2,1)S(1)} custom-call(s32[5]{0:T(128)S(1)} %stack.175.coords, bf16[512,640]{1,0:T(8,128)(2,1)S(1)} %get-tuple-element.427.gmb_ref, bf16[640,512]{1,0:T(8,128)(2,1)S(1)} %copy-done.19, bf16[512,1280]{1,0:T(8,128)(2,1)S(1)} %copy-done.17, bf16[640,512]{1,0:T(8,128)(2,1)S(1)} %get-tuple-element.410.ot_ref.refs_1_, ...), custom_call_target="tpu_custom_call" | custom-call | flops 1258291200 | bytes 7847956 | tf_op jit(solution)/shard_map/attn_bwd/pallas_call | solution.py:442
  200.7 6.6 %attn_bwd.5 = (bf16[3,256,512]{2,1,0:T(8,128)(2,1)S(1)}, bf16[640,512]{1,0:T(8,128)(2,1)S(1)}) custom-call(s32[5]{0:T(128)S(1)} %stack.175.coords, bf16[512,640]{1,0:T(8,128)(2,1)S(1)} %get-tuple-element.427.gmb_ref, bf16[640,512]{1,0:T(8,128)(2,1)S(1)} %copy-done.19, bf16[512,1280]{1,0:T(8,128)(2,1)S(1)} %copy-done.17, ...), custom_call_target="tpu_custom_call" | custom-call | flops 838860800 | bytes 8110100 | tf_op jit(solution)/shard_map/attn_bwd/pallas_call | solution.py:442
  218.0 3.7 %attn_after.2 = (f32[512,640]{1,0:T(8,128)S(1)}, f32[16,640]{1,0:T(8,128)S(1)}) custom-call(bf16[3,384,512]{2,1,0:T(8,128)(2,1)S(1)} %attn_bwd.4.refs_2_.early_ref, bf16[3,256,512]{2,1,0:T(8,128)(2,1)S(1)} %get-tuple-element.457.refs_3_.late_ref, f32[512,640]{1,0:T(8,128)S(1)} %get-tuple-element.458.gm_ref, f32[512,640]{1,0:T(8,128)S(1)} %get-tuple-element.459.x_ref, ...), custom_call_target="tpu_custom_call" | custom-call | flops 1258291200 | bytes 9256960 | tf_op jit(solution)/shard_map/attn_after/pallas_call | solution.py:442
  221.7 6.7 %ffn_bwd.3 = (bf16[512,640]{1,0:T(8,128)(2,1)S(1)}, bf16[512,2560]{1,0:T(8,128)(2,1)S(1)}, f32[512,640]{1,0:T(8,128)S(1)}, bf16[512,640]{1,0:T(8,128)(2,1)S(1)}, f32[16,640]{1,0:T(8,128)S(1)}) custom-call(s32[5]{0:T(128)S(1)} %stack.175.coords, f32[512,640]{1,0:T(8,128)S(1)} %get-tuple-element.460.g_ref, bf16[512,2560]{1,0:T(8,128)(2,1)S(1)} %copy-done.13, ...), custom_call_target="tpu_custom_call" | custom-call | flops 3355443200 | bytes 17121300 | tf_op jit(solution)/shard_map/ffn_bwd/pallas_call | solution.py:442
  235.9 3.5 %grads.17 = (bf16[2,2,2,160,640]{4,3,2,1,0:T(8,128)(2,1)S(1)}, bf16[2,2,160,640]{3,2,1,0:T(8,128)(2,1)S(1)}, bf16[2,2,160,640]{3,2,1,0:T(8,128)(2,1)S(1)}) custom-call(s32[5]{0:T(128)S(1)} %stack.175.coords, bf16[2560,512]{1,0:T(8,128)(2,1)S(1)} %get-tuple-element.455.refs_0_, bf16[512,640]{1,0:T(8,128)(2,1)S(1)} %get-tuple-element.480.refs_1_, ...), custom_call_target="tpu_custom_call" | custom-call | flops 1677721600 | bytes 9830420 | tf_op jit(solution)/shard_map/grads/pallas_call | solution.py:442
  244.1 6.6 %attn_bwd.7 = (bf16[3,256,512]{2,1,0:T(8,128)(2,1)S(1)}, bf16[640,512]{1,0:T(8,128)(2,1)S(1)}) custom-call(s32[5]{0:T(128)S(1)} %stack.175.coords, bf16[512,640]{1,0:T(8,128)(2,1)S(1)} %get-tuple-element.495.gmb_ref, bf16[640,512]{1,0:T(8,128)(2,1)S(1)} %copy-done.23, bf16[512,1280]{1,0:T(8,128)(2,1)S(1)} %copy-done.21, ...), custom_call_target="tpu_custom_call" | custom-call | flops 838860800 | bytes 8110100 | tf_op jit(solution)/shard_map/attn_bwd/pallas_call | solution.py:442
  250.7 9.5 %attn_bwd.6.refs_2_.early_ref = bf16[3,384,512]{2,1,0:T(8,128)(2,1)S(1)} custom-call(s32[5]{0:T(128)S(1)} %stack.175.coords, bf16[512,640]{1,0:T(8,128)(2,1)S(1)} %get-tuple-element.495.gmb_ref, bf16[640,512]{1,0:T(8,128)(2,1)S(1)} %copy-done.23, bf16[512,1280]{1,0:T(8,128)(2,1)S(1)} %copy-done.21, bf16[640,512]{1,0:T(8,128)(2,1)S(1)} %get-tuple-element.498.ot_ref.refs_1_, ...), custom_call_target="tpu_custom_call" | custom-call | flops 1258291200 | bytes 7847956 | tf_op jit(solution)/shard_map/attn_bwd/pallas_call | solution.py:442
  266.5 3.6 %ffn_out.1 = bf16[512,640]{1,0:T(8,128)(2,1)} custom-call(s32[5]{0:T(128)S(1)} %stack.175.coords, f32[512,640]{1,0:T(8,128)S(1)} %get-tuple-element.369.m_ref, bf16[512,2560]{1,0:T(8,128)(2,1)S(1)} %get-tuple-element.526.z_ref, f32[16,640]{1,0:T(8,128)S(1)} %get-tuple-element.670.vec_ref, bf16[2560,640]{1,0:T(8,128)(2,1)S(1)} %bitcast.342), custom_call_target="tpu_custom_call" | custom-call | flops 1677721600 | bytes 7905300 | tf_op jit(solution)/shard_map/ffn_out/pallas_call | solution.py:442
  270.1 4.6 %attn_after.3 = (bf16[512,640]{1,0:T(8,128)(2,1)}, f32[16,640]{1,0:T(8,128)S(1)}) custom-call(bf16[3,384,512]{2,1,0:T(8,128)(2,1)S(1)} %attn_bwd.6.refs_2_.early_ref, bf16[3,256,512]{2,1,0:T(8,128)(2,1)S(1)} %get-tuple-element.536.refs_3_.late_ref, f32[512,640]{1,0:T(8,128)S(1)} %get-tuple-element.519.gm_ref, bf16[512,640]{1,0:T(8,128)(2,1)S(1)} %copy-done.5, ...), custom_call_target="tpu_custom_call" | custom-call | flops 1258291200 | bytes 7946240 | tf_op jit(solution)/shard_map/attn_after/pallas_call | solution.py:442
  274.7 3.7 %grads.18 = bf16[2,2,2,2,80,640]{5,4,3,2,1,0:T(8,128)(2,1)} custom-call(s32[5]{0:T(128)S(1)} %stack.175.coords, bf16[640,512]{1,0:T(8,128)(2,1)S(1)} %get-tuple-element.515.refs_0_, bf16[640,512]{1,0:T(8,128)(2,1)S(1)} %get-tuple-element.498.ot_ref.refs_1_, bf16[3,384,512]{2,1,0:T(8,128)(2,1)S(1)} %attn_bwd.6.refs_2_.early_ref, ...), custom_call_target="tpu_custom_call" | custom-call | flops 838860800 | bytes 5570580 | tf_op jit(solution)/shard_map/grads/pallas_call | solution.py:442
  293.2 7.5 %collective-permute-done.45 = bf16[2,2,2,80,640]{4,3,2,1,0:T(8,128)(2,1)S(1)} collective-permute-done((bf16[2,2,2,80,640]{4,3,2,1,0:T(8,128)(2,1)S(1)}, bf16[2,2,2,80,640]{4,3,2,1,0:T(8,128)(2,1)S(1)}, u32[]{:S(2)}, u32[]{:S(2)}) %collective-permute-start.45) | collective-permute-done | bytes 819232 | tf_op jit(solution)/shard_map/ppermute | solution.py:549
  (373 shorter events, 167.2 us)
Async XLA Ops:
  34.8 14.2 %collective-permute-start.7 = (bf16[2,4,96,640]{3,2,1,0:T(8,128)(2,1)S(1)}, bf16[2,4,96,640]{3,2,1,0:T(8,128)(2,1)S(1)}, u32[]{:S(2)}, u32[]{:S(2)}) collective-permute-start(bf16[2,4,96,640]{3,2,1,0:T(8,128)(2,1)S(1)} %pad_maximum_fusion.2.refs_0_), channel_id=1, source_target_pairs={{0,4},{1,3},{2,6},{3,1},{4,0},{5,7},{6,2},{7,5},{8,12},{9,11},{10,... | collective-permute-start | bytes 2949128 | tf_op jit(solution)/shard_map/ppermute | solution.py:549
  36.3 12.6 %collective-permute-start.8 = (bf16[2,4,96,640]{3,2,1,0:T(8,128)(2,1)S(1)}, bf16[2,4,96,640]{3,2,1,0:T(8,128)(2,1)S(1)}, u32[]{:S(2)}, u32[]{:S(2)}) collective-permute-start(bf16[2,4,96,640]{3,2,1,0:T(8,128)(2,1)S(1)} %pad_maximum_fusion.2.refs_0_), channel_id=1, source_target_pairs={{0,1},{1,0},{2,3},{3,2},{4,5},{5,4},{6,7},{7,6},{8,9},{9,8},{10,11... | collective-permute-start | bytes 2949128 | tf_op jit(solution)/shard_map/ppermute | solution.py:543
  40.9 11.6 %collective-permute-start.12 = (bf16[160,640]{1,0:T(8,128)(2,1)S(1)}, bf16[160,640]{1,0:T(8,128)(2,1)S(1)}, u32[]{:S(2)}, u32[]{:S(2)}) collective-permute-start(bf16[160,640]{1,0:T(8,128)(2,1)S(1)} %pad_maximum_fusion.19), channel_id=1, source_target_pairs={{0,16},{1,9},{2,18},{3,11},{4,20},{5,13},{6,22},{7,15},{8,24},{9,1... | collective-permute-start | bytes 614408 | tf_op jit(solution)/shard_map/ppermute | solution.py:549
  61.5 21.4 %collective-permute-start.16 = (bf16[4,160,640]{2,1,0:T(8,128)(2,1)}, bf16[4,160,640]{2,1,0:T(8,128)(2,1)}, u32[]{:S(2)}, u32[]{:S(2)}) collective-permute-start(bf16[4,160,640]{2,1,0:T(8,128)(2,1)} %pad_maximum_fusion.4), channel_id=1, source_target_pairs={{0,2},{1,5},{2,0},{3,7},{4,6},{5,1},{6,4},{7,3},{8,10},{9,13},{10,... | collective-permute-start | bytes 2457608 | tf_op jit(solution)/shard_map/ppermute | solution.py:549
  64.6 21.1 %collective-permute-start.13 = (bf16[2,4,80,640]{3,2,1,0:T(8,128)(2,1)}, bf16[2,4,80,640]{3,2,1,0:T(8,128)(2,1)}, u32[]{:S(2)}, u32[]{:S(2)}) collective-permute-start(bf16[2,4,80,640]{3,2,1,0:T(8,128)(2,1)} %pad_maximum_fusion.3.refs_0_), channel_id=1, source_target_pairs={{0,4},{1,3},{2,6},{3,1},{4,0},{5,7},{6,2},{7,5},{8,12},{9,11},{10,... | collective-permute-start | bytes 2457608 | tf_op jit(solution)/shard_map/ppermute | solution.py:549
  66.1 19.6 %collective-permute-start.14 = (bf16[2,4,80,640]{3,2,1,0:T(8,128)(2,1)}, bf16[2,4,80,640]{3,2,1,0:T(8,128)(2,1)}, u32[]{:S(2)}, u32[]{:S(2)}) collective-permute-start(bf16[2,4,80,640]{3,2,1,0:T(8,128)(2,1)} %pad_maximum_fusion.3.refs_0_), channel_id=1, source_target_pairs={{0,1},{1,0},{2,3},{3,2},{4,5},{5,4},{6,7},{7,6},{8,9},{9,8},{10,11... | collective-permute-start | bytes 2457608 | tf_op jit(solution)/shard_map/ppermute | solution.py:543
  69.8 14.8 %collective-permute-start.17 = (bf16[2,160,640]{2,1,0:T(8,128)(2,1)}, bf16[2,160,640]{2,1,0:T(8,128)(2,1)S(1)}, u32[]{:S(2)}, u32[]{:S(2)}) collective-permute-start(bf16[2,160,640]{2,1,0:T(8,128)(2,1)} %pad_maximum_fusion.13), channel_id=1, source_target_pairs={{0,8},{1,17},{2,10},{3,19},{4,12},{5,21},{6,14},{7,23},{8,0},{9,25... | collective-permute-start | bytes 1228808 | tf_op jit(solution)/shard_map/ppermute | solution.py:549
  88.2 21.1 %collective-permute-start.19 = (bf16[2,4,160,640]{3,2,1,0:T(8,128)(2,1)S(1)}, bf16[2,4,160,640]{3,2,1,0:T(8,128)(2,1)S(1)}, u32[]{:S(2)}, u32[]{:S(2)}) collective-permute-start(bf16[2,4,160,640]{3,2,1,0:T(8,128)(2,1)S(1)} %pad_maximum_fusion.refs_1_.refs_0_), channel_id=1, source_target_pairs={{0,4},{1,3},{2,6},{3,1},{4,0},{5,7},{6,2},{7,5},{8,12},{9,11},{10,... | collective-permute-start | bytes 4915208 | tf_op jit(solution)/shard_map/ppermute | solution.py:549
  89.8 19.6 %collective-permute-start.20 = (bf16[2,4,160,640]{3,2,1,0:T(8,128)(2,1)S(1)}, bf16[2,4,160,640]{3,2,1,0:T(8,128)(2,1)S(1)}, u32[]{:S(2)}, u32[]{:S(2)}) collective-permute-start(bf16[2,4,160,640]{3,2,1,0:T(8,128)(2,1)S(1)} %pad_maximum_fusion.refs_1_.refs_0_), channel_id=1, source_target_pairs={{0,1},{1,0},{2,3},{3,2},{4,5},{5,4},{6,7},{7,6},{8,9},{9,8},{10,11... | collective-permute-start | bytes 4915208 | tf_op jit(solution)/shard_map/ppermute | solution.py:543
  112.9 12.4 %collective-permute-start.22 = (bf16[4,160,640]{2,1,0:T(8,128)(2,1)S(1)}, bf16[4,160,640]{2,1,0:T(8,128)(2,1)S(1)}, u32[]{:S(2)}, u32[]{:S(2)}) collective-permute-start(bf16[4,160,640]{2,1,0:T(8,128)(2,1)S(1)} %pad_maximum_fusion.5), channel_id=1, source_target_pairs={{0,2},{1,5},{2,0},{3,7},{4,6},{5,1},{6,4},{7,3},{8,10},{9,13},{10,... | collective-permute-start | bytes 2457608 | tf_op jit(solution)/shard_map/ppermute | solution.py:549
  126.9 21.2 %collective-permute-start.23 = (bf16[2,4,160,640]{3,2,1,0:T(8,128)(2,1)S(1)}, bf16[2,4,160,640]{3,2,1,0:T(8,128)(2,1)S(1)}, u32[]{:S(2)}, u32[]{:S(2)}) collective-permute-start(bf16[2,4,160,640]{3,2,1,0:T(8,128)(2,1)S(1)} %pad_maximum_fusion.1.refs_0_), channel_id=1, source_target_pairs={{0,4},{1,3},{2,6},{3,1},{4,0},{5,7},{6,2},{7,5},{8,12},{9,11},{10,... | collective-permute-start | bytes 4915208 | tf_op jit(solution)/shard_map/ppermute | solution.py:549
  128.5 19.6 %collective-permute-start.24 = (bf16[2,4,160,640]{3,2,1,0:T(8,128)(2,1)S(1)}, bf16[2,4,160,640]{3,2,1,0:T(8,128)(2,1)S(1)}, u32[]{:S(2)}, u32[]{:S(2)}) collective-permute-start(bf16[2,4,160,640]{3,2,1,0:T(8,128)(2,1)S(1)} %pad_maximum_fusion.1.refs_0_), channel_id=1, source_target_pairs={{0,1},{1,0},{2,3},{3,2},{4,5},{5,4},{6,7},{7,6},{8,9},{9,8},{10,11... | collective-permute-start | bytes 4915208 | tf_op jit(solution)/shard_map/ppermute | solution.py:543
  166.5 12.4 %collective-permute-start.27 = (bf16[2,2,2,80,640]{4,3,2,1,0:T(8,128)(2,1)S(1)}, bf16[2,2,2,80,640]{4,3,2,1,0:T(8,128)(2,1)S(1)}, u32[]{:S(2)}, u32[]{:S(2)}) collective-permute-start(bf16[2,2,2,80,640]{4,3,2,1,0:T(8,128)(2,1)S(1)} %fusion.6), channel_id=1, source_target_pairs={{0,4},{1,3},{2,6},{3,1},{4,0},{5,7},{6,2},{7,5},{8,12},{9,11},{10,... | collective-permute-start | bytes 2457608 | tf_op jit(solution)/shard_map/ppermute | solution.py:549
  182.8 16.3 %collective-permute-start.29 = (bf16[2,2,2,80,640]{4,3,2,1,0:T(8,128)(2,1)S(1)}, bf16[2,2,2,80,640]{4,3,2,1,0:T(8,128)(2,1)S(1)}, u32[]{:S(2)}, u32[]{:S(2)}) collective-permute-start(bf16[2,2,2,80,640]{4,3,2,1,0:T(8,128)(2,1)S(1)} %fusion.5), channel_id=1, source_target_pairs={{0,4},{1,3},{2,6},{3,1},{4,0},{5,7},{6,2},{7,5},{8,12},{9,11},{10,... | collective-permute-start | bytes 2457608 | tf_op jit(solution)/shard_map/ppermute | solution.py:549
  184.4 12.4 %collective-permute-start.30 = (bf16[2,2,80,640]{3,2,1,0:T(8,128)(2,1)S(1)}, bf16[2,2,80,640]{3,2,1,0:T(8,128)(2,1)S(1)}, u32[]{:S(2)}, u32[]{:S(2)}) collective-permute-start(bf16[2,2,80,640]{3,2,1,0:T(8,128)(2,1)S(1)} %fusion.15), channel_id=1, source_target_pairs={{0,2},{1,5},{2,0},{3,7},{4,6},{5,1},{6,4},{7,3},{8,10},{9,13},{10,... | collective-permute-start | bytes 1228808 | tf_op jit(solution)/shard_map/ppermute | solution.py:549
  214.2 17.6 %collective-permute-start.34 = (bf16[2,2,2,80,640]{4,3,2,1,0:T(8,128)(2,1)S(1)}, bf16[2,2,2,80,640]{4,3,2,1,0:T(8,128)(2,1)S(1)}, u32[]{:S(2)}, u32[]{:S(2)}) collective-permute-start(bf16[2,2,2,80,640]{4,3,2,1,0:T(8,128)(2,1)S(1)} %fusion.4), channel_id=1, source_target_pairs={{0,4},{1,3},{2,6},{3,1},{4,0},{5,7},{6,2},{7,5},{8,12},{9,11},{10,... | collective-permute-start | bytes 2457608 | tf_op jit(solution)/shard_map/ppermute | solution.py:549
  215.8 16.0 %collective-permute-start.35 = (bf16[2,80,640]{2,1,0:T(8,128)(2,1)S(1)}, bf16[2,80,640]{2,1,0:T(8,128)(2,1)S(1)}, u32[]{:S(2)}, u32[]{:S(2)}) collective-permute-start(bf16[2,80,640]{2,1,0:T(8,128)(2,1)S(1)} %fusion.24), channel_id=1, source_target_pairs={{0,8},{1,17},{2,10},{3,19},{4,12},{5,21},{6,14},{7,23},{8,0},{9,25... | collective-permute-start | bytes 614408 | tf_op jit(solution)/shard_map/ppermute | solution.py:549
  217.9 13.9 %collective-permute-start.36 = (bf16[80,640]{1,0:T(8,128)(2,1)S(1)}, bf16[80,640]{1,0:T(8,128)(2,1)S(1)}, u32[]{:S(2)}, u32[]{:S(2)}) collective-permute-start(bf16[80,640]{1,0:T(8,128)(2,1)S(1)} %fusion.35), channel_id=1, source_target_pairs={{0,16},{1,9},{2,18},{3,11},{4,20},{5,13},{6,22},{7,15},{8,24},{9,1... | collective-permute-start | bytes 307208 | tf_op jit(solution)/shard_map/ppermute | solution.py:549
  240.9 21.2 %collective-permute-start.40 = (bf16[2,2,2,160,640]{4,3,2,1,0:T(8,128)(2,1)S(1)}, bf16[2,2,2,160,640]{4,3,2,1,0:T(8,128)(2,1)S(1)}, u32[]{:S(2)}, u32[]{:S(2)}) collective-permute-start(bf16[2,2,2,160,640]{4,3,2,1,0:T(8,128)(2,1)S(1)} %fusion), channel_id=1, source_target_pairs={{0,4},{1,3},{2,6},{3,1},{4,0},{5,7},{6,2},{7,5},{8,12},{9,11},{10,... | collective-permute-start | bytes 4915208 | tf_op jit(solution)/shard_map/ppermute | solution.py:549
  242.0 18.1 %collective-permute-start.41 = (bf16[2,80,640]{2,1,0:T(8,128)(2,1)S(1)}, bf16[2,80,640]{2,1,0:T(8,128)(2,1)S(1)}, u32[]{:S(2)}, u32[]{:S(2)}) collective-permute-start(bf16[2,80,640]{2,1,0:T(8,128)(2,1)S(1)} %fusion.25), channel_id=1, source_target_pairs={{0,8},{1,17},{2,10},{3,19},{4,12},{5,21},{6,14},{7,23},{8,0},{9,25... | collective-permute-start | bytes 614408 | tf_op jit(solution)/shard_map/ppermute | solution.py:549
  262.9 15.6 %collective-permute-start.42 = (bf16[2,2,160,640]{3,2,1,0:T(8,128)(2,1)S(1)}, bf16[2,2,160,640]{3,2,1,0:T(8,128)(2,1)S(1)}, u32[]{:S(2)}, u32[]{:S(2)}) collective-permute-start(bf16[2,2,160,640]{3,2,1,0:T(8,128)(2,1)S(1)} %fusion.3), channel_id=1, source_target_pairs={{0,2},{1,5},{2,0},{3,7},{4,6},{5,1},{6,4},{7,3},{8,10},{9,13},{10,... | collective-permute-start | bytes 2457608 | tf_op jit(solution)/shard_map/ppermute | solution.py:549
  263.8 14.6 %collective-permute-start.43 = (bf16[80,640]{1,0:T(8,128)(2,1)S(1)}, bf16[80,640]{1,0:T(8,128)(2,1)S(1)}, u32[]{:S(2)}, u32[]{:S(2)}) collective-permute-start(bf16[80,640]{1,0:T(8,128)(2,1)S(1)} %fusion.37), channel_id=1, source_target_pairs={{0,16},{1,9},{2,18},{3,11},{4,20},{5,13},{6,22},{7,15},{8,24},{9,1... | collective-permute-start | bytes 307208 | tf_op jit(solution)/shard_map/ppermute | solution.py:549
  281.1 12.1 %collective-permute-start.46 = (bf16[2,160,640]{2,1,0:T(8,128)(2,1)}, bf16[2,160,640]{2,1,0:T(8,128)(2,1)}, u32[]{:S(2)}, u32[]{:S(2)}) collective-permute-start(bf16[2,160,640]{2,1,0:T(8,128)(2,1)} %fusion.16), channel_id=1, source_target_pairs={{0,8},{1,17},{2,10},{3,19},{4,12},{5,21},{6,14},{7,23},{8,0},{9,25... | collective-permute-start | bytes 1228808 | tf_op jit(solution)/shard_map/ppermute | solution.py:549
  288.3 12.4 %collective-permute-start.45 = (bf16[2,2,2,80,640]{4,3,2,1,0:T(8,128)(2,1)S(1)}, bf16[2,2,2,80,640]{4,3,2,1,0:T(8,128)(2,1)S(1)}, u32[]{:S(2)}, u32[]{:S(2)}) collective-permute-start(bf16[2,2,2,80,640]{4,3,2,1,0:T(8,128)(2,1)S(1)} %fusion.1), channel_id=1, source_target_pairs={{0,4},{1,3},{2,6},{3,1},{4,0},{5,7},{6,2},{7,5},{8,12},{9,11},{10,... | collective-permute-start | bytes 2457608 | tf_op jit(solution)/shard_map/ppermute | solution.py:549
  (80 other events, 544.4 us)

commit v7 on v6

--- a/solution.py
+++ b/solution.py
@@ -861,20 +861,20 @@
     second, fourth, core, back[0] = stage(a1.second(got_a1), u1.fourth(got_u1), core, back[0])
 
     got_a1, got_u1, core, rest = stage(step(2, second), step(0, fourth), mate(core), blocks(3, 0))
-    first, third, back[0] = stage(du0.first(core, rest), a1.third(got_a1), back[0])
+    first, third, back[0], hidden = stage(du0.first(core, rest), a1.third(got_a1), back[0], hidden)
 
     got_du0, got_a1 = step(3, first), step(1, third)
     (back[0]["early"],) = attn_bwd(coords, back[0]["gmb"], kept[0], table, whole["attn", 0], EARLY)
     back[0]["late"], back[0]["flip"] = attn_bwd(coords, back[0]["gmb"], kept[0], table, whole["attn", 0], LATE)
-    got_du0, got_a1, back[0] = stage(got_du0, got_a1, back[0])
-    second, fourth, back[0], hidden = stage(du0.second(got_du0), a1.fourth(got_a1), back[0], hidden)
+    output = ffn_out(coords, kept[1], hidden, vectors[1], whole["down", 1])
+    got_du0, got_a1, back[0], output = stage(got_du0, got_a1, back[0], output)
+    second, fourth, back[0] = stage(du0.second(got_du0), a1.fourth(got_a1), back[0])
 
     got_du0, got_a1 = step(2, second), step(0, fourth)
     core = blocks(4, 1)
     grad, more = attn_after(back[0], kept[0], vectors[0], whole["attn", 0], True)
     sums[0] = back[0]["sums"] + more
-    output = ffn_out(coords, kept[1], hidden, vectors[1], whole["down", 1])
-    got_du0, got_a1, core, grad, sums, back[0], output = stage(got_du0, got_a1, core, grad, sums, back[0], output)
+    got_du0, got_a1, core, grad, sums, back[0] = stage(got_du0, got_a1, core, grad, sums, back[0])
     third, core, back[0] = stage(du0.third(got_du0), core, back[0])
 
     got_du0 = step(1, third)

time: 347 us -> 345 us (level)
  no operation moved by 1% of the time
where the time goes in v7:
time: 345 us; the launch traced here: 339 us
  Pallas kernels  134 us (39%)
  waiting for transfers between devices  96 us (28%)
  starting transfers between devices  62 us (18%)
  local copies, waits for them, and re-layouts  22.2 us (6%)
  other arithmetic  21.7 us (6%)
    pallas_call x24, Pallas kernels, call(): pl.pallas_call(kernel, out_shape=[jax.ShapeDtypeStruct(s, t) for s, t in...  134 us
    ppermute x39, waiting for transfers between devices, step(): return lax.ppermute(value, AXES, pairs)  70.9 us
    ppermute x39, starting transfers between devices, step(): return lax.ppermute(value, AXES, pairs)  55.2 us
    ppermute x14, waiting for transfers between devices, mate(): return lax.ppermute(value, 'narrow', [(0, 1), (1, 0)])  14.3 us
    unnamed x104, local copies, waits for them, and re-layouts  10.9 us
    ppermute x9, waiting for transfers between devices, regroup(): lax.ppermute(mine[k], AXES, [(i, i ^ k) for i in range(32)])  10.8 us
  transfers between devices with their start and end apart: 62, of which 31 were waited for; matrix products, arithmetic and copies ran while one was open for 6% of the time, Pallas kernels for 36%

profile of v7, /device:TPU:0, one launch (start us, length us, event | category | flops | bytes accessed | tf_op | source)
XLA Modules:
  0.0 339.0 jit_solution(1669841914125381046)
XLA Ops:
  3.8 4.1 %collective-permute-start = (bf16[96,640]{1,0:T(8,128)(2,1)S(1)}, bf16[96,640]{1,0:T(8,128)(2,1)S(1)}, u32[]{:S(2)}, u32[]{:S(2)}) collective-permute-start(bf16[96,640]{1,0:T(8,128)(2,1)S(1)} %fusion.34), channel_id=1, source_target_pairs={{0,16},{1,9},{2,18},{3,11},{4,20},{5,13},{6,22},{7,15},{8,24},{9,1... | collective-permute-start | bytes 368648 | tf_op jit(solution)/shard_map/ppermute | solution.py:549
  26.8 7.6 %collective-permute-done.6 = bf16[240,640]{1,0:T(8,128)(2,1)S(1)} collective-permute-done((bf16[240,640]{1,0:T(8,128)(2,1)S(1)}, bf16[240,640]{1,0:T(8,128)(2,1)S(1)}, u32[]{:S(2)}, u32[]{:S(2)}) %collective-permute-start.6) | collective-permute-done | bytes 307232 | tf_op jit(solution)/shard_map/ppermute | solution.py:549
  42.9 4.9 %collective-permute-done.9 = bf16[2,80,640]{2,1,0:T(8,128)(2,1)S(1)} collective-permute-done((bf16[2,80,640]{2,1,0:T(8,128)(2,1)}, bf16[2,80,640]{2,1,0:T(8,128)(2,1)S(1)}, u32[]{:S(2)}, u32[]{:S(2)}) %collective-permute-start.9) | collective-permute-done | bytes 204832 | tf_op jit(solution)/shard_map/ppermute | solution.py:549
  55.0 5.2 %collective-permute-done.15 = bf16[2,160,640]{2,1,0:T(8,128)(2,1)S(1)} collective-permute-done((bf16[2,160,640]{2,1,0:T(8,128)(2,1)S(1)}, bf16[2,160,640]{2,1,0:T(8,128)(2,1)S(1)}, u32[]{:S(2)}, u32[]{:S(2)}) %collective-permute-start.15) | collective-permute-done | bytes 409632 | tf_op jit(solution)/shard_map/ppermute | solution.py:549
  69.9 12.9 %collective-permute-done.16 = bf16[4,160,640]{2,1,0:T(8,128)(2,1)} collective-permute-done((bf16[4,160,640]{2,1,0:T(8,128)(2,1)}, bf16[4,160,640]{2,1,0:T(8,128)(2,1)}, u32[]{:S(2)}, u32[]{:S(2)}) %collective-permute-start.16) | collective-permute-done | bytes 819232 | tf_op jit(solution)/shard_map/ppermute | solution.py:549
  89.8 14.2 %attn_fwd.2 = (bf16[640,512]{1,0:T(8,128)(2,1)S(1)}, bf16[640,512]{1,0:T(8,128)(2,1)S(1)}, bf16[512,1280]{1,0:T(8,128)(2,1)S(1)}, bf16[640,512]{1,0:T(8,128)(2,1...) custom-call(s32[5]{0:T(128)S(1)} %stack.175.coords, ...), custom_call_target="tpu_custom_call" | custom-call | flops 2348810240 | bytes 13983764 | tf_op jit(solution)/shard_map/attn_fwd/pallas_call | solution.py:442
  104.0 5.4 %collective-permute-done.19.refs_3_.refs_2_ = bf16[2,4,160,640]{3,2,1,0:T(8,128)(2,1)S(1)} collective-permute-done((bf16[2,4,160,640]{3,2,1,0:T(8,128)(2,1)S(1)}, bf16[2,4,160,640]{3,2,1,0:T(8,128)(2,1)S(1)}, u32[]{:S(2)}, u32[]{:S(2)}) %collective-permute-start.19) | collective-permute-done | bytes 1638432 | tf_op jit(solution)/shard_map/ppermute | solution.py:549
  109.4 3.5 %collective-permute-done.21.refs_4_.refs_3_ = bf16[2,4,160,640]{3,2,1,0:T(8,128)(2,1)S(1)} collective-permute-done((bf16[2,4,160,640]{3,2,1,0:T(8,128)(2,1)S(1)}, bf16[2,4,160,640]{3,2,1,0:T(8,128)(2,1)S(1)}, u32[]{:S(2)}, u32[]{:S(2)}) %collective-permute-start.21) | collective-permute-done | bytes 1638432 | tf_op jit(solution)/shard_map/ppermute | solution.py:543
  114.3 10.9 %ffn_fwd.2 = (f32[512,640]{1,0:T(8,128)S(1)}, bf16[2560,512]{1,0:T(8,128)(2,1)S(1)}, bf16[512,2560]{1,0:T(8,128)(2,1)S(1)}, bf16[4,2,80,2560]{3,2,1,0:T(8,128)(2,1)S(1)}) custom-call(s32[5]{0:T(128)S(1)} %stack.175.coords, f32[512,640]{1,0:T(8,128)S(1)} %get-tuple-element.351.m_ref, bf16[512,640]{1,0:T(8,128)(2,1)S(1)} %get-tuple-element.352.b_ref, ...), custom_call_target="tpu_custom_call" | custom-call | flops 3355443200 | bytes 21667860 | tf_op jit(solution)/shard_map/ffn_fwd/pallas_call | solution.py:442
  128.5 14.0 %attn_fwd.3 = (bf16[640,512]{1,0:T(8,128)(2,1)S(1)}, bf16[640,512]{1,0:T(8,128)(2,1)S(1)}, bf16[512,1280]{1,0:T(8,128)(2,1)S(1)}, bf16[640,512]{1,0:T(8,128)(2,1...) custom-call(s32[5]{0:T(128)S(1)} %stack.175.coords, ...), custom_call_target="tpu_custom_call" | custom-call | flops 2348810240 | bytes 17915924 | tf_op jit(solution)/shard_map/attn_fwd/pallas_call | solution.py:442
  143.3 4.8 %collective-permute-done.23.refs_2_ = bf16[2,4,160,640]{3,2,1,0:T(8,128)(2,1)S(1)} collective-permute-done((bf16[2,4,160,640]{3,2,1,0:T(8,128)(2,1)S(1)}, bf16[2,4,160,640]{3,2,1,0:T(8,128)(2,1)S(1)}, u32[]{:S(2)}, u32[]{:S(2)}) %collective-permute-start.23) | collective-permute-done | bytes 1638432 | tf_op jit(solution)/shard_map/ppermute | solution.py:549
  151.6 9.4 %ffn_fwd.3 = (bf16[512,2560]{1,0:T(8,128)(2,1)S(1)}, bf16[2560,512]{1,0:T(8,128)(2,1)S(1)}, bf16[512,2560]{1,0:T(8,128)(2,1)S(1)}, bf16[4,2,80,2560]{3,2,1,0:T(8...) custom-call(s32[5]{0:T(128)S(1)} %stack.175.coords, f32[512,640]{1,0:T(8,128)S(1)} %get-tuple-element.369.m_ref, ...), custom_call_target="tpu_custom_call" | custom-call | flops 3355443200 | bytes 22978580 | tf_op jit(solution)/shard_map/ffn_fwd/pallas_call | solution.py:442
  168.1 7.8 %ffn_bwd.2 = (bf16[512,640]{1,0:T(8,128)(2,1)}, bf16[512,2560]{1,0:T(8,128)(2,1)S(1)}, f32[512,640]{1,0:T(8,128)S(1)}, bf16[512,640]{1,0:T(8,128)(2,1)S(1)}, f32[16,640]{1,0:T(8,128)S(1)}) custom-call(s32[5]{0:T(128)S(1)} %stack.175.coords, bf16[512,640]{1,0:T(8,128)(2,1)S(1)} %copy-done.4, bf16[512,2560]{1,0:T(8,128)(2,1)S(1)} %copy-done.15, ...), custom_call_target="tpu_custom_call" | custom-call | flops 3355443200 | bytes 16465940 | tf_op jit(solution)/shard_map/ffn_bwd/pallas_call | solution.py:442
  185.0 9.4 %attn_bwd.4.refs_2_.early_ref = bf16[3,384,512]{2,1,0:T(8,128)(2,1)S(1)} custom-call(s32[5]{0:T(128)S(1)} %stack.175.coords, bf16[512,640]{1,0:T(8,128)(2,1)S(1)} %get-tuple-element.427.gmb_ref, bf16[640,512]{1,0:T(8,128)(2,1)S(1)} %copy-done.19, bf16[512,1280]{1,0:T(8,128)(2,1)S(1)} %copy-done.17, bf16[640,512]{1,0:T(8,128)(2,1)S(1)} %get-tuple-element.410.ot_ref.refs_1_, ...), custom_call_target="tpu_custom_call" | custom-call | flops 1258291200 | bytes 7847956 | tf_op jit(solution)/shard_map/attn_bwd/pallas_call | solution.py:442
  200.7 6.6 %attn_bwd.5 = (bf16[3,256,512]{2,1,0:T(8,128)(2,1)S(1)}, bf16[640,512]{1,0:T(8,128)(2,1)S(1)}) custom-call(s32[5]{0:T(128)S(1)} %stack.175.coords, bf16[512,640]{1,0:T(8,128)(2,1)S(1)} %get-tuple-element.427.gmb_ref, bf16[640,512]{1,0:T(8,128)(2,1)S(1)} %copy-done.19, bf16[512,1280]{1,0:T(8,128)(2,1)S(1)} %copy-done.17, ...), custom_call_target="tpu_custom_call" | custom-call | flops 838860800 | bytes 8110100 | tf_op jit(solution)/shard_map/attn_bwd/pallas_call | solution.py:442
  218.0 3.7 %attn_after.2 = (f32[512,640]{1,0:T(8,128)S(1)}, f32[16,640]{1,0:T(8,128)S(1)}) custom-call(bf16[3,384,512]{2,1,0:T(8,128)(2,1)S(1)} %attn_bwd.4.refs_2_.early_ref, bf16[3,256,512]{2,1,0:T(8,128)(2,1)S(1)} %get-tuple-element.457.refs_3_.late_ref, f32[512,640]{1,0:T(8,128)S(1)} %get-tuple-element.458.gm_ref, f32[512,640]{1,0:T(8,128)S(1)} %get-tuple-element.459.x_ref, ...), custom_call_target="tpu_custom_call" | custom-call | flops 1258291200 | bytes 9256960 | tf_op jit(solution)/shard_map/attn_after/pallas_call | solution.py:442
  221.7 6.7 %ffn_bwd.3 = (bf16[512,640]{1,0:T(8,128)(2,1)S(1)}, bf16[512,2560]{1,0:T(8,128)(2,1)S(1)}, f32[512,640]{1,0:T(8,128)S(1)}, bf16[512,640]{1,0:T(8,128)(2,1)S(1)}, f32[16,640]{1,0:T(8,128)S(1)}) custom-call(s32[5]{0:T(128)S(1)} %stack.175.coords, f32[512,640]{1,0:T(8,128)S(1)} %get-tuple-element.460.g_ref, bf16[512,2560]{1,0:T(8,128)(2,1)S(1)} %copy-done.13, ...), custom_call_target="tpu_custom_call" | custom-call | flops 3355443200 | bytes 17121300 | tf_op jit(solution)/shard_map/ffn_bwd/pallas_call | solution.py:442
  235.9 3.5 %grads.17 = (bf16[2,2,2,160,640]{4,3,2,1,0:T(8,128)(2,1)S(1)}, bf16[2,2,160,640]{3,2,1,0:T(8,128)(2,1)S(1)}, bf16[2,2,160,640]{3,2,1,0:T(8,128)(2,1)S(1)}) custom-call(s32[5]{0:T(128)S(1)} %stack.175.coords, bf16[2560,512]{1,0:T(8,128)(2,1)S(1)} %get-tuple-element.455.refs_0_, bf16[512,640]{1,0:T(8,128)(2,1)S(1)} %get-tuple-element.480.refs_1_, ...), custom_call_target="tpu_custom_call" | custom-call | flops 1677721600 | bytes 9830420 | tf_op jit(solution)/shard_map/grads/pallas_call | solution.py:442
  244.1 9.5 %attn_bwd.6.refs_2_.early_ref = bf16[3,384,512]{2,1,0:T(8,128)(2,1)S(1)} custom-call(s32[5]{0:T(128)S(1)} %stack.175.coords, bf16[512,640]{1,0:T(8,128)(2,1)S(1)} %get-tuple-element.495.gmb_ref, bf16[640,512]{1,0:T(8,128)(2,1)S(1)} %copy-done.23, bf16[512,1280]{1,0:T(8,128)(2,1)S(1)} %copy-done.21, bf16[640,512]{1,0:T(8,128)(2,1)S(1)} %get-tuple-element.498.ot_ref.refs_1_, ...), custom_call_target="tpu_custom_call" | custom-call | flops 1258291200 | bytes 7847956 | tf_op jit(solution)/shard_map/attn_bwd/pallas_call | solution.py:442
  253.5 6.6 %attn_bwd.7 = (bf16[3,256,512]{2,1,0:T(8,128)(2,1)S(1)}, bf16[640,512]{1,0:T(8,128)(2,1)S(1)}) custom-call(s32[5]{0:T(128)S(1)} %stack.175.coords, bf16[512,640]{1,0:T(8,128)(2,1)S(1)} %get-tuple-element.495.gmb_ref, bf16[640,512]{1,0:T(8,128)(2,1)S(1)} %copy-done.23, bf16[512,1280]{1,0:T(8,128)(2,1)S(1)} %copy-done.21, ...), custom_call_target="tpu_custom_call" | custom-call | flops 838860800 | bytes 8110100 | tf_op jit(solution)/shard_map/attn_bwd/pallas_call | solution.py:442
  260.1 3.6 %ffn_out.1 = bf16[512,640]{1,0:T(8,128)(2,1)} custom-call(s32[5]{0:T(128)S(1)} %stack.175.coords, f32[512,640]{1,0:T(8,128)S(1)} %get-tuple-element.369.m_ref, bf16[512,2560]{1,0:T(8,128)(2,1)S(1)} %get-tuple-element.505.z_ref, f32[16,640]{1,0:T(8,128)S(1)} %get-tuple-element.670.vec_ref, bf16[2560,640]{1,0:T(8,128)(2,1)S(1)} %bitcast.342), custom_call_target="tpu_custom_call" | custom-call | flops 1677721600 | bytes 7905300 | tf_op jit(solution)/shard_map/ffn_out/pallas_call | solution.py:442
  266.5 4.6 %attn_after.3 = (bf16[512,640]{1,0:T(8,128)(2,1)}, f32[16,640]{1,0:T(8,128)S(1)}) custom-call(bf16[3,384,512]{2,1,0:T(8,128)(2,1)S(1)} %attn_bwd.6.refs_2_.early_ref, bf16[3,256,512]{2,1,0:T(8,128)(2,1)S(1)} %get-tuple-element.536.refs_3_.late_ref, f32[512,640]{1,0:T(8,128)S(1)} %get-tuple-element.522.gm_ref, bf16[512,640]{1,0:T(8,128)(2,1)S(1)} %copy-done.5, ...), custom_call_target="tpu_custom_call" | custom-call | flops 1258291200 | bytes 7946240 | tf_op jit(solution)/shard_map/attn_after/pallas_call | solution.py:442
  271.1 3.7 %grads.18 = bf16[2,2,2,2,80,640]{5,4,3,2,1,0:T(8,128)(2,1)} custom-call(s32[5]{0:T(128)S(1)} %stack.175.coords, bf16[640,512]{1,0:T(8,128)(2,1)S(1)} %get-tuple-element.518.refs_0_, bf16[640,512]{1,0:T(8,128)(2,1)S(1)} %get-tuple-element.498.ot_ref.refs_1_, bf16[3,384,512]{2,1,0:T(8,128)(2,1)S(1)} %attn_bwd.6.refs_2_.early_ref, ...), custom_call_target="tpu_custom_call" | custom-call | flops 838860800 | bytes 5570580 | tf_op jit(solution)/shard_map/grads/pallas_call | solution.py:442
  291.4 7.9 %collective-permute-done.45 = bf16[2,2,2,80,640]{4,3,2,1,0:T(8,128)(2,1)S(1)} collective-permute-done((bf16[2,2,2,80,640]{4,3,2,1,0:T(8,128)(2,1)S(1)}, bf16[2,2,2,80,640]{4,3,2,1,0:T(8,128)(2,1)S(1)}, u32[]{:S(2)}, u32[]{:S(2)}) %collective-permute-start.45) | collective-permute-done | bytes 819232 | tf_op jit(solution)/shard_map/ppermute | solution.py:549
  (373 shorter events, 165.4 us)
Async XLA Ops:
  34.8 14.2 %collective-permute-start.7 = (bf16[2,4,96,640]{3,2,1,0:T(8,128)(2,1)S(1)}, bf16[2,4,96,640]{3,2,1,0:T(8,128)(2,1)S(1)}, u32[]{:S(2)}, u32[]{:S(2)}) collective-permute-start(bf16[2,4,96,640]{3,2,1,0:T(8,128)(2,1)S(1)} %pad_maximum_fusion.2.refs_0_), channel_id=1, source_target_pairs={{0,4},{1,3},{2,6},{3,1},{4,0},{5,7},{6,2},{7,5},{8,12},{9,11},{10,... | collective-permute-start | bytes 2949128 | tf_op jit(solution)/shard_map/ppermute | solution.py:549
  36.3 12.6 %collective-permute-start.8 = (bf16[2,4,96,640]{3,2,1,0:T(8,128)(2,1)S(1)}, bf16[2,4,96,640]{3,2,1,0:T(8,128)(2,1)S(1)}, u32[]{:S(2)}, u32[]{:S(2)}) collective-permute-start(bf16[2,4,96,640]{3,2,1,0:T(8,128)(2,1)S(1)} %pad_maximum_fusion.2.refs_0_), channel_id=1, source_target_pairs={{0,1},{1,0},{2,3},{3,2},{4,5},{5,4},{6,7},{7,6},{8,9},{9,8},{10,11... | collective-permute-start | bytes 2949128 | tf_op jit(solution)/shard_map/ppermute | solution.py:543
  40.9 11.6 %collective-permute-start.12 = (bf16[160,640]{1,0:T(8,128)(2,1)S(1)}, bf16[160,640]{1,0:T(8,128)(2,1)S(1)}, u32[]{:S(2)}, u32[]{:S(2)}) collective-permute-start(bf16[160,640]{1,0:T(8,128)(2,1)S(1)} %pad_maximum_fusion.19), channel_id=1, source_target_pairs={{0,16},{1,9},{2,18},{3,11},{4,20},{5,13},{6,22},{7,15},{8,24},{9,1... | collective-permute-start | bytes 614408 | tf_op jit(solution)/shard_map/ppermute | solution.py:549
  49.0 11.2 %collective-permute-start.15 = (bf16[2,160,640]{2,1,0:T(8,128)(2,1)S(1)}, bf16[2,160,640]{2,1,0:T(8,128)(2,1)S(1)}, u32[]{:S(2)}, u32[]{:S(2)}) collective-permute-start(bf16[2,160,640]{2,1,0:T(8,128)(2,1)S(1)} %slice.466), channel_id=1, source_target_pairs={{0,8},{1,17},{2,10},{3,19},{4,12},{5,21},{6,14},{7,23},{8,0},{9,25... | collective-permute-start | bytes 1228808 | tf_op jit(solution)/shard_map/ppermute | solution.py:549
  61.5 21.4 %collective-permute-start.16 = (bf16[4,160,640]{2,1,0:T(8,128)(2,1)}, bf16[4,160,640]{2,1,0:T(8,128)(2,1)}, u32[]{:S(2)}, u32[]{:S(2)}) collective-permute-start(bf16[4,160,640]{2,1,0:T(8,128)(2,1)} %pad_maximum_fusion.4), channel_id=1, source_target_pairs={{0,2},{1,5},{2,0},{3,7},{4,6},{5,1},{6,4},{7,3},{8,10},{9,13},{10,... | collective-permute-start | bytes 2457608 | tf_op jit(solution)/shard_map/ppermute | solution.py:549
  64.6 21.1 %collective-permute-start.13 = (bf16[2,4,80,640]{3,2,1,0:T(8,128)(2,1)}, bf16[2,4,80,640]{3,2,1,0:T(8,128)(2,1)}, u32[]{:S(2)}, u32[]{:S(2)}) collective-permute-start(bf16[2,4,80,640]{3,2,1,0:T(8,128)(2,1)} %pad_maximum_fusion.3.refs_0_), channel_id=1, source_target_pairs={{0,4},{1,3},{2,6},{3,1},{4,0},{5,7},{6,2},{7,5},{8,12},{9,11},{10,... | collective-permute-start | bytes 2457608 | tf_op jit(solution)/shard_map/ppermute | solution.py:549
  66.1 19.6 %collective-permute-start.14 = (bf16[2,4,80,640]{3,2,1,0:T(8,128)(2,1)}, bf16[2,4,80,640]{3,2,1,0:T(8,128)(2,1)}, u32[]{:S(2)}, u32[]{:S(2)}) collective-permute-start(bf16[2,4,80,640]{3,2,1,0:T(8,128)(2,1)} %pad_maximum_fusion.3.refs_0_), channel_id=1, source_target_pairs={{0,1},{1,0},{2,3},{3,2},{4,5},{5,4},{6,7},{7,6},{8,9},{9,8},{10,11... | collective-permute-start | bytes 2457608 | tf_op jit(solution)/shard_map/ppermute | solution.py:543
  69.8 14.8 %collective-permute-start.17 = (bf16[2,160,640]{2,1,0:T(8,128)(2,1)}, bf16[2,160,640]{2,1,0:T(8,128)(2,1)S(1)}, u32[]{:S(2)}, u32[]{:S(2)}) collective-permute-start(bf16[2,160,640]{2,1,0:T(8,128)(2,1)} %pad_maximum_fusion.13), channel_id=1, source_target_pairs={{0,8},{1,17},{2,10},{3,19},{4,12},{5,21},{6,14},{7,23},{8,0},{9,25... | collective-permute-start | bytes 1228808 | tf_op jit(solution)/shard_map/ppermute | solution.py:549
  88.2 21.1 %collective-permute-start.19 = (bf16[2,4,160,640]{3,2,1,0:T(8,128)(2,1)S(1)}, bf16[2,4,160,640]{3,2,1,0:T(8,128)(2,1)S(1)}, u32[]{:S(2)}, u32[]{:S(2)}) collective-permute-start(bf16[2,4,160,640]{3,2,1,0:T(8,128)(2,1)S(1)} %pad_maximum_fusion.refs_1_.refs_0_), channel_id=1, source_target_pairs={{0,4},{1,3},{2,6},{3,1},{4,0},{5,7},{6,2},{7,5},{8,12},{9,11},{10,... | collective-permute-start | bytes 4915208 | tf_op jit(solution)/shard_map/ppermute | solution.py:549
  89.8 19.6 %collective-permute-start.20 = (bf16[2,4,160,640]{3,2,1,0:T(8,128)(2,1)S(1)}, bf16[2,4,160,640]{3,2,1,0:T(8,128)(2,1)S(1)}, u32[]{:S(2)}, u32[]{:S(2)}) collective-permute-start(bf16[2,4,160,640]{3,2,1,0:T(8,128)(2,1)S(1)} %pad_maximum_fusion.refs_1_.refs_0_), channel_id=1, source_target_pairs={{0,1},{1,0},{2,3},{3,2},{4,5},{5,4},{6,7},{7,6},{8,9},{9,8},{10,11... | collective-permute-start | bytes 4915208 | tf_op jit(solution)/shard_map/ppermute | solution.py:543
  112.9 12.4 %collective-permute-start.22 = (bf16[4,160,640]{2,1,0:T(8,128)(2,1)S(1)}, bf16[4,160,640]{2,1,0:T(8,128)(2,1)S(1)}, u32[]{:S(2)}, u32[]{:S(2)}) collective-permute-start(bf16[4,160,640]{2,1,0:T(8,128)(2,1)S(1)} %pad_maximum_fusion.5), channel_id=1, source_target_pairs={{0,2},{1,5},{2,0},{3,7},{4,6},{5,1},{6,4},{7,3},{8,10},{9,13},{10,... | collective-permute-start | bytes 2457608 | tf_op jit(solution)/shard_map/ppermute | solution.py:549
  126.9 21.2 %collective-permute-start.23 = (bf16[2,4,160,640]{3,2,1,0:T(8,128)(2,1)S(1)}, bf16[2,4,160,640]{3,2,1,0:T(8,128)(2,1)S(1)}, u32[]{:S(2)}, u32[]{:S(2)}) collective-permute-start(bf16[2,4,160,640]{3,2,1,0:T(8,128)(2,1)S(1)} %pad_maximum_fusion.1.refs_0_), channel_id=1, source_target_pairs={{0,4},{1,3},{2,6},{3,1},{4,0},{5,7},{6,2},{7,5},{8,12},{9,11},{10,... | collective-permute-start | bytes 4915208 | tf_op jit(solution)/shard_map/ppermute | solution.py:549
  128.5 19.6 %collective-permute-start.24 = (bf16[2,4,160,640]{3,2,1,0:T(8,128)(2,1)S(1)}, bf16[2,4,160,640]{3,2,1,0:T(8,128)(2,1)S(1)}, u32[]{:S(2)}, u32[]{:S(2)}) collective-permute-start(bf16[2,4,160,640]{3,2,1,0:T(8,128)(2,1)S(1)} %pad_maximum_fusion.1.refs_0_), channel_id=1, source_target_pairs={{0,1},{1,0},{2,3},{3,2},{4,5},{5,4},{6,7},{7,6},{8,9},{9,8},{10,11... | collective-permute-start | bytes 4915208 | tf_op jit(solution)/shard_map/ppermute | solution.py:543
  166.5 12.4 %collective-permute-start.27 = (bf16[2,2,2,80,640]{4,3,2,1,0:T(8,128)(2,1)S(1)}, bf16[2,2,2,80,640]{4,3,2,1,0:T(8,128)(2,1)S(1)}, u32[]{:S(2)}, u32[]{:S(2)}) collective-permute-start(bf16[2,2,2,80,640]{4,3,2,1,0:T(8,128)(2,1)S(1)} %fusion.6), channel_id=1, source_target_pairs={{0,4},{1,3},{2,6},{3,1},{4,0},{5,7},{6,2},{7,5},{8,12},{9,11},{10,... | collective-permute-start | bytes 2457608 | tf_op jit(solution)/shard_map/ppermute | solution.py:549
  182.8 16.3 %collective-permute-start.29 = (bf16[2,2,2,80,640]{4,3,2,1,0:T(8,128)(2,1)S(1)}, bf16[2,2,2,80,640]{4,3,2,1,0:T(8,128)(2,1)S(1)}, u32[]{:S(2)}, u32[]{:S(2)}) collective-permute-start(bf16[2,2,2,80,640]{4,3,2,1,0:T(8,128)(2,1)S(1)} %fusion.5), channel_id=1, source_target_pairs={{0,4},{1,3},{2,6},{3,1},{4,0},{5,7},{6,2},{7,5},{8,12},{9,11},{10,... | collective-permute-start | bytes 2457608 | tf_op jit(solution)/shard_map/ppermute | solution.py:549
  184.4 12.4 %collective-permute-start.30 = (bf16[2,2,80,640]{3,2,1,0:T(8,128)(2,1)S(1)}, bf16[2,2,80,640]{3,2,1,0:T(8,128)(2,1)S(1)}, u32[]{:S(2)}, u32[]{:S(2)}) collective-permute-start(bf16[2,2,80,640]{3,2,1,0:T(8,128)(2,1)S(1)} %fusion.15), channel_id=1, source_target_pairs={{0,2},{1,5},{2,0},{3,7},{4,6},{5,1},{6,4},{7,3},{8,10},{9,13},{10,... | collective-permute-start | bytes 1228808 | tf_op jit(solution)/shard_map/ppermute | solution.py:549
  214.2 17.6 %collective-permute-start.34 = (bf16[2,2,2,80,640]{4,3,2,1,0:T(8,128)(2,1)S(1)}, bf16[2,2,2,80,640]{4,3,2,1,0:T(8,128)(2,1)S(1)}, u32[]{:S(2)}, u32[]{:S(2)}) collective-permute-start(bf16[2,2,2,80,640]{4,3,2,1,0:T(8,128)(2,1)S(1)} %fusion.4), channel_id=1, source_target_pairs={{0,4},{1,3},{2,6},{3,1},{4,0},{5,7},{6,2},{7,5},{8,12},{9,11},{10,... | collective-permute-start | bytes 2457608 | tf_op jit(solution)/shard_map/ppermute | solution.py:549
  215.8 16.0 %collective-permute-start.35 = (bf16[2,80,640]{2,1,0:T(8,128)(2,1)S(1)}, bf16[2,80,640]{2,1,0:T(8,128)(2,1)S(1)}, u32[]{:S(2)}, u32[]{:S(2)}) collective-permute-start(bf16[2,80,640]{2,1,0:T(8,128)(2,1)S(1)} %fusion.24), channel_id=1, source_target_pairs={{0,8},{1,17},{2,10},{3,19},{4,12},{5,21},{6,14},{7,23},{8,0},{9,25... | collective-permute-start | bytes 614408 | tf_op jit(solution)/shard_map/ppermute | solution.py:549
  217.9 13.9 %collective-permute-start.36 = (bf16[80,640]{1,0:T(8,128)(2,1)S(1)}, bf16[80,640]{1,0:T(8,128)(2,1)S(1)}, u32[]{:S(2)}, u32[]{:S(2)}) collective-permute-start(bf16[80,640]{1,0:T(8,128)(2,1)S(1)} %fusion.35), channel_id=1, source_target_pairs={{0,16},{1,9},{2,18},{3,11},{4,20},{5,13},{6,22},{7,15},{8,24},{9,1... | collective-permute-start | bytes 307208 | tf_op jit(solution)/shard_map/ppermute | solution.py:549
  240.9 22.8 %collective-permute-start.40 = (bf16[2,2,2,160,640]{4,3,2,1,0:T(8,128)(2,1)S(1)}, bf16[2,2,2,160,640]{4,3,2,1,0:T(8,128)(2,1)S(1)}, u32[]{:S(2)}, u32[]{:S(2)}) collective-permute-start(bf16[2,2,2,160,640]{4,3,2,1,0:T(8,128)(2,1)S(1)} %fusion), channel_id=1, source_target_pairs={{0,4},{1,3},{2,6},{3,1},{4,0},{5,7},{6,2},{7,5},{8,12},{9,11},{10,... | collective-permute-start | bytes 4915208 | tf_op jit(solution)/shard_map/ppermute | solution.py:549
  242.0 21.7 %collective-permute-start.41 = (bf16[2,80,640]{2,1,0:T(8,128)(2,1)S(1)}, bf16[2,80,640]{2,1,0:T(8,128)(2,1)S(1)}, u32[]{:S(2)}, u32[]{:S(2)}) collective-permute-start(bf16[2,80,640]{2,1,0:T(8,128)(2,1)S(1)} %fusion.25), channel_id=1, source_target_pairs={{0,8},{1,17},{2,10},{3,19},{4,12},{5,21},{6,14},{7,23},{8,0},{9,25... | collective-permute-start | bytes 614408 | tf_op jit(solution)/shard_map/ppermute | solution.py:549
  264.5 12.3 %collective-permute-start.42 = (bf16[2,2,160,640]{3,2,1,0:T(8,128)(2,1)S(1)}, bf16[2,2,160,640]{3,2,1,0:T(8,128)(2,1)S(1)}, u32[]{:S(2)}, u32[]{:S(2)}) collective-permute-start(bf16[2,2,160,640]{3,2,1,0:T(8,128)(2,1)S(1)} %fusion.2), channel_id=1, source_target_pairs={{0,2},{1,5},{2,0},{3,7},{4,6},{5,1},{6,4},{7,3},{8,10},{9,13},{10,... | collective-permute-start | bytes 2457608 | tf_op jit(solution)/shard_map/ppermute | solution.py:549
  279.3 12.1 %collective-permute-start.46 = (bf16[2,160,640]{2,1,0:T(8,128)(2,1)}, bf16[2,160,640]{2,1,0:T(8,128)(2,1)}, u32[]{:S(2)}, u32[]{:S(2)}) collective-permute-start(bf16[2,160,640]{2,1,0:T(8,128)(2,1)} %fusion.16), channel_id=1, source_target_pairs={{0,8},{1,17},{2,10},{3,19},{4,12},{5,21},{6,14},{7,23},{8,0},{9,25... | collective-permute-start | bytes 1228808 | tf_op jit(solution)/shard_map/ppermute | solution.py:549
  286.9 12.4 %collective-permute-start.45 = (bf16[2,2,2,80,640]{4,3,2,1,0:T(8,128)(2,1)S(1)}, bf16[2,2,2,80,640]{4,3,2,1,0:T(8,128)(2,1)S(1)}, u32[]{:S(2)}, u32[]{:S(2)}) collective-permute-start(bf16[2,2,2,80,640]{4,3,2,1,0:T(8,128)(2,1)S(1)} %fusion.1), channel_id=1, source_target_pairs={{0,4},{1,3},{2,6},{3,1},{4,0},{5,7},{6,2},{7,5},{8,12},{9,11},{10,... | collective-permute-start | bytes 2457608 | tf_op jit(solution)/shard_map/ppermute | solution.py:549
  (80 other events, 531.3 us)
